TPU v7x, 32 devices: a whole 2x2x4 slice. The times are simulated.
32 devices in a mesh: shot: 2 (over y), gx: 4 (over z), gy: 2 (over x), gz: 2 (over core).
Axes of the slice: x: 2, y: 2, z: 4, core: 2. Of those that a mesh axis runs over, the one named last changes fastest.
Arguments:
- stored: float32 [8, 16, 64, 256], P('shot', 'gx', 'gy', 'gz'), parts along dimension 0, may hold values from -6 to 6
- adjoint_end: float32 [8, 16, 64, 256], P('shot', 'gx', 'gy', 'gz'), parts along dimension 0, may hold values from -6 to 6
- labels: int32 [16, 64, 256], P('gx', 'gy', 'gz'), may hold values from 0 to 7
- tissue: float32 [3, 8], replicated, may hold values from 0 to 2, as said below
- source_cells: int32 [128, 3], P('shot'), parts along dimension 0, may hold values from 0 to 255, as said below
- source_wave: float32 [4, 128], P(None, 'shot'), parts along dimension 1, may hold values from -6 to 6
- receiver_cells: int32 [1024, 3], replicated, may hold values from 0 to 255, as said below
- receiver_wave: float32 [4, 2048], P(None, 'shot'), parts along dimension 1, may hold values from -6 to 6
Outputs:
- gradient: float32 [4, 16, 64, 256], P('shot', 'gx', 'gy', 'gz'), parts along dimension 0
- adjoint_start: float32 [8, 16, 64, 256], P('shot', 'gx', 'gy', 'gz'), parts along dimension 0
There are 2 independent parts, one for each index of `shot`. A program takes and returns all parts, laid end to end along the dimension named above; an argument that names none is the same for every part. Nothing has to cross between parts.
Inputs may be any that keep to these rules, and one draw needn't show every extreme that they name: `tissue`: row 0 is the Courant number, row 1 the relative density, row 2 the absorption per step. `source_cells`: each row is a cell (x, y, z) of the grid; cells may repeat. `receiver_cells`: each row is a cell (x, y, z) of the grid; cells may repeat.
All inputs are finite; a program needn't handle non-finite values.
Results may differ from a plain program's by a relative error of at most 0.00002.
Values sent between devices are 32-bit elements; how exact they have to be, the bound alone decides.
No kernel may reach another device: no remote copies, remote signals or barrier semaphores. Data moves between devices by JAX's collectives and lax.ppermute only.
A program may use at most 64 MiB of HBM per device.

v0:
```python
import jax
import jax.numpy as jnp
from jax import lax
from jax.sharding import PartitionSpec as P

STEPS = 4


def with_halo(block, sides, width):
    for axis, dim in sides:
        count = lax.axis_size(axis)
        forward = [(i, i + 1) for i in range(count - 1)]
        backward = [(target, source) for source, target in forward]
        low = lax.ppermute(
            lax.slice_in_dim(block, block.shape[dim] - width, None, axis=dim), axis, forward
        )
        high = lax.ppermute(lax.slice_in_dim(block, 0, width, axis=dim), axis, backward)
        block = jnp.concatenate([low, block, high], axis=dim)
    return block


def from_partner(block, axis, apart):
    count = lax.axis_size(axis)
    route = []
    for low in range(count):
        high = low | 1 << apart
        if high != low and high < count:
            route += [(low, high), (high, low)]
    return lax.ppermute(block, axis, route)


def shifted(values, along, offset):
    length = values.shape[along]
    pad_width = [(0, 0)] * values.ndim
    if offset > 0:
        pad_width[along] = (0, offset)
        padded = jnp.pad(values, pad_width)
        return lax.slice_in_dim(padded, offset, offset + length, axis=along)
    pad_width[along] = (-offset, 0)
    padded = jnp.pad(values, pad_width)
    return lax.slice_in_dim(padded, 0, length, axis=along)


def grad_up(values):
    return jnp.stack([shifted(values, along, 1) - values for along in range(3)], 0)


def div_down(velocity):
    result = velocity[0] - shifted(velocity[0], 0, -1)
    result = result + (velocity[1] - shifted(velocity[1], 1, -1))
    return result + (velocity[2] - shifted(velocity[2], 2, -1))


def coefficients(labels, tissue):
    sound_speed = jnp.zeros(labels.shape, jnp.float32)
    density = jnp.zeros(labels.shape, jnp.float32)
    absorb = jnp.zeros(labels.shape, jnp.float32)
    for label_id in range(tissue.shape[1]):
        picked = (labels == label_id).astype(jnp.float32)
        sound_speed = sound_speed + picked * tissue[0, label_id]
        density = density + picked * tissue[1, label_id]
        absorb = absorb + picked * tissue[2, label_id]
    return jnp.stack([density * sound_speed, sound_speed / density, 1.0 - absorb], 0)


def inject(grid_shape, cell_list, amounts, anchor):
    relative = cell_list - anchor[None, :]
    inside = jnp.ones(relative.shape[0], bool)
    for along in range(3):
        inside = inside & (relative[:, along] >= 0) & (relative[:, along] < grid_shape[along])
    total_cells = grid_shape[0] * grid_shape[1] * grid_shape[2]
    flat_index = (relative[:, 0] * grid_shape[1] + relative[:, 1]) * grid_shape[2] + relative[:, 2]
    flat_index = jnp.where(inside, flat_index, total_cells)
    result = jnp.zeros((total_cells,), jnp.float32).at[flat_index].add(amounts, mode="drop")
    return result.reshape(grid_shape)


def forward_step(pressure, velocity, tissue_grid, source_add):
    slopes_now = grad_up(pressure)
    velocity = velocity - tissue_grid[1] * slopes_now
    spread = div_down(velocity)
    pressure = tissue_grid[2] * (pressure - tissue_grid[0] * spread) + source_add
    return (pressure, velocity, slopes_now, spread)


def adjoint_step(pressure_adj, velocity_adj, tissue_grid, receiver_add):
    pressure_adj = pressure_adj + receiver_add
    scaled = tissue_grid[0] * tissue_grid[2] * pressure_adj
    velocity_adj = velocity_adj + grad_up(scaled)
    return (pressure_adj, velocity_adj)


def widened(wave_state, margin):
    extended = with_halo(wave_state, (("gx", 1), ("gy", 2), ("gz", 3)), margin)
    return (extended[0], extended[1:])


def interior(values, margin, cells_x, cells_y, cells_z):
    return values[
        ..., margin : margin + cells_x, margin : margin + cells_y, margin : margin + cells_z
    ]


def local(
    stored, adjoint_end, labels, tissue, source_cells, source_wave, receiver_cells, receiver_wave
):
    margin = 1
    cells_x, cells_y, cells_z = (stored.shape[1], stored.shape[2], stored.shape[3])
    top_bit = lax.axis_size("gx").bit_length() - 2
    wave_state = from_partner(stored, "gx", top_bit)
    tissue_grid = coefficients(labels, tissue)
    tissue_grid = with_halo(tissue_grid, (("gx", 1), ("gy", 2), ("gz", 3)), margin)
    anchor = jnp.stack(
        [
            lax.axis_index("gx") * cells_x - margin,
            lax.axis_index("gy") * cells_y - margin,
            lax.axis_index("gz") * cells_z - margin,
        ]
    )
    grid_shape = tissue_grid.shape[1:]
    slope_list = [None] * STEPS
    spread_list = [None] * STEPS
    for opening in range(0, STEPS, margin):
        pressure, velocity = widened(wave_state, margin)
        for counter in range(opening, opening + margin):
            source_add = inject(grid_shape, source_cells, source_wave[counter], anchor)
            pressure, velocity, slopes_now, spread = forward_step(
                pressure, velocity, tissue_grid, source_add
            )
            slope_list[counter] = interior(slopes_now, margin, cells_x, cells_y, cells_z)
            spread_list[counter] = interior(spread, margin, cells_x, cells_y, cells_z)
        wave_state = interior(
            jnp.concatenate([pressure[None], velocity], 0), margin, cells_x, cells_y, cells_z
        )
    damping_inner = interior(tissue_grid[2], margin, cells_x, cells_y, cells_z)
    grad_stiff = jnp.zeros((cells_x, cells_y, cells_z), jnp.float32)
    grad_buoy = jnp.zeros((cells_x, cells_y, cells_z), jnp.float32)
    adjoint_state = adjoint_end
    for opening in range(STEPS - 1, -1, -margin):
        pressure_adj, velocity_adj = widened(adjoint_state, margin)
        for counter in range(opening, opening - margin, -1):
            receiver_add = inject(grid_shape, receiver_cells, receiver_wave[counter], anchor)
            pressure_adj, velocity_adj = adjoint_step(
                pressure_adj, velocity_adj, tissue_grid, receiver_add
            )
            pressure_inner = interior(pressure_adj, margin, cells_x, cells_y, cells_z)
            velocity_inner = interior(velocity_adj, margin, cells_x, cells_y, cells_z)
            grad_stiff = grad_stiff - damping_inner * pressure_inner * spread_list[counter]
            slopes_now = slope_list[counter]
            grad_buoy = grad_buoy - (
                velocity_inner[0] * slopes_now[0]
                + velocity_inner[1] * slopes_now[1]
                + velocity_inner[2] * slopes_now[2]
            )
            pressure_adj = tissue_grid[2] * pressure_adj + div_down(tissue_grid[1] * velocity_adj)
        adjoint_state = interior(
            jnp.concatenate([pressure_adj[None], velocity_adj], 0),
            margin,
            cells_x,
            cells_y,
            cells_z,
        )
    gradient = jnp.stack([grad_stiff, grad_buoy], 0)
    return (gradient, adjoint_state)


def solution(mesh):
    return jax.shard_map(
        local,
        mesh=mesh,
        in_specs=(
            P("shot", "gx", "gy", "gz"),
            P("shot", "gx", "gy", "gz"),
            P("gx", "gy", "gz"),
            P(),
            P("shot", None),
            P(None, "shot"),
            P(),
            P(None, "shot"),
        ),
        out_specs=(P("shot", "gx", "gy", "gz"), P("shot", "gx", "gy", "gz")),
        check_vma=False,
    )
```

profile of v0, /device:TPU:8, one launch (start us, length us, event | category | flops | bytes accessed | tf_op | source)
XLA Modules:
  0.0 270.9 jit_solution(7163594841171655268)
XLA Ops:
  6.1 10.1 %multiply_bitcast_fusion = (f32[1,4,32,128]{3,2,1,0:T(8,128)S(1)}, pred[4,32,128]{2,1,0:T(8,128)(4,1)S(1)}, pred[4,32,128]{2,1,0:T(8,128)(4,1)S(1)}, pred[4,32,1...) fusion(f32[]{:T(128)} %bitcast.7, f32[]{:T(128)} %bitcast.6, ...), kind=kLoop, calls=%fused_computation.258 | loop fusion | flops 638976 | bytes 262208 | tf_op jit(solution)/shard_map/stack | solution.py:63
  16.1 10.0 %divide_bitcast_fusion = f32[1,4,32,128]{3,2,1,0:T(8,128)S(1)} fusion(pred[4,32,128]{2,1,0:T(8,128)(4,1)S(1)} %get-tuple-element.33, f32[]{:T(128)} %bitcast.7, pred[4,32,128]{2,1,0:T(8,128)(4,1)S(1)} %get-tuple-element.32, f32[]{:T(128)} %bitcast.6, pred[4,32,128]{2,1,0:T(8,128)(4,1)S(1)} %get-tuple-element.31, f32[]{:T(128)} %bitcast.5, ...), kind=kLoop, calls=%fused_computation.257 | loop fusion | flops 507904 | bytes 196672 | tf_op jit(solution)/shard_map/stack | solution.py:63
  26.2 5.2 %subtract_bitcast_fusion.16 = f32[1,4,32,128]{3,2,1,0:T(8,128)S(1)} fusion(pred[4,32,128]{2,1,0:T(8,128)(4,1)S(1)} %get-tuple-element.33, pred[4,32,128]{2,1,0:T(8,128)(4,1)S(1)} %get-tuple-element.32, pred[4,32,128]{2,1,0:T(8,128)(4,1)S(1)} %get-tuple-element.31, pred[4,32,128]{2,1,0:T(8,128)(4,1)S(1)} %get-tuple-element.30, ...), kind=kLoop, calls=%fused_computation.256 | loop fusion | flops 262144 | bytes 196640 | tf_op jit(solution)/shard_map/stack | solution.py:63
  33.8 3.5 %collective-permute-start = (f32[3,1,32,128]{3,2,1,0:T(8,128)S(1)}, f32[3,1,32,128]{3,2,1,0:T(8,128)S(1)}, u32[]{:S(2)}, u32[]{:S(2)}) collective-permute-start(f32[3,1,32,128]{3,2,1,0:T(8,128)S(1)} %get-tuple-element.139), channel_id=1, source_target_pairs={{0,4},{4,8},{8,12},{1,5},{5,9},{9,13},{2,6},{6,10},{10,14},{3,7},{... | collective-permute-start | bytes 147464 | tf_op jit(solution)/shard_map/ppermute | solution.py:14
  39.8 3.9 %collective-permute-start.7 = (f32[4,1,32,128]{3,2,1,0:T(8,128)S(1)}, f32[4,1,32,128]{3,2,1,0:T(8,128)S(1)}, u32[]{:S(2)}, u32[]{:S(2)}) collective-permute-start(f32[4,1,32,128]{3,2,1,0:T(8,128)S(1)} %get-tuple-element.110), channel_id=1, source_target_pairs={{4,0},{8,4},{12,8},{5,1},{9,5},{13,9},{6,2},{10,6},{14,10},{7,3},{... | collective-permute-start | bytes 196616 | tf_op jit(solution)/shard_map/ppermute | solution.py:17
  47.4 4.5 %collective-permute-start.2 = (f32[3,6,1,128]{3,2,1,0:T(1,128)S(1)}, f32[3,6,1,128]{3,2,1,0:T(1,128)S(1)}, u32[]{:S(2)}, u32[]{:S(2)}) collective-permute-start(f32[3,6,1,128]{3,2,1,0:T(1,128)S(1)} %get-tuple-element.108), channel_id=1, source_target_pairs={{0,2},{1,3},{4,6},{5,7},{8,10},{9,11},{12,14},{13,15},{16,18},{17,... | collective-permute-start | bytes 27656 | tf_op jit(solution)/shard_map/ppermute | solution.py:14
  55.5 3.8 %collective-permute-start.4 = (f32[3,6,34,1]{3,2,1,0:T(8,128)S(1)}, f32[3,6,34,1]{3,2,1,0:T(8,128)}, u32[]{:S(2)}, u32[]{:S(2)}) collective-permute-start(f32[3,6,34,1]{3,2,1,0:T(8,128)S(1)} %get-tuple-element.106), channel_id=1, source_target_pairs={{0,1},{2,3},{4,5},{6,7},{8,9},{10,11},{12,13},{14,15},{16,17},{18,... | collective-permute-start | bytes 7352 | tf_op jit(solution)/shard_map/ppermute | solution.py:14
  59.3 7.1 %scatter_custom_fusion = f32[26520]{0:T(1024)S(1)} fusion(s32[1024]{0:T(1024)S(1)} %bitcast.218, f32[1024]{0:T(1024)S(1)} %bitcast.225, f32[]{:T(128)} %constant.63.clone.1), kind=kCustom, calls=%fused_computation.273 | custom fusion | flops 1024 | bytes 106084 | tf_op jit(solution)/shard_map/scatter-add | solution.py:74
  66.6 7.1 %scatter_custom_fusion.6 = f32[26520]{0:T(1024)S(1)} fusion(s32[1024]{0:T(1024)S(1)} %bitcast.219, f32[1024]{0:T(1024)S(1)} %bitcast.224, f32[]{:T(128)} %constant.63.clone.1), kind=kCustom, calls=%fused_computation.261 | custom fusion | flops 1024 | bytes 106084 | tf_op jit(solution)/shard_map/scatter-add | solution.py:74
  73.8 7.1 %scatter_custom_fusion.5 = f32[26520]{0:T(1024)S(1)} fusion(s32[1024]{0:T(1024)S(1)} %bitcast.220, f32[1024]{0:T(1024)S(1)} %bitcast.223, f32[]{:T(128)} %constant.63.clone.1), kind=kCustom, calls=%fused_computation.263 | custom fusion | flops 1024 | bytes 106084 | tf_op jit(solution)/shard_map/scatter-add | solution.py:74
  81.1 7.1 %scatter_custom_fusion.4 = f32[26520]{0:T(1024)S(1)} fusion(s32[1024]{0:T(1024)S(1)} %bitcast.221, f32[1024]{0:T(1024)S(1)} %bitcast.222, f32[]{:T(128)} %constant.63.clone.1), kind=kCustom, calls=%fused_computation.265 | custom fusion | flops 1024 | bytes 106084 | tf_op jit(solution)/shard_map/scatter-add | solution.py:74
  94.3 4.5 %collective-permute-start.8 = (f32[4,6,1,128]{3,2,1,0:T(1,128)S(1)}, f32[4,6,1,128]{3,2,1,0:T(1,128)S(1)}, u32[]{:S(2)}, u32[]{:S(2)}) collective-permute-start(f32[4,6,1,128]{3,2,1,0:T(1,128)S(1)} %get-tuple-element.102), channel_id=1, source_target_pairs={{0,2},{1,3},{4,6},{5,7},{8,10},{9,11},{12,14},{13,15},{16,18},{17,... | collective-permute-start | bytes 36872 | tf_op jit(solution)/shard_map/ppermute | solution.py:14
  106.9 3.9 %collective-permute-start.14 = (f32[4,1,32,128]{3,2,1,0:T(8,128)S(1)}, f32[4,1,32,128]{3,2,1,0:T(8,128)S(1)}, u32[]{:S(2)}, u32[]{:S(2)}) collective-permute-start(f32[4,1,32,128]{3,2,1,0:T(8,128)S(1)} %get-tuple-element.112), channel_id=1, source_target_pairs={{4,0},{8,4},{12,8},{5,1},{9,5},{13,9},{6,2},{10,6},{14,10},{7,3},{... | collective-permute-start | bytes 196616 | tf_op jit(solution)/shard_map/ppermute | solution.py:17
  114.4 4.5 %collective-permute-start.15 = (f32[4,6,1,128]{3,2,1,0:T(1,128)S(1)}, f32[4,6,1,128]{3,2,1,0:T(1,128)S(1)}, u32[]{:S(2)}, u32[]{:S(2)}) collective-permute-start(f32[4,6,1,128]{3,2,1,0:T(1,128)S(1)} %get-tuple-element.104), channel_id=1, source_target_pairs={{0,2},{1,3},{4,6},{5,7},{8,10},{9,11},{12,14},{13,15},{16,18},{17,... | collective-permute-start | bytes 36872 | tf_op jit(solution)/shard_map/ppermute | solution.py:14
  121.8 3.3 %collective-permute-start.17 = (f32[4,6,34,1]{3,2,1,0:T(8,128)S(1)}, f32[4,6,34,1]{3,2,1,0:T(8,128)S(1)}, u32[]{:S(2)}, u32[]{:S(2)}) collective-permute-start(f32[4,6,34,1]{3,2,1,0:T(8,128)S(1)} %get-tuple-element.88), channel_id=1, source_target_pairs={{0,1},{2,3},{4,5},{6,7},{8,9},{10,11},{12,13},{14,15},{16,17},{18,... | collective-permute-start | bytes 9800 | tf_op jit(solution)/shard_map/ppermute | solution.py:14
  128.9 3.9 %collective-permute-start.38 = (f32[4,1,32,128]{3,2,1,0:T(8,128)S(1)}, f32[4,1,32,128]{3,2,1,0:T(8,128)S(1)}, u32[]{:S(2)}, u32[]{:S(2)}) collective-permute-start(f32[4,1,32,128]{3,2,1,0:T(8,128)S(1)} %get-tuple-element.45), channel_id=1, source_target_pairs={{4,0},{8,4},{12,8},{5,1},{9,5},{13,9},{6,2},{10,6},{14,10},{7,3},{... | collective-permute-start | bytes 196616 | tf_op jit(solution)/shard_map/ppermute | solution.py:17
  134.8 3.9 %collective-permute-start.20 = (f32[4,1,32,128]{3,2,1,0:T(8,128)S(1)}, f32[4,1,32,128]{3,2,1,0:T(8,128)S(1)}, u32[]{:S(2)}, u32[]{:S(2)}) collective-permute-start(f32[4,1,32,128]{3,2,1,0:T(8,128)S(1)} %get-tuple-element.39), channel_id=1, source_target_pairs={{4,0},{8,4},{12,8},{5,1},{9,5},{13,9},{6,2},{10,6},{14,10},{7,3},{... | collective-permute-start | bytes 196616 | tf_op jit(solution)/shard_map/ppermute | solution.py:17
  142.3 4.5 %collective-permute-start.39 = (f32[4,6,1,128]{3,2,1,0:T(1,128)S(1)}, f32[4,6,1,128]{3,2,1,0:T(1,128)S(1)}, u32[]{:S(2)}, u32[]{:S(2)}) collective-permute-start(f32[4,6,1,128]{3,2,1,0:T(1,128)S(1)} %get-tuple-element.100), channel_id=1, source_target_pairs={{0,2},{1,3},{4,6},{5,7},{8,10},{9,11},{12,14},{13,15},{16,18},{17,... | collective-permute-start | bytes 36872 | tf_op jit(solution)/shard_map/ppermute | solution.py:14
  148.2 4.5 %collective-permute-start.21 = (f32[4,6,1,128]{3,2,1,0:T(1,128)S(1)}, f32[4,6,1,128]{3,2,1,0:T(1,128)S(1)}, u32[]{:S(2)}, u32[]{:S(2)}) collective-permute-start(f32[4,6,1,128]{3,2,1,0:T(1,128)S(1)} %get-tuple-element.94), channel_id=1, source_target_pairs={{0,2},{1,3},{4,6},{5,7},{8,10},{9,11},{12,14},{13,15},{16,18},{17,... | collective-permute-start | bytes 36872 | tf_op jit(solution)/shard_map/ppermute | solution.py:14
  154.3 3.1 %collective-permute-start.41 = (f32[4,6,34,1]{3,2,1,0:T(8,128)S(1)}, f32[4,6,34,1]{3,2,1,0:T(8,128)S(1)}, u32[]{:S(2)}, u32[]{:S(2)}) collective-permute-start(f32[4,6,34,1]{3,2,1,0:T(8,128)S(1)} %get-tuple-element.84), channel_id=1, source_target_pairs={{0,1},{2,3},{4,5},{6,7},{8,9},{10,11},{12,13},{14,15},{16,17},{18,... | collective-permute-start | bytes 9800 | tf_op jit(solution)/shard_map/ppermute | solution.py:14
  163.3 3.9 %collective-permute-start.44 = (f32[4,1,32,128]{3,2,1,0:T(8,128)S(1)}, f32[4,1,32,128]{3,2,1,0:T(8,128)S(1)}, u32[]{:S(2)}, u32[]{:S(2)}) collective-permute-start(f32[4,1,32,128]{3,2,1,0:T(8,128)S(1)} %get-tuple-element.43), channel_id=1, source_target_pairs={{4,0},{8,4},{12,8},{5,1},{9,5},{13,9},{6,2},{10,6},{14,10},{7,3},{... | collective-permute-start | bytes 196616 | tf_op jit(solution)/shard_map/ppermute | solution.py:17
  169.4 3.9 %collective-permute-done.43 = f32[4,1,32,128]{3,2,1,0:T(8,128)S(1)} collective-permute-done((f32[4,1,32,128]{3,2,1,0:T(8,128)S(1)}, f32[4,1,32,128]{3,2,1,0:T(8,128)S(1)}, u32[]{:S(2)}, u32[]{:S(2)}) %collective-permute-start.43) | collective-permute-done | bytes 65568 | tf_op jit(solution)/shard_map/ppermute | solution.py:14
  174.7 4.5 %collective-permute-start.45 = (f32[4,6,1,128]{3,2,1,0:T(1,128)S(1)}, f32[4,6,1,128]{3,2,1,0:T(1,128)S(1)}, u32[]{:S(2)}, u32[]{:S(2)}) collective-permute-start(f32[4,6,1,128]{3,2,1,0:T(1,128)S(1)} %get-tuple-element.98), channel_id=1, source_target_pairs={{0,2},{1,3},{4,6},{5,7},{8,10},{9,11},{12,14},{13,15},{16,18},{17,... | collective-permute-start | bytes 36872 | tf_op jit(solution)/shard_map/ppermute | solution.py:14
  182.2 3.1 %collective-permute-start.47 = (f32[4,6,34,1]{3,2,1,0:T(8,128)S(1)}, f32[4,6,34,1]{3,2,1,0:T(8,128)S(1)}, u32[]{:S(2)}, u32[]{:S(2)}) collective-permute-start(f32[4,6,34,1]{3,2,1,0:T(8,128)S(1)} %get-tuple-element.82), channel_id=1, source_target_pairs={{0,1},{2,3},{4,5},{6,7},{8,9},{10,11},{12,13},{14,15},{16,17},{18,... | collective-permute-start | bytes 9800 | tf_op jit(solution)/shard_map/ppermute | solution.py:14
  189.8 3.9 %collective-permute-start.49 = (f32[4,1,32,128]{3,2,1,0:T(8,128)S(1)}, f32[4,1,32,128]{3,2,1,0:T(8,128)S(1)}, u32[]{:S(2)}, u32[]{:S(2)}) collective-permute-start(f32[4,1,32,128]{3,2,1,0:T(8,128)S(1)} %get-tuple-element.40), channel_id=1, source_target_pairs={{0,4},{4,8},{8,12},{1,5},{5,9},{9,13},{2,6},{6,10},{10,14},{3,7},{... | collective-permute-start | bytes 196616 | tf_op jit(solution)/shard_map/ppermute | solution.py:14
  197.4 4.5 %collective-permute-start.51 = (f32[4,6,1,128]{3,2,1,0:T(1,128)S(1)}, f32[4,6,1,128]{3,2,1,0:T(1,128)S(1)}, u32[]{:S(2)}, u32[]{:S(2)}) collective-permute-start(f32[4,6,1,128]{3,2,1,0:T(1,128)S(1)} %get-tuple-element.96), channel_id=1, source_target_pairs={{0,2},{1,3},{4,6},{5,7},{8,10},{9,11},{12,14},{13,15},{16,18},{17,... | collective-permute-start | bytes 36872 | tf_op jit(solution)/shard_map/ppermute | solution.py:14
  215.1 3.9 %collective-permute-start.25 = (f32[4,1,32,128]{3,2,1,0:T(8,128)S(1)}, f32[4,1,32,128]{3,2,1,0:T(8,128)S(1)}, u32[]{:S(2)}, u32[]{:S(2)}) collective-permute-start(f32[4,1,32,128]{3,2,1,0:T(8,128)S(1)} %get-tuple-element.36), channel_id=1, source_target_pairs={{0,4},{4,8},{8,12},{1,5},{5,9},{9,13},{2,6},{6,10},{10,14},{3,7},{... | collective-permute-start | bytes 196616 | tf_op jit(solution)/shard_map/ppermute | solution.py:14
  222.7 4.5 %collective-permute-start.27 = (f32[4,6,1,128]{3,2,1,0:T(1,128)S(1)}, f32[4,6,1,128]{3,2,1,0:T(1,128)S(1)}, u32[]{:S(2)}, u32[]{:S(2)}) collective-permute-start(f32[4,6,1,128]{3,2,1,0:T(1,128)S(1)} %get-tuple-element.92), channel_id=1, source_target_pairs={{0,2},{1,3},{4,6},{5,7},{8,10},{9,11},{12,14},{13,15},{16,18},{17,... | collective-permute-start | bytes 36872 | tf_op jit(solution)/shard_map/ppermute | solution.py:14
  231.1 4.6 %collective-permute-start.29 = (f32[4,6,34,1]{3,2,1,0:T(8,128)}, f32[4,6,34,1]{3,2,1,0:T(8,128)}, u32[]{:S(2)}, u32[]{:S(2)}) collective-permute-start(f32[4,6,34,1]{3,2,1,0:T(8,128)} %get-tuple-element.76), channel_id=1, source_target_pairs={{0,1},{2,3},{4,5},{6,7},{8,9},{10,11},{12,13},{14,15},{16,17},{18,... | collective-permute-start | bytes 9800 | tf_op jit(solution)/shard_map/ppermute | solution.py:14
  245.7 4.1 %collective-permute-start.31 = (f32[4,1,32,128]{3,2,1,0:T(8,128)S(1)}, f32[4,1,32,128]{3,2,1,0:T(8,128)S(1)}, u32[]{:S(2)}, u32[]{:S(2)}) collective-permute-start(f32[4,1,32,128]{3,2,1,0:T(8,128)S(1)} %get-tuple-element.34), channel_id=1, source_target_pairs={{0,4},{4,8},{8,12},{1,5},{5,9},{9,13},{2,6},{6,10},{10,14},{3,7},{... | collective-permute-start | bytes 196616 | tf_op jit(solution)/shard_map/ppermute | solution.py:14
  253.2 4.5 %collective-permute-start.33 = (f32[4,6,1,128]{3,2,1,0:T(1,128)S(1)}, f32[4,6,1,128]{3,2,1,0:T(1,128)S(1)}, u32[]{:S(2)}, u32[]{:S(2)}) collective-permute-start(f32[4,6,1,128]{3,2,1,0:T(1,128)S(1)} %get-tuple-element.90), channel_id=1, source_target_pairs={{0,2},{1,3},{4,6},{5,7},{8,10},{9,11},{12,14},{13,15},{16,18},{17,... | collective-permute-start | bytes 36872 | tf_op jit(solution)/shard_map/ppermute | solution.py:14
  260.9 3.1 %collective-permute-start.35 = (f32[4,6,34,1]{3,2,1,0:T(8,128)S(1)}, f32[4,6,34,1]{3,2,1,0:T(8,128)S(1)}, u32[]{:S(2)}, u32[]{:S(2)}) collective-permute-start(f32[4,6,34,1]{3,2,1,0:T(8,128)S(1)} %get-tuple-element.74), channel_id=1, source_target_pairs={{0,1},{2,3},{4,5},{6,7},{8,9},{10,11},{12,13},{14,15},{16,17},{18,... | collective-permute-start | bytes 9800 | tf_op jit(solution)/shard_map/ppermute | solution.py:14
  (243 shorter events, 114.5 us)
Async XLA Ops:
  0.6 99.7 %collective-permute-start.12 = (f32[4,4,32,128]{3,2,1,0:T(8,128)}, f32[4,4,32,128]{3,2,1,0:T(8,128)S(1)}, u32[]{:S(2)}, u32[]{:S(2)}) collective-permute-start(f32[4,4,32,128]{3,2,1,0:T(8,128)} %param.8), channel_id=1, source_target_pairs={{0,8},{8,0},{4,12},{12,4},{1,9},{9,1},{5,13},{13,5},{2,10},{10,2},... | collective-permute-start | bytes 786440 | tf_op jit(solution)/shard_map/ppermute | solution.py:29
  31.4 14.6 %collective-permute-start.1 = (f32[3,1,32,128]{3,2,1,0:T(8,128)S(1)}, f32[3,1,32,128]{3,2,1,0:T(8,128)S(1)}, u32[]{:S(2)}, u32[]{:S(2)}) collective-permute-start(f32[3,1,32,128]{3,2,1,0:T(8,128)S(1)} %get-tuple-element.140), channel_id=1, source_target_pairs={{4,0},{8,4},{12,8},{5,1},{9,5},{13,9},{6,2},{10,6},{14,10},{7,3},{... | collective-permute-start | bytes 147464 | tf_op jit(solution)/shard_map/ppermute | solution.py:17
  33.8 12.3 %collective-permute-start = (f32[3,1,32,128]{3,2,1,0:T(8,128)S(1)}, f32[3,1,32,128]{3,2,1,0:T(8,128)S(1)}, u32[]{:S(2)}, u32[]{:S(2)}) collective-permute-start(f32[3,1,32,128]{3,2,1,0:T(8,128)S(1)} %get-tuple-element.139), channel_id=1, source_target_pairs={{0,4},{4,8},{8,12},{1,5},{5,9},{9,13},{2,6},{6,10},{10,14},{3,7},{... | collective-permute-start | bytes 147464 | tf_op jit(solution)/shard_map/ppermute | solution.py:14
  37.9 55.0 %collective-permute-start.6 = (f32[4,1,32,128]{3,2,1,0:T(8,128)}, f32[4,1,32,128]{3,2,1,0:T(8,128)S(1)}, u32[]{:S(2)}, u32[]{:S(2)}) collective-permute-start(f32[4,1,32,128]{3,2,1,0:T(8,128)} %get-tuple-element.111), channel_id=1, source_target_pairs={{0,4},{4,8},{8,12},{1,5},{5,9},{9,13},{2,6},{6,10},{10,14},{3,7},{... | collective-permute-start | bytes 196616 | tf_op jit(solution)/shard_map/ppermute | solution.py:14
  39.8 53.1 %collective-permute-start.7 = (f32[4,1,32,128]{3,2,1,0:T(8,128)S(1)}, f32[4,1,32,128]{3,2,1,0:T(8,128)S(1)}, u32[]{:S(2)}, u32[]{:S(2)}) collective-permute-start(f32[4,1,32,128]{3,2,1,0:T(8,128)S(1)} %get-tuple-element.110), channel_id=1, source_target_pairs={{4,0},{8,4},{12,8},{5,1},{9,5},{13,9},{6,2},{10,6},{14,10},{7,3},{... | collective-permute-start | bytes 196616 | tf_op jit(solution)/shard_map/ppermute | solution.py:17
  54.2 37.3 %collective-permute-start.5 = (f32[3,6,34,1]{3,2,1,0:T(8,128)}, f32[3,6,34,1]{3,2,1,0:T(8,128)S(1)}, u32[]{:S(2)}, u32[]{:S(2)}) collective-permute-start(f32[3,6,34,1]{3,2,1,0:T(8,128)} %get-tuple-element.107), channel_id=1, source_target_pairs={{1,0},{3,2},{5,4},{7,6},{9,8},{11,10},{13,12},{15,14},{17,16},{19,... | collective-permute-start | bytes 7352 | tf_op jit(solution)/shard_map/ppermute | solution.py:17
  55.5 36.0 %collective-permute-start.4 = (f32[3,6,34,1]{3,2,1,0:T(8,128)S(1)}, f32[3,6,34,1]{3,2,1,0:T(8,128)}, u32[]{:S(2)}, u32[]{:S(2)}) collective-permute-start(f32[3,6,34,1]{3,2,1,0:T(8,128)S(1)} %get-tuple-element.106), channel_id=1, source_target_pairs={{0,1},{2,3},{4,5},{6,7},{8,9},{10,11},{12,13},{14,15},{16,17},{18,... | collective-permute-start | bytes 7352 | tf_op jit(solution)/shard_map/ppermute | solution.py:14
  93.0 6.6 %collective-permute-start.9 = (f32[4,6,1,128]{3,2,1,0:T(1,128)S(1)}, f32[4,6,1,128]{3,2,1,0:T(1,128)S(1)}, u32[]{:S(2)}, u32[]{:S(2)}) collective-permute-start(f32[4,6,1,128]{3,2,1,0:T(1,128)S(1)} %get-tuple-element.103), channel_id=1, source_target_pairs={{2,0},{3,1},{6,4},{7,5},{10,8},{11,9},{14,12},{15,13},{18,16},{19,... | collective-permute-start | bytes 36872 | tf_op jit(solution)/shard_map/ppermute | solution.py:17
  100.3 10.4 %collective-permute-start.13 = (f32[4,1,32,128]{3,2,1,0:T(8,128)S(1)}, f32[4,1,32,128]{3,2,1,0:T(8,128)S(1)}, u32[]{:S(2)}, u32[]{:S(2)}) collective-permute-start(f32[4,1,32,128]{3,2,1,0:T(8,128)S(1)} %get-tuple-element.113), channel_id=1, source_target_pairs={{0,4},{4,8},{8,12},{1,5},{5,9},{9,13},{2,6},{6,10},{10,14},{3,7},{... | collective-permute-start | bytes 196616 | tf_op jit(solution)/shard_map/ppermute | solution.py:14
  102.5 16.4 %collective-permute-start.11 = (f32[4,6,34,1]{3,2,1,0:T(8,128)S(1)}, f32[4,6,34,1]{3,2,1,0:T(8,128)S(1)}, u32[]{:S(2)}, u32[]{:S(2)}) collective-permute-start(f32[4,6,34,1]{3,2,1,0:T(8,128)S(1)} %get-tuple-element.87), channel_id=1, source_target_pairs={{1,0},{3,2},{5,4},{7,6},{9,8},{11,10},{13,12},{15,14},{17,16},{19,... | collective-permute-start | bytes 9800 | tf_op jit(solution)/shard_map/ppermute | solution.py:17
  103.8 15.1 %collective-permute-start.10 = (f32[4,6,34,1]{3,2,1,0:T(8,128)S(1)}, f32[4,6,34,1]{3,2,1,0:T(8,128)S(1)}, u32[]{:S(2)}, u32[]{:S(2)}) collective-permute-start(f32[4,6,34,1]{3,2,1,0:T(8,128)S(1)} %get-tuple-element.86), channel_id=1, source_target_pairs={{0,1},{2,3},{4,5},{6,7},{8,9},{10,11},{12,13},{14,15},{16,17},{18,... | collective-permute-start | bytes 9800 | tf_op jit(solution)/shard_map/ppermute | solution.py:14
  128.9 12.1 %collective-permute-start.38 = (f32[4,1,32,128]{3,2,1,0:T(8,128)S(1)}, f32[4,1,32,128]{3,2,1,0:T(8,128)S(1)}, u32[]{:S(2)}, u32[]{:S(2)}) collective-permute-start(f32[4,1,32,128]{3,2,1,0:T(8,128)S(1)} %get-tuple-element.45), channel_id=1, source_target_pairs={{4,0},{8,4},{12,8},{5,1},{9,5},{13,9},{6,2},{10,6},{14,10},{7,3},{... | collective-permute-start | bytes 196616 | tf_op jit(solution)/shard_map/ppermute | solution.py:17
  132.8 8.1 %collective-permute-start.37 = (f32[4,1,32,128]{3,2,1,0:T(8,128)S(1)}, f32[4,1,32,128]{3,2,1,0:T(8,128)S(1)}, u32[]{:S(2)}, u32[]{:S(2)}) collective-permute-start(f32[4,1,32,128]{3,2,1,0:T(8,128)S(1)} %get-tuple-element.44), channel_id=1, source_target_pairs={{0,4},{4,8},{8,12},{1,5},{5,9},{9,13},{2,6},{6,10},{10,14},{3,7},{... | collective-permute-start | bytes 196616 | tf_op jit(solution)/shard_map/ppermute | solution.py:14
  134.8 12.0 %collective-permute-start.20 = (f32[4,1,32,128]{3,2,1,0:T(8,128)S(1)}, f32[4,1,32,128]{3,2,1,0:T(8,128)S(1)}, u32[]{:S(2)}, u32[]{:S(2)}) collective-permute-start(f32[4,1,32,128]{3,2,1,0:T(8,128)S(1)} %get-tuple-element.39), channel_id=1, source_target_pairs={{4,0},{8,4},{12,8},{5,1},{9,5},{13,9},{6,2},{10,6},{14,10},{7,3},{... | collective-permute-start | bytes 196616 | tf_op jit(solution)/shard_map/ppermute | solution.py:17
  138.8 8.1 %collective-permute-start.19 = (f32[4,1,32,128]{3,2,1,0:T(8,128)S(1)}, f32[4,1,32,128]{3,2,1,0:T(8,128)S(1)}, u32[]{:S(2)}, u32[]{:S(2)}) collective-permute-start(f32[4,1,32,128]{3,2,1,0:T(8,128)S(1)} %get-tuple-element.38), channel_id=1, source_target_pairs={{0,4},{4,8},{8,12},{1,5},{5,9},{9,13},{2,6},{6,10},{10,14},{3,7},{... | collective-permute-start | bytes 196616 | tf_op jit(solution)/shard_map/ppermute | solution.py:14
  141.0 11.8 %collective-permute-start.40 = (f32[4,6,1,128]{3,2,1,0:T(1,128)S(1)}, f32[4,6,1,128]{3,2,1,0:T(1,128)S(1)}, u32[]{:S(2)}, u32[]{:S(2)}) collective-permute-start(f32[4,6,1,128]{3,2,1,0:T(1,128)S(1)} %get-tuple-element.101), channel_id=1, source_target_pairs={{2,0},{3,1},{6,4},{7,5},{10,8},{11,9},{14,12},{15,13},{18,16},{19,... | collective-permute-start | bytes 36872 | tf_op jit(solution)/shard_map/ppermute | solution.py:17
  142.3 10.5 %collective-permute-start.39 = (f32[4,6,1,128]{3,2,1,0:T(1,128)S(1)}, f32[4,6,1,128]{3,2,1,0:T(1,128)S(1)}, u32[]{:S(2)}, u32[]{:S(2)}) collective-permute-start(f32[4,6,1,128]{3,2,1,0:T(1,128)S(1)} %get-tuple-element.100), channel_id=1, source_target_pairs={{0,2},{1,3},{4,6},{5,7},{8,10},{9,11},{12,14},{13,15},{16,18},{17,... | collective-permute-start | bytes 36872 | tf_op jit(solution)/shard_map/ppermute | solution.py:14
  146.9 10.5 %collective-permute-start.22 = (f32[4,6,1,128]{3,2,1,0:T(1,128)S(1)}, f32[4,6,1,128]{3,2,1,0:T(1,128)S(1)}, u32[]{:S(2)}, u32[]{:S(2)}) collective-permute-start(f32[4,6,1,128]{3,2,1,0:T(1,128)S(1)} %get-tuple-element.95), channel_id=1, source_target_pairs={{2,0},{3,1},{6,4},{7,5},{10,8},{11,9},{14,12},{15,13},{18,16},{19,... | collective-permute-start | bytes 36872 | tf_op jit(solution)/shard_map/ppermute | solution.py:17
  148.2 9.2 %collective-permute-start.21 = (f32[4,6,1,128]{3,2,1,0:T(1,128)S(1)}, f32[4,6,1,128]{3,2,1,0:T(1,128)S(1)}, u32[]{:S(2)}, u32[]{:S(2)}) collective-permute-start(f32[4,6,1,128]{3,2,1,0:T(1,128)S(1)} %get-tuple-element.94), channel_id=1, source_target_pairs={{0,2},{1,3},{4,6},{5,7},{8,10},{9,11},{12,14},{13,15},{16,18},{17,... | collective-permute-start | bytes 36872 | tf_op jit(solution)/shard_map/ppermute | solution.py:14
  153.0 9.1 %collective-permute-start.42 = (f32[4,6,34,1]{3,2,1,0:T(8,128)S(1)}, f32[4,6,34,1]{3,2,1,0:T(8,128)S(1)}, u32[]{:S(2)}, u32[]{:S(2)}) collective-permute-start(f32[4,6,34,1]{3,2,1,0:T(8,128)S(1)} %get-tuple-element.85), channel_id=1, source_target_pairs={{1,0},{3,2},{5,4},{7,6},{9,8},{11,10},{13,12},{15,14},{17,16},{19,... | collective-permute-start | bytes 9800 | tf_op jit(solution)/shard_map/ppermute | solution.py:17
  154.3 7.8 %collective-permute-start.41 = (f32[4,6,34,1]{3,2,1,0:T(8,128)S(1)}, f32[4,6,34,1]{3,2,1,0:T(8,128)S(1)}, u32[]{:S(2)}, u32[]{:S(2)}) collective-permute-start(f32[4,6,34,1]{3,2,1,0:T(8,128)S(1)} %get-tuple-element.84), channel_id=1, source_target_pairs={{0,1},{2,3},{4,5},{6,7},{8,9},{10,11},{12,13},{14,15},{16,17},{18,... | collective-permute-start | bytes 9800 | tf_op jit(solution)/shard_map/ppermute | solution.py:14
  157.7 21.5 %collective-permute-start.24 = (f32[4,6,34,1]{3,2,1,0:T(8,128)S(1)}, f32[4,6,34,1]{3,2,1,0:T(8,128)S(1)}, u32[]{:S(2)}, u32[]{:S(2)}) collective-permute-start(f32[4,6,34,1]{3,2,1,0:T(8,128)S(1)} %get-tuple-element.79), channel_id=1, source_target_pairs={{1,0},{3,2},{5,4},{7,6},{9,8},{11,10},{13,12},{15,14},{17,16},{19,... | collective-permute-start | bytes 9800 | tf_op jit(solution)/shard_map/ppermute | solution.py:17
  159.0 20.3 %collective-permute-start.23 = (f32[4,6,34,1]{3,2,1,0:T(8,128)S(1)}, f32[4,6,34,1]{3,2,1,0:T(8,128)S(1)}, u32[]{:S(2)}, u32[]{:S(2)}) collective-permute-start(f32[4,6,34,1]{3,2,1,0:T(8,128)S(1)} %get-tuple-element.78), channel_id=1, source_target_pairs={{0,1},{2,3},{4,5},{6,7},{8,9},{10,11},{12,13},{14,15},{16,17},{18,... | collective-permute-start | bytes 9800 | tf_op jit(solution)/shard_map/ppermute | solution.py:14
  167.2 6.2 %collective-permute-start.43 = (f32[4,1,32,128]{3,2,1,0:T(8,128)S(1)}, f32[4,1,32,128]{3,2,1,0:T(8,128)S(1)}, u32[]{:S(2)}, u32[]{:S(2)}) collective-permute-start(f32[4,1,32,128]{3,2,1,0:T(8,128)S(1)} %get-tuple-element.42), channel_id=1, source_target_pairs={{0,4},{4,8},{8,12},{1,5},{5,9},{9,13},{2,6},{6,10},{10,14},{3,7},{... | collective-permute-start | bytes 196616 | tf_op jit(solution)/shard_map/ppermute | solution.py:14
  187.9 6.3 %collective-permute-start.50 = (f32[4,1,32,128]{3,2,1,0:T(8,128)S(1)}, f32[4,1,32,128]{3,2,1,0:T(8,128)S(1)}, u32[]{:S(2)}, u32[]{:S(2)}) collective-permute-start(f32[4,1,32,128]{3,2,1,0:T(8,128)S(1)} %get-tuple-element.41), channel_id=1, source_target_pairs={{4,0},{8,4},{12,8},{5,1},{9,5},{13,9},{6,2},{10,6},{14,10},{7,3},{... | collective-permute-start | bytes 196616 | tf_op jit(solution)/shard_map/ppermute | solution.py:17
  189.8 6.3 %collective-permute-start.49 = (f32[4,1,32,128]{3,2,1,0:T(8,128)S(1)}, f32[4,1,32,128]{3,2,1,0:T(8,128)S(1)}, u32[]{:S(2)}, u32[]{:S(2)}) collective-permute-start(f32[4,1,32,128]{3,2,1,0:T(8,128)S(1)} %get-tuple-element.40), channel_id=1, source_target_pairs={{0,4},{4,8},{8,12},{1,5},{5,9},{9,13},{2,6},{6,10},{10,14},{3,7},{... | collective-permute-start | bytes 196616 | tf_op jit(solution)/shard_map/ppermute | solution.py:14
  196.1 6.4 %collective-permute-start.52 = (f32[4,6,1,128]{3,2,1,0:T(1,128)S(1)}, f32[4,6,1,128]{3,2,1,0:T(1,128)S(1)}, u32[]{:S(2)}, u32[]{:S(2)}) collective-permute-start(f32[4,6,1,128]{3,2,1,0:T(1,128)S(1)} %get-tuple-element.97), channel_id=1, source_target_pairs={{2,0},{3,1},{6,4},{7,5},{10,8},{11,9},{14,12},{15,13},{18,16},{19,... | collective-permute-start | bytes 36872 | tf_op jit(solution)/shard_map/ppermute | solution.py:17
  213.2 6.5 %collective-permute-start.26 = (f32[4,1,32,128]{3,2,1,0:T(8,128)S(1)}, f32[4,1,32,128]{3,2,1,0:T(8,128)S(1)}, u32[]{:S(2)}, u32[]{:S(2)}) collective-permute-start(f32[4,1,32,128]{3,2,1,0:T(8,128)S(1)} %get-tuple-element.37), channel_id=1, source_target_pairs={{4,0},{8,4},{12,8},{5,1},{9,5},{13,9},{6,2},{10,6},{14,10},{7,3},{... | collective-permute-start | bytes 196616 | tf_op jit(solution)/shard_map/ppermute | solution.py:17
  215.1 6.3 %collective-permute-start.25 = (f32[4,1,32,128]{3,2,1,0:T(8,128)S(1)}, f32[4,1,32,128]{3,2,1,0:T(8,128)S(1)}, u32[]{:S(2)}, u32[]{:S(2)}) collective-permute-start(f32[4,1,32,128]{3,2,1,0:T(8,128)S(1)} %get-tuple-element.36), channel_id=1, source_target_pairs={{0,4},{4,8},{8,12},{1,5},{5,9},{9,13},{2,6},{6,10},{10,14},{3,7},{... | collective-permute-start | bytes 196616 | tf_op jit(solution)/shard_map/ppermute | solution.py:14
  229.8 9.3 %collective-permute-start.30 = (f32[4,6,34,1]{3,2,1,0:T(8,128)}, f32[4,6,34,1]{3,2,1,0:T(8,128)}, u32[]{:S(2)}, u32[]{:S(2)}) collective-permute-start(f32[4,6,34,1]{3,2,1,0:T(8,128)} %get-tuple-element.77), channel_id=1, source_target_pairs={{1,0},{3,2},{5,4},{7,6},{9,8},{11,10},{13,12},{15,14},{17,16},{19,... | collective-permute-start | bytes 9800 | tf_op jit(solution)/shard_map/ppermute | solution.py:17
  231.1 8.0 %collective-permute-start.29 = (f32[4,6,34,1]{3,2,1,0:T(8,128)}, f32[4,6,34,1]{3,2,1,0:T(8,128)}, u32[]{:S(2)}, u32[]{:S(2)}) collective-permute-start(f32[4,6,34,1]{3,2,1,0:T(8,128)} %get-tuple-element.76), channel_id=1, source_target_pairs={{0,1},{2,3},{4,5},{6,7},{8,9},{10,11},{12,13},{14,15},{16,17},{18,... | collective-permute-start | bytes 9800 | tf_op jit(solution)/shard_map/ppermute | solution.py:14
  243.8 6.2 %collective-permute-start.32 = (f32[4,1,32,128]{3,2,1,0:T(8,128)S(1)}, f32[4,1,32,128]{3,2,1,0:T(8,128)S(1)}, u32[]{:S(2)}, u32[]{:S(2)}) collective-permute-start(f32[4,1,32,128]{3,2,1,0:T(8,128)S(1)} %get-tuple-element.35), channel_id=1, source_target_pairs={{4,0},{8,4},{12,8},{5,1},{9,5},{13,9},{6,2},{10,6},{14,10},{7,3},{... | collective-permute-start | bytes 196616 | tf_op jit(solution)/shard_map/ppermute | solution.py:17
  (46 other events, 239.6 us)
where the time goes:
time: 275 us; the launch traced here: 271 us
  starting transfers between devices  150 us (55%)
  other arithmetic  77.7 us (28%)
  waiting for transfers between devices  24.8 us (9%)
  local copies, waits for them, and re-layouts  16.4 us (6%)
    ppermute x27, starting transfers between devices, with_halo(): lax.ppermute(lax.slice_in_dim(block, block.shape[dim] - width, None, axis...  96.2 us
    ppermute x27, starting transfers between devices, with_halo(): lax.ppermute(lax.slice_in_dim(block, 0, width, axis=dim), axis, backward)  51.1 us
    scatter-add x7, other arithmetic, inject(): jnp.zeros((total_cells,), jnp.float32).at[flat_index]  31.8 us
    another operation x3, other arithmetic, coefficients(): jnp.stack([density * sound_speed, sound_speed / density, 1.0 - absorb], 0)  25.3 us
    ppermute x27, waiting for transfers between devices, with_halo(): lax.ppermute(lax.slice_in_dim(block, block.shape[dim] - width, None, axis...  21.7 us
  transfers between devices with their start and end apart: 55, of which 19 were waited for; matrix products, arithmetic and copies ran while one was open for 27% of the time, Pallas kernels for 0%

commit v1 on v0

v1 whole, which is shorter than its diff:
```python
import jax
import jax.numpy as jnp
from jax import lax
from jax.experimental import pallas as pl
from jax.experimental.pallas import tpu as pltpu
from jax.sharding import PartitionSpec as P

STEPS = 4
MARGIN = 4
BX, BY, BZ = 4, 32, 128
EX, EY = BX + 2 * MARGIN, BY + 2 * MARGIN
STRIP = 2 * MARGIN
F32 = jnp.float32
BF16 = jnp.bfloat16
VMEM_LIMIT = 48 * 1024 * 1024


def lanes(shape):
    return lax.broadcasted_iota(jnp.int32, shape, len(shape) - 1)


def rows(shape):
    return lax.broadcasted_iota(jnp.int32, shape, len(shape) - 2)


def pack_kernel(stored_ref, adj_ref, lab_ref, al_ref, ep_ref, strip_ref):
    gz = lax.axis_index("gz")
    lane = lanes((BY, BZ))
    row = rows((8, BZ))

    def plane(field, x):
        if field < 4:
            return stored_ref[field, x]
        if field < 8:
            return adj_ref[field - 4, x]
        return lab_ref[x].astype(F32) + 1.0

    for group in range(3):
        strip = jnp.zeros((BY, BZ), F32)
        for slot in range(4 if group < 2 else 1):
            field = group * 4 + slot
            for x in range(BX):
                block = plane(field, x)
                if field >= 4:
                    al_ref[field - 4, x] = block
                ep_ref[field * BX + x] = jnp.where(row < MARGIN, block[0:8], block[BY - 8 : BY])
                base = slot * BX * STRIP + x * STRIP
                rolled = pltpu.roll(block, (base + MARGIN) % BZ, 1)
                first = base + MARGIN * gz
                strip = jnp.where((lane >= first) & (lane < first + MARGIN), rolled, strip)
        strip_ref[group] = strip
        ep_ref[9 * BX + group] = jnp.where(row < MARGIN, strip[0:8], strip[BY - 8 : BY])


def merge_kernel(up_ref, down_ref, strip_ref, other_ref, dup_ref, ddown_ref, xw_ref, xa_ref):
    row = rows((8, BZ))

    def halo(index):
        return jnp.where(row < MARGIN, up_ref[index], down_ref[index])

    for index in range(4 * BX):
        xw_ref[index] = halo(index)
    for index in range(5 * BX):
        xa_ref[index] = halo(4 * BX + index)
    for group in range(3):
        target, first = ((xw_ref, 4 * BX), (xa_ref, 5 * BX), (xa_ref, 5 * BX + 5))[group]
        for tile in range(4):
            sl = slice(tile * 8, tile * 8 + 8)
            target[first + tile] = strip_ref[group, sl] + other_ref[group, sl]
        diagonal = jnp.where(row < MARGIN, dup_ref[group], ddown_ref[group])
        target[first + 4] = halo(9 * BX + group) + diagonal


def split(values):
    high = values.astype(BF16)
    rest = values - high.astype(F32)
    middle = rest.astype(BF16)
    low = (rest - middle.astype(F32)).astype(BF16)
    return high, middle, low


def inject_points(table_ref, count, width, out_ref, strip_out_ref, waves):
    gx, gy, gz = (lax.axis_index(name) for name in ("gx", "gy", "gz"))
    cut = BZ * lax.axis_size("gz") // 2 - MARGIN
    for start in range(0, count, width):
        sl = slice(start, start + width)
        cell_x = table_ref[0:1, sl].astype(jnp.int32) - (gx * BX - MARGIN)
        cell_y = table_ref[1:2, sl].astype(jnp.int32) - gy * BY
        cell_z = table_ref[2:3, sl].astype(jnp.int32)
        in_x = (cell_x >= 0) & (cell_x < EX)
        in_y = (cell_y >= -MARGIN) & (cell_y < BY + MARGIN)
        row = jnp.where(cell_y < 0, cell_y + EY, cell_y)
        flat = jnp.where(in_x & in_y, cell_x * EY + row, -1)
        row = jnp.where(in_y, row, -1)
        zz = cell_z - cut
        in_strip = in_x & (zz >= 0) & (zz < STRIP)
        strip_lane = jnp.where(in_strip, cell_x * STRIP + zz, -1)
        here = (rows((EX * EY, width)) == flat).astype(F32).astype(BF16)
        at_z = rows((BZ, width)) == (cell_z - gz * BZ)
        at_strip = (rows((BZ, width)) == strip_lane).astype(F32).astype(BF16)
        at_row = rows((EY, width)) == row
        for wave in range(waves):
            total = None
            strip_total = None
            for part in split(table_ref[4 + wave : 5 + wave, sl]):
                part = part.astype(F32)
                term = lax.dot_general(
                    here,
                    jnp.where(at_z, part, 0.0).astype(BF16),
                    (((1,), (1,)), ((), ())),
                    preferred_element_type=F32,
                )
                total = term if total is None else total + term
                term = lax.dot_general(
                    jnp.where(at_row, part, 0.0).astype(BF16),
                    at_strip,
                    (((1,), (1,)), ((), ())),
                    preferred_element_type=F32,
                )
                strip_total = term if strip_total is None else strip_total + term
            if start > 0:
                total = total + out_ref[wave]
                strip_total = strip_total + strip_out_ref[wave]
            out_ref[wave] = total
            strip_out_ref[wave] = strip_total


def inject_kernel(receivers_ref, sources_ref, r_ref, rs_ref, s_ref, ss_ref):
    inject_points(receivers_ref, receivers_ref.shape[1], 256, r_ref, rs_ref, STEPS)
    inject_points(sources_ref, sources_ref.shape[1], 128, s_ref, ss_ref, STEPS - 1)


def strip_of(packed, block, slot):
    lane = lanes(packed.shape)
    width = BX * STRIP
    shift = (block * width - slot * width) % BZ
    moved = pltpu.roll(packed, shift, 1) if shift else packed
    return jnp.where((lane >= block * width) & (lane < (block + 1) * width), moved, 0.0)


def y_up(v):
    return pltpu.roll(v, EY - 1, 0)


def y_down(v):
    return pltpu.roll(v, 1, 0)


def z_up(v, strip, x):
    edge = pltpu.roll(strip, (BZ - 1 - (x * STRIP + MARGIN)) % BZ, 1)
    return jnp.where(lanes(v.shape) == BZ - 1, edge, pltpu.roll(v, BZ - 1, 1))


def z_down(v, strip, x):
    edge = pltpu.roll(strip, (BZ - (x * STRIP + MARGIN - 1)) % BZ, 1)
    return jnp.where(lanes(v.shape) == 0, edge, pltpu.roll(v, 1, 1))


def coefficient_values(labels, tissue_ref):
    stiffness = jnp.zeros(labels.shape, F32)
    buoyancy = jnp.zeros(labels.shape, F32)
    damping = jnp.zeros(labels.shape, F32)
    for index in range(tissue_ref.shape[1]):
        picked = labels == float(index + 1)
        speed = tissue_ref[0, index]
        density = tissue_ref[1, index]
        ratio = (jnp.full((8, BZ), speed, F32) / jnp.full((8, BZ), density, F32))[0:1, :]
        stiffness = jnp.where(picked, density * speed, stiffness)
        buoyancy = jnp.where(picked, ratio, buoyancy)
        damping = jnp.where(picked, 1.0 - tissue_ref[2, index], damping)
    return stiffness, buoyancy, damping


def adjoint_kernel(
    al, al_low, al_high, xa, xa_low, xa_high, r_ref, rs_ref, tissue_ref,
    out_ref, hist_ref, coef_ref, coef_strip_ref,
    field, strip, sem,
):
    gz = lax.axis_index("gz")
    cut_up = jnp.where(gz == lax.axis_size("gz") // 2 - 1, 1.0, 0.0)
    cut_down = jnp.where(gz == lax.axis_size("gz") // 2, 1.0, 0.0)
    copies = []
    for block, (own, extra) in enumerate(((al_low, xa_low), (al, xa), (al_high, xa_high))):
        planes = pl.ds(block * BX, BX)
        copies.append(pltpu.make_async_copy(own, field.at[:, planes, pl.ds(0, BY), :], sem))
        for index in range(5):
            copies.append(
                pltpu.make_async_copy(
                    extra.at[pl.ds(index * BX, BX)],
                    field.at[index, planes, pl.ds(BY, 8), :],
                    sem,
                )
            )
        for group in range(2):
            copies.append(
                pltpu.make_async_copy(
                    extra.at[pl.ds(5 * BX + 5 * group, 5)], strip.at[block, group], sem
                )
            )
    for copy in copies:
        copy.start()
    for copy in copies:
        copy.wait()

    for x in range(EX):
        for index, values in enumerate(coefficient_values(field[4, x], tissue_ref)):
            coef_ref[index, x] = values
    packed = [[strip[b, g].reshape(EY, BZ) for g in range(2)] for b in range(3)]
    label_strip = sum(strip_of(packed[b][1], b, 0) for b in range(3))
    stiff_s, buoy_s, damp_s = coefficient_values(label_strip, tissue_ref)
    coef_strip_ref[0], coef_strip_ref[1], coef_strip_ref[2] = stiff_s, buoy_s, damp_s
    q_s, wx_s, wy_s, wz_s = (
        sum(strip_of(packed[b][0], b, slot) for b in range(3)) for slot in range(4)
    )

    for step in range(1, STEPS + 1):
        k = STEPS - step
        q_s = q_s + rs_ref[k]
        u_s = stiff_s * damp_s * q_s
        wx_s = wx_s + (pltpu.roll(u_s, BZ - STRIP, 1) - u_s)
        wy_s = wy_s + (y_up(u_s) - u_s)
        wz_s = wz_s + (pltpu.roll(u_s, BZ - 1, 1) - u_s)
        bx_s, by_s, bz_s = buoy_s * wx_s, buoy_s * wy_s, buoy_s * wz_s
        spread = (bx_s - pltpu.roll(bx_s, STRIP, 1)) + (by_s - y_down(by_s))
        spread = spread + (bz_s - pltpu.roll(bz_s, 1, 1))
        q_s = damp_s * q_s + spread
        edge_up = u_s * cut_up
        edge_down = bz_s * cut_down

        def injected(x):
            value = field[0, x] + r_ref[k, x]
            return value, coef_ref[0, x] * coef_ref[2, x] * value

        bx_below = None
        q_now, u_now = injected(step - 1)
        for x in range(step - 1, EX - step):
            q_next, u_next = injected(x + 1)
            wx = field[1, x] + (u_next - u_now)
            field[1, x] = wx
            bx = coef_ref[1, x] * wx
            if x >= step:
                wy = field[2, x] + (y_up(u_now) - u_now)
                wz = field[3, x] + (z_up(u_now, edge_up, x) - u_now)
                field[2, x] = wy
                field[3, x] = wz
                damped = coef_ref[2, x] * q_now
                if BX <= x < 2 * BX:
                    hist_ref[k, 0, x - BX] = damped[0:BY]
                    hist_ref[k, 1, x - BX] = wx[0:BY]
                    hist_ref[k, 2, x - BX] = wy[0:BY]
                    hist_ref[k, 3, x - BX] = wz[0:BY]
                by = coef_ref[1, x] * wy
                bz = coef_ref[1, x] * wz
                spread = (bx - bx_below) + (by - y_down(by))
                spread = spread + (bz - z_down(bz, edge_down, x))
                field[0, x] = damped + spread
            bx_below = bx
            q_now, u_now = q_next, u_next

    for index in range(4):
        for x in range(BX):
            out_ref[index, x] = field[index, BX + x, 0:BY]


def forward_kernel(
    ag, agx, coef_ref, coef_strip_ref, s_ref, ss_ref, hist_ref, grad_ref, field, strip, sem
):
    gx = lax.axis_index("gx")
    gz = lax.axis_index("gz")
    count = ag.shape[0]
    cut_up = jnp.where(gz == lax.axis_size("gz") // 2 - 1, 1.0, 0.0)
    cut_down = jnp.where(gz == lax.axis_size("gz") // 2, 1.0, 0.0)

    def copies(block):
        source = lax.rem(gx - 1 + block + count + count // 2, count)
        planes = pl.ds(block * BX, BX)
        result = [
            pltpu.make_async_copy(ag.at[source], field.at[:, planes, pl.ds(0, BY), :], sem)
        ]
        for index in range(4):
            result.append(
                pltpu.make_async_copy(
                    agx.at[source, pl.ds(index * BX, BX)],
                    field.at[index, planes, pl.ds(BY, 8), :],
                    sem,
                )
            )
        result.append(
            pltpu.make_async_copy(agx.at[source, pl.ds(4 * BX, 5)], strip.at[block], sem)
        )
        return result

    inside = (gx > 0, None, gx < count - 1)

    def start(block):
        for copy in copies(block):
            copy.start()

    def clear(block):
        planes = slice(block * BX, block * BX + BX)
        field[:, planes] = jnp.zeros((4, BX, EY, BZ), F32)
        strip[block] = jnp.zeros((5, 8, BZ), F32)

    def finish(block):
        for copy in copies(block):
            copy.wait()

    start(1)
    for block in (0, 2):
        pl.when(inside[block])(lambda block=block: start(block))
        pl.when(jnp.logical_not(inside[block]))(lambda block=block: clear(block))
    finish(1)
    for block in (0, 2):
        pl.when(inside[block])(lambda block=block: finish(block))

    packed = [strip[b].reshape(EY, BZ) for b in range(3)]
    stiff_s, buoy_s, damp_s = coef_strip_ref[0], coef_strip_ref[1], coef_strip_ref[2]
    p_s, vx_s, vy_s, vz_s = (
        sum(strip_of(packed[b], b, slot) for b in range(3)) for slot in range(4)
    )

    for step in range(1, STEPS + 1):
        k = step - 1
        edge_up = p_s * cut_up
        vx_s = vx_s - buoy_s * (pltpu.roll(p_s, BZ - STRIP, 1) - p_s)
        vy_s = vy_s - buoy_s * (y_up(p_s) - p_s)
        vz_s = vz_s - buoy_s * (pltpu.roll(p_s, BZ - 1, 1) - p_s)
        edge_down = vz_s * cut_down
        if step < STEPS:
            spread = (vx_s - pltpu.roll(vx_s, STRIP, 1)) + (vy_s - y_down(vy_s))
            spread = spread + (vz_s - pltpu.roll(vz_s, 1, 1))
            p_s = damp_s * (p_s - stiff_s * spread) + ss_ref[k]

        vx_below = None
        p_now = field[0, step - 1]
        for x in range(step - 1, EX - step):
            p_next = field[0, x + 1]
            buoyancy = coef_ref[1, x]
            slope_x = p_next - p_now
            vx = field[1, x] - buoyancy * slope_x
            field[1, x] = vx
            if x >= step:
                slope_y = y_up(p_now) - p_now
                slope_z = z_up(p_now, edge_up, x) - p_now
                vy = field[2, x] - buoyancy * slope_y
                vz = field[3, x] - buoyancy * slope_z
                field[2, x] = vy
                field[3, x] = vz
                spread = (vx - vx_below) + (vy - y_down(vy))
                spread = spread + (vz - z_down(vz, edge_down, x))
                if step < STEPS:
                    field[0, x] = (
                        coef_ref[2, x] * (p_now - coef_ref[0, x] * spread) + s_ref[k, x]
                    )
                if BX <= x < 2 * BX:
                    own = x - BX
                    term = hist_ref[k, 0, own] * spread[0:BY]
                    grad_s = -term if k == 0 else grad_ref[0, own] - term
                    grad_ref[0, own] = grad_s
                    term = hist_ref[k, 1, own] * slope_x[0:BY]
                    term = term + hist_ref[k, 2, own] * slope_y[0:BY]
                    term = term + hist_ref[k, 3, own] * slope_z[0:BY]
                    grad_ref[1, own] = -term if k == 0 else grad_ref[1, own] - term
            vx_below = vx
            p_now = p_next


def shape(*dims):
    return jax.ShapeDtypeStruct(dims, F32)


def call(kernel, outs, operands, scratch=(), any_operands=(), smem_operands=(), bytes_moved=1 << 20):
    def spec(index):
        if index in any_operands:
            return pl.BlockSpec(memory_space=pl.ANY)
        if index in smem_operands:
            return pl.BlockSpec(memory_space=pltpu.SMEM)
        return pl.BlockSpec(memory_space=pltpu.VMEM)

    return pl.pallas_call(
        kernel,
        out_shape=outs,
        in_specs=[spec(index) for index in range(len(operands))],
        out_specs=[pl.BlockSpec(memory_space=pltpu.VMEM)] * len(outs),
        scratch_shapes=list(scratch),
        compiler_params=pltpu.CompilerParams(vmem_limit_bytes=VMEM_LIMIT),
        cost_estimate=pl.CostEstimate(flops=1 << 24, bytes_accessed=bytes_moved, transcendentals=0),
    )(*operands)


def from_sides(array, axes):
    count = lax.axis_size("gy")

    def route(offset):
        pairs = []
        for target in range(count):
            source = target + offset
            if 0 <= source < count:
                if "gz" in axes:
                    pairs += [(2 * source + z, 2 * target + 1 - z) for z in range(2)]
                else:
                    pairs.append((source, target))
        return pairs

    if count == 2:
        both = lax.ppermute(array, axes, route(1) + route(-1))
        me = lax.axis_index("gy")
        return both * (me == 0).astype(F32), both * (me == 1).astype(F32)
    return lax.ppermute(array, axes, route(1)), lax.ppermute(array, axes, route(-1))


def along_x(array):
    count = lax.axis_size("gx")
    forward = [(i, i + 1) for i in range(count - 1)]
    backward = [(i + 1, i) for i in range(count - 1)]
    return lax.ppermute(array, "gx", forward), lax.ppermute(array, "gx", backward)


def table(cells, wave, width):
    short = width - cells.shape[0]
    places = jnp.pad(cells.T.astype(F32), ((0, 1), (0, short)), constant_values=-1000.0)
    return jnp.concatenate([places, jnp.pad(wave, ((0, 0), (0, short)))], 0)


def local(
    stored, adjoint_end, labels, tissue, source_cells, source_wave, receiver_cells, receiver_wave
):
    assert lax.axis_size("gz") == 2 and labels.shape == (BX, BY, BZ)
    gathered = lax.all_gather(stored, "gx")
    al, edges, strips = call(
        pack_kernel,
        [shape(5, BX, BY, BZ), shape(9 * BX + 3, 8, BZ), shape(3, BY, BZ)],
        [stored, adjoint_end, labels],
    )
    al_low, al_high = along_x(al)
    other = lax.ppermute(strips, "gz", [(0, 1), (1, 0)])
    up, down = from_sides(edges, "gy")
    diagonal_up, diagonal_down = from_sides(edges[9 * BX :], ("gy", "gz"))
    xw, xa = call(
        merge_kernel,
        [shape(4 * BX + 5, 8, BZ), shape(5 * BX + 10, 8, BZ)],
        [up, down, strips, other, diagonal_up, diagonal_down],
    )
    gathered_x = lax.all_gather(xw, "gx")
    xa_low, xa_high = along_x(xa)
    receivers = table(receiver_cells, receiver_wave, -(-receiver_cells.shape[0] // 256) * 256)
    sources = table(source_cells, source_wave, -(-source_cells.shape[0] // 128) * 128)
    r, rs, s, ss = call(
        inject_kernel,
        [
            shape(STEPS, EX * EY, BZ),
            shape(STEPS, EY, BZ),
            shape(STEPS - 1, EX * EY, BZ),
            shape(STEPS - 1, EY, BZ),
        ],
        [receivers, sources],
    )
    r = r.reshape(STEPS, EX, EY, BZ)
    s = s.reshape(STEPS - 1, EX, EY, BZ)
    adjoint_start, hist, coef, coef_strip = call(
        adjoint_kernel,
        [
            shape(4, BX, BY, BZ),
            shape(STEPS, 4, BX, BY, BZ),
            shape(3, EX, EY, BZ),
            shape(3, EY, BZ),
        ],
        [al, al_low, al_high, xa, xa_low, xa_high, r, rs, tissue],
        scratch=[
            pltpu.VMEM((5, EX, EY, BZ), F32),
            pltpu.VMEM((3, 2, 5, 8, BZ), F32),
            pltpu.SemaphoreType.DMA,
        ],
        any_operands=range(6),
        smem_operands=(8,),
    )
    (gradient,) = call(
        forward_kernel,
        [shape(2, BX, BY, BZ)],
        [gathered, gathered_x, coef, coef_strip, s, ss, hist],
        scratch=[
            pltpu.VMEM((4, EX, EY, BZ), F32),
            pltpu.VMEM((3, 5, 8, BZ), F32),
            pltpu.SemaphoreType.DMA,
        ],
        any_operands=range(2),
    )
    return gradient, adjoint_start


def solution(mesh):
    return jax.shard_map(
        local,
        mesh=mesh,
        in_specs=(
            P("shot", "gx", "gy", "gz"),
            P("shot", "gx", "gy", "gz"),
            P("gx", "gy", "gz"),
            P(),
            P("shot", None),
            P(None, "shot"),
            P(),
            P(None, "shot"),
        ),
        out_specs=(P("shot", "gx", "gy", "gz"), P("shot", "gx", "gy", "gz")),
        check_vma=False,
    )
```

time: 275 us -> 76 us (0.28)
  the two profiles are of different devices: /device:TPU:8 before, /device:TPU:0 now
where the time goes in v1:
time: 76 us; the launch traced here: 75.4 us
  blocking collectives  24.7 us (32%)
  starting transfers between devices  14.3 us (19%)
  between operations  14.2 us (19%)
  Pallas kernels  11.6 us (15%)
  local copies, waits for them, and re-layouts  9.82 us (13%)
    all_gather x1, blocking collectives, local(): gathered_x = lax.all_gather(xw, 'gx')  24.7 us
    pallas_call x5, Pallas kernels, call(): pl.pallas_call(kernel, out_shape=outs, in_specs=[spec(index) for index in...  11.6 us
    unnamed x30, local copies, waits for them, and re-layouts  9.82 us
    ppermute x2, starting transfers between devices, along_x(): lax.ppermute(array, 'gx', forward)  9.49 us
    ppermute x2, starting transfers between devices, along_x(): lax.ppermute(array, 'gx', backward)  2.58 us
    ppermute x2, starting transfers between devices, from_sides(): both = lax.ppermute(array, axes, route(1) + route(-1))  1.56 us
  transfers between devices with their start and end apart: 8, of which 0 were waited for; matrix products, arithmetic and copies ran while one was open for 0% of the time, Pallas kernels for 11%

profile of v1, /device:TPU:0, one launch (start us, length us, event | category | flops | bytes accessed | tf_op | source)
XLA Modules:
  0.0 75.4 jit_solution(11269679222070750816)
XLA Ops:
  7.2 0.0 all-gather.4.cloned.1.call-start
  7.2 0.7 all-gather.4.cloned.1.call-update
  7.9 0.2 copy-done
  8.1 0.9 %copy-done.4 = f32[4,4,32,128]{3,2,1,0:T(8,128)S(1)} copy-done((f32[4,4,32,128]{3,2,1,0:T(8,128)S(1)}, f32[4,4,32,128]{3,2,1,0:T(8,128)}, u32[]{:S(2)}) %copy-start.4) | copy-done | bytes 262168
  9.1 0.8 %copy-done.5 = s32[4,32,128]{2,1,0:T(8,128)S(1)} copy-done((s32[4,32,128]{2,1,0:T(8,128)S(1)}, s32[4,32,128]{2,1,0:T(8,128)}, u32[]{:S(2)}) %copy-start.5) | copy-done | bytes 65560
  9.9 0.2 shard_map.95
  10.1 0.0 copy-start.11
  10.1 4.9 %collective-permute-start.3 = (f32[5,4,32,128]{3,2,1,0:T(8,128)S(1)}, f32[5,4,32,128]{3,2,1,0:T(8,128)S(1)}, u32[]{:S(2)}, u32[]{:S(2)}) collective-permute-start(f32[5,4,32,128]{3,2,1,0:T(8,128)S(1)} %get-tuple-element.18.al), channel_id=1, source_target_pairs={{0,4},{4,8},{8,12},{1,5},{5,9},{9,13},{2,6},{6,10},{10,14},{3,7},{... | collective-permute-start | bytes 983048 | tf_op jit(solution)/shard_map/ppermute | solution.py:416
  15.1 1.3 %collective-permute-start.4 = (f32[5,4,32,128]{3,2,1,0:T(8,128)S(1)}, f32[5,4,32,128]{3,2,1,0:T(8,128)S(1)}, u32[]{:S(2)}, u32[]{:S(2)}) collective-permute-start(f32[5,4,32,128]{3,2,1,0:T(8,128)S(1)} %get-tuple-element.18.al), channel_id=1, source_target_pairs={{4,0},{8,4},{12,8},{5,1},{9,5},{13,9},{6,2},{10,6},{14,10},{7,3},{... | collective-permute-start | bytes 983048 | tf_op jit(solution)/shard_map/ppermute | solution.py:416
  16.4 1.6 %collective-permute-start = (f32[39,8,128]{2,1,0:T(8,128)S(1)}, f32[39,8,128]{2,1,0:T(8,128)S(1)}, u32[]{:S(2)}, u32[]{:S(2)}) collective-permute-start(f32[39,8,128]{2,1,0:T(8,128)S(1)} %get-tuple-element.15), channel_id=1, source_target_pairs={{2,0},{0,2},{3,1},{1,3},{6,4},{4,6},{7,5},{5,7},{10,8},{8,10},{11,... | collective-permute-start | bytes 479240 | tf_op jit(solution)/shard_map/ppermute | solution.py:406
  18.0 0.6 collective-permute-start.1
  18.6 0.1 copy-done.12
  18.7 0.7 copy-done.13
  19.4 0.7 copy-done.14
  20.1 4.6 %shard_map.97 = (f32[4,480,128]{2,1,0:T(8,128)S(1)}, f32[4,40,128]{2,1,0:T(8,128)S(1)}, f32[3,480,128]{2,1,0:T(8,128)S(1)}, f32[3,40,128]{2,1,0:T(8,128)S(1)}) custom-call(f32[8,1024]{1,0:T(8,128)S(1)} %select_maximum_fusion.receivers_ref, f32[8,128]{1,0:T(8,128)S(1)} %select_maximum_fusion.1.sources_ref), custom_call_target="tpu_custom_call" | custom-call | flops 16777216 | bytes 1048576 | tf_op jit(solution)/shard_map/pallas_call | solution.py:380
  24.7 0.0 collective-permute-done
  24.7 0.5 copy-done.6
  25.2 0.0 collective-permute-done.1.other_ref
  25.3 4.5 %collective-permute-start.5 = (f32[30,8,128]{2,1,0:T(8,128)S(1)}, f32[30,8,128]{2,1,0:T(8,128)S(1)}, u32[]{:S(2)}, u32[]{:S(2)}) collective-permute-start(f32[30,8,128]{2,1,0:T(8,128)S(1)} %get-tuple-element.19.xa), channel_id=1, source_target_pairs={{0,4},{4,8},{8,12},{1,5},{5,9},{9,13},{2,6},{6,10},{10,14},{3,7},{... | collective-permute-start | bytes 368648 | tf_op jit(solution)/shard_map/ppermute | solution.py:416
  29.8 1.3 %collective-permute-start.6 = (f32[30,8,128]{2,1,0:T(8,128)S(1)}, f32[30,8,128]{2,1,0:T(8,128)S(1)}, u32[]{:S(2)}, u32[]{:S(2)}) collective-permute-start(f32[30,8,128]{2,1,0:T(8,128)S(1)} %get-tuple-element.19.xa), channel_id=1, source_target_pairs={{4,0},{8,4},{12,8},{5,1},{9,5},{13,9},{6,2},{10,6},{14,10},{7,3},{... | collective-permute-start | bytes 368648 | tf_op jit(solution)/shard_map/ppermute | solution.py:416
  31.1 24.7 %all-gather.1 = f32[84,8,128]{2,1,0:T(8,128)S(1)} all-gather(f32[21,8,128]{2,1,0:T(8,128)S(1)} %get-tuple-element.17), channel_id=3, replica_groups=mesh['shot'=2,'gx'=4,'gy'=2,'gz'=2] {'gx'}, dimensions={0}, use_global_device_ids=true | all-gather | bytes 430080 | tf_op jit(solution)/shard_map/all_gather | solution.py:444
  55.9 0.0 collective-permute-done.3.al_low
  55.9 0.7 copy-done.2
  56.6 0.7 copy-done.10
  57.3 1.0 %copy-done.3 = f32[5,4,32,128]{3,2,1,0:T(8,128)S(1)} copy-done((f32[5,4,32,128]{3,2,1,0:T(8,128)S(1)}, f32[5,4,32,128]{3,2,1,0:T(8,128)}, u32[]{:S(2)}) %copy-start.3) | copy-done | bytes 327704
  58.3 3.7 %shard_map.98 = (f32[4,4,32,128]{3,2,1,0:T(8,128)}, f32[4,4,4,32,128]{4,3,2,1,0:T(8,128)S(1)}, f32[3,12,40,128]{3,2,1,0:T(8,128)S(1)}, f32[3,40,128]{2,1,0:T(8,128)S(1)}) custom-call(f32[5,4,32,128]{3,2,1,0:T(8,128)S(1)} %get-tuple-element.18.al, f32[5,4,32,128]{3,2,1,0:T(8,128)S(1)} %collective-permute-done.3.al_low, f32[5,4,32,128]{3,2,1,0:T(8,128)S(1)} %copy-done.3, ...), custom_call_target="tpu_custom_call" | custom-call | flops 16777216 | bytes 1048576 | tf_op jit(solution)/shard_map/pallas_call | solution.py:380
  62.0 0.0 copy-start.8
  62.0 0.6 copy-done.8
  62.6 1.2 %copy-done.1 = f32[16,4,32,128]{3,2,1,0:T(8,128)S(1)} copy-done((f32[16,4,32,128]{3,2,1,0:T(8,128)S(1)}, f32[16,4,32,128]{3,2,1,0:T(8,128)}, u32[]{:S(2)}) %copy-start.1) | copy-done | bytes 1048600
  63.9 0.8 %copy-done.7 = f32[3,40,128]{2,1,0:T(8,128)S(1)} copy-done((f32[3,40,128]{2,1,0:T(8,128)S(1)}, f32[3,40,128]{2,1,0:T(8,128)}, u32[]{:S(2)}) %copy-start.7) | copy-done | bytes 61464
  64.7 0.8 %copy-done.9 = f32[3,40,128]{2,1,0:T(8,128)S(1)} copy-done((f32[3,40,128]{2,1,0:T(8,128)S(1)}, f32[3,40,128]{2,1,0:T(8,128)}, u32[]{:S(2)}) %copy-start.9) | copy-done | bytes 61464
  65.5 3.0 %shard_map.99 = f32[2,4,32,128]{3,2,1,0:T(8,128)} custom-call(f32[4,4,4,32,128]{4,3,2,1,0:T(8,128)S(1)} %bitcast.9, f32[4,21,8,128]{3,2,1,0:T(8,128)S(1)} %bitcast.8, f32[3,12,40,128]{3,2,1,0:T(8,128)S(1)} %get-tuple-element.22.coef_ref, f32[3,40,128]{2,1,0:T(8,128)S(1)} %copy-done.9, f32[3,12,40,128]{3,2,1,0:T(8,128)S(1)} %bitcast.11, ...), custom_call_target="tpu_custom_call" | custom-call | flops 16777216 | bytes 1048576 | tf_op jit(solution)/shard_map/pallas_call | solution.py:380
  (28 shorter events, 0.1 us)
Async XLA Ops:
  7.2 1.0 %copy-start = (f32[4,4,32,128]{3,2,1,0:T(8,128)S(1)}, f32[4,4,32,128]{3,2,1,0:T(8,128)}, u32[]{:S(2)}) copy-start(f32[4,4,32,128]{3,2,1,0:T(8,128)} %stored_ref.1) | copy-start | bytes 786436
  7.2 55.5 %all-gather.4.cloned.1.call-start = ((), (), s32[]{:S(2)}) async-start(), calls=%async_computation | async-start | bytes 1310720 | tf_op jit(solution)/shard_map/all_gather | solution.py:429
  8.1 0.9 %copy-start.4 = (f32[4,4,32,128]{3,2,1,0:T(8,128)S(1)}, f32[4,4,32,128]{3,2,1,0:T(8,128)}, u32[]{:S(2)}) copy-start(f32[4,4,32,128]{3,2,1,0:T(8,128)} %adj_ref.1) | copy-start | bytes 786436
  9.1 0.8 %copy-start.5 = (s32[4,32,128]{2,1,0:T(8,128)S(1)}, s32[4,32,128]{2,1,0:T(8,128)}, u32[]{:S(2)}) copy-start(s32[4,32,128]{2,1,0:T(8,128)} %lab_ref.1) | copy-start | bytes 196612
  10.1 8.5 %copy-start.11 = (s32[1024,3]{0,1:T(4,128)S(1)}, s32[1024,3]{0,1:T(4,128)}, u32[]{:S(2)}) copy-start(s32[1024,3]{0,1:T(4,128)} %param.14) | copy-start | bytes 36868
  10.1 45.7 %collective-permute-start.3 = (f32[5,4,32,128]{3,2,1,0:T(8,128)S(1)}, f32[5,4,32,128]{3,2,1,0:T(8,128)S(1)}, u32[]{:S(2)}, u32[]{:S(2)}) collective-permute-start(f32[5,4,32,128]{3,2,1,0:T(8,128)S(1)} %get-tuple-element.18.al), channel_id=1, source_target_pairs={{0,4},{4,8},{8,12},{1,5},{5,9},{9,13},{2,6},{6,10},{10,14},{3,7},{... | collective-permute-start | bytes 983048 | tf_op jit(solution)/shard_map/ppermute | solution.py:416
  15.1 40.8 %collective-permute-start.4 = (f32[5,4,32,128]{3,2,1,0:T(8,128)S(1)}, f32[5,4,32,128]{3,2,1,0:T(8,128)S(1)}, u32[]{:S(2)}, u32[]{:S(2)}) collective-permute-start(f32[5,4,32,128]{3,2,1,0:T(8,128)S(1)} %get-tuple-element.18.al), channel_id=1, source_target_pairs={{4,0},{8,4},{12,8},{5,1},{9,5},{13,9},{6,2},{10,6},{14,10},{7,3},{... | collective-permute-start | bytes 983048 | tf_op jit(solution)/shard_map/ppermute | solution.py:416
  16.4 8.3 %collective-permute-start = (f32[39,8,128]{2,1,0:T(8,128)S(1)}, f32[39,8,128]{2,1,0:T(8,128)S(1)}, u32[]{:S(2)}, u32[]{:S(2)}) collective-permute-start(f32[39,8,128]{2,1,0:T(8,128)S(1)} %get-tuple-element.15), channel_id=1, source_target_pairs={{2,0},{0,2},{3,1},{1,3},{6,4},{4,6},{7,5},{5,7},{10,8},{8,10},{11,... | collective-permute-start | bytes 479240 | tf_op jit(solution)/shard_map/ppermute | solution.py:406
  18.0 6.7 %collective-permute-start.2 = (f32[3,8,128]{2,1,0:T(8,128)S(1)}, f32[3,8,128]{2,1,0:T(8,128)S(1)}, u32[]{:S(2)}, u32[]{:S(2)}) collective-permute-start(f32[3,8,128]{2,1,0:T(8,128)S(1)} %slice.3), channel_id=1, source_target_pairs={{2,1},{3,0},{0,3},{1,2},{6,5},{7,4},{4,7},{5,6},{10,9},{11,8},{8,1... | collective-permute-start | bytes 36872 | tf_op jit(solution)/shard_map/ppermute | solution.py:406
  18.0 0.7 copy-start.12
  18.0 7.3 %collective-permute-start.1 = (f32[3,32,128]{2,1,0:T(8,128)S(1)}, f32[3,32,128]{2,1,0:T(8,128)S(1)}, u32[]{:S(2)}, u32[]{:S(2)}) collective-permute-start(f32[3,32,128]{2,1,0:T(8,128)S(1)} %get-tuple-element.16.strip_ref), channel_id=1, source_target_pairs={{0,1},{1,0},{2,3},{3,2},{4,5},{5,4},{6,7},{7,6},{8,9},{9,8},{10,11... | collective-permute-start | bytes 147464 | tf_op jit(solution)/shard_map/ppermute | solution.py:436
  18.7 0.7 copy-start.13
  19.4 0.7 copy-start.14
  24.6 0.6 copy-start.6
  25.3 30.6 %collective-permute-start.5 = (f32[30,8,128]{2,1,0:T(8,128)S(1)}, f32[30,8,128]{2,1,0:T(8,128)S(1)}, u32[]{:S(2)}, u32[]{:S(2)}) collective-permute-start(f32[30,8,128]{2,1,0:T(8,128)S(1)} %get-tuple-element.19.xa), channel_id=1, source_target_pairs={{0,4},{4,8},{8,12},{1,5},{5,9},{9,13},{2,6},{6,10},{10,14},{3,7},{... | collective-permute-start | bytes 368648 | tf_op jit(solution)/shard_map/ppermute | solution.py:416
  29.8 26.1 %collective-permute-start.6 = (f32[30,8,128]{2,1,0:T(8,128)S(1)}, f32[30,8,128]{2,1,0:T(8,128)S(1)}, u32[]{:S(2)}, u32[]{:S(2)}) collective-permute-start(f32[30,8,128]{2,1,0:T(8,128)S(1)} %get-tuple-element.19.xa), channel_id=1, source_target_pairs={{4,0},{8,4},{12,8},{5,1},{9,5},{13,9},{6,2},{10,6},{14,10},{7,3},{... | collective-permute-start | bytes 368648 | tf_op jit(solution)/shard_map/ppermute | solution.py:416
  55.9 0.7 copy-start.2
  56.6 0.7 copy-start.10
  57.3 1.0 %copy-start.3 = (f32[5,4,32,128]{3,2,1,0:T(8,128)S(1)}, f32[5,4,32,128]{3,2,1,0:T(8,128)}, u32[]{:S(2)}) copy-start(f32[5,4,32,128]{3,2,1,0:T(8,128)} %copy-done.2) | copy-start | bytes 983044
  62.0 0.6 copy-start.8
  62.6 1.2 %copy-start.1 = (f32[16,4,32,128]{3,2,1,0:T(8,128)S(1)}, f32[16,4,32,128]{3,2,1,0:T(8,128)}, u32[]{:S(2)}) copy-start(f32[16,4,32,128]{3,2,1,0:T(8,128)} %all-gather.4.cloned.1.call-done) | copy-start | bytes 3145732
  63.9 0.8 %copy-start.7 = (f32[3,40,128]{2,1,0:T(8,128)S(1)}, f32[3,40,128]{2,1,0:T(8,128)}, u32[]{:S(2)}) copy-start(f32[3,40,128]{2,1,0:T(8,128)} %copy-done.6) | copy-start | bytes 184324
  64.7 0.8 %copy-start.9 = (f32[3,40,128]{2,1,0:T(8,128)S(1)}, f32[3,40,128]{2,1,0:T(8,128)}, u32[]{:S(2)}) copy-start(f32[3,40,128]{2,1,0:T(8,128)} %copy-done.8) | copy-start | bytes 184324
Sparse Core Ops, SparseCore 0:
  9.6 39.0 all-gather.3

commit v2 on v1

v2 whole, which is shorter than its diff:
```python
import jax
import jax.numpy as jnp
from jax import lax
from jax.experimental import pallas as pl
from jax.experimental.pallas import tpu as pltpu
from jax.sharding import PartitionSpec as P

STEPS = 4
MARGIN = 4
BX, BY, BZ = 4, 32, 128
EX, EY = BX + 2 * MARGIN, BY + 2 * MARGIN
STRIP = 2 * MARGIN
F32 = jnp.float32
BF16 = jnp.bfloat16
VMEM_LIMIT = 16 * 1024 * 1024
OWN_ROWS = BX * BY + 2 * BX * 8 + EY
ADJ_ROWS_OWN = BX * BY + 3 * BX * 8 + EY
WAVE_ROWS = 3 * BY + 5 * 8 + EY
ADJ_ROWS = 3 * BY + 8 * 8 + EY


def lanes(shape):
    return lax.broadcasted_iota(jnp.int32, shape, len(shape) - 1)


def rows(shape):
    return lax.broadcasted_iota(jnp.int32, shape, len(shape) - 2)


def run(copies):
    for copy in copies:
        copy.start()
    for copy in copies:
        copy.wait()


def class_values(tissue_ref, index):
    speed = jnp.full((1, BZ), tissue_ref[0, index], F32)
    density = jnp.full((1, BZ), tissue_ref[1, index], F32)
    damping = 1.0 - jnp.full((1, BZ), tissue_ref[2, index], F32)
    return density * speed, speed / density, damping


def buoyancy_of(labels, tissue_ref):
    result = jnp.zeros(labels.shape, F32)
    for index in range(tissue_ref.shape[1]):
        result = jnp.where(labels == float(index + 1), class_values(tissue_ref, index)[1], result)
    return result


def coefficients(labels, tissue_ref):
    stiffness = jnp.zeros(labels.shape, F32)
    buoyancy = jnp.zeros(labels.shape, F32)
    damping = jnp.zeros(labels.shape, F32)
    for index in range(tissue_ref.shape[1]):
        picked = labels == float(index + 1)
        values = class_values(tissue_ref, index)
        stiffness = jnp.where(picked, values[0], stiffness)
        buoyancy = jnp.where(picked, values[1], buoyancy)
        damping = jnp.where(picked, values[2], damping)
    return stiffness, buoyancy, damping


def face_kernel(
    stored_hbm, adj_hbm, lab_hbm, tissue_hbm,
    p_ref, ql_ref, face_x_ref, face_y_ref, face_z_ref,
    stored, adj, lab, tissue, sem,
):
    run([
        pltpu.make_async_copy(stored_hbm, stored, sem),
        pltpu.make_async_copy(adj_hbm, adj, sem),
        pltpu.make_async_copy(lab_hbm, lab, sem),
        pltpu.make_async_copy(tissue_hbm, tissue, sem),
    ])
    lane = lanes((BY, BZ))
    row = rows((8, BZ))
    face_y = jnp.zeros((8, BZ), F32)
    face_z = jnp.zeros((BY, BZ), F32)
    for x in range(BX):
        labels = lab[x].astype(F32) + 1.0
        buoyancy = buoyancy_of(labels, tissue)
        plane = slice(x * BY, x * BY + BY)
        p_ref[plane] = stored[0, x]
        ql_ref[plane] = adj[0, x]
        ql_ref[x * BY + BX * BY : (x + 1) * BY + BX * BY] = labels
        for kind, (v, factor) in enumerate(((stored, None), (adj, buoyancy))):
            vx, vy, vz = v[1, x], v[2, x, BY - 8 : BY], v[3, x]
            if factor is not None:
                vx, vy, vz = factor * vx, factor[BY - 8 : BY] * vy, factor * vz
            if x == BX - 1:
                face_x_ref[kind * BY : kind * BY + BY] = vx
            index = kind * BX + x
            face_y = jnp.where(row == index, pltpu.roll(vy, (index + 1) % 8, 0), face_y)
            face_z = jnp.where(lane == index, pltpu.roll(vz, index + 1, 1), face_z)
    face_y_ref[...] = face_y
    face_z_ref[...] = face_z


def pack_kernel(
    stored_hbm, adj_hbm, lab_hbm, tissue_hbm, face_x, face_y, face_z,
    s_ref, t_ref, edge_ref, corner_ref, strip_ref,
    stored, adj, lab, tissue, sem,
):
    run([
        pltpu.make_async_copy(stored_hbm, stored, sem),
        pltpu.make_async_copy(adj_hbm, adj, sem),
        pltpu.make_async_copy(lab_hbm, lab, sem),
        pltpu.make_async_copy(tissue_hbm, tissue, sem),
    ])
    gx, gy, gz = (lax.axis_index(name) for name in ("gx", "gy", "gz"))
    count = lax.axis_size("gx")
    lane = lanes((BY, BZ))
    row = rows((BY, BZ))
    tile_row = rows((8, BZ))
    below = (
        jnp.where(gx == count // 2, 0.0, 1.0),
        jnp.where(gx == 0, 0.0, 1.0),
    )
    has_y = jnp.where(gy == 0, 0.0, 1.0)
    has_z = jnp.where(gz == 0, 0.0, 1.0)
    planes = [[None] * BX for _ in range(5)]
    previous = [face_x[kind * BY : kind * BY + BY] * below[kind] for kind in range(2)]
    tile_y = face_y[...] * has_y
    tile_z = face_z[...] * has_z
    for x in range(BX):
        labels = lab[x].astype(F32) + 1.0
        buoyancy = buoyancy_of(labels, tissue)
        planes[0][x] = stored[0, x]
        planes[2][x] = adj[0, x]
        planes[4][x] = labels
        for kind, v in enumerate((stored, adj)):
            vx, vy, vz = v[1, x], v[2, x], v[3, x]
            if kind == 1:
                vx, vy, vz = buoyancy * vx, buoyancy * vy, buoyancy * vz
            index = kind * BX + x
            row_below = tile_y[index : index + 1]
            lane_below = pltpu.roll(tile_z, (BZ - index) % BZ, 1) if index else tile_z
            y_below = jnp.where(row == 0, row_below, pltpu.roll(vy, 1, 0))
            z_below = jnp.where(lane == 0, lane_below, pltpu.roll(vz, 1, 1))
            spread = ((vx - previous[kind]) + (vy - y_below)) + (vz - z_below)
            previous[kind] = vx
            (s_ref, t_ref)[kind][x * BY : x * BY + BY] = spread
            planes[1 + 2 * kind][x] = spread

    strips = [jnp.zeros((BY, BZ), F32) for _ in range(2)]
    for field in range(5):
        group, slot = (0, field) if field < 2 else (1, field - 2)
        for x in range(BX):
            block = planes[field][x]
            tile = jnp.where(tile_row < MARGIN, block[0:8], block[BY - 8 : BY])
            index = field * BX + x
            edge_ref[index * 8 : index * 8 + 8] = tile
            base = slot * BX * STRIP + x * STRIP
            rolled = pltpu.roll(block, base + MARGIN, 1)
            first = base + MARGIN * gz
            strips[group] = jnp.where(
                (lane >= first) & (lane < first + MARGIN), rolled, strips[group]
            )
    for group in range(2):
        strip = strips[group]
        strip_ref[group * BY : group * BY + BY] = strip
        tile = jnp.where(tile_row < MARGIN, strip[0:8], strip[BY - 8 : BY])
        index = 5 * BX + group
        edge_ref[index * 8 : index * 8 + 8] = tile
        corner_ref[group * 8 : group * 8 + 8] = tile


def merge_kernel(
    up_ref, down_ref, strip_ref, other_ref, corner_up_ref, corner_down_ref, s_ref, t_ref,
    own_ref, high_ref, low_ref, adj_own_ref, even_ref, odd_ref,
    halo_ref,
):
    gx, gy = lax.axis_index("gx"), lax.axis_index("gy")
    row = rows((8, BZ))
    take_up = (row < MARGIN) & (gy < lax.axis_size("gy") - 1)
    take_down = (row >= MARGIN) & (gy > 0)

    def halo(up, down, index):
        sl = slice(index * 8, index * 8 + 8)
        return jnp.where(take_up, up[sl], jnp.where(take_down, down[sl], 0.0))

    for index in range(5 * BX):
        halo_ref[index] = halo(up_ref, down_ref, index)
    own_ref[0 : BX * BY] = s_ref[...]
    for index in range(2 * BX):
        start = BX * BY + index * 8
        own_ref[start : start + 8] = halo_ref[index]
    high_ref[0 : 3 * BY] = s_ref[0 : 3 * BY]
    low_ref[0 : 3 * BY] = s_ref[BY : 4 * BY]
    for place, (high, low) in enumerate(((0, 1), (1, 2), (2, 3), (4, 6), (5, 7))):
        start = 3 * BY + place * 8
        high_ref[start : start + 8] = halo_ref[high]
        low_ref[start : start + 8] = halo_ref[low]
    adj_own_ref[0 : BX * BY] = t_ref[...]
    for index in range(3 * BX):
        start = BX * BY + index * 8
        adj_own_ref[start : start + 8] = halo_ref[2 * BX + index]
    parity = lax.rem(gx, 2)
    for first, target in ((1 - parity, even_ref), (parity, odd_ref)):
        for place in range(3):
            target[place * BY : place * BY + BY] = t_ref[
                pl.ds(pl.multiple_of((first + place) * BY, BY), BY)
            ]
        indices = [2 * BX + first, 2 * BX + first + 1, 2 * BX + first + 2]
        indices += [3 * BX + 2 * first, 3 * BX + 2 * first + 1]
        indices += [4 * BX + first, 4 * BX + first + 1, 4 * BX + first + 2]
        for place, index in enumerate(indices):
            start = 3 * BY + place * 8
            target[start : start + 8] = halo_ref[index]
    for group, targets in enumerate(((own_ref, high_ref, low_ref), (adj_own_ref, even_ref, odd_ref))):
        strip = strip_ref[group * BY : group * BY + BY] + other_ref[group * BY : group * BY + BY]
        tile = halo(up_ref, down_ref, 5 * BX + group) + halo(corner_up_ref, corner_down_ref, group)
        for target in targets:
            start = target.shape[0] - EY
            target[start : start + BY] = strip
            target[start + BY : start + EY] = tile


def split(values):
    high = values.astype(BF16)
    rest = values - high.astype(F32)
    middle = rest.astype(BF16)
    low = (rest - middle.astype(F32)).astype(BF16)
    return high, middle, low


def inject_points(cells, wave_ref, width, out_ref, strip_out_ref, waves):
    gx, gy, gz = (lax.axis_index(name) for name in ("gx", "gy", "gz"))
    cut = BZ * lax.axis_size("gz") // 2 - MARGIN
    for start in range(0, cells.shape[1], width):
        sl = slice(start, start + width)
        cell_x = cells[0:1, sl] - (gx * BX - MARGIN)
        cell_y = cells[1:2, sl] - gy * BY
        cell_z = cells[2:3, sl]
        in_x = (cell_x >= 0) & (cell_x < EX)
        in_y = (cell_y >= -MARGIN) & (cell_y < BY + MARGIN)
        row = jnp.where(cell_y < 0, cell_y + EY, cell_y)
        flat = jnp.where(in_x & in_y, cell_x * EY + row, -1)
        row = jnp.where(in_y, row, -1)
        zz = cell_z - cut
        in_strip = in_x & (zz >= 0) & (zz < STRIP)
        strip_lane = jnp.where(in_strip, cell_x * STRIP + zz, -1)
        here = (rows((EX * EY, width)) == flat).astype(F32).astype(BF16)
        at_z = rows((BZ, width)) == (cell_z - gz * BZ)
        at_strip = (rows((BZ, width)) == strip_lane).astype(F32).astype(BF16)
        at_row = rows((EY, width)) == row
        for wave in range(waves):
            total = None
            strip_total = None
            for part in split(wave_ref[wave : wave + 1, sl]):
                part = part.astype(F32)
                term = lax.dot_general(
                    here,
                    jnp.where(at_z, part, 0.0).astype(BF16),
                    (((1,), (1,)), ((), ())),
                    preferred_element_type=F32,
                )
                total = term if total is None else total + term
                term = lax.dot_general(
                    jnp.where(at_row, part, 0.0).astype(BF16),
                    at_strip,
                    (((1,), (1,)), ((), ())),
                    preferred_element_type=F32,
                )
                strip_total = term if strip_total is None else strip_total + term
            if start > 0:
                total = total + out_ref[wave]
                strip_total = strip_total + strip_out_ref[wave]
            out_ref[wave] = total
            strip_out_ref[wave] = strip_total


def inject_kernel(
    receiver_hbm, receiver_wave_hbm, source_hbm, source_wave_hbm,
    r_ref, rs_ref, s_ref, ss_ref,
    receivers, receiver_wave, sources, source_wave, sem,
):
    run([
        pltpu.make_async_copy(receiver_hbm, receivers, sem),
        pltpu.make_async_copy(receiver_wave_hbm, receiver_wave, sem),
        pltpu.make_async_copy(source_hbm, sources, sem),
        pltpu.make_async_copy(source_wave_hbm, source_wave, sem),
    ])
    inject_points(receivers, receiver_wave, 256, r_ref, rs_ref, STEPS)
    inject_points(sources, source_wave, sources.shape[1], s_ref, ss_ref, STEPS - 1)


def strip_of(packed, block, slot):
    lane = lanes(packed.shape)
    width = BX * STRIP
    shift = (block * width - slot * width) % BZ
    moved = pltpu.roll(packed, shift, 1) if shift else packed
    return jnp.where((lane >= block * width) & (lane < (block + 1) * width), moved, 0.0)


def y_up(v):
    return pltpu.roll(v, EY - 1, 0)


def y_down(v):
    return pltpu.roll(v, 1, 0)


def z_up(v, strip, x):
    edge = pltpu.roll(strip, (BZ - 1 - (x * STRIP + MARGIN)) % BZ, 1)
    return jnp.where(lanes(v.shape) == BZ - 1, edge, pltpu.roll(v, BZ - 1, 1))


def z_down(v, strip, x):
    edge = pltpu.roll(strip, (BZ - (x * STRIP + MARGIN - 1)) % BZ, 1)
    return jnp.where(lanes(v.shape) == 0, edge, pltpu.roll(v, 1, 1))


def strip_flux(values, buoyancy):
    flux_x = buoyancy * (pltpu.roll(values, BZ - STRIP, 1) - values)
    flux_y = buoyancy * (y_up(values) - values)
    flux_z = buoyancy * (pltpu.roll(values, BZ - 1, 1) - values)
    spread = (flux_x - pltpu.roll(flux_x, STRIP, 1)) + (flux_y - y_down(flux_y))
    return flux_z, spread + (flux_z - pltpu.roll(flux_z, 1, 1))


def cut_flags():
    gz, half = lax.axis_index("gz"), lax.axis_size("gz") // 2
    return jnp.where(gz == half - 1, 1.0, 0.0), jnp.where(gz == half, 1.0, 0.0)


def adjoint_kernel(
    ql, ql_even, ql_odd, late, late_even, late_odd, adj_hbm, r_ref, rs_ref, tissue_hbm,
    out_ref, hist_ref, coef_ref, coef_strip_ref,
    field, strip, tissue, sem,
):
    gx, count = lax.axis_index("gx"), lax.axis_size("gx")
    cut_up, cut_down = cut_flags()

    def plane_copies(source, first, rows_of, index, planes):
        return [
            pltpu.make_async_copy(
                source.at[pl.ds(first + i * rows_of, rows_of)],
                field.at[index, plane, pl.ds(0 if rows_of == BY else BY, rows_of), :],
                sem,
            )
            for i, plane in enumerate(planes)
        ]

    def own_copies():
        planes = range(BX, 2 * BX)
        copies = [
            pltpu.make_async_copy(adj_hbm.at[pl.ds(1, 3)], out_ref.at[pl.ds(1, 3)], sem),
            pltpu.make_async_copy(tissue_hbm, tissue, sem),
            pltpu.make_async_copy(late.at[pl.ds(ADJ_ROWS_OWN - EY, EY)], strip.at[1], sem),
        ]
        copies += plane_copies(ql, 0, BY, 0, planes) + plane_copies(ql, BX * BY, BY, 2, planes)
        copies += plane_copies(late, 0, BY, 1, planes)
        for index in range(3):
            copies += plane_copies(late, BX * BY + index * BX * 8, 8, index, planes)
        return copies

    def side_copies(raw, extra, block):
        first = 1 if block == 0 else 2 * BX
        planes = range(block * BX, block * BX + BX)
        copies = [pltpu.make_async_copy(extra.at[pl.ds(ADJ_ROWS - EY, EY)], strip.at[block], sem)]
        copies += plane_copies(raw, 0, BY, 0, planes) + plane_copies(raw, BX * BY, BY, 2, planes)
        copies += plane_copies(extra, 0, BY, 1, range(first, first + 3))
        copies += plane_copies(extra, 3 * BY, 8, 0, range(first, first + 3))
        near = first + 1 if block == 0 else first
        copies += plane_copies(extra, 3 * BY + 24, 8, 1, range(near, near + 2))
        copies += plane_copies(extra, 3 * BY + 40, 8, 2, range(first, first + 3))
        return copies

    def clear(block):
        planes = slice(block * BX, block * BX + BX)
        field[:, planes] = jnp.zeros((3, BX, EY, BZ), F32)
        strip[block] = jnp.zeros((EY, BZ), F32)

    def both(even, act):
        for raw, extra, block in (
            (ql_even, late_even, 2 if even else 0),
            (ql_odd, late_odd, 0 if even else 2),
        ):
            inside = gx > 0 if block == 0 else gx < count - 1
            act(side_copies(raw, extra, block), inside, block)

    def start(copies, inside, block):
        @pl.when(inside)
        def _():
            for copy in copies:
                copy.start()

        @pl.when(jnp.logical_not(inside))
        def _():
            clear(block)

    def finish(copies, inside, block):
        @pl.when(inside)
        def _():
            for copy in copies:
                copy.wait()

    is_even = lax.rem(gx, 2) == 0
    for copy in own_copies():
        copy.start()
    for act in (start, finish):
        pl.when(is_even)(lambda: both(True, act))
        pl.when(jnp.logical_not(is_even))(lambda: both(False, act))
    for copy in own_copies():
        copy.wait()

    for x in range(EX):
        for index, values in enumerate(coefficients(field[2, x], tissue)):
            coef_ref[index, x] = values
    packed = [strip[block] for block in range(3)]
    q_s, t_s, label_s = (
        sum(strip_of(packed[block], block, slot) for block in range(3)) for slot in range(3)
    )
    stiff_s, buoy_s, damp_s = coefficients(label_s, tissue)
    coef_strip_ref[0], coef_strip_ref[1], coef_strip_ref[2] = stiff_s, buoy_s, damp_s

    for step in range(1, STEPS + 1):
        k = STEPS - step
        q_s = q_s + rs_ref[k]
        u_s = stiff_s * damp_s * q_s
        flux_s, spread = strip_flux(u_s, buoy_s)
        t_s = t_s + spread
        q_s = damp_s * q_s + t_s
        edge_up = u_s * cut_up
        edge_down = flux_s * cut_down

        def injected(x):
            value = field[0, x] + r_ref[k, x]
            return value, coef_ref[0, x] * coef_ref[2, x] * value

        flux_below = None
        q_now, u_now = injected(step - 1)
        for x in range(step - 1, EX - step):
            q_next, u_next = injected(x + 1)
            buoyancy = coef_ref[1, x]
            slope_x = u_next - u_now
            flux_x = buoyancy * slope_x
            if x >= step:
                slope_y = y_up(u_now) - u_now
                slope_z = z_up(u_now, edge_up, x) - u_now
                flux_y = buoyancy * slope_y
                flux_z = buoyancy * slope_z
                spread = (flux_x - flux_below) + (flux_y - y_down(flux_y))
                spread = spread + (flux_z - z_down(flux_z, edge_down, x))
                damped = coef_ref[2, x] * q_now
                if BX <= x < 2 * BX:
                    own = x - BX
                    hist_ref[k, 0, own] = damped[0:BY]
                    for index, slope in enumerate((slope_x, slope_y, slope_z)):
                        w = out_ref[1 + index, own] + slope[0:BY]
                        out_ref[1 + index, own] = w
                        hist_ref[k, 1 + index, own] = w
                t = field[1, x] + spread
                field[1, x] = t
                field[0, x] = damped + t
            flux_below = flux_x
            q_now, u_now = q_next, u_next

    for x in range(BX):
        out_ref[0, x] = field[0, BX + x, 0:BY]


def forward_kernel(
    p, p_high, p_low, late, late_high, late_low,
    coef_ref, coef_strip_ref, s_ref, ss_ref, hist_ref,
    grad_ref,
    field, strip, sem,
):
    gx, count = lax.axis_index("gx"), lax.axis_size("gx")
    cut_up, cut_down = cut_flags()

    def plane_copies(source, first, rows_of, index, planes):
        return [
            pltpu.make_async_copy(
                source.at[pl.ds(first + i * rows_of, rows_of)],
                field.at[index, plane, pl.ds(0 if rows_of == BY else BY, rows_of), :],
                sem,
            )
            for i, plane in enumerate(planes)
        ]

    def own_copies():
        planes = range(BX, 2 * BX)
        copies = [pltpu.make_async_copy(late.at[pl.ds(OWN_ROWS - EY, EY)], strip.at[1], sem)]
        copies += plane_copies(p, 0, BY, 0, planes) + plane_copies(late, 0, BY, 1, planes)
        for index in range(2):
            copies += plane_copies(late, BX * BY + index * BX * 8, 8, index, planes)
        return copies

    def side_copies(raw, extra, block):
        first = 1 if block == 0 else 2 * BX
        near = first + 1 if block == 0 else first
        copies = [pltpu.make_async_copy(extra.at[pl.ds(WAVE_ROWS - EY, EY)], strip.at[block], sem)]
        copies += plane_copies(raw, 0, BY, 0, range(block * BX, block * BX + BX))
        copies += plane_copies(extra, 0, BY, 1, range(first, first + 3))
        copies += plane_copies(extra, 3 * BY, 8, 0, range(first, first + 3))
        copies += plane_copies(extra, 3 * BY + 24, 8, 1, range(near, near + 2))
        return copies

    def clear(block):
        planes = slice(block * BX, block * BX + BX)
        field[:, planes] = jnp.zeros((2, BX, EY, BZ), F32)
        strip[block] = jnp.zeros((EY, BZ), F32)

    sides = ((p_low, late_low, 0, gx > 0), (p_high, late_high, 2, gx < count - 1))
    for copy in own_copies():
        copy.start()
    for raw, extra, block, inside in sides:

        @pl.when(inside)
        def _(raw=raw, extra=extra, block=block):
            for copy in side_copies(raw, extra, block):
                copy.start()

        @pl.when(jnp.logical_not(inside))
        def _(block=block):
            clear(block)

    for copy in own_copies():
        copy.wait()
    for raw, extra, block, inside in sides:

        @pl.when(inside)
        def _(raw=raw, extra=extra, block=block):
            for copy in side_copies(raw, extra, block):
                copy.wait()

    packed = [strip[block] for block in range(3)]
    p_s, s_s = (
        sum(strip_of(packed[block], block, slot) for block in range(3)) for slot in range(2)
    )
    stiff_s, buoy_s, damp_s = coef_strip_ref[0], coef_strip_ref[1], coef_strip_ref[2]

    for step in range(1, STEPS + 1):
        k = step - 1
        edge_up = p_s * cut_up
        flux_s, spread = strip_flux(p_s, buoy_s)
        edge_down = flux_s * cut_down
        if step < STEPS:
            s_s = s_s - spread
            p_s = damp_s * (p_s - stiff_s * s_s) + ss_ref[k]

        flux_below = None
        p_now = field[0, step - 1]
        for x in range(step - 1, EX - step):
            p_next = field[0, x + 1]
            buoyancy = coef_ref[1, x]
            slope_x = p_next - p_now
            flux_x = buoyancy * slope_x
            if x >= step:
                slope_y = y_up(p_now) - p_now
                slope_z = z_up(p_now, edge_up, x) - p_now
                flux_y = buoyancy * slope_y
                flux_z = buoyancy * slope_z
                spread = (flux_x - flux_below) + (flux_y - y_down(flux_y))
                spread = spread + (flux_z - z_down(flux_z, edge_down, x))
                spread = field[1, x] - spread
                if step < STEPS:
                    field[1, x] = spread
                    field[0, x] = (
                        coef_ref[2, x] * (p_now - coef_ref[0, x] * spread) + s_ref[k, x]
                    )
                if BX <= x < 2 * BX:
                    own = x - BX
                    term = hist_ref[k, 0, own] * spread[0:BY]
                    grad_ref[0, own] = -term if k == 0 else grad_ref[0, own] - term
                    term = hist_ref[k, 1, own] * slope_x[0:BY]
                    term = term + hist_ref[k, 2, own] * slope_y[0:BY]
                    term = term + hist_ref[k, 3, own] * slope_z[0:BY]
                    grad_ref[1, own] = -term if k == 0 else grad_ref[1, own] - term
            flux_below = flux_x
            p_now = p_next


def shape(*dims):
    return jax.ShapeDtypeStruct(dims, F32)


def call(kernel, outs, operands, scratch, places=""):
    spaces = {"h": pltpu.HBM, "a": pl.ANY, "v": pltpu.VMEM}
    return pl.pallas_call(
        kernel,
        out_shape=outs,
        in_specs=[pl.BlockSpec(memory_space=spaces[place]) for place in places],
        out_specs=[pl.BlockSpec(memory_space=pltpu.VMEM)] * len(outs),
        scratch_shapes=scratch,
        compiler_params=pltpu.CompilerParams(vmem_limit_bytes=VMEM_LIMIT),
        cost_estimate=pl.CostEstimate(flops=1 << 24, bytes_accessed=1 << 20, transcendentals=0),
    )(*operands)


def from_sides(array, axes):
    count = lax.axis_size("gy")

    def route(offset):
        pairs = []
        for target in range(count):
            source = target + offset
            if 0 <= source < count:
                if "gz" in axes:
                    pairs += [(2 * source + z, 2 * target + 1 - z) for z in range(2)]
                else:
                    pairs.append((source, target))
        return pairs

    if count == 2:
        both = lax.ppermute(array, axes, route(1) + route(-1))
        return both, both
    return lax.ppermute(array, axes, route(1)), lax.ppermute(array, axes, route(-1))


def rotated(array, axis, offset):
    count = lax.axis_size(axis)
    return lax.ppermute(array, axis, [((i + offset) % count, i) for i in range(count)])


def paired(array, odd):
    count = lax.axis_size("gx")
    pairs = []
    for i in range(count):
        partner = i ^ 1 if not odd else ((i - 1) ^ 1) + 1
        pairs.append((partner if 0 <= partner < count else i, i))
    return lax.ppermute(array, "gx", pairs)


def local(
    stored, adjoint_end, labels, tissue, source_cells, source_wave, receiver_cells, receiver_wave
):
    assert lax.axis_size("gz") == 2 and labels.shape == (BX, BY, BZ)
    half = lax.axis_size("gx") // 2
    block_scratch = [
        pltpu.VMEM((4, BX, BY, BZ), F32),
        pltpu.VMEM((4, BX, BY, BZ), F32),
        pltpu.VMEM((BX, BY, BZ), jnp.int32),
        pltpu.SMEM(tissue.shape, F32),
        pltpu.SemaphoreType.DMA,
    ]
    arguments = [stored, adjoint_end, labels, tissue]
    p, ql, face_x, face_y, face_z = call(
        face_kernel,
        [shape(BX * BY, BZ), shape(2 * BX * BY, BZ), shape(2 * BY, BZ), shape(8, BZ), shape(BY, BZ)],
        arguments,
        block_scratch,
        "hhhh",
    )
    face_x = rotated(face_x, "gx", -1)
    face_y = rotated(face_y, "gy", -1)
    face_z = rotated(face_z, "gz", -1)
    p_own, p_high, p_low = (rotated(p, "gx", half + offset) for offset in (0, 1, -1))
    ql_even, ql_odd = paired(ql, False), paired(ql, True)
    receivers, sources = receiver_cells.T, source_cells.T
    r, rs, src, src_strip = call(
        inject_kernel,
        [
            shape(STEPS, EX * EY, BZ),
            shape(STEPS, EY, BZ),
            shape(STEPS - 1, EX * EY, BZ),
            shape(STEPS - 1, EY, BZ),
        ],
        [receivers, receiver_wave, sources, source_wave],
        [
            pltpu.VMEM(receivers.shape, jnp.int32),
            pltpu.VMEM(receiver_wave.shape, F32),
            pltpu.VMEM(sources.shape, jnp.int32),
            pltpu.VMEM(source_wave.shape, F32),
            pltpu.SemaphoreType.DMA,
        ],
        "hhhh",
    )
    r = r.reshape(STEPS, EX, EY, BZ)
    src = src.reshape(STEPS - 1, EX, EY, BZ)
    s, t, edges, corners, strips = call(
        pack_kernel,
        [
            shape(BX * BY, BZ),
            shape(BX * BY, BZ),
            shape((5 * BX + 2) * 8, BZ),
            shape(16, BZ),
            shape(2 * BY, BZ),
        ],
        arguments + [face_x, face_y, face_z],
        block_scratch,
        "hhhhvvv",
    )
    other = rotated(strips, "gz", 1)
    up, down = from_sides(edges, "gy")
    corner_up, corner_down = from_sides(corners, ("gy", "gz"))
    late, late_for_low, late_for_high, adj_late, adj_even, adj_odd = call(
        merge_kernel,
        [
            shape(OWN_ROWS, BZ),
            shape(WAVE_ROWS, BZ),
            shape(WAVE_ROWS, BZ),
            shape(ADJ_ROWS_OWN, BZ),
            shape(ADJ_ROWS, BZ),
            shape(ADJ_ROWS, BZ),
        ],
        [up, down, strips, other, corner_up, corner_down, s, t],
        [pltpu.VMEM((5 * BX, 8, BZ), F32)],
        "vvvvvvvv",
    )
    late_own = rotated(late, "gx", half)
    late_high = rotated(late_for_low, "gx", half + 1)
    late_low = rotated(late_for_high, "gx", half - 1)
    adj_even, adj_odd = paired(adj_even, False), paired(adj_odd, True)
    adjoint_start, hist, coef, coef_strip = call(
        adjoint_kernel,
        [
            shape(4, BX, BY, BZ),
            shape(STEPS, 4, BX, BY, BZ),
            shape(3, EX, EY, BZ),
            shape(3, EY, BZ),
        ],
        [ql, ql_even, ql_odd, adj_late, adj_even, adj_odd, adjoint_end, r, rs, tissue],
        [
            pltpu.VMEM((3, EX, EY, BZ), F32),
            pltpu.VMEM((3, EY, BZ), F32),
            pltpu.SMEM(tissue.shape, F32),
            pltpu.SemaphoreType.DMA,
        ],
        "aaaaaahvvh",
    )
    (gradient,) = call(
        forward_kernel,
        [shape(2, BX, BY, BZ)],
        [p_own, p_high, p_low, late_own, late_high, late_low, coef, coef_strip, src, src_strip, hist],
        [
            pltpu.VMEM((2, EX, EY, BZ), F32),
            pltpu.VMEM((3, EY, BZ), F32),
            pltpu.SemaphoreType.DMA,
        ],
        "aaaaaavvvvv",
    )
    return gradient, adjoint_start


def solution(mesh):
    return jax.shard_map(
        local,
        mesh=mesh,
        in_specs=(
            P("shot", "gx", "gy", "gz"),
            P("shot", "gx", "gy", "gz"),
            P("gx", "gy", "gz"),
            P(),
            P("shot", None),
            P(None, "shot"),
            P(),
            P(None, "shot"),
        ),
        out_specs=(P("shot", "gx", "gy", "gz"), P("shot", "gx", "gy", "gz")),
        check_vma=False,
    )
```

time: 76 us -> 49.3 us (0.65)
  blocking collectives: 24.7 us -> 0 us
  between operations: 14.2 us -> 0.82 us
  starting transfers between devices: 14.3 us -> 23.8 us
  waiting for transfers between devices: 0.7 us -> 7.02 us
  local copies, waits for them, and re-layouts: 9.82 us -> 4.11 us
  Pallas kernels: 11.6 us -> 13.3 us
    all_gather x1 -> x0, blocking collectives: 24.7 us -> none  [local(): gathered_x = lax.all_gather(xw, 'gx')]
    ppermute x5 -> x14, starting transfers between devices: 12.7 us -> 21.3 us  [the longest x10 18.9 us: rotated(): lax.ppermute(array, axis, [((i + offset) % count, i) for i in range(count)])]
    unnamed x30 -> x20, local copies, waits for them, and re-layouts: 9.82 us -> 4.11 us
    ppermute x5 -> x14, waiting for transfers between devices: 0.01 us -> 4.52 us  [the longest x10 4.51 us: rotated(): lax.ppermute(array, axis, [((i + offset) % count, i) for i in range(count)])]
    ppermute x2, waiting for transfers between devices: 0.01 us -> 2.49 us  [from_sides(): both = lax.ppermute(array, axes, route(1) + route(-1))]
    pallas_call x5 -> x6, Pallas kernels: 11.6 us -> 13.3 us  [call(): pl.pallas_call(kernel, out_shape=outs, in_specs=[pl.BlockSpec(memory_spac...]
    ppermute x2, starting transfers between devices: 1.56 us -> 2.42 us  [from_sides(): both = lax.ppermute(array, axes, route(1) + route(-1))]
  transfers between devices with their start and end apart: 8 -> 16, of which waited for: 0 -> 4; matrix products, arithmetic and copies ran while one was open for 0% -> 0% of each run, Pallas kernels for 11% -> 17%
where the time goes in v2:
time: 49.3 us; the launch traced here: 49 us
  starting transfers between devices  23.8 us (48%)
  Pallas kernels  13.3 us (27%)
  waiting for transfers between devices  7.02 us (14%)
  local copies, waits for them, and re-layouts  4.11 us (8%)
  between operations  0.82 us (2%)
    ppermute x10, starting transfers between devices, rotated(): lax.ppermute(array, axis, [((i + offset) % count, i) for i in range(count)])  18.9 us
    pallas_call x6, Pallas kernels, call(): pl.pallas_call(kernel, out_shape=outs, in_specs=[pl.BlockSpec(memory_spac...  13.3 us
    ppermute x10, waiting for transfers between devices, rotated(): lax.ppermute(array, axis, [((i + offset) % count, i) for i in range(count)])  4.51 us
    unnamed x20, local copies, waits for them, and re-layouts  4.11 us
    ppermute x2, waiting for transfers between devices, from_sides(): both = lax.ppermute(array, axes, route(1) + route(-1))  2.49 us
    ppermute x4, starting transfers between devices, paired(): return lax.ppermute(array, 'gx', pairs)  2.45 us
    ppermute x2, starting transfers between devices, from_sides(): both = lax.ppermute(array, axes, route(1) + route(-1))  2.42 us
  transfers between devices with their start and end apart: 16, of which 4 were waited for; matrix products, arithmetic and copies ran while one was open for 0% of the time, Pallas kernels for 17%

profile of v2, /device:TPU:0, one launch (start us, length us, event | category | flops | bytes accessed | tf_op | source)
XLA Modules:
  0.0 49.0 jit_solution(1592044202158935427)
XLA Ops:
  0.6 0.0 copy-start
  0.6 0.9 %copy-done = f32[4,4,32,128]{3,2,1,0:T(8,128)S(1)} copy-done((f32[4,4,32,128]{3,2,1,0:T(8,128)S(1)}, f32[4,4,32,128]{3,2,1,0:T(8,128)}, u32[]{:S(2)}) %copy-start) | copy-done | bytes 262168
  1.6 0.9 %copy-done.2 = f32[4,4,32,128]{3,2,1,0:T(8,128)S(1)} copy-done((f32[4,4,32,128]{3,2,1,0:T(8,128)S(1)}, f32[4,4,32,128]{3,2,1,0:T(8,128)}, u32[]{:S(2)}) %copy-start.2) | copy-done | bytes 262168
  2.5 0.8 %copy-done.3 = s32[4,32,128]{2,1,0:T(8,128)S(1)} copy-done((s32[4,32,128]{2,1,0:T(8,128)S(1)}, s32[4,32,128]{2,1,0:T(8,128)}, u32[]{:S(2)}) %copy-start.3) | copy-done | bytes 65560
  3.4 0.7 %copy-done.4 = f32[3,8]{1,0:T(4,128)S(1)} copy-done((f32[3,8]{1,0:T(4,128)S(1)}, f32[3,8]{1,0:T(4,128)}, u32[]{:S(2)}) %copy-start.4) | copy-done | bytes 120
  4.1 0.8 %shard_map.95 = (f32[128,128]{1,0:T(8,128)S(1)}, f32[256,128]{1,0:T(8,128)S(1)}, f32[64,128]{1,0:T(8,128)S(1)}, f32[8,128]{1,0:T(8,128)S(1)}, f32[32,128]{1,0:T(8,128)S(1)}) custom-call(f32[4,4,32,128]{3,2,1,0:T(8,128)S(1)} %copy-done.2, f32[4,4,32,128]{3,2,1,0:T(8,128)S(1)} %copy-done, s32[4,32,128]{2,1,0:T(8,128)S(1)} %copy-done.3, f32[3,8]{1,0:T(4,128)S(1)} %copy-done.4), custom_call_target="tpu_custom_call" | custom-call | flops 16777216 | bytes 1048576 | tf_op jit(solution)/shard_map/pallas_call | solution.py:582
  4.9 3.1 %collective-permute-start.3 = (f32[64,128]{1,0:T(8,128)S(1)}, f32[64,128]{1,0:T(8,128)S(1)}, u32[]{:S(2)}, u32[]{:S(2)}) collective-permute-start(f32[64,128]{1,0:T(8,128)S(1)} %get-tuple-element.27), channel_id=1, source_target_pairs={{12,0},{0,4},{4,8},{8,12},{13,1},{1,5},{5,9},{9,13},{14,2},{2,6},{... | collective-permute-start | bytes 98312 | tf_op jit(solution)/shard_map/ppermute | solution.py:615
  7.9 1.5 %collective-permute-start.4 = (f32[8,128]{1,0:T(8,128)S(1)}, f32[8,128]{1,0:T(8,128)S(1)}, u32[]{:S(2)}, u32[]{:S(2)}) collective-permute-start(f32[8,128]{1,0:T(8,128)S(1)} %get-tuple-element.28), channel_id=1, source_target_pairs={{2,0},{0,2},{3,1},{1,3},{6,4},{4,6},{7,5},{5,7},{10,8},{8,10},{11,... | collective-permute-start | bytes 12296 | tf_op jit(solution)/shard_map/ppermute | solution.py:615
  9.4 2.1 %collective-permute-done.4.face_y = f32[8,128]{1,0:T(8,128)S(1)} collective-permute-done((f32[8,128]{1,0:T(8,128)S(1)}, f32[8,128]{1,0:T(8,128)S(1)}, u32[]{:S(2)}, u32[]{:S(2)}) %collective-permute-start.4) | collective-permute-done | bytes 4128 | tf_op jit(solution)/shard_map/ppermute | solution.py:615
  11.6 0.3 collective-permute-done.3.face_x
  11.9 0.9 %shard_map.96 = (f32[128,128]{1,0:T(8,128)S(1)}, f32[128,128]{1,0:T(8,128)S(1)}, f32[176,128]{1,0:T(8,128)S(1)}, f32[16,128]{1,0:T(8,128)S(1)}, f32[64,128]{1,0:T(8,128)S(1)}) custom-call(f32[4,4,32,128]{3,2,1,0:T(8,128)S(1)} %copy-done.2, f32[4,4,32,128]{3,2,1,0:T(8,128)S(1)} %copy-done, s32[4,32,128]{2,1,0:T(8,128)S(1)} %copy-done.3, ...), custom_call_target="tpu_custom_call" | custom-call | flops 16777216 | bytes 1048576 | tf_op jit(solution)/shard_map/pallas_call | solution.py:582
  12.8 0.0 copy-start.1
  12.8 1.8 %collective-permute-start.6 = (f32[176,128]{1,0:T(8,128)S(1)}, f32[176,128]{1,0:T(8,128)S(1)}, u32[]{:S(2)}, u32[]{:S(2)}) collective-permute-start(f32[176,128]{1,0:T(8,128)S(1)} %get-tuple-element.30), channel_id=1, source_target_pairs={{2,0},{0,2},{3,1},{1,3},{6,4},{4,6},{7,5},{5,7},{10,8},{8,10},{11,... | collective-permute-start | bytes 270344 | tf_op jit(solution)/shard_map/ppermute | solution.py:608
  14.6 1.1 %collective-permute-start.12 = (f32[256,128]{1,0:T(8,128)S(1)}, f32[256,128]{1,0:T(8,128)S(1)}, u32[]{:S(2)}, u32[]{:S(2)}) collective-permute-start(f32[256,128]{1,0:T(8,128)S(1)} %get-tuple-element.38.ql), channel_id=1, source_target_pairs={{4,0},{0,4},{12,8},{8,12},{5,1},{1,5},{13,9},{9,13},{6,2},{2,6},{1... | collective-permute-start | bytes 393224 | tf_op jit(solution)/shard_map/ppermute | solution.py:624
  15.6 0.7 %collective-permute-start.13 = (f32[256,128]{1,0:T(8,128)S(1)}, f32[256,128]{1,0:T(8,128)S(1)}, u32[]{:S(2)}, u32[]{:S(2)}) collective-permute-start(f32[256,128]{1,0:T(8,128)S(1)} %get-tuple-element.38.ql), channel_id=1, source_target_pairs={{0,0},{8,4},{4,8},{12,12},{1,1},{9,5},{5,9},{13,13},{2,2},{10,6},{... | collective-permute-start | bytes 393224 | tf_op jit(solution)/shard_map/ppermute | solution.py:624
  16.3 0.1 collective-permute-start.7
  16.4 0.7 %collective-permute-start.8 = (f32[16,128]{1,0:T(8,128)S(1)}, f32[16,128]{1,0:T(8,128)S(1)}, u32[]{:S(2)}, u32[]{:S(2)}) collective-permute-start(f32[16,128]{1,0:T(8,128)S(1)} %get-tuple-element.32), channel_id=1, source_target_pairs={{2,1},{3,0},{0,3},{1,2},{6,5},{7,4},{4,7},{5,6},{10,9},{11,8},{8,1... | collective-permute-start | bytes 24584 | tf_op jit(solution)/shard_map/ppermute | solution.py:608
  17.0 2.5 %collective-permute-done.8.corner_up_ref.corner_down_ref = f32[16,128]{1,0:T(8,128)S(1)} collective-permute-done((f32[16,128]{1,0:T(8,128)S(1)}, f32[16,128]{1,0:T(8,128)S(1)}, u32[]{:S(2)}, u32[]{:S(2)}) %collective-permute-start.8) | collective-permute-done | bytes 8224 | tf_op jit(solution)/shard_map/ppermute | solution.py:608
  19.5 3.7 %collective-permute-start = (f32[128,128]{1,0:T(8,128)S(1)}, f32[128,128]{1,0:T(8,128)S(1)}, u32[]{:S(2)}, u32[]{:S(2)}) collective-permute-start(f32[128,128]{1,0:T(8,128)S(1)} %get-tuple-element.26), channel_id=1, source_target_pairs={{8,0},{12,4},{0,8},{4,12},{9,1},{13,5},{1,9},{5,13},{10,2},{14,6},... | collective-permute-start | bytes 196616 | tf_op jit(solution)/shard_map/ppermute | solution.py:615
  23.2 0.1 shard_map.97
  23.3 0.1 collective-permute-start.14
  23.4 0.7 %collective-permute-start.15 = (f32[200,128]{1,0:T(8,128)S(1)}, f32[200,128]{1,0:T(8,128)S(1)}, u32[]{:S(2)}, u32[]{:S(2)}) collective-permute-start(f32[200,128]{1,0:T(8,128)S(1)} %get-tuple-element.41), channel_id=1, source_target_pairs={{0,0},{8,4},{4,8},{12,12},{1,1},{9,5},{5,9},{13,13},{2,2},{10,6},{... | collective-permute-start | bytes 307208 | tf_op jit(solution)/shard_map/ppermute | solution.py:624
  24.0 2.1 %collective-permute-done.p = f32[128,128]{1,0:T(8,128)S(1)} collective-permute-done((f32[128,128]{1,0:T(8,128)S(1)}, f32[128,128]{1,0:T(8,128)S(1)}, u32[]{:S(2)}, u32[]{:S(2)}) %collective-permute-start) | collective-permute-done | bytes 65568 | tf_op jit(solution)/shard_map/ppermute | solution.py:615
  26.1 3.0 %collective-permute-start.9 = (f32[232,128]{1,0:T(8,128)S(1)}, f32[232,128]{1,0:T(8,128)S(1)}, u32[]{:S(2)}, u32[]{:S(2)}) collective-permute-start(f32[232,128]{1,0:T(8,128)S(1)} %get-tuple-element.35), channel_id=1, source_target_pairs={{8,0},{12,4},{0,8},{4,12},{9,1},{13,5},{1,9},{5,13},{10,2},{14,6},... | collective-permute-start | bytes 356360 | tf_op jit(solution)/shard_map/ppermute | solution.py:615
  29.1 0.0 copy-start.8
  29.1 3.8 %collective-permute-start.11 = (f32[176,128]{1,0:T(8,128)S(1)}, f32[176,128]{1,0:T(8,128)S(1)}, u32[]{:S(2)}, u32[]{:S(2)}) collective-permute-start(f32[176,128]{1,0:T(8,128)S(1)} %get-tuple-element.37), channel_id=1, source_target_pairs={{4,0},{8,4},{12,8},{0,12},{5,1},{9,5},{13,9},{1,13},{6,2},{10,6},{... | collective-permute-start | bytes 270344 | tf_op jit(solution)/shard_map/ppermute | solution.py:615
  32.9 3.8 %collective-permute-start.2 = (f32[128,128]{1,0:T(8,128)S(1)}, f32[128,128]{1,0:T(8,128)S(1)}, u32[]{:S(2)}, u32[]{:S(2)}) collective-permute-start(f32[128,128]{1,0:T(8,128)S(1)} %get-tuple-element.26), channel_id=1, source_target_pairs={{4,0},{8,4},{12,8},{0,12},{5,1},{9,5},{13,9},{1,13},{6,2},{10,6},{... | collective-permute-start | bytes 196616 | tf_op jit(solution)/shard_map/ppermute | solution.py:615
  36.7 4.6 %shard_map.98 = (f32[4,480,128]{2,1,0:T(8,128)S(1)}, f32[4,40,128]{2,1,0:T(8,128)S(1)}, f32[3,480,128]{2,1,0:T(8,128)S(1)}, f32[3,40,128]{2,1,0:T(8,128)S(1)}) custom-call(s32[3,1024]{1,0:T(4,128)S(1)} %bitcast.6, f32[4,1024]{1,0:T(4,128)S(1)} %copy-done.7, s32[3,64]{1,0:T(4,128)S(1)} %bitcast.7, f32[4,64]{1,0:T(4,128)S(1)} %copy-done.9), custom_call_target="tpu_custom_call" | custom-call | flops 16777216 | bytes 1048576 | tf_op jit(solution)/shard_map/pallas_call | solution.py:582
  41.4 0.0 copy-start.5
  41.4 0.7 %copy-done.5 = f32[3,8]{1,0:T(4,128)S(1)} copy-done((f32[3,8]{1,0:T(4,128)S(1)}, f32[3,8]{1,0:T(4,128)}, u32[]{:S(2)}) %copy-start.5) | copy-done | bytes 120
  42.1 3.7 %shard_map.99 = (f32[4,4,32,128]{3,2,1,0:T(8,128)}, f32[4,4,4,32,128]{4,3,2,1,0:T(8,128)S(1)}, f32[3,12,40,128]{3,2,1,0:T(8,128)S(1)}, f32[3,40,128]{2,1,0:T(8,128)S(1)}) custom-call(f32[256,128]{1,0:T(8,128)S(1)} %get-tuple-element.38.ql, f32[256,128]{1,0:T(8,128)S(1)} %collective-permute-done.12.ql_even, f32[256,128]{1,0:T(8,128)S(1)} %collective-permute-done.13.ql_odd, ...), custom_call_target="tpu_custom_call" | custom-call | flops 16777216 | bytes 1048576 | tf_op jit(solution)/shard_map/pallas_call | solution.py:582
  45.8 3.2 %shard_map.100 = f32[2,4,32,128]{3,2,1,0:T(8,128)} custom-call(f32[128,128]{1,0:T(8,128)S(1)} %collective-permute-done.p, f32[128,128]{1,0:T(8,128)S(1)} %collective-permute-done.1.p_high, f32[128,128]{1,0:T(8,128)S(1)} %collective-permute-done.2.p_low, f32[232,128]{1,0:T(8,128)S(1)} %collective-permute-done.9.late, ...), custom_call_target="tpu_custom_call" | custom-call | flops 16777216 | bytes 1048576 | tf_op jit(solution)/shard_map/pallas_call | solution.py:582
  (26 shorter events, 0.1 us)
Async XLA Ops:
  0.6 1.0 %copy-start = (f32[4,4,32,128]{3,2,1,0:T(8,128)S(1)}, f32[4,4,32,128]{3,2,1,0:T(8,128)}, u32[]{:S(2)}) copy-start(f32[4,4,32,128]{3,2,1,0:T(8,128)} %adj_hbm.5) | copy-start | bytes 786436
  1.6 0.9 %copy-start.2 = (f32[4,4,32,128]{3,2,1,0:T(8,128)S(1)}, f32[4,4,32,128]{3,2,1,0:T(8,128)}, u32[]{:S(2)}) copy-start(f32[4,4,32,128]{3,2,1,0:T(8,128)} %stored_hbm.3) | copy-start | bytes 786436
  2.5 0.8 %copy-start.3 = (s32[4,32,128]{2,1,0:T(8,128)S(1)}, s32[4,32,128]{2,1,0:T(8,128)}, u32[]{:S(2)}) copy-start(s32[4,32,128]{2,1,0:T(8,128)} %lab_hbm.3) | copy-start | bytes 196612
  3.4 0.7 %copy-start.4 = (f32[3,8]{1,0:T(4,128)S(1)}, f32[3,8]{1,0:T(4,128)}, u32[]{:S(2)}) copy-start(f32[3,8]{1,0:T(4,128)} %tissue_hbm.5) | copy-start | bytes 292
  4.9 7.0 %collective-permute-start.3 = (f32[64,128]{1,0:T(8,128)S(1)}, f32[64,128]{1,0:T(8,128)S(1)}, u32[]{:S(2)}, u32[]{:S(2)}) collective-permute-start(f32[64,128]{1,0:T(8,128)S(1)} %get-tuple-element.27), channel_id=1, source_target_pairs={{12,0},{0,4},{4,8},{8,12},{13,1},{1,5},{5,9},{9,13},{14,2},{2,6},{... | collective-permute-start | bytes 98312 | tf_op jit(solution)/shard_map/ppermute | solution.py:615
  7.9 3.6 %collective-permute-start.5 = (f32[32,128]{1,0:T(8,128)S(1)}, f32[32,128]{1,0:T(8,128)S(1)}, u32[]{:S(2)}, u32[]{:S(2)}) collective-permute-start(f32[32,128]{1,0:T(8,128)S(1)} %get-tuple-element.29), channel_id=1, source_target_pairs={{1,0},{0,1},{3,2},{2,3},{5,4},{4,5},{7,6},{6,7},{9,8},{8,9},{11,10... | collective-permute-start | bytes 49160 | tf_op jit(solution)/shard_map/ppermute | solution.py:615
  7.9 3.6 %collective-permute-start.4 = (f32[8,128]{1,0:T(8,128)S(1)}, f32[8,128]{1,0:T(8,128)S(1)}, u32[]{:S(2)}, u32[]{:S(2)}) collective-permute-start(f32[8,128]{1,0:T(8,128)S(1)} %get-tuple-element.28), channel_id=1, source_target_pairs={{2,0},{0,2},{3,1},{1,3},{6,4},{4,6},{7,5},{5,7},{10,8},{8,10},{11,... | collective-permute-start | bytes 12296 | tf_op jit(solution)/shard_map/ppermute | solution.py:615
  12.8 28.6 %copy-start.1 = (f32[4,4,32,128]{3,2,1,0:T(8,128)S(1)}, f32[4,4,32,128]{3,2,1,0:T(8,128)}, u32[]{:S(2)}) copy-start(f32[4,4,32,128]{3,2,1,0:T(8,128)} %adj_hbm.5) | copy-start | bytes 786436
  12.8 10.4 %collective-permute-start.6 = (f32[176,128]{1,0:T(8,128)S(1)}, f32[176,128]{1,0:T(8,128)S(1)}, u32[]{:S(2)}, u32[]{:S(2)}) collective-permute-start(f32[176,128]{1,0:T(8,128)S(1)} %get-tuple-element.30), channel_id=1, source_target_pairs={{2,0},{0,2},{3,1},{1,3},{6,4},{4,6},{7,5},{5,7},{10,8},{8,10},{11,... | collective-permute-start | bytes 270344 | tf_op jit(solution)/shard_map/ppermute | solution.py:608
  14.6 14.5 %collective-permute-start.12 = (f32[256,128]{1,0:T(8,128)S(1)}, f32[256,128]{1,0:T(8,128)S(1)}, u32[]{:S(2)}, u32[]{:S(2)}) collective-permute-start(f32[256,128]{1,0:T(8,128)S(1)} %get-tuple-element.38.ql), channel_id=1, source_target_pairs={{4,0},{0,4},{12,8},{8,12},{5,1},{1,5},{13,9},{9,13},{6,2},{2,6},{1... | collective-permute-start | bytes 393224 | tf_op jit(solution)/shard_map/ppermute | solution.py:624
  15.6 13.4 %collective-permute-start.13 = (f32[256,128]{1,0:T(8,128)S(1)}, f32[256,128]{1,0:T(8,128)S(1)}, u32[]{:S(2)}, u32[]{:S(2)}) collective-permute-start(f32[256,128]{1,0:T(8,128)S(1)} %get-tuple-element.38.ql), channel_id=1, source_target_pairs={{0,0},{8,4},{4,8},{12,12},{1,1},{9,5},{5,9},{13,13},{2,2},{10,6},{... | collective-permute-start | bytes 393224 | tf_op jit(solution)/shard_map/ppermute | solution.py:624
  16.3 6.9 %collective-permute-start.7 = (f32[64,128]{1,0:T(8,128)S(1)}, f32[64,128]{1,0:T(8,128)S(1)}, u32[]{:S(2)}, u32[]{:S(2)}) collective-permute-start(f32[64,128]{1,0:T(8,128)S(1)} %get-tuple-element.31.strip_ref), channel_id=1, source_target_pairs={{1,0},{0,1},{3,2},{2,3},{5,4},{4,5},{7,6},{6,7},{9,8},{8,9},{11,10... | collective-permute-start | bytes 98312 | tf_op jit(solution)/shard_map/ppermute | solution.py:615
  16.4 3.1 %collective-permute-start.8 = (f32[16,128]{1,0:T(8,128)S(1)}, f32[16,128]{1,0:T(8,128)S(1)}, u32[]{:S(2)}, u32[]{:S(2)}) collective-permute-start(f32[16,128]{1,0:T(8,128)S(1)} %get-tuple-element.32), channel_id=1, source_target_pairs={{2,1},{3,0},{0,3},{1,2},{6,5},{7,4},{4,7},{5,6},{10,9},{11,8},{8,1... | collective-permute-start | bytes 24584 | tf_op jit(solution)/shard_map/ppermute | solution.py:608
  19.5 6.6 %collective-permute-start = (f32[128,128]{1,0:T(8,128)S(1)}, f32[128,128]{1,0:T(8,128)S(1)}, u32[]{:S(2)}, u32[]{:S(2)}) collective-permute-start(f32[128,128]{1,0:T(8,128)S(1)} %get-tuple-element.26), channel_id=1, source_target_pairs={{8,0},{12,4},{0,8},{4,12},{9,1},{13,5},{1,9},{5,13},{10,2},{14,6},... | collective-permute-start | bytes 196616 | tf_op jit(solution)/shard_map/ppermute | solution.py:615
  23.2 13.5 %copy-start.6 = (s32[1024,3]{0,1:T(4,128)S(1)}, s32[1024,3]{0,1:T(4,128)}, u32[]{:S(2)}) copy-start(s32[1024,3]{0,1:T(4,128)} %param.14) | copy-start | bytes 36868
  23.2 13.5 %copy-start.7 = (f32[4,1024]{1,0:T(4,128)S(1)}, f32[4,1024]{1,0:T(4,128)}, u32[]{:S(2)}) copy-start(f32[4,1024]{1,0:T(4,128)} %receiver_wave_hbm.1) | copy-start | bytes 49156
  23.3 9.6 %collective-permute-start.14 = (f32[200,128]{1,0:T(8,128)S(1)}, f32[200,128]{1,0:T(8,128)S(1)}, u32[]{:S(2)}, u32[]{:S(2)}) collective-permute-start(f32[200,128]{1,0:T(8,128)S(1)} %get-tuple-element.40), channel_id=1, source_target_pairs={{4,0},{0,4},{12,8},{8,12},{5,1},{1,5},{13,9},{9,13},{6,2},{2,6},{1... | collective-permute-start | bytes 307208 | tf_op jit(solution)/shard_map/ppermute | solution.py:624
  23.4 9.5 %collective-permute-start.15 = (f32[200,128]{1,0:T(8,128)S(1)}, f32[200,128]{1,0:T(8,128)S(1)}, u32[]{:S(2)}, u32[]{:S(2)}) collective-permute-start(f32[200,128]{1,0:T(8,128)S(1)} %get-tuple-element.41), channel_id=1, source_target_pairs={{0,0},{8,4},{4,8},{12,12},{1,1},{9,5},{5,9},{13,13},{2,2},{10,6},{... | collective-permute-start | bytes 307208 | tf_op jit(solution)/shard_map/ppermute | solution.py:624
  26.1 19.7 %collective-permute-start.9 = (f32[232,128]{1,0:T(8,128)S(1)}, f32[232,128]{1,0:T(8,128)S(1)}, u32[]{:S(2)}, u32[]{:S(2)}) collective-permute-start(f32[232,128]{1,0:T(8,128)S(1)} %get-tuple-element.35), channel_id=1, source_target_pairs={{8,0},{12,4},{0,8},{4,12},{9,1},{13,5},{1,9},{5,13},{10,2},{14,6},... | collective-permute-start | bytes 356360 | tf_op jit(solution)/shard_map/ppermute | solution.py:615
  29.1 16.7 %collective-permute-start.10 = (f32[176,128]{1,0:T(8,128)S(1)}, f32[176,128]{1,0:T(8,128)S(1)}, u32[]{:S(2)}, u32[]{:S(2)}) collective-permute-start(f32[176,128]{1,0:T(8,128)S(1)} %get-tuple-element.36), channel_id=1, source_target_pairs={{12,0},{0,4},{4,8},{8,12},{13,1},{1,5},{5,9},{9,13},{14,2},{2,6},{... | collective-permute-start | bytes 270344 | tf_op jit(solution)/shard_map/ppermute | solution.py:615
  29.1 7.7 %copy-start.9 = (f32[4,64]{1,0:T(4,128)S(1)}, f32[4,64]{1,0:T(4,128)}, u32[]{:S(2)}) copy-start(f32[4,64]{1,0:T(4,128)} %source_wave_hbm.1) | copy-start | bytes 3076
  29.1 7.7 %copy-start.8 = (s32[64,3]{0,1:T(4,128)S(1)}, s32[64,3]{0,1:T(4,128)}, u32[]{:S(2)}) copy-start(s32[64,3]{0,1:T(4,128)} %param.12) | copy-start | bytes 2308
  29.1 16.7 %collective-permute-start.11 = (f32[176,128]{1,0:T(8,128)S(1)}, f32[176,128]{1,0:T(8,128)S(1)}, u32[]{:S(2)}, u32[]{:S(2)}) collective-permute-start(f32[176,128]{1,0:T(8,128)S(1)} %get-tuple-element.37), channel_id=1, source_target_pairs={{4,0},{8,4},{12,8},{0,12},{5,1},{9,5},{13,9},{1,13},{6,2},{10,6},{... | collective-permute-start | bytes 270344 | tf_op jit(solution)/shard_map/ppermute | solution.py:615
  32.9 12.9 %collective-permute-start.1 = (f32[128,128]{1,0:T(8,128)S(1)}, f32[128,128]{1,0:T(8,128)S(1)}, u32[]{:S(2)}, u32[]{:S(2)}) collective-permute-start(f32[128,128]{1,0:T(8,128)S(1)} %get-tuple-element.26), channel_id=1, source_target_pairs={{12,0},{0,4},{4,8},{8,12},{13,1},{1,5},{5,9},{9,13},{14,2},{2,6},{... | collective-permute-start | bytes 196616 | tf_op jit(solution)/shard_map/ppermute | solution.py:615
  32.9 12.9 %collective-permute-start.2 = (f32[128,128]{1,0:T(8,128)S(1)}, f32[128,128]{1,0:T(8,128)S(1)}, u32[]{:S(2)}, u32[]{:S(2)}) collective-permute-start(f32[128,128]{1,0:T(8,128)S(1)} %get-tuple-element.26), channel_id=1, source_target_pairs={{4,0},{8,4},{12,8},{0,12},{5,1},{9,5},{13,9},{1,13},{6,2},{10,6},{... | collective-permute-start | bytes 196616 | tf_op jit(solution)/shard_map/ppermute | solution.py:615
  41.4 0.7 %copy-start.5 = (f32[3,8]{1,0:T(4,128)S(1)}, f32[3,8]{1,0:T(4,128)}, u32[]{:S(2)}) copy-start(f32[3,8]{1,0:T(4,128)} %tissue_hbm.5) | copy-start | bytes 292

commit v3 on v2

v3 whole, which is shorter than its diff:
```python
import jax
import jax.numpy as jnp
from jax import lax
from jax.experimental import pallas as pl
from jax.experimental.pallas import tpu as pltpu
from jax.sharding import PartitionSpec as P

STEPS = 4
MARGIN = 4
BX, BY, BZ = 4, 32, 128
EX, EY = BX + 2 * MARGIN, BY + 2 * MARGIN
STRIP = 2 * MARGIN
F32 = jnp.float32
BF16 = jnp.bfloat16
VMEM_LIMIT = 16 * 1024 * 1024
PLANES = BX * BY
OWN_ROWS = PLANES + 2 * BX * 8 + EY
ADJ_OWN_ROWS = PLANES + 3 * BX * 8 + EY
WAVE_ROWS = 3 * BY + 5 * 8 + EY
ADJ_ROWS = 3 * BY + 8 * 8 + EY


def lanes(shape):
    return lax.broadcasted_iota(jnp.int32, shape, len(shape) - 1)


def rows(shape):
    return lax.broadcasted_iota(jnp.int32, shape, len(shape) - 2)


def run(copies):
    for copy in copies:
        copy.start()
    for copy in copies:
        copy.wait()


def class_values(tissue_ref, index):
    speed = jnp.full((1, BZ), tissue_ref[0, index], F32)
    density = jnp.full((1, BZ), tissue_ref[1, index], F32)
    damping = 1.0 - jnp.full((1, BZ), tissue_ref[2, index], F32)
    return density * speed, speed / density, damping


def buoyancy_of(labels, tissue_ref):
    result = jnp.zeros(labels.shape, F32)
    for index in range(tissue_ref.shape[1]):
        result = jnp.where(labels == float(index + 1), class_values(tissue_ref, index)[1], result)
    return result


def coefficients(labels, tissue_ref):
    stiffness = jnp.zeros(labels.shape, F32)
    buoyancy = jnp.zeros(labels.shape, F32)
    damping = jnp.zeros(labels.shape, F32)
    for index in range(tissue_ref.shape[1]):
        picked = labels == float(index + 1)
        values = class_values(tissue_ref, index)
        stiffness = jnp.where(picked, values[0], stiffness)
        buoyancy = jnp.where(picked, values[1], buoyancy)
        damping = jnp.where(picked, values[2], damping)
    return stiffness, buoyancy, damping


def face_kernel(
    stored_hbm, adj_hbm, lab_hbm, tissue_hbm,
    p_ref, raw_ref, s_ref, t_ref, face_x_ref, face_y_ref, face_z_ref,
    stored, adj, lab, tissue, sem,
):
    run([
        pltpu.make_async_copy(stored_hbm, stored, sem),
        pltpu.make_async_copy(adj_hbm, adj, sem),
        pltpu.make_async_copy(lab_hbm, lab, sem),
        pltpu.make_async_copy(tissue_hbm, tissue, sem),
    ])
    lane = lanes((BY, BZ))
    row = rows((BY, BZ))
    tile_row = rows((8, BZ))
    face_y = jnp.zeros((8, BZ), F32)
    face_z = jnp.zeros((BY, BZ), F32)
    previous = [None, None]
    for x in range(BX):
        labels = lab[x].astype(F32) + 1.0
        buoyancy = buoyancy_of(labels, tissue)
        plane = slice(x * BY, x * BY + BY)
        p_ref[plane] = stored[0, x]
        for index, values in enumerate((stored[0, x], adj[0, x], labels)):
            raw_ref[index * PLANES + x * BY : index * PLANES + x * BY + BY] = values
        for kind, v in enumerate((stored, adj)):
            vx, vy, vz = v[1, x], v[2, x], v[3, x]
            if kind == 1:
                vx, vy, vz = buoyancy * vx, buoyancy * vy, buoyancy * vz
            y_below = pltpu.roll(vy, 1, 0)
            z_below = pltpu.roll(vz, 1, 1)
            index = kind * BX + x
            last = pltpu.roll(vy[BY - 8 : BY], (index + 1) % 8, 0)
            face_y = jnp.where(tile_row == index, last, face_y)
            face_z = jnp.where(lane == index, pltpu.roll(vz, index + 1, 1), face_z)
            spread = vx if x == 0 else vx - previous[kind]
            spread = spread + (vy - jnp.where(row == 0, 0.0, y_below))
            spread = spread + (vz - jnp.where(lane == 0, 0.0, z_below))
            (s_ref, t_ref)[kind][plane] = spread
            previous[kind] = vx
    for kind in range(2):
        face_x_ref[kind * BY : kind * BY + BY] = previous[kind]
    face_y_ref[...] = face_y
    face_z_ref[...] = face_z


def pack_kernel(
    raw_ref, s_in, t_in, face_x, face_y, face_z, _,
    s_ref, t_ref, edge_ref, corner_ref, strip_ref,
):
    gx, gy, gz = (lax.axis_index(name) for name in ("gx", "gy", "gz"))
    count = lax.axis_size("gx")
    lane = lanes((BY, BZ))
    row = rows((BY, BZ))
    tile_row = rows((8, BZ))
    below = (
        jnp.where(gx == count // 2, 0.0, 1.0),
        jnp.where(gx == 0, 0.0, 1.0),
    )
    tile_y = face_y[...] * jnp.where(gy == 0, 0.0, 1.0)
    tile_z = face_z[...] * jnp.where(gz == 0, 0.0, 1.0)
    strips = [jnp.zeros((BY, BZ), F32) for _ in range(2)]
    for field in range(5):
        group, slot = (0, field) if field < 2 else (1, field - 2)
        for x in range(BX):
            plane = slice(x * BY, x * BY + BY)
            if field in (1, 3):
                kind = field // 2
                block = (s_in, t_in)[kind][plane]
                if x == 0:
                    block = block - face_x[kind * BY : kind * BY + BY] * below[kind]
                index = kind * BX + x
                lane_below = pltpu.roll(tile_z, (BZ - index) % BZ, 1) if index else tile_z
                block = block - jnp.where(row == 0, tile_y[index : index + 1], 0.0)
                block = block - jnp.where(lane == 0, lane_below, 0.0)
                (s_ref, t_ref)[kind][plane] = block
            else:
                first = field // 2 * PLANES + x * BY
                block = raw_ref[first : first + BY]
            tile = jnp.where(tile_row < MARGIN, block[0:8], block[BY - 8 : BY])
            index = field * BX + x
            edge_ref[index * 8 : index * 8 + 8] = tile
            base = slot * BX * STRIP + x * STRIP
            rolled = pltpu.roll(block, base + MARGIN, 1)
            first = base + MARGIN * gz
            strips[group] = jnp.where(
                (lane >= first) & (lane < first + MARGIN), rolled, strips[group]
            )
    for group in range(2):
        strip = strips[group]
        strip_ref[group * BY : group * BY + BY] = strip
        tile = jnp.where(tile_row < MARGIN, strip[0:8], strip[BY - 8 : BY])
        index = 5 * BX + group
        edge_ref[index * 8 : index * 8 + 8] = tile
        corner_ref[group * 8 : group * 8 + 8] = tile


def merge_kernel(
    up_ref, down_ref, strip_ref, other_ref, corner_up_ref, corner_down_ref, s_ref, t_ref,
    _a, _b, _c, _d,
    own_ref, adj_own_ref, to_next_ref, to_last_ref,
):
    gy = lax.axis_index("gy")
    row = rows((8, BZ))
    take_up = (row < MARGIN) & (gy < lax.axis_size("gy") - 1)
    take_down = (row >= MARGIN) & (gy > 0)

    def halo(up, down, index):
        sl = slice(index * 8, index * 8 + 8)
        return jnp.where(take_up, up[sl], jnp.where(take_down, down[sl], 0.0))

    tiles = [halo(up_ref, down_ref, index) for index in range(5 * BX)]
    strips = []
    for group in range(2):
        sl = slice(group * BY, group * BY + BY)
        tile = halo(up_ref, down_ref, 5 * BX + group) + halo(corner_up_ref, corner_down_ref, group)
        strips.append((strip_ref[sl] + other_ref[sl], tile))

    def put(target, base, planes, chosen, strip):
        target[base : base + planes.shape[0]] = planes
        base += planes.shape[0]
        for index in chosen:
            target[base : base + 8] = tiles[index]
            base += 8
        target[base : base + BY] = strip[0]
        target[base + BY : base + EY] = strip[1]

    put(own_ref, 0, s_ref[...], range(2 * BX), strips[0])
    put(adj_own_ref, 0, t_ref[...], range(2 * BX, 5 * BX), strips[1])
    above, below = s_ref[0 : 3 * BY], s_ref[BY:PLANES]
    put(to_next_ref, 0, above, (0, 1, 2, 4, 5), strips[0])
    put(to_last_ref, 0, below, (1, 2, 3, 6, 7), strips[0])
    above, below = t_ref[0 : 3 * BY], t_ref[BY:PLANES]
    put(to_next_ref, WAVE_ROWS, below, (9, 10, 11, 14, 15, 17, 18, 19), strips[1])
    put(to_last_ref, WAVE_ROWS, above, (8, 9, 10, 12, 13, 16, 17, 18), strips[1])


def split(values):
    high = values.astype(BF16)
    rest = values - high.astype(F32)
    middle = rest.astype(BF16)
    low = (rest - middle.astype(F32)).astype(BF16)
    return high, middle, low


def places(cells, sl):
    gx, gy, gz = (lax.axis_index(name) for name in ("gx", "gy", "gz"))
    cut = BZ * lax.axis_size("gz") // 2 - MARGIN
    cell_x = cells[0:1, sl] - (gx * BX - MARGIN)
    cell_y = cells[1:2, sl] - gy * BY
    cell_z = cells[2:3, sl]
    in_x = (cell_x >= 0) & (cell_x < EX)
    in_y = (cell_y >= -MARGIN) & (cell_y < BY + MARGIN)
    row = jnp.where(cell_y < 0, cell_y + EY, cell_y)
    flat = jnp.where(in_x & in_y, cell_x * EY + row, -1)
    row = jnp.where(in_y, row, -1)
    zz = cell_z - cut
    in_strip = in_x & (zz >= 0) & (zz < STRIP)
    strip_lane = jnp.where(in_strip, cell_x * STRIP + zz, -1)
    return flat, cell_z - gz * BZ, row, strip_lane


def hits(count, index):
    return rows((count, index.shape[1])) == index


def product(left, right):
    return lax.dot_general(
        left, right, (((1,), (1,)), ((), ())), preferred_element_type=F32
    )


def inject_points(cells, wave_ref, width, waves, out_ref, strip_out_ref):
    count = len(waves)
    for start in range(0, cells.shape[1], width):
        sl = slice(start, start + width)
        flat, z, row, strip_lane = places(cells, sl)
        here = hits(EX * EY, flat).astype(F32).astype(BF16)
        at_strip = hits(BZ, strip_lane).astype(F32).astype(BF16)
        at_z, at_row = hits(BZ, z), hits(EY, row)
        total = strip_total = None
        parts = [split(wave_ref[wave : wave + 1, sl]) for wave in waves]
        for part in range(3):
            amounts = [parts[wave][part].astype(F32) for wave in range(count)]
            right = jnp.concatenate([jnp.where(at_z, a, 0.0) for a in amounts], 0).astype(BF16)
            left = jnp.concatenate([jnp.where(at_row, a, 0.0) for a in amounts], 0).astype(BF16)
            term, strip_term = product(here, right), product(left, at_strip)
            total = term if part == 0 else total + term
            strip_total = strip_term if part == 0 else strip_total + strip_term
        for wave in range(count):
            value = total[:, wave * BZ : wave * BZ + BZ]
            strip_value = strip_total[wave * EY : wave * EY + EY]
            if start > 0:
                value = value + out_ref[wave]
                strip_value = strip_value + strip_out_ref[wave]
            out_ref[wave] = value
            strip_out_ref[wave] = strip_value


def late_kernel(
    receiver_hbm, receiver_wave_hbm, _, r_ref, rs_ref, receivers, receiver_wave, sem
):
    run([
        pltpu.make_async_copy(receiver_hbm, receivers, sem),
        pltpu.make_async_copy(receiver_wave_hbm, receiver_wave, sem),
    ])
    inject_points(receivers, receiver_wave, 256, (2, 3), r_ref, rs_ref)


def early_kernel(
    receiver_hbm, receiver_wave_hbm, source_hbm, source_wave_hbm, _,
    r_ref, rs_ref, s_ref, ss_ref,
    receivers, receiver_wave, sources, source_wave, sem,
):
    run([
        pltpu.make_async_copy(receiver_hbm, receivers, sem),
        pltpu.make_async_copy(receiver_wave_hbm, receiver_wave, sem),
        pltpu.make_async_copy(source_hbm, sources, sem),
        pltpu.make_async_copy(source_wave_hbm, source_wave, sem),
    ])
    inject_points(receivers, receiver_wave, 256, (0, 1), r_ref, rs_ref)
    inject_points(sources, source_wave, sources.shape[1], (0, 1, 2), s_ref, ss_ref)


def strip_of(packed, block, slot):
    lane = lanes(packed.shape)
    width = BX * STRIP
    shift = (block * width - slot * width) % BZ
    moved = pltpu.roll(packed, shift, 1) if shift else packed
    return jnp.where((lane >= block * width) & (lane < (block + 1) * width), moved, 0.0)


def y_up(v):
    return pltpu.roll(v, EY - 1, 0)


def y_down(v):
    return pltpu.roll(v, 1, 0)


def z_up(v, strip, x):
    edge = pltpu.roll(strip, (BZ - 1 - (x * STRIP + MARGIN)) % BZ, 1)
    return jnp.where(lanes(v.shape) == BZ - 1, edge, pltpu.roll(v, BZ - 1, 1))


def z_down(v, strip, x):
    edge = pltpu.roll(strip, (BZ - (x * STRIP + MARGIN - 1)) % BZ, 1)
    return jnp.where(lanes(v.shape) == 0, edge, pltpu.roll(v, 1, 1))


def strip_flux(values, buoyancy):
    flux_x = buoyancy * (pltpu.roll(values, BZ - STRIP, 1) - values)
    flux_y = buoyancy * (y_up(values) - values)
    flux_z = buoyancy * (pltpu.roll(values, BZ - 1, 1) - values)
    spread = (flux_x - pltpu.roll(flux_x, STRIP, 1)) + (flux_y - y_down(flux_y))
    return flux_z, spread + (flux_z - pltpu.roll(flux_z, 1, 1))


def cut_flags():
    gz, half = lax.axis_index("gz"), lax.axis_size("gz") // 2
    return jnp.where(gz == half - 1, 1.0, 0.0), jnp.where(gz == half, 1.0, 0.0)


def widened(blocks, flags, x, raw_first, tile_firsts):
    block, plane = divmod(x, BX)
    main, tiles = blocks[block]
    tile_first = tile_firsts[block][plane]
    if tile_first is None:
        tile = jnp.zeros((8, BZ), F32)
    else:
        tile = tiles[tile_first : tile_first + 8]
    first = raw_first[block][plane]
    if first is None:
        return jnp.zeros((EY, BZ), F32)
    value = jnp.concatenate([main[first : first + BY], tile], 0)
    return value if block == 1 else value * flags[block]


def series(base, wanted, step):
    result = [None] * BX
    for place, plane in enumerate(wanted):
        result[plane] = base + place * step
    return result


def side_flags():
    gx = lax.axis_index("gx")
    low = jnp.where(gx > 0, 1.0, 0.0)
    high = jnp.where(gx < lax.axis_size("gx") - 1, 1.0, 0.0)
    return low, None, high


def whole_strip(packed, flags, slot):
    parts = [strip_of(packed[block], block, slot) for block in range(3)]
    return parts[1] + parts[0] * flags[0] + parts[2] * flags[2]


def adjoint_kernel(
    raw_low, raw_own, raw_high, low, own, high, adj_hbm, ra_ref, rsa_ref, rb_ref, rsb_ref,
    tissue_hbm,
    out_ref, hist_ref, coef_ref, coef_strip_ref,
    field, tissue, sem, w_sem,
):
    w_copy = pltpu.make_async_copy(adj_hbm.at[pl.ds(1, 3)], out_ref.at[pl.ds(1, 3)], w_sem)
    w_copy.start()
    run([pltpu.make_async_copy(tissue_hbm, tissue, sem)])
    cut_up, cut_down = cut_flags()
    flags = side_flags()
    r_refs = ((ra_ref, 0), (ra_ref, 1), (rb_ref, 0), (rb_ref, 1))
    rs_refs = ((rsa_ref, 0), (rsa_ref, 1), (rsb_ref, 0), (rsb_ref, 1))
    every, lows, highs = range(BX), range(1, BX), range(BX - 1)
    base = WAVE_ROWS
    raws = (raw_low, raw_own, raw_high)
    lates = (low, own, high)

    def initial(index, x):
        tile = 3 * BY + base
        tiles = {
            0: (series(tile, lows, 8), series(PLANES, every, 8), series(tile, highs, 8)),
            1: (
                series(tile + 24, lows[1:], 8),
                series(PLANES + 32, every, 8),
                series(tile + 24, highs[:2], 8),
            ),
            2: (series(tile + 40, lows, 8), series(PLANES + 64, every, 8), series(tile + 40, highs, 8)),
        }[index]
        if index == 1:
            mains = lates
            firsts = (series(base, lows, BY), series(0, every, BY), series(base, highs, BY))
        else:
            mains = raws
            firsts = [series(PLANES * (1 if index == 0 else 2), every, BY)] * 3
        return widened(list(zip(mains, lates)), flags, x, firsts, tiles)

    for x in range(EX):
        for index, values in enumerate(coefficients(initial(2, x), tissue)):
            coef_ref[index, x] = values
    packed = [
        low[base + ADJ_ROWS - EY : base + ADJ_ROWS],
        own[ADJ_OWN_ROWS - EY : ADJ_OWN_ROWS],
        high[base + ADJ_ROWS - EY : base + ADJ_ROWS],
    ]
    q_s, t_s, label_s = (whole_strip(packed, flags, slot) for slot in range(3))
    stiff_s, buoy_s, damp_s = coefficients(label_s, tissue)
    coef_strip_ref[0], coef_strip_ref[1], coef_strip_ref[2] = stiff_s, buoy_s, damp_s
    w_copy.wait()

    for step in range(1, STEPS + 1):
        k = STEPS - step
        rs_ref, place = rs_refs[k]
        q_s = q_s + rs_ref[place]
        u_s = stiff_s * damp_s * q_s
        flux_s, spread = strip_flux(u_s, buoy_s)
        t_s = t_s + spread
        q_s = damp_s * q_s + t_s
        edge_up = u_s * cut_up
        edge_down = flux_s * cut_down

        def injected(x):
            r_ref, place = r_refs[k]
            value = initial(0, x) if step == 1 else field[0, x]
            value = value + r_ref[place, x]
            return value, coef_ref[0, x] * coef_ref[2, x] * value

        flux_below = None
        q_now, u_now = injected(step - 1)
        for x in range(step - 1, EX - step):
            q_next, u_next = injected(x + 1)
            buoyancy = coef_ref[1, x]
            slope_x = u_next - u_now
            flux_x = buoyancy * slope_x
            if x >= step:
                slope_y = y_up(u_now) - u_now
                slope_z = z_up(u_now, edge_up, x) - u_now
                flux_y = buoyancy * slope_y
                flux_z = buoyancy * slope_z
                spread = (flux_x - flux_below) + (flux_y - y_down(flux_y))
                spread = spread + (flux_z - z_down(flux_z, edge_down, x))
                damped = coef_ref[2, x] * q_now
                if BX <= x < 2 * BX:
                    place = x - BX
                    hist_ref[k, 0, place] = damped[0:BY]
                    for index, slope in enumerate((slope_x, slope_y, slope_z)):
                        w = out_ref[1 + index, place] + slope[0:BY]
                        out_ref[1 + index, place] = w
                        hist_ref[k, 1 + index, place] = w
                t = (initial(1, x) if step == 1 else field[1, x]) + spread
                if step < STEPS:
                    field[1, x] = t
                    field[0, x] = damped + t
                else:
                    out_ref[0, x - BX] = (damped + t)[0:BY]
            flux_below = flux_x
            q_now, u_now = q_next, u_next


def forward_kernel(
    raw_low, p_own, raw_high, low, own, high,
    coef_ref, coef_strip_ref, s_ref, ss_ref, hist_ref,
    grad_ref,
    field,
):
    cut_up, cut_down = cut_flags()
    flags = side_flags()
    every, lows, highs = range(BX), range(1, BX), range(BX - 1)
    raws = (raw_low, p_own, raw_high)
    lates = (low, own, high)

    def initial(index, x):
        tile = 3 * BY
        if index == 0:
            tiles = (series(tile, lows, 8), series(PLANES, every, 8), series(tile, highs, 8))
            return widened(list(zip(raws, lates)), flags, x, [series(0, every, BY)] * 3, tiles)
        tiles = (
            series(tile + 24, lows[1:], 8),
            series(PLANES + 32, every, 8),
            series(tile + 24, highs[:2], 8),
        )
        firsts = (series(0, lows, BY), series(0, every, BY), series(0, highs, BY))
        return widened(list(zip(lates, lates)), flags, x, firsts, tiles)

    packed = [
        low[WAVE_ROWS - EY : WAVE_ROWS],
        own[OWN_ROWS - EY : OWN_ROWS],
        high[WAVE_ROWS - EY : WAVE_ROWS],
    ]
    p_s, s_s = (whole_strip(packed, flags, slot) for slot in range(2))
    stiff_s, buoy_s, damp_s = coef_strip_ref[0], coef_strip_ref[1], coef_strip_ref[2]

    for step in range(1, STEPS + 1):
        k = step - 1
        edge_up = p_s * cut_up
        flux_s, spread = strip_flux(p_s, buoy_s)
        edge_down = flux_s * cut_down
        if step < STEPS:
            s_s = s_s - spread
            p_s = damp_s * (p_s - stiff_s * s_s) + ss_ref[k]

        def pressure(x):
            return initial(0, x) if step == 1 else field[0, x]

        flux_below = None
        p_now = pressure(step - 1)
        for x in range(step - 1, EX - step):
            p_next = pressure(x + 1)
            buoyancy = coef_ref[1, x]
            slope_x = p_next - p_now
            flux_x = buoyancy * slope_x
            if x >= step:
                slope_y = y_up(p_now) - p_now
                slope_z = z_up(p_now, edge_up, x) - p_now
                flux_y = buoyancy * slope_y
                flux_z = buoyancy * slope_z
                spread = (flux_x - flux_below) + (flux_y - y_down(flux_y))
                spread = spread + (flux_z - z_down(flux_z, edge_down, x))
                spread = (initial(1, x) if step == 1 else field[1, x]) - spread
                if step < STEPS:
                    field[1, x] = spread
                    field[0, x] = (
                        coef_ref[2, x] * (p_now - coef_ref[0, x] * spread) + s_ref[k, x]
                    )
                if BX <= x < 2 * BX:
                    place = x - BX
                    term = hist_ref[k, 0, place] * spread[0:BY]
                    grad_ref[0, place] = -term if k == 0 else grad_ref[0, place] - term
                    term = hist_ref[k, 1, place] * slope_x[0:BY]
                    term = term + hist_ref[k, 2, place] * slope_y[0:BY]
                    term = term + hist_ref[k, 3, place] * slope_z[0:BY]
                    grad_ref[1, place] = -term if k == 0 else grad_ref[1, place] - term
            flux_below = flux_x
            p_now = p_next


def shape(*dims):
    return jax.ShapeDtypeStruct(dims, F32)


def call(kernel, outs, operands, scratch, places):
    spaces = {"h": pltpu.HBM, "a": pl.ANY, "v": pltpu.VMEM}
    operands = [
        pltpu.with_memory_space_constraint(operand, pltpu.HBM) if place == "h" else operand
        for operand, place in zip(operands, places)
    ]
    return pl.pallas_call(
        kernel,
        out_shape=outs,
        in_specs=[pl.BlockSpec(memory_space=spaces[place]) for place in places],
        out_specs=[pl.BlockSpec(memory_space=pltpu.VMEM)] * len(outs),
        scratch_shapes=scratch,
        compiler_params=pltpu.CompilerParams(vmem_limit_bytes=VMEM_LIMIT),
        cost_estimate=pl.CostEstimate(flops=1 << 24, bytes_accessed=1 << 20, transcendentals=0),
    )(*operands)


def from_sides(array, axes):
    count = lax.axis_size("gy")

    def route(offset):
        pairs = []
        for target in range(count):
            source = target + offset
            if 0 <= source < count:
                if "gz" in axes:
                    pairs += [(2 * source + z, 2 * target + 1 - z) for z in range(2)]
                else:
                    pairs.append((source, target))
        return pairs

    if count == 2:
        both = lax.ppermute(array, axes, route(1) + route(-1))
        return both, both
    return lax.ppermute(array, axes, route(1)), lax.ppermute(array, axes, route(-1))


def rotated(array, axis, offset):
    count = lax.axis_size(axis)
    return lax.ppermute(array, axis, [((i + offset) % count, i) for i in range(count)])


def neighbours(to_next, to_last, cut):
    count = lax.axis_size("gx")
    if count == 4:
        return rotated(to_next, "gx", -1), rotated(to_last, "gx", 1)
    half = count // 2
    return (
        jnp.concatenate(
            [rotated(to_next[:cut], "gx", half + 1), rotated(to_next[cut:], "gx", -1)], 0
        ),
        jnp.concatenate(
            [rotated(to_last[:cut], "gx", half - 1), rotated(to_last[cut:], "gx", 1)], 0
        ),
    )


def local(
    stored, adjoint_end, labels, tissue, source_cells, source_wave, receiver_cells, receiver_wave
):
    assert lax.axis_size("gz") == 2 and labels.shape == (BX, BY, BZ)
    half = lax.axis_size("gx") // 2
    p, raw, s, t, face_x, face_y, face_z = call(
        face_kernel,
        [
            shape(PLANES, BZ),
            shape(3 * PLANES, BZ),
            shape(PLANES, BZ),
            shape(PLANES, BZ),
            shape(2 * BY, BZ),
            shape(8, BZ),
            shape(BY, BZ),
        ],
        [stored, adjoint_end, labels, tissue],
        [
            pltpu.VMEM(stored.shape, F32),
            pltpu.VMEM(adjoint_end.shape, F32),
            pltpu.VMEM(labels.shape, jnp.int32),
            pltpu.SMEM(tissue.shape, F32),
            pltpu.SemaphoreType.DMA,
        ],
        "hhhh",
    )
    receivers, sources = receiver_cells.T, source_cells.T
    point_scratch = [
        pltpu.VMEM(receivers.shape, jnp.int32),
        pltpu.VMEM(receiver_wave.shape, F32),
        pltpu.VMEM(sources.shape, jnp.int32),
        pltpu.VMEM(source_wave.shape, F32),
    ]
    rb, rsb = call(
        late_kernel,
        [shape(2, EX * EY, BZ), shape(2, EY, BZ)],
        [receivers, receiver_wave, face_y],
        point_scratch[:2] + [pltpu.SemaphoreType.DMA],
        "hha",
    )
    face_x = rotated(face_x, "gx", -1)
    face_y = rotated(face_y, "gy", -1)
    face_z = rotated(face_z, "gz", -1)
    p_own = rotated(p, "gx", half)
    raw_prev, raw_next = neighbours(raw, raw, PLANES)
    s, t, edges, corners, strips = call(
        pack_kernel,
        [
            shape(PLANES, BZ),
            shape(PLANES, BZ),
            shape((5 * BX + 2) * 8, BZ),
            shape(16, BZ),
            shape(2 * BY, BZ),
        ],
        [raw, s, t, face_x, face_y, face_z, rsb],
        [],
        "vvvvvva",
    )
    ra, rsa, src, src_strip = call(
        early_kernel,
        [
            shape(2, EX * EY, BZ),
            shape(2, EY, BZ),
            shape(STEPS - 1, EX * EY, BZ),
            shape(STEPS - 1, EY, BZ),
        ],
        [receivers, receiver_wave, sources, source_wave, corners],
        point_scratch + [pltpu.SemaphoreType.DMA],
        "hhhha",
    )
    ra, rb = ra.reshape(2, EX, EY, BZ), rb.reshape(2, EX, EY, BZ)
    src = src.reshape(STEPS - 1, EX, EY, BZ)
    other = rotated(strips, "gz", 1)
    up, down = from_sides(edges, "gy")
    corner_up, corner_down = from_sides(corners, ("gy", "gz"))
    late, adj_own, to_next, to_last = call(
        merge_kernel,
        [
            shape(OWN_ROWS, BZ),
            shape(ADJ_OWN_ROWS, BZ),
            shape(WAVE_ROWS + ADJ_ROWS, BZ),
            shape(WAVE_ROWS + ADJ_ROWS, BZ),
        ],
        [up, down, strips, other, corner_up, corner_down, s, t, rsa, p_own, raw_prev, raw_next],
        [],
        "vvvvvvvvaaaa",
    )
    late_prev, late_next = neighbours(to_next, to_last, WAVE_ROWS)
    late_own = rotated(late, "gx", half)
    adjoint_start, hist, coef, coef_strip = call(
        adjoint_kernel,
        [
            shape(4, BX, BY, BZ),
            shape(STEPS, 4, BX, BY, BZ),
            shape(3, EX, EY, BZ),
            shape(3, EY, BZ),
        ],
        [
            raw_prev, raw, raw_next, late_prev, adj_own, late_next,
            adjoint_end, ra, rsa, rb, rsb, tissue,
        ],
        [
            pltpu.VMEM((2, EX, EY, BZ), F32),
            pltpu.SMEM(tissue.shape, F32),
            pltpu.SemaphoreType.DMA,
            pltpu.SemaphoreType.DMA,
        ],
        "vvvvvvhvvvvh",
    )
    (gradient,) = call(
        forward_kernel,
        [shape(2, BX, BY, BZ)],
        [
            raw_next, p_own, raw_prev, late_next, late_own, late_prev,
            coef, coef_strip, src, src_strip, hist,
        ],
        [pltpu.VMEM((2, EX, EY, BZ), F32)],
        "vvvvvvvvvvv",
    )
    return gradient, adjoint_start


def solution(mesh):
    return jax.shard_map(
        local,
        mesh=mesh,
        in_specs=(
            P("shot", "gx", "gy", "gz"),
            P("shot", "gx", "gy", "gz"),
            P("gx", "gy", "gz"),
            P(),
            P("shot", None),
            P(None, "shot"),
            P(),
            P(None, "shot"),
        ),
        out_specs=(P("shot", "gx", "gy", "gz"), P("shot", "gx", "gy", "gz")),
        check_vma=False,
    )
```

time: 49.3 us -> 45.5 us (0.923)
  waiting for transfers between devices: 7.02 us -> 18.5 us
  starting transfers between devices: 23.8 us -> 13.4 us
  local copies, waits for them, and re-layouts: 4.11 us -> 0 us
  Pallas kernels: 13.3 us -> 12.5 us
    ppermute x10, waiting for transfers between devices: 4.51 us -> 15.4 us  [rotated(): lax.ppermute(array, axis, [((i + offset) % count, i) for i in range(count)])]
    ppermute x10, starting transfers between devices: 18.9 us -> 11.8 us  [rotated(): lax.ppermute(array, axis, [((i + offset) % count, i) for i in range(count)])]
    unnamed x20 -> x0, local copies, waits for them, and re-layouts: 4.11 us -> none
    ppermute x4 -> x0, starting transfers between devices: 2.45 us -> none  [paired(): return lax.ppermute(array, 'gx', pairs)]
    ppermute x2, starting transfers between devices: 2.42 us -> 1.56 us  [from_sides(): both = lax.ppermute(array, axes, route(1) + route(-1))]
    pallas_call x6 -> x7, Pallas kernels: 13.3 us -> 12.5 us  [call(): pl.pallas_call(kernel, out_shape=outs, in_specs=[pl.BlockSpec(memory_spac...]
    ppermute x2, waiting for transfers between devices: 2.49 us -> 3.08 us  [from_sides(): both = lax.ppermute(array, axes, route(1) + route(-1))]
  transfers between devices with their start and end apart: 16 -> 12, of which waited for: 4 -> 4; matrix products, arithmetic and copies ran while one was open for 0% -> 0% of each run, Pallas kernels for 17% -> 19%
where the time goes in v3:
time: 45.5 us; the launch traced here: 45 us
  waiting for transfers between devices  18.5 us (41%)
  starting transfers between devices  13.4 us (29%)
  Pallas kernels  12.5 us (27%)
  between operations  0.75 us (2%)
    ppermute x10, waiting for transfers between devices, rotated(): lax.ppermute(array, axis, [((i + offset) % count, i) for i in range(count)])  15.4 us
    pallas_call x7, Pallas kernels, call(): pl.pallas_call(kernel, out_shape=outs, in_specs=[pl.BlockSpec(memory_spac...  12.5 us
    ppermute x10, starting transfers between devices, rotated(): lax.ppermute(array, axis, [((i + offset) % count, i) for i in range(count)])  11.8 us
    ppermute x2, waiting for transfers between devices, from_sides(): both = lax.ppermute(array, axes, route(1) + route(-1))  3.08 us
    ppermute x2, starting transfers between devices, from_sides(): both = lax.ppermute(array, axes, route(1) + route(-1))  1.56 us
  transfers between devices with their start and end apart: 12, of which 4 were waited for; matrix products, arithmetic and copies ran while one was open for 0% of the time, Pallas kernels for 19%

profile of v3, /device:TPU:0, one launch (start us, length us, event | category | flops | bytes accessed | tf_op | source)
XLA Modules:
  0.0 45.0 jit_solution(3140692502757760852)
XLA Ops:
  0.6 1.2 %shard_map.95 = (f32[128,128]{1,0:T(8,128)S(1)}, f32[384,128]{1,0:T(8,128)S(1)}, f32[128,128]{1,0:T(8,128)S(1)}, f32[128,128]{1,0:T(8,128)S(1)}, f32[64,128]{1,0...) custom-call(f32[4,4,32,128]{3,2,1,0:T(8,128)} %stored_hbm.1, f32[4,4,32,128]{3,2,1,0:T(8,128)} %adj_hbm.3, ...), custom_call_target="tpu_custom_call" | custom-call | flops 16777216 | bytes 1048576 | tf_op jit(solution)/shard_map/pallas_call | solution.py:547
  1.8 3.1 %collective-permute-start.2 = (f32[384,128]{1,0:T(8,128)S(1)}, f32[384,128]{1,0:T(8,128)S(1)}, u32[]{:S(2)}, u32[]{:S(2)}) collective-permute-start(f32[384,128]{1,0:T(8,128)S(1)} %get-tuple-element.28.raw_ref.raw_own), channel_id=1, source_target_pairs={{12,0},{0,4},{4,8},{8,12},{13,1},{1,5},{5,9},{9,13},{14,2},{2,6},{... | collective-permute-start | bytes 589832 | tf_op jit(solution)/shard_map/ppermute | solution.py:580
  4.9 2.1 %collective-permute-start = (f32[384,128]{1,0:T(8,128)S(1)}, f32[384,128]{1,0:T(8,128)S(1)}, u32[]{:S(2)}, u32[]{:S(2)}) collective-permute-start(f32[384,128]{1,0:T(8,128)S(1)} %get-tuple-element.28.raw_ref.raw_own), channel_id=1, source_target_pairs={{4,0},{8,4},{12,8},{0,12},{5,1},{9,5},{13,9},{1,13},{6,2},{10,6},{... | collective-permute-start | bytes 589832 | tf_op jit(solution)/shard_map/ppermute | solution.py:580
  7.0 0.0 collective-permute-start.3
  7.0 0.0 collective-permute-start.5
  7.0 1.6 %collective-permute-start.4 = (f32[8,128]{1,0:T(8,128)S(1)}, f32[8,128]{1,0:T(8,128)S(1)}, u32[]{:S(2)}, u32[]{:S(2)}) collective-permute-start(f32[8,128]{1,0:T(8,128)S(1)} %get-tuple-element.33._), channel_id=1, source_target_pairs={{2,0},{0,2},{3,1},{1,3},{6,4},{4,6},{7,5},{5,7},{10,8},{8,10},{11,... | collective-permute-start | bytes 12296 | tf_op jit(solution)/shard_map/ppermute | solution.py:580
  8.6 2.0 %shard_map.96 = (f32[2,480,128]{2,1,0:T(8,128)S(1)}, f32[2,40,128]{2,1,0:T(8,128)S(1)}) custom-call(s32[3,1024]{1,0:T(4,128)} %bitcast.8, f32[4,1024]{1,0:T(4,128)} %receiver_wave_hbm.3, f32[8,128]{1,0:T(8,128)S(1)} %get-tuple-element.33._), custom_call_target="tpu_custom_call" | custom-call | flops 16777216 | bytes 1048576 | tf_op jit(solution)/shard_map/pallas_call | solution.py:547
  10.6 0.0 collective-permute-done.4.face_y
  10.7 0.0 collective-permute-done.5.face_z
  10.7 6.1 %collective-permute-done.3.face_x = f32[64,128]{1,0:T(8,128)S(1)} collective-permute-done((f32[64,128]{1,0:T(8,128)S(1)}, f32[64,128]{1,0:T(8,128)S(1)}, u32[]{:S(2)}, u32[]{:S(2)}) %collective-permute-start.3) | collective-permute-done | bytes 32800 | tf_op jit(solution)/shard_map/ppermute | solution.py:580
  16.8 0.2 shard_map.97
  17.0 1.6 %collective-permute-start.6 = (f32[176,128]{1,0:T(8,128)S(1)}, f32[176,128]{1,0:T(8,128)S(1)}, u32[]{:S(2)}, u32[]{:S(2)}) collective-permute-start(f32[176,128]{1,0:T(8,128)S(1)} %get-tuple-element.36), channel_id=1, source_target_pairs={{2,0},{0,2},{3,1},{1,3},{6,4},{4,6},{7,5},{5,7},{10,8},{8,10},{11,... | collective-permute-start | bytes 270344 | tf_op jit(solution)/shard_map/ppermute | solution.py:573
  18.6 0.7 %collective-permute-start.1 = (f32[128,128]{1,0:T(8,128)S(1)}, f32[128,128]{1,0:T(8,128)S(1)}, u32[]{:S(2)}, u32[]{:S(2)}) collective-permute-start(f32[128,128]{1,0:T(8,128)S(1)} %get-tuple-element.29), channel_id=1, source_target_pairs={{8,0},{12,4},{0,8},{4,12},{9,1},{13,5},{1,9},{5,13},{10,2},{14,6},... | collective-permute-start | bytes 196616 | tf_op jit(solution)/shard_map/ppermute | solution.py:580
  19.3 0.0 collective-permute-start.8
  19.3 3.1 %collective-permute-done.8.corner_up_ref.corner_down_ref = f32[16,128]{1,0:T(8,128)S(1)} collective-permute-done((f32[16,128]{1,0:T(8,128)S(1)}, f32[16,128]{1,0:T(8,128)S(1)}, u32[]{:S(2)}, u32[]{:S(2)}) %collective-permute-start.8) | collective-permute-done | bytes 8224 | tf_op jit(solution)/shard_map/ppermute | solution.py:573
  22.3 0.0 collective-permute-start.7
  22.3 2.3 %shard_map.98 = (f32[2,480,128]{2,1,0:T(8,128)S(1)}, f32[2,40,128]{2,1,0:T(8,128)S(1)}, f32[3,480,128]{2,1,0:T(8,128)S(1)}, f32[3,40,128]{2,1,0:T(8,128)S(1)}) custom-call(s32[3,1024]{1,0:T(4,128)} %bitcast.9, f32[4,1024]{1,0:T(4,128)} %receiver_wave_hbm.3, s32[3,64]{1,0:T(4,128)} %bitcast.10, f32[4,64]{1,0:T(4,128)} %source_wave_hbm.1, ...), custom_call_target="tpu_custom_call" | custom-call | flops 16777216 | bytes 1048576 | tf_op jit(solution)/shard_map/pallas_call | solution.py:547
  24.7 0.0 collective-permute-done.1._b.p_own
  24.7 0.0 collective-permute-done.7.other_ref
  24.7 0.0 collective-permute-done.6.up_ref.down_ref
  24.7 0.0 collective-permute-done.2._c.raw_low.raw_high
  24.7 0.0 collective-permute-done._d.raw_high.raw_low
  24.7 0.1 shard_map.99
  24.8 1.4 %collective-permute-start.9 = (f32[376,128]{1,0:T(8,128)S(1)}, f32[376,128]{1,0:T(8,128)S(1)}, u32[]{:S(2)}, u32[]{:S(2)}) collective-permute-start(f32[376,128]{1,0:T(8,128)S(1)} %get-tuple-element.42), channel_id=1, source_target_pairs={{4,0},{8,4},{12,8},{0,12},{5,1},{9,5},{13,9},{1,13},{6,2},{10,6},{... | collective-permute-start | bytes 577544 | tf_op jit(solution)/shard_map/ppermute | solution.py:580
  26.2 0.7 %collective-permute-start.11 = (f32[376,128]{1,0:T(8,128)S(1)}, f32[376,128]{1,0:T(8,128)S(1)}, u32[]{:S(2)}, u32[]{:S(2)}) collective-permute-start(f32[376,128]{1,0:T(8,128)S(1)} %get-tuple-element.44), channel_id=1, source_target_pairs={{12,0},{0,4},{4,8},{8,12},{13,1},{1,5},{5,9},{9,13},{14,2},{2,6},{... | collective-permute-start | bytes 577544 | tf_op jit(solution)/shard_map/ppermute | solution.py:580
  26.9 2.2 %collective-permute-start.10 = (f32[232,128]{1,0:T(8,128)S(1)}, f32[232,128]{1,0:T(8,128)S(1)}, u32[]{:S(2)}, u32[]{:S(2)}) collective-permute-start(f32[232,128]{1,0:T(8,128)S(1)} %get-tuple-element.43), channel_id=1, source_target_pairs={{8,0},{12,4},{0,8},{4,12},{9,1},{13,5},{1,9},{5,13},{10,2},{14,6},... | collective-permute-start | bytes 356360 | tf_op jit(solution)/shard_map/ppermute | solution.py:580
  29.1 3.0 %collective-permute-done.9.high.low = f32[376,128]{1,0:T(8,128)S(1)} collective-permute-done((f32[376,128]{1,0:T(8,128)S(1)}, f32[376,128]{1,0:T(8,128)S(1)}, u32[]{:S(2)}, u32[]{:S(2)}) %collective-permute-start.9) | collective-permute-done | bytes 192544 | tf_op jit(solution)/shard_map/ppermute | solution.py:580
  32.1 6.3 %collective-permute-done.11.low.high = f32[376,128]{1,0:T(8,128)S(1)} collective-permute-done((f32[376,128]{1,0:T(8,128)S(1)}, f32[376,128]{1,0:T(8,128)S(1)}, u32[]{:S(2)}, u32[]{:S(2)}) %collective-permute-start.11) | collective-permute-done | bytes 192544 | tf_op jit(solution)/shard_map/ppermute | solution.py:580
  38.4 4.0 %shard_map.100 = (f32[4,4,32,128]{3,2,1,0:T(8,128)}, f32[4,4,4,32,128]{4,3,2,1,0:T(8,128)S(1)}, f32[3,12,40,128]{3,2,1,0:T(8,128)S(1)}, f32[3,40,128]{2,1,0:T(8,128)S(1)}) custom-call(f32[384,128]{1,0:T(8,128)S(1)} %collective-permute-done.2._c.raw_low.raw_high, f32[384,128]{1,0:T(8,128)S(1)} %get-tuple-element.28.raw_ref.raw_own, ...), custom_call_target="tpu_custom_call" | custom-call | flops 16777216 | bytes 1048576 | tf_op jit(solution)/shard_map/pallas_call | solution.py:547
  42.4 0.0 collective-permute-done.10.own
  42.4 2.6 %shard_map.101 = f32[2,4,32,128]{3,2,1,0:T(8,128)} custom-call(f32[384,128]{1,0:T(8,128)S(1)} %collective-permute-done._d.raw_high.raw_low, f32[128,128]{1,0:T(8,128)S(1)} %collective-permute-done.1._b.p_own, f32[384,128]{1,0:T(8,128)S(1)} %collective-permute-done.2._c.raw_low.raw_high, f32[376,128]{1,0:T(8,128)S(1)} %collective-permute-done.9.high.low, ...), custom_call_target="tpu_custom_call" | custom-call | flops 16777216 | bytes 1048576 | tf_op jit(solution)/shard_map/pallas_call | solution.py:547
Async XLA Ops:
  1.8 22.9 %collective-permute-start.2 = (f32[384,128]{1,0:T(8,128)S(1)}, f32[384,128]{1,0:T(8,128)S(1)}, u32[]{:S(2)}, u32[]{:S(2)}) collective-permute-start(f32[384,128]{1,0:T(8,128)S(1)} %get-tuple-element.28.raw_ref.raw_own), channel_id=1, source_target_pairs={{12,0},{0,4},{4,8},{8,12},{13,1},{1,5},{5,9},{9,13},{14,2},{2,6},{... | collective-permute-start | bytes 589832 | tf_op jit(solution)/shard_map/ppermute | solution.py:580
  4.9 19.8 %collective-permute-start = (f32[384,128]{1,0:T(8,128)S(1)}, f32[384,128]{1,0:T(8,128)S(1)}, u32[]{:S(2)}, u32[]{:S(2)}) collective-permute-start(f32[384,128]{1,0:T(8,128)S(1)} %get-tuple-element.28.raw_ref.raw_own), channel_id=1, source_target_pairs={{4,0},{8,4},{12,8},{0,12},{5,1},{9,5},{13,9},{1,13},{6,2},{10,6},{... | collective-permute-start | bytes 589832 | tf_op jit(solution)/shard_map/ppermute | solution.py:580
  7.0 9.8 %collective-permute-start.3 = (f32[64,128]{1,0:T(8,128)S(1)}, f32[64,128]{1,0:T(8,128)S(1)}, u32[]{:S(2)}, u32[]{:S(2)}) collective-permute-start(f32[64,128]{1,0:T(8,128)S(1)} %get-tuple-element.32), channel_id=1, source_target_pairs={{12,0},{0,4},{4,8},{8,12},{13,1},{1,5},{5,9},{9,13},{14,2},{2,6},{... | collective-permute-start | bytes 98312 | tf_op jit(solution)/shard_map/ppermute | solution.py:580
  7.0 3.7 %collective-permute-start.5 = (f32[32,128]{1,0:T(8,128)S(1)}, f32[32,128]{1,0:T(8,128)S(1)}, u32[]{:S(2)}, u32[]{:S(2)}) collective-permute-start(f32[32,128]{1,0:T(8,128)S(1)} %get-tuple-element.34), channel_id=1, source_target_pairs={{1,0},{0,1},{3,2},{2,3},{5,4},{4,5},{7,6},{6,7},{9,8},{8,9},{11,10... | collective-permute-start | bytes 49160 | tf_op jit(solution)/shard_map/ppermute | solution.py:580
  7.0 3.6 %collective-permute-start.4 = (f32[8,128]{1,0:T(8,128)S(1)}, f32[8,128]{1,0:T(8,128)S(1)}, u32[]{:S(2)}, u32[]{:S(2)}) collective-permute-start(f32[8,128]{1,0:T(8,128)S(1)} %get-tuple-element.33._), channel_id=1, source_target_pairs={{2,0},{0,2},{3,1},{1,3},{6,4},{4,6},{7,5},{5,7},{10,8},{8,10},{11,... | collective-permute-start | bytes 12296 | tf_op jit(solution)/shard_map/ppermute | solution.py:580
  17.0 7.7 %collective-permute-start.6 = (f32[176,128]{1,0:T(8,128)S(1)}, f32[176,128]{1,0:T(8,128)S(1)}, u32[]{:S(2)}, u32[]{:S(2)}) collective-permute-start(f32[176,128]{1,0:T(8,128)S(1)} %get-tuple-element.36), channel_id=1, source_target_pairs={{2,0},{0,2},{3,1},{1,3},{6,4},{4,6},{7,5},{5,7},{10,8},{8,10},{11,... | collective-permute-start | bytes 270344 | tf_op jit(solution)/shard_map/ppermute | solution.py:573
  18.6 6.1 %collective-permute-start.1 = (f32[128,128]{1,0:T(8,128)S(1)}, f32[128,128]{1,0:T(8,128)S(1)}, u32[]{:S(2)}, u32[]{:S(2)}) collective-permute-start(f32[128,128]{1,0:T(8,128)S(1)} %get-tuple-element.29), channel_id=1, source_target_pairs={{8,0},{12,4},{0,8},{4,12},{9,1},{13,5},{1,9},{5,13},{10,2},{14,6},... | collective-permute-start | bytes 196616 | tf_op jit(solution)/shard_map/ppermute | solution.py:580
  19.3 3.1 %collective-permute-start.8 = (f32[16,128]{1,0:T(8,128)S(1)}, f32[16,128]{1,0:T(8,128)S(1)}, u32[]{:S(2)}, u32[]{:S(2)}) collective-permute-start(f32[16,128]{1,0:T(8,128)S(1)} %get-tuple-element.38._), channel_id=1, source_target_pairs={{2,1},{3,0},{0,3},{1,2},{6,5},{7,4},{4,7},{5,6},{10,9},{11,8},{8,1... | collective-permute-start | bytes 24584 | tf_op jit(solution)/shard_map/ppermute | solution.py:573
  22.3 2.4 %collective-permute-start.7 = (f32[64,128]{1,0:T(8,128)S(1)}, f32[64,128]{1,0:T(8,128)S(1)}, u32[]{:S(2)}, u32[]{:S(2)}) collective-permute-start(f32[64,128]{1,0:T(8,128)S(1)} %get-tuple-element.37.strip_ref), channel_id=1, source_target_pairs={{1,0},{0,1},{3,2},{2,3},{5,4},{4,5},{7,6},{6,7},{9,8},{8,9},{11,10... | collective-permute-start | bytes 98312 | tf_op jit(solution)/shard_map/ppermute | solution.py:580
  24.8 7.3 %collective-permute-start.9 = (f32[376,128]{1,0:T(8,128)S(1)}, f32[376,128]{1,0:T(8,128)S(1)}, u32[]{:S(2)}, u32[]{:S(2)}) collective-permute-start(f32[376,128]{1,0:T(8,128)S(1)} %get-tuple-element.42), channel_id=1, source_target_pairs={{4,0},{8,4},{12,8},{0,12},{5,1},{9,5},{13,9},{1,13},{6,2},{10,6},{... | collective-permute-start | bytes 577544 | tf_op jit(solution)/shard_map/ppermute | solution.py:580
  26.2 12.1 %collective-permute-start.11 = (f32[376,128]{1,0:T(8,128)S(1)}, f32[376,128]{1,0:T(8,128)S(1)}, u32[]{:S(2)}, u32[]{:S(2)}) collective-permute-start(f32[376,128]{1,0:T(8,128)S(1)} %get-tuple-element.44), channel_id=1, source_target_pairs={{12,0},{0,4},{4,8},{8,12},{13,1},{1,5},{5,9},{9,13},{14,2},{2,6},{... | collective-permute-start | bytes 577544 | tf_op jit(solution)/shard_map/ppermute | solution.py:580
  26.9 15.5 %collective-permute-start.10 = (f32[232,128]{1,0:T(8,128)S(1)}, f32[232,128]{1,0:T(8,128)S(1)}, u32[]{:S(2)}, u32[]{:S(2)}) collective-permute-start(f32[232,128]{1,0:T(8,128)S(1)} %get-tuple-element.43), channel_id=1, source_target_pairs={{8,0},{12,4},{0,8},{4,12},{9,1},{13,5},{1,9},{5,13},{10,2},{14,6},... | collective-permute-start | bytes 356360 | tf_op jit(solution)/shard_map/ppermute | solution.py:580

commit v4 on v3

--- a/solution.py
+++ b/solution.py
@@ -14,10 +14,10 @@
 BF16 = jnp.bfloat16
 VMEM_LIMIT = 16 * 1024 * 1024
 PLANES = BX * BY
-OWN_ROWS = PLANES + 2 * BX * 8 + EY
-ADJ_OWN_ROWS = PLANES + 3 * BX * 8 + EY
-WAVE_ROWS = 3 * BY + 5 * 8 + EY
-ADJ_ROWS = 3 * BY + 8 * 8 + EY
+WAVE_EDGE_ROWS = 2 * BX * 8 + EY
+ADJ_EDGE_ROWS = 3 * BX * 8 + EY
+WAVE_ROWS = PLANES + 3 * BY + 5 * 8 + EY
+ADJ_ROWS = 2 * PLANES + 3 * BY + 8 * 8 + EY
 
 
 def lanes(shape):
@@ -35,44 +35,42 @@
         copy.wait()
 
 
-def class_values(tissue_ref, index):
-    speed = jnp.full((1, BZ), tissue_ref[0, index], F32)
-    density = jnp.full((1, BZ), tissue_ref[1, index], F32)
-    damping = 1.0 - jnp.full((1, BZ), tissue_ref[2, index], F32)
-    return density * speed, speed / density, damping
-
-
-def buoyancy_of(labels, tissue_ref):
+def coefficients(labels, table_ref):
+    result = [jnp.zeros(labels.shape, F32) for _ in range(3)]
+    for index in range(8):
+        picked = labels == float(index + 1)
+        for kind in range(3):
+            row = kind * 8 + index
+            result[kind] = jnp.where(picked, table_ref[row : row + 1], result[kind])
+    return result
+
+
+def buoyancy_of(labels, table_ref):
     result = jnp.zeros(labels.shape, F32)
-    for index in range(tissue_ref.shape[1]):
-        result = jnp.where(labels == float(index + 1), class_values(tissue_ref, index)[1], result)
+    for index in range(8):
+        result = jnp.where(labels == float(index + 1), table_ref[8 + index : 9 + index], result)
     return result
 
 
-def coefficients(labels, tissue_ref):
-    stiffness = jnp.zeros(labels.shape, F32)
-    buoyancy = jnp.zeros(labels.shape, F32)
-    damping = jnp.zeros(labels.shape, F32)
-    for index in range(tissue_ref.shape[1]):
-        picked = labels == float(index + 1)
-        values = class_values(tissue_ref, index)
-        stiffness = jnp.where(picked, values[0], stiffness)
-        buoyancy = jnp.where(picked, values[1], buoyancy)
-        damping = jnp.where(picked, values[2], damping)
-    return stiffness, buoyancy, damping
-
-
 def face_kernel(
-    stored_hbm, adj_hbm, lab_hbm, tissue_hbm,
-    p_ref, raw_ref, s_ref, t_ref, face_x_ref, face_y_ref, face_z_ref,
+    stored_hbm, adj_hbm, lab_hbm, tissue_hbm, rc_hbm, rw_hbm, sc_hbm, sw_hbm,
+    raw_ref, s_ref, t_ref, face_x_ref, face_y_ref, face_z_ref, table_ref,
+    rc_ref, rw_ref, sc_ref, sw_ref,
     stored, adj, lab, tissue, sem,
 ):
     run([
-        pltpu.make_async_copy(stored_hbm, stored, sem),
-        pltpu.make_async_copy(adj_hbm, adj, sem),
-        pltpu.make_async_copy(lab_hbm, lab, sem),
-        pltpu.make_async_copy(tissue_hbm, tissue, sem),
+        pltpu.make_async_copy(source, target, sem)
+        for source, target in (
+            (stored_hbm, stored), (adj_hbm, adj), (lab_hbm, lab), (tissue_hbm, tissue),
+            (rc_hbm, rc_ref), (rw_hbm, rw_ref), (sc_hbm, sc_ref), (sw_hbm, sw_ref),
+        )
     ])
+    for index in range(tissue.shape[1]):
+        speed = jnp.full((1, BZ), tissue[0, index], F32)
+        density = jnp.full((1, BZ), tissue[1, index], F32)
+        table_ref[index : index + 1] = density * speed
+        table_ref[8 + index : 9 + index] = speed / density
+        table_ref[16 + index : 17 + index] = 1.0 - jnp.full((1, BZ), tissue[2, index], F32)
     lane = lanes((BY, BZ))
     row = rows((BY, BZ))
     tile_row = rows((8, BZ))
@@ -81,9 +79,8 @@
     previous = [None, None]
     for x in range(BX):
         labels = lab[x].astype(F32) + 1.0
-        buoyancy = buoyancy_of(labels, tissue)
+        buoyancy = buoyancy_of(labels, table_ref)
         plane = slice(x * BY, x * BY + BY)
-        p_ref[plane] = stored[0, x]
         for index, values in enumerate((stored[0, x], adj[0, x], labels)):
             raw_ref[index * PLANES + x * BY : index * PLANES + x * BY + BY] = values
         for kind, v in enumerate((stored, adj)):
@@ -109,7 +106,7 @@
 
 def pack_kernel(
     raw_ref, s_in, t_in, face_x, face_y, face_z, _,
-    s_ref, t_ref, edge_ref, corner_ref, strip_ref,
+    wave_ref, t_ref, edge_ref, corner_ref, strip_ref,
 ):
     gx, gy, gz = (lax.axis_index(name) for name in ("gx", "gy", "gz"))
     count = lax.axis_size("gx")
@@ -136,10 +133,15 @@
                 lane_below = pltpu.roll(tile_z, (BZ - index) % BZ, 1) if index else tile_z
                 block = block - jnp.where(row == 0, tile_y[index : index + 1], 0.0)
                 block = block - jnp.where(lane == 0, lane_below, 0.0)
-                (s_ref, t_ref)[kind][plane] = block
+                if kind == 0:
+                    wave_ref[PLANES + x * BY : PLANES + x * BY + BY] = block
+                else:
+                    t_ref[plane] = block
             else:
                 first = field // 2 * PLANES + x * BY
                 block = raw_ref[first : first + BY]
+                if field == 0:
+                    wave_ref[plane] = block
             tile = jnp.where(tile_row < MARGIN, block[0:8], block[BY - 8 : BY])
             index = field * BX + x
             edge_ref[index * 8 : index * 8 + 8] = tile
@@ -158,10 +160,19 @@
         corner_ref[group * 8 : group * 8 + 8] = tile
 
 
+def copy_rows(target, base, source, first, count):
+    target[base : base + count] = source[pl.ds(pl.multiple_of(first, 8), count)]
+    return base + count
+
+
+def pair_planes():
+    parity = lax.rem(lax.axis_index("gx"), 2)
+    return 1 - parity, parity
+
+
 def merge_kernel(
-    up_ref, down_ref, strip_ref, other_ref, corner_up_ref, corner_down_ref, s_ref, t_ref,
-    _a, _b, _c, _d,
-    own_ref, adj_own_ref, to_next_ref, to_last_ref,
+    up_ref, down_ref, strip_ref, other_ref, corner_up_ref, corner_down_ref, raw_ref, t_ref, _,
+    wave_edge_ref, adj_edge_ref, even_ref, odd_ref,
 ):
     gy = lax.axis_index("gy")
     row = rows((8, BZ))
@@ -172,30 +183,31 @@
         sl = slice(index * 8, index * 8 + 8)
         return jnp.where(take_up, up[sl], jnp.where(take_down, down[sl], 0.0))
 
-    tiles = [halo(up_ref, down_ref, index) for index in range(5 * BX)]
-    strips = []
-    for group in range(2):
+    for index in range(5 * BX):
+        target, place = (wave_edge_ref, index) if index < 8 else (adj_edge_ref, index - 8)
+        target[place * 8 : place * 8 + 8] = halo(up_ref, down_ref, index)
+    for group, target in enumerate((wave_edge_ref, adj_edge_ref)):
+        base = target.shape[0] - EY
         sl = slice(group * BY, group * BY + BY)
+        target[base : base + BY] = strip_ref[sl] + other_ref[sl]
         tile = halo(up_ref, down_ref, 5 * BX + group) + halo(corner_up_ref, corner_down_ref, group)
-        strips.append((strip_ref[sl] + other_ref[sl], tile))
-
-    def put(target, base, planes, chosen, strip):
-        target[base : base + planes.shape[0]] = planes
-        base += planes.shape[0]
-        for index in chosen:
-            target[base : base + 8] = tiles[index]
-            base += 8
-        target[base : base + BY] = strip[0]
-        target[base + BY : base + EY] = strip[1]
-
-    put(own_ref, 0, s_ref[...], range(2 * BX), strips[0])
-    put(adj_own_ref, 0, t_ref[...], range(2 * BX, 5 * BX), strips[1])
-    above, below = s_ref[0 : 3 * BY], s_ref[BY:PLANES]
-    put(to_next_ref, 0, above, (0, 1, 2, 4, 5), strips[0])
-    put(to_last_ref, 0, below, (1, 2, 3, 6, 7), strips[0])
-    above, below = t_ref[0 : 3 * BY], t_ref[BY:PLANES]
-    put(to_next_ref, WAVE_ROWS, below, (9, 10, 11, 14, 15, 17, 18, 19), strips[1])
-    put(to_last_ref, WAVE_ROWS, above, (8, 9, 10, 12, 13, 16, 17, 18), strips[1])
+        target[base + BY : base + EY] = tile
+    for target, first in zip((even_ref, odd_ref), pair_planes()):
+        base = copy_rows(target, 0, raw_ref, PLANES, 2 * PLANES)
+        base = copy_rows(target, base, t_ref, first * BY, 3 * BY)
+        base = copy_rows(target, base, adj_edge_ref, first * 8, 24)
+        base = copy_rows(target, base, adj_edge_ref, 32 + first * 16, 16)
+        base = copy_rows(target, base, adj_edge_ref, 64 + first * 8, 24)
+        copy_rows(target, base, adj_edge_ref, ADJ_EDGE_ROWS - EY, EY)
+
+
+def join_kernel(wave_ref, edge_ref, even_ref, odd_ref):
+    for target, first in zip((even_ref, odd_ref), pair_planes()):
+        base = copy_rows(target, 0, wave_ref, 0, PLANES)
+        base = copy_rows(target, base, wave_ref, PLANES + first * BY, 3 * BY)
+        base = copy_rows(target, base, edge_ref, first * 8, 24)
+        base = copy_rows(target, base, edge_ref, 32 + first * 16, 16)
+        copy_rows(target, base, edge_ref, WAVE_EDGE_ROWS - EY, EY)
 
 
 def split(values):
@@ -233,12 +245,12 @@
     )
 
 
-def inject_points(cells, wave_ref, width, waves, out_ref, strip_out_ref):
-    count = len(waves)
+def inject_points(cells, wave_ref, width, waves, planes, out_ref, strip_out_ref):
+    count, low, total_rows = len(waves), planes[0] * EY, (planes[1] - planes[0]) * EY
     for start in range(0, cells.shape[1], width):
         sl = slice(start, start + width)
         flat, z, row, strip_lane = places(cells, sl)
-        here = hits(EX * EY, flat).astype(F32).astype(BF16)
+        here = hits(total_rows, flat - low).astype(F32).astype(BF16)
         at_strip = hits(BZ, strip_lane).astype(F32).astype(BF16)
         at_z, at_row = hits(BZ, z), hits(EY, row)
         total = strip_total = None
@@ -260,29 +272,19 @@
             strip_out_ref[wave] = strip_value
 
 
-def late_kernel(
-    receiver_hbm, receiver_wave_hbm, _, r_ref, rs_ref, receivers, receiver_wave, sem
+LATE_PLANES, EARLY_PLANES, SOURCE_PLANES = (0, EX), (2, EX - 2), (1, EX - 1)
+
+
+def late_kernel(receivers, receiver_wave, r_ref, rs_ref):
+    inject_points(receivers, receiver_wave, 256, (2, 3), LATE_PLANES, r_ref, rs_ref)
+
+
+def early_kernel(
+    receivers, receiver_wave, sources, source_wave, _, r_ref, rs_ref, s_ref, ss_ref
 ):
-    run([
-        pltpu.make_async_copy(receiver_hbm, receivers, sem),
-        pltpu.make_async_copy(receiver_wave_hbm, receiver_wave, sem),
-    ])
-    inject_points(receivers, receiver_wave, 256, (2, 3), r_ref, rs_ref)
-
-
-def early_kernel(
-    receiver_hbm, receiver_wave_hbm, source_hbm, source_wave_hbm, _,
-    r_ref, rs_ref, s_ref, ss_ref,
-    receivers, receiver_wave, sources, source_wave, sem,
-):
-    run([
-        pltpu.make_async_copy(receiver_hbm, receivers, sem),
-        pltpu.make_async_copy(receiver_wave_hbm, receiver_wave, sem),
-        pltpu.make_async_copy(source_hbm, sources, sem),
-        pltpu.make_async_copy(source_wave_hbm, source_wave, sem),
-    ])
-    inject_points(receivers, receiver_wave, 256, (0, 1), r_ref, rs_ref)
-    inject_points(sources, source_wave, sources.shape[1], (0, 1, 2), s_ref, ss_ref)
+    inject_points(receivers, receiver_wave, 256, (0, 1), EARLY_PLANES, r_ref, rs_ref)
+    width = sources.shape[1]
+    inject_points(sources, source_wave, width, (0, 1, 2), SOURCE_PLANES, s_ref, ss_ref)
 
 
 def strip_of(packed, block, slot):
@@ -324,87 +326,79 @@
     return jnp.where(gz == half - 1, 1.0, 0.0), jnp.where(gz == half, 1.0, 0.0)
 
 
-def widened(blocks, flags, x, raw_first, tile_firsts):
-    block, plane = divmod(x, BX)
-    main, tiles = blocks[block]
-    tile_first = tile_firsts[block][plane]
-    if tile_first is None:
-        tile = jnp.zeros((8, BZ), F32)
-    else:
-        tile = tiles[tile_first : tile_first + 8]
-    first = raw_first[block][plane]
-    if first is None:
-        return jnp.zeros((EY, BZ), F32)
-    value = jnp.concatenate([main[first : first + BY], tile], 0)
-    return value if block == 1 else value * flags[block]
-
-
-def series(base, wanted, step):
-    result = [None] * BX
-    for place, plane in enumerate(wanted):
-        result[plane] = base + place * step
-    return result
-
-
-def side_flags():
+def sides():
     gx = lax.axis_index("gx")
     low = jnp.where(gx > 0, 1.0, 0.0)
     high = jnp.where(gx < lax.axis_size("gx") - 1, 1.0, 0.0)
-    return low, None, high
-
-
-def whole_strip(packed, flags, slot):
-    parts = [strip_of(packed[block], block, slot) for block in range(3)]
-    return parts[1] + parts[0] * flags[0] + parts[2] * flags[2]
+    return low, high, lax.rem(gx, 2) == 0
+
+
+def from_side(messages, first, count, block, side):
+    even, odd = (message[first : first + count] for message in messages)
+    low, high, even_above = side
+    if block == 0:
+        return jnp.where(even_above, odd, even) * low
+    return jnp.where(even_above, even, odd) * high
+
+
+def side_rows(base, wanted, step, block):
+    planes = range(BX - wanted, BX) if block == 0 else range(wanted)
+    return {plane: base + place * step for place, plane in enumerate(planes)}
+
+
+def widened(own, own_tiles, messages, x, layout, side):
+    block, plane = divmod(x, BX)
+    if block == 1:
+        main = own[0][own[1] + plane * BY : own[1] + plane * BY + BY]
+        tile = own_tiles[0][own_tiles[1] + plane * 8 : own_tiles[1] + plane * 8 + 8]
+        return jnp.concatenate([main, tile], 0)
+    parts = []
+    for (base, wanted), count in zip(layout, (BY, 8)):
+        first = side_rows(base, wanted, count, block).get(plane)
+        if first is None:
+            parts.append(jnp.zeros((count, BZ), F32))
+        else:
+            parts.append(from_side(messages, first, count, block, side))
+    return jnp.concatenate(parts, 0)
+
+
+def whole_strip(own, messages, first, slot, side):
+    low = from_side(messages, first, EY, 0, side)
+    high = from_side(messages, first, EY, 2, side)
+    return strip_of(low, 0, slot) + strip_of(own, 1, slot) + strip_of(high, 2, slot)
 
 
 def adjoint_kernel(
-    raw_low, raw_own, raw_high, low, own, high, adj_hbm, ra_ref, rsa_ref, rb_ref, rsb_ref,
-    tissue_hbm,
+    raw_ref, t_ref, edge_ref, even, odd, adj_hbm, ra_ref, rsa_ref, rb_ref, rsb_ref, table_ref,
     out_ref, hist_ref, coef_ref, coef_strip_ref,
-    field, tissue, sem, w_sem,
+    field, w_sem,
 ):
     w_copy = pltpu.make_async_copy(adj_hbm.at[pl.ds(1, 3)], out_ref.at[pl.ds(1, 3)], w_sem)
     w_copy.start()
-    run([pltpu.make_async_copy(tissue_hbm, tissue, sem)])
     cut_up, cut_down = cut_flags()
-    flags = side_flags()
+    side = sides()
+    messages = (even, odd)
     r_refs = ((ra_ref, 0), (ra_ref, 1), (rb_ref, 0), (rb_ref, 1))
     rs_refs = ((rsa_ref, 0), (rsa_ref, 1), (rsb_ref, 0), (rsb_ref, 1))
-    every, lows, highs = range(BX), range(1, BX), range(BX - 1)
-    base = WAVE_ROWS
-    raws = (raw_low, raw_own, raw_high)
-    lates = (low, own, high)
+    tiles = 2 * PLANES + 3 * BY
 
     def initial(index, x):
-        tile = 3 * BY + base
-        tiles = {
-            0: (series(tile, lows, 8), series(PLANES, every, 8), series(tile, highs, 8)),
-            1: (
-                series(tile + 24, lows[1:], 8),
-                series(PLANES + 32, every, 8),
-                series(tile + 24, highs[:2], 8),
-            ),
-            2: (series(tile + 40, lows, 8), series(PLANES + 64, every, 8), series(tile + 40, highs, 8)),
-        }[index]
-        if index == 1:
-            mains = lates
-            firsts = (series(base, lows, BY), series(0, every, BY), series(base, highs, BY))
-        else:
-            mains = raws
-            firsts = [series(PLANES * (1 if index == 0 else 2), every, BY)] * 3
-        return widened(list(zip(mains, lates)), flags, x, firsts, tiles)
+        own = ((raw_ref, PLANES), (t_ref, 0), (raw_ref, 2 * PLANES))[index]
+        layout = (
+            ((0, 4), (tiles, 3)),
+            ((2 * PLANES, 3), (tiles + 24, 2)),
+            ((PLANES, 4), (tiles + 40, 3)),
+        )[index]
+        return widened(own, (edge_ref, 32 * index), messages, x, layout, side)
 
     for x in range(EX):
-        for index, values in enumerate(coefficients(initial(2, x), tissue)):
-            coef_ref[index, x] = values
-    packed = [
-        low[base + ADJ_ROWS - EY : base + ADJ_ROWS],
-        own[ADJ_OWN_ROWS - EY : ADJ_OWN_ROWS],
-        high[base + ADJ_ROWS - EY : base + ADJ_ROWS],
-    ]
-    q_s, t_s, label_s = (whole_strip(packed, flags, slot) for slot in range(3))
-    stiff_s, buoy_s, damp_s = coefficients(label_s, tissue)
+        stiff, buoy, damp = coefficients(initial(2, x), table_ref)
+        coef_ref[0, x], coef_ref[1, x], coef_ref[2, x] = stiff, buoy, damp
+    own_strip = edge_ref[ADJ_EDGE_ROWS - EY : ADJ_EDGE_ROWS]
+    q_s, t_s, label_s = (
+        whole_strip(own_strip, messages, ADJ_ROWS - EY, slot, side) for slot in range(3)
+    )
+    stiff_s, buoy_s, damp_s = coefficients(label_s, table_ref)
     coef_strip_ref[0], coef_strip_ref[1], coef_strip_ref[2] = stiff_s, buoy_s, damp_s
     w_copy.wait()
 
@@ -422,7 +416,7 @@
         def injected(x):
             r_ref, place = r_refs[k]
             value = initial(0, x) if step == 1 else field[0, x]
-            value = value + r_ref[place, x]
+            value = value + r_ref[place, x - (EARLY_PLANES if k < 2 else LATE_PLANES)[0]]
             return value, coef_ref[0, x] * coef_ref[2, x] * value
 
         flux_below = None
@@ -458,36 +452,24 @@
 
 
 def forward_kernel(
-    raw_low, p_own, raw_high, low, own, high,
-    coef_ref, coef_strip_ref, s_ref, ss_ref, hist_ref,
+    wave_ref, edge_ref, even, odd, coef_ref, coef_strip_ref, s_ref, ss_ref, hist_ref,
     grad_ref,
     field,
 ):
     cut_up, cut_down = cut_flags()
-    flags = side_flags()
-    every, lows, highs = range(BX), range(1, BX), range(BX - 1)
-    raws = (raw_low, p_own, raw_high)
-    lates = (low, own, high)
+    side = sides()
+    messages = (even, odd)
+    tiles = PLANES + 3 * BY
 
     def initial(index, x):
-        tile = 3 * BY
-        if index == 0:
-            tiles = (series(tile, lows, 8), series(PLANES, every, 8), series(tile, highs, 8))
-            return widened(list(zip(raws, lates)), flags, x, [series(0, every, BY)] * 3, tiles)
-        tiles = (
-            series(tile + 24, lows[1:], 8),
-            series(PLANES + 32, every, 8),
-            series(tile + 24, highs[:2], 8),
-        )
-        firsts = (series(0, lows, BY), series(0, every, BY), series(0, highs, BY))
-        return widened(list(zip(lates, lates)), flags, x, firsts, tiles)
-
-    packed = [
-        low[WAVE_ROWS - EY : WAVE_ROWS],
-        own[OWN_ROWS - EY : OWN_ROWS],
-        high[WAVE_ROWS - EY : WAVE_ROWS],
-    ]
-    p_s, s_s = (whole_strip(packed, flags, slot) for slot in range(2))
+        layout = (((0, 4), (tiles, 3)), ((PLANES, 3), (tiles + 24, 2)))[index]
+        own = (wave_ref, PLANES * index)
+        return widened(own, (edge_ref, 32 * index), messages, x, layout, side)
+
+    own_strip = edge_ref[WAVE_EDGE_ROWS - EY : WAVE_EDGE_ROWS]
+    p_s, s_s = (
+        whole_strip(own_strip, messages, WAVE_ROWS - EY, slot, side) for slot in range(2)
+    )
     stiff_s, buoy_s, damp_s = coef_strip_ref[0], coef_strip_ref[1], coef_strip_ref[2]
 
     for step in range(1, STEPS + 1):
@@ -520,7 +502,8 @@
                 if step < STEPS:
                     field[1, x] = spread
                     field[0, x] = (
-                        coef_ref[2, x] * (p_now - coef_ref[0, x] * spread) + s_ref[k, x]
+                        coef_ref[2, x] * (p_now - coef_ref[0, x] * spread)
+                        + s_ref[k, x - SOURCE_PLANES[0]]
                     )
                 if BX <= x < 2 * BX:
                     place = x - BX
@@ -580,38 +563,37 @@
     return lax.ppermute(array, axis, [((i + offset) % count, i) for i in range(count)])
 
 
-def neighbours(to_next, to_last, cut):
+def paired(array, odd):
     count = lax.axis_size("gx")
-    if count == 4:
-        return rotated(to_next, "gx", -1), rotated(to_last, "gx", 1)
-    half = count // 2
-    return (
-        jnp.concatenate(
-            [rotated(to_next[:cut], "gx", half + 1), rotated(to_next[cut:], "gx", -1)], 0
-        ),
-        jnp.concatenate(
-            [rotated(to_last[:cut], "gx", half - 1), rotated(to_last[cut:], "gx", 1)], 0
-        ),
-    )
+    pairs = []
+    for i in range(count):
+        partner = ((i - 1) ^ 1) + 1 if odd else i ^ 1
+        pairs.append((partner if 0 <= partner < count else i, i))
+    return lax.ppermute(array, "gx", pairs)
 
 
 def local(
     stored, adjoint_end, labels, tissue, source_cells, source_wave, receiver_cells, receiver_wave
 ):
-    assert lax.axis_size("gz") == 2 and labels.shape == (BX, BY, BZ)
+    assert lax.axis_size("gz") == 2 and labels.shape == (BX, BY, BZ) and tissue.shape[1] == 8
     half = lax.axis_size("gx") // 2
-    p, raw, s, t, face_x, face_y, face_z = call(
+    arguments = [
+        stored, adjoint_end, labels, tissue,
+        receiver_cells.T, receiver_wave, source_cells.T, source_wave,
+    ]
+    raw, s, t, face_x, face_y, face_z, table, receivers, receiver_wave, sources, source_wave = call(
         face_kernel,
         [
-            shape(PLANES, BZ),
             shape(3 * PLANES, BZ),
             shape(PLANES, BZ),
             shape(PLANES, BZ),
             shape(2 * BY, BZ),
             shape(8, BZ),
             shape(BY, BZ),
-        ],
-        [stored, adjoint_end, labels, tissue],
+            shape(24, BZ),
+        ]
+        + [jax.ShapeDtypeStruct(array.shape, array.dtype) for array in arguments[4:]],
+        arguments,
         [
             pltpu.VMEM(stored.shape, F32),
             pltpu.VMEM(adjoint_end.shape, F32),
@@ -619,31 +601,22 @@
             pltpu.SMEM(tissue.shape, F32),
             pltpu.SemaphoreType.DMA,
         ],
-        "hhhh",
-    )
-    receivers, sources = receiver_cells.T, source_cells.T
-    point_scratch = [
-        pltpu.VMEM(receivers.shape, jnp.int32),
-        pltpu.VMEM(receiver_wave.shape, F32),
-        pltpu.VMEM(sources.shape, jnp.int32),
-        pltpu.VMEM(source_wave.shape, F32),
-    ]
+        "hhhhhhhh",
+    )
     rb, rsb = call(
         late_kernel,
         [shape(2, EX * EY, BZ), shape(2, EY, BZ)],
-        [receivers, receiver_wave, face_y],
-        point_scratch[:2] + [pltpu.SemaphoreType.DMA],
-        "hha",
+        [receivers, receiver_wave],
+        [],
+        "vv",
     )
     face_x = rotated(face_x, "gx", -1)
     face_y = rotated(face_y, "gy", -1)
     face_z = rotated(face_z, "gz", -1)
-    p_own = rotated(p, "gx", half)
-    raw_prev, raw_next = neighbours(raw, raw, PLANES)
-    s, t, edges, corners, strips = call(
+    wave, t, edges, corners, strips = call(
         pack_kernel,
         [
-            shape(PLANES, BZ),
+            shape(2 * PLANES, BZ),
             shape(PLANES, BZ),
             shape((5 * BX + 2) * 8, BZ),
             shape(16, BZ),
@@ -653,37 +626,47 @@
         [],
         "vvvvvva",
     )
+    wave = rotated(wave, "gx", half)
+    early_planes, source_planes = (last - first for first, last in (EARLY_PLANES, SOURCE_PLANES))
     ra, rsa, src, src_strip = call(
         early_kernel,
         [
-            shape(2, EX * EY, BZ),
+            shape(2, early_planes * EY, BZ),
             shape(2, EY, BZ),
-            shape(STEPS - 1, EX * EY, BZ),
+            shape(STEPS - 1, source_planes * EY, BZ),
             shape(STEPS - 1, EY, BZ),
         ],
         [receivers, receiver_wave, sources, source_wave, corners],
-        point_scratch + [pltpu.SemaphoreType.DMA],
-        "hhhha",
-    )
-    ra, rb = ra.reshape(2, EX, EY, BZ), rb.reshape(2, EX, EY, BZ)
-    src = src.reshape(STEPS - 1, EX, EY, BZ)
+        [],
+        "vvvva",
+    )
+    ra, rb = ra.reshape(2, early_planes, EY, BZ), rb.reshape(2, EX, EY, BZ)
+    src = src.reshape(STEPS - 1, source_planes, EY, BZ)
     other = rotated(strips, "gz", 1)
     up, down = from_sides(edges, "gy")
     corner_up, corner_down = from_sides(corners, ("gy", "gz"))
-    late, adj_own, to_next, to_last = call(
+    wave_edge, adj_edge, even, odd = call(
         merge_kernel,
         [
-            shape(OWN_ROWS, BZ),
-            shape(ADJ_OWN_ROWS, BZ),
-            shape(WAVE_ROWS + ADJ_ROWS, BZ),
-            shape(WAVE_ROWS + ADJ_ROWS, BZ),
+            shape(WAVE_EDGE_ROWS, BZ),
+            shape(ADJ_EDGE_ROWS, BZ),
+            shape(ADJ_ROWS, BZ),
+            shape(ADJ_ROWS, BZ),
         ],
-        [up, down, strips, other, corner_up, corner_down, s, t, rsa, p_own, raw_prev, raw_next],
+        [up, down, strips, other, corner_up, corner_down, raw, t, rsa],
         [],
-        "vvvvvvvvaaaa",
-    )
-    late_prev, late_next = neighbours(to_next, to_last, WAVE_ROWS)
-    late_own = rotated(late, "gx", half)
+        "vvvvvvvva",
+    )
+    wave_edge = rotated(wave_edge, "gx", half)
+    even, odd = paired(even, False), paired(odd, True)
+    wave_even, wave_odd = call(
+        join_kernel,
+        [shape(WAVE_ROWS, BZ), shape(WAVE_ROWS, BZ)],
+        [wave, wave_edge],
+        [],
+        "vv",
+    )
+    wave_even, wave_odd = paired(wave_even, False), paired(wave_odd, True)
     adjoint_start, hist, coef, coef_strip = call(
         adjoint_kernel,
         [
@@ -692,27 +675,16 @@
             shape(3, EX, EY, BZ),
             shape(3, EY, BZ),
         ],
-        [
-            raw_prev, raw, raw_next, late_prev, adj_own, late_next,
-            adjoint_end, ra, rsa, rb, rsb, tissue,
-        ],
-        [
-            pltpu.VMEM((2, EX, EY, BZ), F32),
-            pltpu.SMEM(tissue.shape, F32),
-            pltpu.SemaphoreType.DMA,
-            pltpu.SemaphoreType.DMA,
-        ],
-        "vvvvvvhvvvvh",
+        [raw, t, adj_edge, even, odd, adjoint_end, ra, rsa, rb, rsb, table],
+        [pltpu.VMEM((2, EX, EY, BZ), F32), pltpu.SemaphoreType.DMA],
+        "vvvvvhvvvvv",
     )
     (gradient,) = call(
         forward_kernel,
         [shape(2, BX, BY, BZ)],
-        [
-            raw_next, p_own, raw_prev, late_next, late_own, late_prev,
-            coef, coef_strip, src, src_strip, hist,
-        ],
+        [wave, wave_edge, wave_even, wave_odd, coef, coef_strip, src, src_strip, hist],
         [pltpu.VMEM((2, EX, EY, BZ), F32)],
-        "vvvvvvvvvvv",
+        "vvvvvvvvv",
     )
     return gradient, adjoint_start
 

time: 45.5 us -> 38.9 us (0.85)
  the two profiles are of different devices: /device:TPU:0 before, /device:TPU:8 now
where the time goes in v4:
time: 38.9 us; the launch traced here: 38.8 us
  starting transfers between devices  16.8 us (43%)
  waiting for transfers between devices  10.8 us (28%)
  Pallas kernels  10.4 us (27%)
  between operations  0.74 us (2%)
    pallas_call x8, Pallas kernels, call(): pl.pallas_call(kernel, out_shape=outs, in_specs=[pl.BlockSpec(memory_spac...  10.4 us
    ppermute x4, starting transfers between devices, paired(): return lax.ppermute(array, 'gx', pairs)  10 us
    ppermute x6, waiting for transfers between devices, rotated(): lax.ppermute(array, axis, [((i + offset) % count, i) for i in range(count)])  8.68 us
    ppermute x6, starting transfers between devices, rotated(): lax.ppermute(array, axis, [((i + offset) % count, i) for i in range(count)])  4.5 us
    ppermute x2, starting transfers between devices, from_sides(): both = lax.ppermute(array, axes, route(1) + route(-1))  2.2 us
    ppermute x2, waiting for transfers between devices, from_sides(): both = lax.ppermute(array, axes, route(1) + route(-1))  1.16 us
    ppermute x4, waiting for transfers between devices, paired(): return lax.ppermute(array, 'gx', pairs)  1 us
  transfers between devices with their start and end apart: 12, of which 4 were waited for; matrix products, arithmetic and copies ran while one was open for 0% of the time, Pallas kernels for 17%

profile of v4, /device:TPU:8, one launch (start us, length us, event | category | flops | bytes accessed | tf_op | source)
XLA Modules:
  0.0 38.8 jit_solution(12482416952601112880)
XLA Ops:
  0.6 1.2 %shard_map.95 = (f32[384,128]{1,0:T(8,128)S(1)}, f32[128,128]{1,0:T(8,128)S(1)}, f32[128,128]{1,0:T(8,128)S(1)}, f32[64,128]{1,0:T(8,128)S(1)}, f32[8,128]{1,0:T...) custom-call(f32[4,4,32,128]{3,2,1,0:T(8,128)} %stored_hbm.1, ...), custom_call_target="tpu_custom_call" | custom-call | flops 16777216 | bytes 1048576 | tf_op jit(solution)/shard_map/pallas_call | solution.py:530
  1.8 1.6 %collective-permute-start = (f32[64,128]{1,0:T(8,128)S(1)}, f32[64,128]{1,0:T(8,128)S(1)}, u32[]{:S(2)}, u32[]{:S(2)}) collective-permute-start(f32[64,128]{1,0:T(8,128)S(1)} %get-tuple-element.37), channel_id=1, source_target_pairs={{12,0},{0,4},{4,8},{8,12},{13,1},{1,5},{5,9},{9,13},{14,2},{2,6},{... | collective-permute-start | bytes 98312 | tf_op jit(solution)/shard_map/ppermute | solution.py:563
  3.5 0.0 collective-permute-start.2
  3.5 1.5 %collective-permute-start.1 = (f32[8,128]{1,0:T(8,128)S(1)}, f32[8,128]{1,0:T(8,128)S(1)}, u32[]{:S(2)}, u32[]{:S(2)}) collective-permute-start(f32[8,128]{1,0:T(8,128)S(1)} %get-tuple-element.38), channel_id=1, source_target_pairs={{2,0},{0,2},{3,1},{1,3},{6,4},{4,6},{7,5},{5,7},{10,8},{8,10},{11,... | collective-permute-start | bytes 12296 | tf_op jit(solution)/shard_map/ppermute | solution.py:563
  5.0 1.2 %shard_map.96 = (f32[2,480,128]{2,1,0:T(8,128)S(1)}, f32[2,40,128]{2,1,0:T(8,128)S(1)}) custom-call(s32[3,1024]{1,0:T(4,128)S(1)} %get-tuple-element.40.receivers, f32[4,1024]{1,0:T(4,128)S(1)} %get-tuple-element.41.receiver_wave), custom_call_target="tpu_custom_call" | custom-call | flops 16777216 | bytes 1048576 | tf_op jit(solution)/shard_map/pallas_call | solution.py:530
  6.2 0.9 %collective-permute-done.1.face_y = f32[8,128]{1,0:T(8,128)S(1)} collective-permute-done((f32[8,128]{1,0:T(8,128)S(1)}, f32[8,128]{1,0:T(8,128)S(1)}, u32[]{:S(2)}, u32[]{:S(2)}) %collective-permute-start.1) | collective-permute-done | bytes 4128 | tf_op jit(solution)/shard_map/ppermute | solution.py:563
  7.1 0.0 collective-permute-done.2.face_z
  7.1 0.0 collective-permute-done.face_x
  7.1 0.2 shard_map.97
  7.3 1.6 %collective-permute-start.4 = (f32[176,128]{1,0:T(8,128)S(1)}, f32[176,128]{1,0:T(8,128)S(1)}, u32[]{:S(2)}, u32[]{:S(2)}) collective-permute-start(f32[176,128]{1,0:T(8,128)S(1)} %get-tuple-element.44), channel_id=1, source_target_pairs={{2,0},{0,2},{3,1},{1,3},{6,4},{4,6},{7,5},{5,7},{10,8},{8,10},{11,... | collective-permute-start | bytes 270344 | tf_op jit(solution)/shard_map/ppermute | solution.py:556
  8.9 1.3 %collective-permute-start.3 = (f32[256,128]{1,0:T(8,128)S(1)}, f32[256,128]{1,0:T(8,128)S(1)}, u32[]{:S(2)}, u32[]{:S(2)}) collective-permute-start(f32[256,128]{1,0:T(8,128)S(1)} %get-tuple-element.43), channel_id=1, source_target_pairs={{8,0},{12,4},{0,8},{4,12},{9,1},{13,5},{1,9},{5,13},{10,2},{14,6},... | collective-permute-start | bytes 393224 | tf_op jit(solution)/shard_map/ppermute | solution.py:563
  10.2 0.0 collective-permute-start.5
  10.2 0.6 %collective-permute-start.6 = (f32[16,128]{1,0:T(8,128)S(1)}, f32[16,128]{1,0:T(8,128)S(1)}, u32[]{:S(2)}, u32[]{:S(2)}) collective-permute-start(f32[16,128]{1,0:T(8,128)S(1)} %get-tuple-element.46._), channel_id=1, source_target_pairs={{2,1},{3,0},{0,3},{1,2},{6,5},{7,4},{4,7},{5,6},{10,9},{11,8},{8,1... | collective-permute-start | bytes 24584 | tf_op jit(solution)/shard_map/ppermute | solution.py:556
  10.8 1.3 %shard_map.98 = (f32[2,320,128]{2,1,0:T(8,128)S(1)}, f32[2,40,128]{2,1,0:T(8,128)S(1)}, f32[3,400,128]{2,1,0:T(8,128)S(1)}, f32[3,40,128]{2,1,0:T(8,128)S(1)}) custom-call(s32[3,1024]{1,0:T(4,128)S(1)} %get-tuple-element.40.receivers, f32[4,1024]{1,0:T(4,128)S(1)} %get-tuple-element.41.receiver_wave, s32[3,64]{1,0:T(4,128)S(1)} %get-tuple-element.48.sources, ...), custom_call_target="tpu_custom_call" | custom-call | flops 16777216 | bytes 1048576 | tf_op jit(solution)/shard_map/pallas_call | solution.py:530
  12.1 1.2 %collective-permute-done.6.corner_up_ref.corner_down_ref = f32[16,128]{1,0:T(8,128)S(1)} collective-permute-done((f32[16,128]{1,0:T(8,128)S(1)}, f32[16,128]{1,0:T(8,128)S(1)}, u32[]{:S(2)}, u32[]{:S(2)}) %collective-permute-start.6) | collective-permute-done | bytes 8224 | tf_op jit(solution)/shard_map/ppermute | solution.py:556
  13.3 0.0 collective-permute-done.5.other_ref
  13.3 0.0 collective-permute-done.4.up_ref.down_ref
  13.3 1.8 %collective-permute-start.10 = (f32[456,128]{1,0:T(8,128)S(1)}, f32[456,128]{1,0:T(8,128)S(1)}, u32[]{:S(2)}, u32[]{:S(2)}) collective-permute-start(f32[456,128]{1,0:T(8,128)S(1)} %get-tuple-element.55), channel_id=1, source_target_pairs={{4,0},{0,4},{12,8},{8,12},{5,1},{1,5},{13,9},{9,13},{6,2},{2,6},{1... | collective-permute-start | bytes 700424 | tf_op jit(solution)/shard_map/ppermute | solution.py:572
  15.1 2.3 %collective-permute-start.11 = (f32[456,128]{1,0:T(8,128)S(1)}, f32[456,128]{1,0:T(8,128)S(1)}, u32[]{:S(2)}, u32[]{:S(2)}) collective-permute-start(f32[456,128]{1,0:T(8,128)S(1)} %get-tuple-element.56), channel_id=1, source_target_pairs={{0,0},{8,4},{4,8},{12,12},{1,1},{9,5},{5,9},{13,13},{2,2},{10,6},{... | collective-permute-start | bytes 700424 | tf_op jit(solution)/shard_map/ppermute | solution.py:572
  17.5 0.1 collective-permute-start.7
  17.6 0.0 collective-permute-done.3.wave_ref
  17.6 7.8 %collective-permute-done.7.edge_ref = f32[104,128]{1,0:T(8,128)S(1)} collective-permute-done((f32[104,128]{1,0:T(8,128)S(1)}, f32[104,128]{1,0:T(8,128)S(1)}, u32[]{:S(2)}, u32[]{:S(2)}) %collective-permute-start.7) | collective-permute-done | bytes 53280 | tf_op jit(solution)/shard_map/ppermute | solution.py:563
  25.4 3.6 %collective-permute-start.8 = (f32[304,128]{1,0:T(8,128)S(1)}, f32[304,128]{1,0:T(8,128)S(1)}, u32[]{:S(2)}, u32[]{:S(2)}) collective-permute-start(f32[304,128]{1,0:T(8,128)S(1)} %get-tuple-element.52), channel_id=1, source_target_pairs={{4,0},{0,4},{12,8},{8,12},{5,1},{1,5},{13,9},{9,13},{6,2},{2,6},{1... | collective-permute-start | bytes 466952 | tf_op jit(solution)/shard_map/ppermute | solution.py:572
  29.0 2.3 %collective-permute-start.9 = (f32[304,128]{1,0:T(8,128)S(1)}, f32[304,128]{1,0:T(8,128)S(1)}, u32[]{:S(2)}, u32[]{:S(2)}) collective-permute-start(f32[304,128]{1,0:T(8,128)S(1)} %get-tuple-element.53), channel_id=1, source_target_pairs={{0,0},{8,4},{4,8},{12,12},{1,1},{9,5},{5,9},{13,13},{2,2},{10,6},{... | collective-permute-start | bytes 466952 | tf_op jit(solution)/shard_map/ppermute | solution.py:572
  31.3 0.0 collective-permute-done.10.even
  31.3 0.0 collective-permute-done.11.odd
  31.3 3.9 %shard_map.101 = (f32[4,4,32,128]{3,2,1,0:T(8,128)}, f32[4,4,4,32,128]{4,3,2,1,0:T(8,128)S(1)}, f32[3,12,40,128]{3,2,1,0:T(8,128)S(1)}, f32[3,40,128]{2,1,0:T(8,128)S(1)}) custom-call(f32[384,128]{1,0:T(8,128)S(1)} %get-tuple-element.34.raw_ref, f32[128,128]{1,0:T(8,128)S(1)} %get-tuple-element.47.t_ref, f32[136,128]{1,0:T(8,128)S(1)} %get-tuple-element.54.edge_ref, ...), custom_call_target="tpu_custom_call" | custom-call | flops 16777216 | bytes 1048576 | tf_op jit(solution)/shard_map/pallas_call | solution.py:530
  35.2 0.0 collective-permute-done.8.even
  35.2 1.0 %collective-permute-done.9.odd = f32[304,128]{1,0:T(8,128)S(1)} collective-permute-done((f32[304,128]{1,0:T(8,128)S(1)}, f32[304,128]{1,0:T(8,128)S(1)}, u32[]{:S(2)}, u32[]{:S(2)}) %collective-permute-start.9) | collective-permute-done | bytes 155680 | tf_op jit(solution)/shard_map/ppermute | solution.py:572
  36.2 2.5 %shard_map.102 = f32[2,4,32,128]{3,2,1,0:T(8,128)} custom-call(f32[256,128]{1,0:T(8,128)S(1)} %collective-permute-done.3.wave_ref, f32[104,128]{1,0:T(8,128)S(1)} %collective-permute-done.7.edge_ref, f32[304,128]{1,0:T(8,128)S(1)} %collective-permute-done.8.even, f32[304,128]{1,0:T(8,128)S(1)} %collective-permute-done.9.odd, ...), custom_call_target="tpu_custom_call" | custom-call | flops 16777216 | bytes 1048576 | tf_op jit(solution)/shard_map/pallas_call | solution.py:530
  (2 shorter events, 0.1 us)
Async XLA Ops:
  1.8 5.2 %collective-permute-start = (f32[64,128]{1,0:T(8,128)S(1)}, f32[64,128]{1,0:T(8,128)S(1)}, u32[]{:S(2)}, u32[]{:S(2)}) collective-permute-start(f32[64,128]{1,0:T(8,128)S(1)} %get-tuple-element.37), channel_id=1, source_target_pairs={{12,0},{0,4},{4,8},{8,12},{13,1},{1,5},{5,9},{9,13},{14,2},{2,6},{... | collective-permute-start | bytes 98312 | tf_op jit(solution)/shard_map/ppermute | solution.py:563
  3.5 3.6 %collective-permute-start.2 = (f32[32,128]{1,0:T(8,128)S(1)}, f32[32,128]{1,0:T(8,128)S(1)}, u32[]{:S(2)}, u32[]{:S(2)}) collective-permute-start(f32[32,128]{1,0:T(8,128)S(1)} %get-tuple-element.39), channel_id=1, source_target_pairs={{1,0},{0,1},{3,2},{2,3},{5,4},{4,5},{7,6},{6,7},{9,8},{8,9},{11,10... | collective-permute-start | bytes 49160 | tf_op jit(solution)/shard_map/ppermute | solution.py:563
  3.5 3.6 %collective-permute-start.1 = (f32[8,128]{1,0:T(8,128)S(1)}, f32[8,128]{1,0:T(8,128)S(1)}, u32[]{:S(2)}, u32[]{:S(2)}) collective-permute-start(f32[8,128]{1,0:T(8,128)S(1)} %get-tuple-element.38), channel_id=1, source_target_pairs={{2,0},{0,2},{3,1},{1,3},{6,4},{4,6},{7,5},{5,7},{10,8},{8,10},{11,... | collective-permute-start | bytes 12296 | tf_op jit(solution)/shard_map/ppermute | solution.py:563
  7.3 6.0 %collective-permute-start.4 = (f32[176,128]{1,0:T(8,128)S(1)}, f32[176,128]{1,0:T(8,128)S(1)}, u32[]{:S(2)}, u32[]{:S(2)}) collective-permute-start(f32[176,128]{1,0:T(8,128)S(1)} %get-tuple-element.44), channel_id=1, source_target_pairs={{2,0},{0,2},{3,1},{1,3},{6,4},{4,6},{7,5},{5,7},{10,8},{8,10},{11,... | collective-permute-start | bytes 270344 | tf_op jit(solution)/shard_map/ppermute | solution.py:556
  8.9 8.7 %collective-permute-start.3 = (f32[256,128]{1,0:T(8,128)S(1)}, f32[256,128]{1,0:T(8,128)S(1)}, u32[]{:S(2)}, u32[]{:S(2)}) collective-permute-start(f32[256,128]{1,0:T(8,128)S(1)} %get-tuple-element.43), channel_id=1, source_target_pairs={{8,0},{12,4},{0,8},{4,12},{9,1},{13,5},{1,9},{5,13},{10,2},{14,6},... | collective-permute-start | bytes 393224 | tf_op jit(solution)/shard_map/ppermute | solution.py:563
  10.2 3.1 %collective-permute-start.5 = (f32[64,128]{1,0:T(8,128)S(1)}, f32[64,128]{1,0:T(8,128)S(1)}, u32[]{:S(2)}, u32[]{:S(2)}) collective-permute-start(f32[64,128]{1,0:T(8,128)S(1)} %get-tuple-element.45.strip_ref), channel_id=1, source_target_pairs={{1,0},{0,1},{3,2},{2,3},{5,4},{4,5},{7,6},{6,7},{9,8},{8,9},{11,10... | collective-permute-start | bytes 98312 | tf_op jit(solution)/shard_map/ppermute | solution.py:563
  10.2 3.1 %collective-permute-start.6 = (f32[16,128]{1,0:T(8,128)S(1)}, f32[16,128]{1,0:T(8,128)S(1)}, u32[]{:S(2)}, u32[]{:S(2)}) collective-permute-start(f32[16,128]{1,0:T(8,128)S(1)} %get-tuple-element.46._), channel_id=1, source_target_pairs={{2,1},{3,0},{0,3},{1,2},{6,5},{7,4},{4,7},{5,6},{10,9},{11,8},{8,1... | collective-permute-start | bytes 24584 | tf_op jit(solution)/shard_map/ppermute | solution.py:556
  13.3 18.0 %collective-permute-start.10 = (f32[456,128]{1,0:T(8,128)S(1)}, f32[456,128]{1,0:T(8,128)S(1)}, u32[]{:S(2)}, u32[]{:S(2)}) collective-permute-start(f32[456,128]{1,0:T(8,128)S(1)} %get-tuple-element.55), channel_id=1, source_target_pairs={{4,0},{0,4},{12,8},{8,12},{5,1},{1,5},{13,9},{9,13},{6,2},{2,6},{1... | collective-permute-start | bytes 700424 | tf_op jit(solution)/shard_map/ppermute | solution.py:572
  15.1 16.2 %collective-permute-start.11 = (f32[456,128]{1,0:T(8,128)S(1)}, f32[456,128]{1,0:T(8,128)S(1)}, u32[]{:S(2)}, u32[]{:S(2)}) collective-permute-start(f32[456,128]{1,0:T(8,128)S(1)} %get-tuple-element.56), channel_id=1, source_target_pairs={{0,0},{8,4},{4,8},{12,12},{1,1},{9,5},{5,9},{13,13},{2,2},{10,6},{... | collective-permute-start | bytes 700424 | tf_op jit(solution)/shard_map/ppermute | solution.py:572
  17.5 7.9 %collective-permute-start.7 = (f32[104,128]{1,0:T(8,128)S(1)}, f32[104,128]{1,0:T(8,128)S(1)}, u32[]{:S(2)}, u32[]{:S(2)}) collective-permute-start(f32[104,128]{1,0:T(8,128)S(1)} %get-tuple-element.51), channel_id=1, source_target_pairs={{8,0},{12,4},{0,8},{4,12},{9,1},{13,5},{1,9},{5,13},{10,2},{14,6},... | collective-permute-start | bytes 159752 | tf_op jit(solution)/shard_map/ppermute | solution.py:563
  25.4 9.8 %collective-permute-start.8 = (f32[304,128]{1,0:T(8,128)S(1)}, f32[304,128]{1,0:T(8,128)S(1)}, u32[]{:S(2)}, u32[]{:S(2)}) collective-permute-start(f32[304,128]{1,0:T(8,128)S(1)} %get-tuple-element.52), channel_id=1, source_target_pairs={{4,0},{0,4},{12,8},{8,12},{5,1},{1,5},{13,9},{9,13},{6,2},{2,6},{1... | collective-permute-start | bytes 466952 | tf_op jit(solution)/shard_map/ppermute | solution.py:572
  29.0 7.3 %collective-permute-start.9 = (f32[304,128]{1,0:T(8,128)S(1)}, f32[304,128]{1,0:T(8,128)S(1)}, u32[]{:S(2)}, u32[]{:S(2)}) collective-permute-start(f32[304,128]{1,0:T(8,128)S(1)} %get-tuple-element.53), channel_id=1, source_target_pairs={{0,0},{8,4},{4,8},{12,12},{1,1},{9,5},{5,9},{13,13},{2,2},{10,6},{... | collective-permute-start | bytes 466952 | tf_op jit(solution)/shard_map/ppermute | solution.py:572

commit v5 on v4

--- a/solution.py
+++ b/solution.py
@@ -104,44 +104,41 @@
     face_z_ref[...] = face_z
 
 
-def pack_kernel(
-    raw_ref, s_in, t_in, face_x, face_y, face_z, _,
-    wave_ref, t_ref, edge_ref, corner_ref, strip_ref,
-):
+def fix_kernel(raw_ref, s_in, t_in, face_x, face_y, face_z, _, wave_ref, t_ref):
     gx, gy, gz = (lax.axis_index(name) for name in ("gx", "gy", "gz"))
-    count = lax.axis_size("gx")
     lane = lanes((BY, BZ))
     row = rows((BY, BZ))
-    tile_row = rows((8, BZ))
     below = (
-        jnp.where(gx == count // 2, 0.0, 1.0),
+        jnp.where(gx == lax.axis_size("gx") // 2, 0.0, 1.0),
         jnp.where(gx == 0, 0.0, 1.0),
     )
     tile_y = face_y[...] * jnp.where(gy == 0, 0.0, 1.0)
     tile_z = face_z[...] * jnp.where(gz == 0, 0.0, 1.0)
+    wave_ref[0:PLANES] = raw_ref[0:PLANES]
+    for kind, (source, target, base) in enumerate(((s_in, wave_ref, PLANES), (t_in, t_ref, 0))):
+        for x in range(BX):
+            block = source[x * BY : x * BY + BY]
+            if x == 0:
+                block = block - face_x[kind * BY : kind * BY + BY] * below[kind]
+            index = kind * BX + x
+            lane_below = pltpu.roll(tile_z, (BZ - index) % BZ, 1) if index else tile_z
+            block = block - jnp.where(row == 0, tile_y[index : index + 1], 0.0)
+            block = block - jnp.where(lane == 0, lane_below, 0.0)
+            target[base + x * BY : base + x * BY + BY] = block
+
+
+def edge_kernel(raw_ref, wave_ref, t_ref, edge_ref, corner_ref, strip_ref):
+    gz = lax.axis_index("gz")
+    lane = lanes((BY, BZ))
+    tile_row = rows((8, BZ))
     strips = [jnp.zeros((BY, BZ), F32) for _ in range(2)]
-    for field in range(5):
+    sources = (
+        (wave_ref, 0), (wave_ref, PLANES), (raw_ref, PLANES), (t_ref, 0), (raw_ref, 2 * PLANES)
+    )
+    for field, (source, first_row) in enumerate(sources):
         group, slot = (0, field) if field < 2 else (1, field - 2)
         for x in range(BX):
-            plane = slice(x * BY, x * BY + BY)
-            if field in (1, 3):
-                kind = field // 2
-                block = (s_in, t_in)[kind][plane]
-                if x == 0:
-                    block = block - face_x[kind * BY : kind * BY + BY] * below[kind]
-                index = kind * BX + x
-                lane_below = pltpu.roll(tile_z, (BZ - index) % BZ, 1) if index else tile_z
-                block = block - jnp.where(row == 0, tile_y[index : index + 1], 0.0)
-                block = block - jnp.where(lane == 0, lane_below, 0.0)
-                if kind == 0:
-                    wave_ref[PLANES + x * BY : PLANES + x * BY + BY] = block
-                else:
-                    t_ref[plane] = block
-            else:
-                first = field // 2 * PLANES + x * BY
-                block = raw_ref[first : first + BY]
-                if field == 0:
-                    wave_ref[plane] = block
+            block = source[first_row + x * BY : first_row + x * BY + BY]
             tile = jnp.where(tile_row < MARGIN, block[0:8], block[BY - 8 : BY])
             index = field * BX + x
             edge_ref[index * 8 : index * 8 + 8] = tile
@@ -171,8 +168,8 @@
 
 
 def merge_kernel(
-    up_ref, down_ref, strip_ref, other_ref, corner_up_ref, corner_down_ref, raw_ref, t_ref, _,
-    wave_edge_ref, adj_edge_ref, even_ref, odd_ref,
+    up_ref, down_ref, strip_ref, other_ref, corner_up_ref, corner_down_ref, _a, _b,
+    wave_edge_ref, adj_edge_ref,
 ):
     gy = lax.axis_index("gy")
     row = rows((8, BZ))
@@ -192,6 +189,9 @@
         target[base : base + BY] = strip_ref[sl] + other_ref[sl]
         tile = halo(up_ref, down_ref, 5 * BX + group) + halo(corner_up_ref, corner_down_ref, group)
         target[base + BY : base + EY] = tile
+
+
+def adjoint_join_kernel(raw_ref, t_ref, adj_edge_ref, _, even_ref, odd_ref):
     for target, first in zip((even_ref, odd_ref), pair_planes()):
         base = copy_rows(target, 0, raw_ref, PLANES, 2 * PLANES)
         base = copy_rows(target, base, t_ref, first * BY, 3 * BY)
@@ -279,10 +279,11 @@
     inject_points(receivers, receiver_wave, 256, (2, 3), LATE_PLANES, r_ref, rs_ref)
 
 
-def early_kernel(
-    receivers, receiver_wave, sources, source_wave, _, r_ref, rs_ref, s_ref, ss_ref
-):
+def early_kernel(receivers, receiver_wave, _, r_ref, rs_ref):
     inject_points(receivers, receiver_wave, 256, (0, 1), EARLY_PLANES, r_ref, rs_ref)
+
+
+def source_kernel(sources, source_wave, _, s_ref, ss_ref):
     width = sources.shape[1]
     inject_points(sources, source_wave, width, (0, 1, 2), SOURCE_PLANES, s_ref, ss_ref)
 
@@ -613,51 +614,56 @@
     face_x = rotated(face_x, "gx", -1)
     face_y = rotated(face_y, "gy", -1)
     face_z = rotated(face_z, "gz", -1)
-    wave, t, edges, corners, strips = call(
-        pack_kernel,
-        [
-            shape(2 * PLANES, BZ),
-            shape(PLANES, BZ),
-            shape((5 * BX + 2) * 8, BZ),
-            shape(16, BZ),
-            shape(2 * BY, BZ),
-        ],
+    wave, t = call(
+        fix_kernel,
+        [shape(2 * PLANES, BZ), shape(PLANES, BZ)],
         [raw, s, t, face_x, face_y, face_z, rsb],
         [],
         "vvvvvva",
     )
+    edges, corners, strips = call(
+        edge_kernel,
+        [shape((5 * BX + 2) * 8, BZ), shape(16, BZ), shape(2 * BY, BZ)],
+        [raw, wave, t],
+        [],
+        "vvv",
+    )
     wave = rotated(wave, "gx", half)
     early_planes, source_planes = (last - first for first, last in (EARLY_PLANES, SOURCE_PLANES))
-    ra, rsa, src, src_strip = call(
+    ra, rsa = call(
         early_kernel,
-        [
-            shape(2, early_planes * EY, BZ),
-            shape(2, EY, BZ),
-            shape(STEPS - 1, source_planes * EY, BZ),
-            shape(STEPS - 1, EY, BZ),
-        ],
-        [receivers, receiver_wave, sources, source_wave, corners],
+        [shape(2, early_planes * EY, BZ), shape(2, EY, BZ)],
+        [receivers, receiver_wave, corners],
         [],
-        "vvvva",
+        "vva",
     )
     ra, rb = ra.reshape(2, early_planes, EY, BZ), rb.reshape(2, EX, EY, BZ)
-    src = src.reshape(STEPS - 1, source_planes, EY, BZ)
     other = rotated(strips, "gz", 1)
     up, down = from_sides(edges, "gy")
     corner_up, corner_down = from_sides(corners, ("gy", "gz"))
-    wave_edge, adj_edge, even, odd = call(
+    wave_edge, adj_edge = call(
         merge_kernel,
-        [
-            shape(WAVE_EDGE_ROWS, BZ),
-            shape(ADJ_EDGE_ROWS, BZ),
-            shape(ADJ_ROWS, BZ),
-            shape(ADJ_ROWS, BZ),
-        ],
-        [up, down, strips, other, corner_up, corner_down, raw, t, rsa],
+        [shape(WAVE_EDGE_ROWS, BZ), shape(ADJ_EDGE_ROWS, BZ)],
+        [up, down, strips, other, corner_up, corner_down, rsa, wave],
         [],
-        "vvvvvvvva",
+        "vvvvvvaa",
     )
     wave_edge = rotated(wave_edge, "gx", half)
+    src, src_strip = call(
+        source_kernel,
+        [shape(STEPS - 1, source_planes * EY, BZ), shape(STEPS - 1, EY, BZ)],
+        [sources, source_wave, adj_edge],
+        [],
+        "vva",
+    )
+    src = src.reshape(STEPS - 1, source_planes, EY, BZ)
+    even, odd = call(
+        adjoint_join_kernel,
+        [shape(ADJ_ROWS, BZ), shape(ADJ_ROWS, BZ)],
+        [raw, t, adj_edge, wave_edge],
+        [],
+        "vvva",
+    )
     even, odd = paired(even, False), paired(odd, True)
     wave_even, wave_odd = call(
         join_kernel,

time: 38.9 us -> 37.9 us (0.974)
  waiting for transfers between devices: 10.8 us -> 7.76 us
  starting transfers between devices: 16.8 us -> 18.5 us
    ppermute x6, waiting for transfers between devices: 8.68 us -> 3.19 us  [rotated(): lax.ppermute(array, axis, [((i + offset) % count, i) for i in range(count)])]
    ppermute x6, starting transfers between devices: 4.5 us -> 7.94 us  [rotated(): lax.ppermute(array, axis, [((i + offset) % count, i) for i in range(count)])]
    ppermute x4, waiting for transfers between devices: 1 us -> 3.12 us  [paired(): return lax.ppermute(array, 'gx', pairs)]
    ppermute x4, starting transfers between devices: 10 us -> 8.36 us  [paired(): return lax.ppermute(array, 'gx', pairs)]
    pallas_call x8 -> x11, Pallas kernels: 10.4 us -> 10.7 us  [call(): pl.pallas_call(kernel, out_shape=outs, in_specs=[pl.BlockSpec(memory_spac...]
  transfers between devices with their start and end apart: 12 -> 12, of which waited for: 4 -> 5; matrix products, arithmetic and copies ran while one was open for 0% -> 0% of each run, Pallas kernels for 17% -> 18%
where the time goes in v5:
time: 37.9 us; the launch traced here: 37.8 us
  starting transfers between devices  18.5 us (49%)
  Pallas kernels  10.7 us (28%)
  waiting for transfers between devices  7.76 us (20%)
  between operations  0.74 us (2%)
    pallas_call x11, Pallas kernels, call(): pl.pallas_call(kernel, out_shape=outs, in_specs=[pl.BlockSpec(memory_spac...  10.7 us
    ppermute x4, starting transfers between devices, paired(): return lax.ppermute(array, 'gx', pairs)  8.36 us
    ppermute x6, starting transfers between devices, rotated(): lax.ppermute(array, axis, [((i + offset) % count, i) for i in range(count)])  7.94 us
    ppermute x6, waiting for transfers between devices, rotated(): lax.ppermute(array, axis, [((i + offset) % count, i) for i in range(count)])  3.19 us
    ppermute x4, waiting for transfers between devices, paired(): return lax.ppermute(array, 'gx', pairs)  3.12 us
    ppermute x2, starting transfers between devices, from_sides(): both = lax.ppermute(array, axes, route(1) + route(-1))  2.2 us
    ppermute x2, waiting for transfers between devices, from_sides(): both = lax.ppermute(array, axes, route(1) + route(-1))  1.45 us
  transfers between devices with their start and end apart: 12, of which 5 were waited for; matrix products, arithmetic and copies ran while one was open for 0% of the time, Pallas kernels for 18%

profile of v5, /device:TPU:8, one launch (start us, length us, event | category | flops | bytes accessed | tf_op | source)
XLA Modules:
  0.0 37.8 jit_solution(7250984691250668515)
XLA Ops:
  0.6 1.2 %shard_map.95 = (f32[384,128]{1,0:T(8,128)S(1)}, f32[128,128]{1,0:T(8,128)S(1)}, f32[128,128]{1,0:T(8,128)S(1)}, f32[64,128]{1,0:T(8,128)S(1)}, f32[8,128]{1,0:T...) custom-call(f32[4,4,32,128]{3,2,1,0:T(8,128)} %stored_hbm.1, ...), custom_call_target="tpu_custom_call" | custom-call | flops 16777216 | bytes 1048576 | tf_op jit(solution)/shard_map/pallas_call | solution.py:531
  1.8 1.6 %collective-permute-start = (f32[64,128]{1,0:T(8,128)S(1)}, f32[64,128]{1,0:T(8,128)S(1)}, u32[]{:S(2)}, u32[]{:S(2)}) collective-permute-start(f32[64,128]{1,0:T(8,128)S(1)} %get-tuple-element.37), channel_id=1, source_target_pairs={{12,0},{0,4},{4,8},{8,12},{13,1},{1,5},{5,9},{9,13},{14,2},{2,6},{... | collective-permute-start | bytes 98312 | tf_op jit(solution)/shard_map/ppermute | solution.py:564
  3.5 0.0 collective-permute-start.2
  3.5 1.5 %collective-permute-start.1 = (f32[8,128]{1,0:T(8,128)S(1)}, f32[8,128]{1,0:T(8,128)S(1)}, u32[]{:S(2)}, u32[]{:S(2)}) collective-permute-start(f32[8,128]{1,0:T(8,128)S(1)} %get-tuple-element.38), channel_id=1, source_target_pairs={{2,0},{0,2},{3,1},{1,3},{6,4},{4,6},{7,5},{5,7},{10,8},{8,10},{11,... | collective-permute-start | bytes 12296 | tf_op jit(solution)/shard_map/ppermute | solution.py:564
  5.0 1.2 %shard_map.96 = (f32[2,480,128]{2,1,0:T(8,128)S(1)}, f32[2,40,128]{2,1,0:T(8,128)S(1)}) custom-call(s32[3,1024]{1,0:T(4,128)S(1)} %get-tuple-element.40.receivers, f32[4,1024]{1,0:T(4,128)S(1)} %get-tuple-element.41.receiver_wave), custom_call_target="tpu_custom_call" | custom-call | flops 16777216 | bytes 1048576 | tf_op jit(solution)/shard_map/pallas_call | solution.py:531
  6.2 0.9 %collective-permute-done.1.face_y = f32[8,128]{1,0:T(8,128)S(1)} collective-permute-done((f32[8,128]{1,0:T(8,128)S(1)}, f32[8,128]{1,0:T(8,128)S(1)}, u32[]{:S(2)}, u32[]{:S(2)}) %collective-permute-start.1) | collective-permute-done | bytes 4128 | tf_op jit(solution)/shard_map/ppermute | solution.py:564
  7.1 0.0 collective-permute-done.2.face_z
  7.1 0.0 collective-permute-done.face_x
  7.1 0.1 shard_map.97
  7.2 1.4 %collective-permute-start.3 = (f32[256,128]{1,0:T(8,128)S(1)}, f32[256,128]{1,0:T(8,128)S(1)}, u32[]{:S(2)}, u32[]{:S(2)}) collective-permute-start(f32[256,128]{1,0:T(8,128)S(1)} %get-tuple-element.43.wave_ref), channel_id=1, source_target_pairs={{8,0},{12,4},{0,8},{4,12},{9,1},{13,5},{1,9},{5,13},{10,2},{14,6},... | collective-permute-start | bytes 393224 | tf_op jit(solution)/shard_map/ppermute | solution.py:564
  8.6 0.1 shard_map.98
  8.7 1.6 %collective-permute-start.4 = (f32[176,128]{1,0:T(8,128)S(1)}, f32[176,128]{1,0:T(8,128)S(1)}, u32[]{:S(2)}, u32[]{:S(2)}) collective-permute-start(f32[176,128]{1,0:T(8,128)S(1)} %get-tuple-element.45), channel_id=1, source_target_pairs={{2,0},{0,2},{3,1},{1,3},{6,4},{4,6},{7,5},{5,7},{10,8},{8,10},{11,... | collective-permute-start | bytes 270344 | tf_op jit(solution)/shard_map/ppermute | solution.py:557
  10.3 0.0 collective-permute-start.5
  10.3 0.6 %collective-permute-start.6 = (f32[16,128]{1,0:T(8,128)S(1)}, f32[16,128]{1,0:T(8,128)S(1)}, u32[]{:S(2)}, u32[]{:S(2)}) collective-permute-start(f32[16,128]{1,0:T(8,128)S(1)} %get-tuple-element.47._), channel_id=1, source_target_pairs={{2,1},{3,0},{0,3},{1,2},{6,5},{7,4},{4,7},{5,6},{10,9},{11,8},{8,1... | collective-permute-start | bytes 24584 | tf_op jit(solution)/shard_map/ppermute | solution.py:557
  10.9 1.0 %shard_map.99 = (f32[2,320,128]{2,1,0:T(8,128)S(1)}, f32[2,40,128]{2,1,0:T(8,128)S(1)}) custom-call(s32[3,1024]{1,0:T(4,128)S(1)} %get-tuple-element.40.receivers, f32[4,1024]{1,0:T(4,128)S(1)} %get-tuple-element.41.receiver_wave, f32[16,128]{1,0:T(8,128)S(1)} %get-tuple-element.47._), custom_call_target="tpu_custom_call" | custom-call | flops 16777216 | bytes 1048576 | tf_op jit(solution)/shard_map/pallas_call | solution.py:531
  12.0 1.5 %collective-permute-done.6.corner_up_ref.corner_down_ref = f32[16,128]{1,0:T(8,128)S(1)} collective-permute-done((f32[16,128]{1,0:T(8,128)S(1)}, f32[16,128]{1,0:T(8,128)S(1)}, u32[]{:S(2)}, u32[]{:S(2)}) %collective-permute-start.6) | collective-permute-done | bytes 8224 | tf_op jit(solution)/shard_map/ppermute | solution.py:557
  13.4 0.0 collective-permute-done.5.other_ref
  13.4 0.0 collective-permute-done.4.up_ref.down_ref
  13.4 0.2 collective-permute-done.3._b.wave_ref
  13.6 3.4 %collective-permute-start.7 = (f32[104,128]{1,0:T(8,128)S(1)}, f32[104,128]{1,0:T(8,128)S(1)}, u32[]{:S(2)}, u32[]{:S(2)}) collective-permute-start(f32[104,128]{1,0:T(8,128)S(1)} %get-tuple-element.49), channel_id=1, source_target_pairs={{8,0},{12,4},{0,8},{4,12},{9,1},{13,5},{1,9},{5,13},{10,2},{14,6},... | collective-permute-start | bytes 159752 | tf_op jit(solution)/shard_map/ppermute | solution.py:564
  17.1 2.1 %collective-permute-done.7.edge_ref._ = f32[104,128]{1,0:T(8,128)S(1)} collective-permute-done((f32[104,128]{1,0:T(8,128)S(1)}, f32[104,128]{1,0:T(8,128)S(1)}, u32[]{:S(2)}, u32[]{:S(2)}) %collective-permute-start.7) | collective-permute-done | bytes 53280 | tf_op jit(solution)/shard_map/ppermute | solution.py:564
  19.2 2.5 %collective-permute-start.10 = (f32[456,128]{1,0:T(8,128)S(1)}, f32[456,128]{1,0:T(8,128)S(1)}, u32[]{:S(2)}, u32[]{:S(2)}) collective-permute-start(f32[456,128]{1,0:T(8,128)S(1)} %get-tuple-element.53), channel_id=1, source_target_pairs={{4,0},{0,4},{12,8},{8,12},{5,1},{1,5},{13,9},{9,13},{6,2},{2,6},{1... | collective-permute-start | bytes 700424 | tf_op jit(solution)/shard_map/ppermute | solution.py:573
  21.7 3.0 %collective-permute-start.11 = (f32[456,128]{1,0:T(8,128)S(1)}, f32[456,128]{1,0:T(8,128)S(1)}, u32[]{:S(2)}, u32[]{:S(2)}) collective-permute-start(f32[456,128]{1,0:T(8,128)S(1)} %get-tuple-element.54), channel_id=1, source_target_pairs={{0,0},{8,4},{4,8},{12,12},{1,1},{9,5},{5,9},{13,13},{2,2},{10,6},{... | collective-permute-start | bytes 700424 | tf_op jit(solution)/shard_map/ppermute | solution.py:573
  24.7 0.1 collective-permute-start.8
  24.8 2.8 %collective-permute-start.9 = (f32[304,128]{1,0:T(8,128)S(1)}, f32[304,128]{1,0:T(8,128)S(1)}, u32[]{:S(2)}, u32[]{:S(2)}) collective-permute-start(f32[304,128]{1,0:T(8,128)S(1)} %get-tuple-element.51), channel_id=1, source_target_pairs={{0,0},{8,4},{4,8},{12,12},{1,1},{9,5},{5,9},{13,13},{2,2},{10,6},{... | collective-permute-start | bytes 466952 | tf_op jit(solution)/shard_map/ppermute | solution.py:573
  27.7 0.5 %shard_map.104 = (f32[3,400,128]{2,1,0:T(8,128)S(1)}, f32[3,40,128]{2,1,0:T(8,128)S(1)}) custom-call(s32[3,64]{1,0:T(4,128)S(1)} %get-tuple-element.60.sources, f32[4,64]{1,0:T(4,128)S(1)} %get-tuple-element.61.source_wave, f32[136,128]{1,0:T(8,128)S(1)} %get-tuple-element.52.adj_edge_ref.edge_ref._), custom_call_target="tpu_custom_call" | custom-call | flops 16777216 | bytes 1048576 | tf_op jit(solution)/shard_map/pallas_call | solution.py:531
  28.2 0.0 collective-permute-done.10.even
  28.2 3.1 %collective-permute-done.11.odd = f32[456,128]{1,0:T(8,128)S(1)} collective-permute-done((f32[456,128]{1,0:T(8,128)S(1)}, f32[456,128]{1,0:T(8,128)S(1)}, u32[]{:S(2)}, u32[]{:S(2)}) %collective-permute-start.11) | collective-permute-done | bytes 233504 | tf_op jit(solution)/shard_map/ppermute | solution.py:573
  31.3 3.9 %shard_map.103 = (f32[4,4,32,128]{3,2,1,0:T(8,128)}, f32[4,4,4,32,128]{4,3,2,1,0:T(8,128)S(1)}, f32[3,12,40,128]{3,2,1,0:T(8,128)S(1)}, f32[3,40,128]{2,1,0:T(8,128)S(1)}) custom-call(f32[384,128]{1,0:T(8,128)S(1)} %get-tuple-element.34.raw_ref, f32[128,128]{1,0:T(8,128)S(1)} %get-tuple-element.44.t_ref, ...), custom_call_target="tpu_custom_call" | custom-call | flops 16777216 | bytes 1048576 | tf_op jit(solution)/shard_map/pallas_call | solution.py:531
  35.2 0.0 collective-permute-done.8.even
  35.2 0.0 collective-permute-done.9.odd
  35.2 2.5 %shard_map.105 = f32[2,4,32,128]{3,2,1,0:T(8,128)} custom-call(f32[256,128]{1,0:T(8,128)S(1)} %collective-permute-done.3._b.wave_ref, f32[104,128]{1,0:T(8,128)S(1)} %collective-permute-done.7.edge_ref._, f32[304,128]{1,0:T(8,128)S(1)} %collective-permute-done.8.even, f32[304,128]{1,0:T(8,128)S(1)} %collective-permute-done.9.odd, ...), custom_call_target="tpu_custom_call" | custom-call | flops 16777216 | bytes 1048576 | tf_op jit(solution)/shard_map/pallas_call | solution.py:531
  (3 shorter events, 0.1 us)
Async XLA Ops:
  1.8 5.2 %collective-permute-start = (f32[64,128]{1,0:T(8,128)S(1)}, f32[64,128]{1,0:T(8,128)S(1)}, u32[]{:S(2)}, u32[]{:S(2)}) collective-permute-start(f32[64,128]{1,0:T(8,128)S(1)} %get-tuple-element.37), channel_id=1, source_target_pairs={{12,0},{0,4},{4,8},{8,12},{13,1},{1,5},{5,9},{9,13},{14,2},{2,6},{... | collective-permute-start | bytes 98312 | tf_op jit(solution)/shard_map/ppermute | solution.py:564
  3.5 3.6 %collective-permute-start.2 = (f32[32,128]{1,0:T(8,128)S(1)}, f32[32,128]{1,0:T(8,128)S(1)}, u32[]{:S(2)}, u32[]{:S(2)}) collective-permute-start(f32[32,128]{1,0:T(8,128)S(1)} %get-tuple-element.39), channel_id=1, source_target_pairs={{1,0},{0,1},{3,2},{2,3},{5,4},{4,5},{7,6},{6,7},{9,8},{8,9},{11,10... | collective-permute-start | bytes 49160 | tf_op jit(solution)/shard_map/ppermute | solution.py:564
  3.5 3.6 %collective-permute-start.1 = (f32[8,128]{1,0:T(8,128)S(1)}, f32[8,128]{1,0:T(8,128)S(1)}, u32[]{:S(2)}, u32[]{:S(2)}) collective-permute-start(f32[8,128]{1,0:T(8,128)S(1)} %get-tuple-element.38), channel_id=1, source_target_pairs={{2,0},{0,2},{3,1},{1,3},{6,4},{4,6},{7,5},{5,7},{10,8},{8,10},{11,... | collective-permute-start | bytes 12296 | tf_op jit(solution)/shard_map/ppermute | solution.py:564
  7.2 6.4 %collective-permute-start.3 = (f32[256,128]{1,0:T(8,128)S(1)}, f32[256,128]{1,0:T(8,128)S(1)}, u32[]{:S(2)}, u32[]{:S(2)}) collective-permute-start(f32[256,128]{1,0:T(8,128)S(1)} %get-tuple-element.43.wave_ref), channel_id=1, source_target_pairs={{8,0},{12,4},{0,8},{4,12},{9,1},{13,5},{1,9},{5,13},{10,2},{14,6},... | collective-permute-start | bytes 393224 | tf_op jit(solution)/shard_map/ppermute | solution.py:564
  8.7 4.7 %collective-permute-start.4 = (f32[176,128]{1,0:T(8,128)S(1)}, f32[176,128]{1,0:T(8,128)S(1)}, u32[]{:S(2)}, u32[]{:S(2)}) collective-permute-start(f32[176,128]{1,0:T(8,128)S(1)} %get-tuple-element.45), channel_id=1, source_target_pairs={{2,0},{0,2},{3,1},{1,3},{6,4},{4,6},{7,5},{5,7},{10,8},{8,10},{11,... | collective-permute-start | bytes 270344 | tf_op jit(solution)/shard_map/ppermute | solution.py:557
  10.3 3.1 %collective-permute-start.5 = (f32[64,128]{1,0:T(8,128)S(1)}, f32[64,128]{1,0:T(8,128)S(1)}, u32[]{:S(2)}, u32[]{:S(2)}) collective-permute-start(f32[64,128]{1,0:T(8,128)S(1)} %get-tuple-element.46.strip_ref), channel_id=1, source_target_pairs={{1,0},{0,1},{3,2},{2,3},{5,4},{4,5},{7,6},{6,7},{9,8},{8,9},{11,10... | collective-permute-start | bytes 98312 | tf_op jit(solution)/shard_map/ppermute | solution.py:564
  10.3 3.1 %collective-permute-start.6 = (f32[16,128]{1,0:T(8,128)S(1)}, f32[16,128]{1,0:T(8,128)S(1)}, u32[]{:S(2)}, u32[]{:S(2)}) collective-permute-start(f32[16,128]{1,0:T(8,128)S(1)} %get-tuple-element.47._), channel_id=1, source_target_pairs={{2,1},{3,0},{0,3},{1,2},{6,5},{7,4},{4,7},{5,6},{10,9},{11,8},{8,1... | collective-permute-start | bytes 24584 | tf_op jit(solution)/shard_map/ppermute | solution.py:557
  13.6 5.6 %collective-permute-start.7 = (f32[104,128]{1,0:T(8,128)S(1)}, f32[104,128]{1,0:T(8,128)S(1)}, u32[]{:S(2)}, u32[]{:S(2)}) collective-permute-start(f32[104,128]{1,0:T(8,128)S(1)} %get-tuple-element.49), channel_id=1, source_target_pairs={{8,0},{12,4},{0,8},{4,12},{9,1},{13,5},{1,9},{5,13},{10,2},{14,6},... | collective-permute-start | bytes 159752 | tf_op jit(solution)/shard_map/ppermute | solution.py:564
  19.2 9.0 %collective-permute-start.10 = (f32[456,128]{1,0:T(8,128)S(1)}, f32[456,128]{1,0:T(8,128)S(1)}, u32[]{:S(2)}, u32[]{:S(2)}) collective-permute-start(f32[456,128]{1,0:T(8,128)S(1)} %get-tuple-element.53), channel_id=1, source_target_pairs={{4,0},{0,4},{12,8},{8,12},{5,1},{1,5},{13,9},{9,13},{6,2},{2,6},{1... | collective-permute-start | bytes 700424 | tf_op jit(solution)/shard_map/ppermute | solution.py:573
  21.7 9.6 %collective-permute-start.11 = (f32[456,128]{1,0:T(8,128)S(1)}, f32[456,128]{1,0:T(8,128)S(1)}, u32[]{:S(2)}, u32[]{:S(2)}) collective-permute-start(f32[456,128]{1,0:T(8,128)S(1)} %get-tuple-element.54), channel_id=1, source_target_pairs={{0,0},{8,4},{4,8},{12,12},{1,1},{9,5},{5,9},{13,13},{2,2},{10,6},{... | collective-permute-start | bytes 700424 | tf_op jit(solution)/shard_map/ppermute | solution.py:573
  24.7 10.5 %collective-permute-start.8 = (f32[304,128]{1,0:T(8,128)S(1)}, f32[304,128]{1,0:T(8,128)S(1)}, u32[]{:S(2)}, u32[]{:S(2)}) collective-permute-start(f32[304,128]{1,0:T(8,128)S(1)} %get-tuple-element.50), channel_id=1, source_target_pairs={{4,0},{0,4},{12,8},{8,12},{5,1},{1,5},{13,9},{9,13},{6,2},{2,6},{1... | collective-permute-start | bytes 466952 | tf_op jit(solution)/shard_map/ppermute | solution.py:573
  24.8 10.4 %collective-permute-start.9 = (f32[304,128]{1,0:T(8,128)S(1)}, f32[304,128]{1,0:T(8,128)S(1)}, u32[]{:S(2)}, u32[]{:S(2)}) collective-permute-start(f32[304,128]{1,0:T(8,128)S(1)} %get-tuple-element.51), channel_id=1, source_target_pairs={{0,0},{8,4},{4,8},{12,12},{1,1},{9,5},{5,9},{13,13},{2,2},{10,6},{... | collective-permute-start | bytes 466952 | tf_op jit(solution)/shard_map/ppermute | solution.py:573

commit v6 on v5

--- a/solution.py
+++ b/solution.py
@@ -14,10 +14,10 @@
 BF16 = jnp.bfloat16
 VMEM_LIMIT = 16 * 1024 * 1024
 PLANES = BX * BY
-WAVE_EDGE_ROWS = 2 * BX * 8 + EY
-ADJ_EDGE_ROWS = 3 * BX * 8 + EY
-WAVE_ROWS = PLANES + 3 * BY + 5 * 8 + EY
-ADJ_ROWS = 2 * PLANES + 3 * BY + 8 * 8 + EY
+WAVE_OWN = (PLANES, PLANES + BY, PLANES + BY + 9 * 8)
+ADJ_OWN = (PLANES, PLANES + BY, PLANES + BY + 13 * 8)
+WAVE_SIDE = (PLANES + 3 * BY, PLANES + 4 * BY, PLANES + 4 * BY + 6 * 8)
+ADJ_SIDE = (3 * BY, 4 * BY, 4 * BY + 9 * 8)
 
 
 def lanes(shape):
@@ -52,12 +52,16 @@
     return result
 
 
-def face_kernel(
+def half_turn(tile):
+    return pltpu.roll(tile, MARGIN, 0)
+
+
+def load_kernel(
     stored_hbm, adj_hbm, lab_hbm, tissue_hbm, rc_hbm, rw_hbm, sc_hbm, sw_hbm,
-    raw_ref, s_ref, t_ref, face_x_ref, face_y_ref, face_z_ref, table_ref,
-    rc_ref, rw_ref, sc_ref, sw_ref,
-    stored, adj, lab, tissue, sem,
+    p_ref, ql_ref, s_ref, t_ref, last_x_ref, last_y_ref, strip_ref, table_ref,
+    rc_ref, rw_ref, sc_ref, sw_ref, *rest,
 ):
+    *sends, stored, adj, lab, tissue, sem = rest
     run([
         pltpu.make_async_copy(source, target, sem)
         for source, target in (
@@ -71,90 +75,67 @@
         table_ref[index : index + 1] = density * speed
         table_ref[8 + index : 9 + index] = speed / density
         table_ref[16 + index : 17 + index] = 1.0 - jnp.full((1, BZ), tissue[2, index], F32)
+    gy, gz = lax.axis_index("gy"), lax.axis_index("gz")
     lane = lanes((BY, BZ))
     row = rows((BY, BZ))
     tile_row = rows((8, BZ))
-    face_y = jnp.zeros((8, BZ), F32)
-    face_z = jnp.zeros((BY, BZ), F32)
+    strips = [jnp.zeros((BY, BZ), F32) for _ in range(3)]
+    tiles = [None] * 39
     previous = [None, None]
+
+    def edge_tile(block):
+        return jnp.where(tile_row < MARGIN, block[0:8], block[BY - 8 : BY])
+
     for x in range(BX):
         labels = lab[x].astype(F32) + 1.0
         buoyancy = buoyancy_of(labels, table_ref)
         plane = slice(x * BY, x * BY + BY)
-        for index, values in enumerate((stored[0, x], adj[0, x], labels)):
-            raw_ref[index * PLANES + x * BY : index * PLANES + x * BY + BY] = values
-        for kind, v in enumerate((stored, adj)):
-            vx, vy, vz = v[1, x], v[2, x], v[3, x]
-            if kind == 1:
-                vx, vy, vz = buoyancy * vx, buoyancy * vy, buoyancy * vz
-            y_below = pltpu.roll(vy, 1, 0)
-            z_below = pltpu.roll(vz, 1, 1)
-            index = kind * BX + x
-            last = pltpu.roll(vy[BY - 8 : BY], (index + 1) % 8, 0)
-            face_y = jnp.where(tile_row == index, last, face_y)
-            face_z = jnp.where(lane == index, pltpu.roll(vz, index + 1, 1), face_z)
-            spread = vx if x == 0 else vx - previous[kind]
-            spread = spread + (vy - jnp.where(row == 0, 0.0, y_below))
-            spread = spread + (vz - jnp.where(lane == 0, 0.0, z_below))
-            (s_ref, t_ref)[kind][plane] = spread
-            previous[kind] = vx
-    for kind in range(2):
-        face_x_ref[kind * BY : kind * BY + BY] = previous[kind]
-    face_y_ref[...] = face_y
-    face_z_ref[...] = face_z
-
-
-def fix_kernel(raw_ref, s_in, t_in, face_x, face_y, face_z, _, wave_ref, t_ref):
-    gx, gy, gz = (lax.axis_index(name) for name in ("gx", "gy", "gz"))
-    lane = lanes((BY, BZ))
-    row = rows((BY, BZ))
-    below = (
-        jnp.where(gx == lax.axis_size("gx") // 2, 0.0, 1.0),
-        jnp.where(gx == 0, 0.0, 1.0),
-    )
-    tile_y = face_y[...] * jnp.where(gy == 0, 0.0, 1.0)
-    tile_z = face_z[...] * jnp.where(gz == 0, 0.0, 1.0)
-    wave_ref[0:PLANES] = raw_ref[0:PLANES]
-    for kind, (source, target, base) in enumerate(((s_in, wave_ref, PLANES), (t_in, t_ref, 0))):
-        for x in range(BX):
-            block = source[x * BY : x * BY + BY]
-            if x == 0:
-                block = block - face_x[kind * BY : kind * BY + BY] * below[kind]
-            index = kind * BX + x
-            lane_below = pltpu.roll(tile_z, (BZ - index) % BZ, 1) if index else tile_z
-            block = block - jnp.where(row == 0, tile_y[index : index + 1], 0.0)
-            block = block - jnp.where(lane == 0, lane_below, 0.0)
-            target[base + x * BY : base + x * BY + BY] = block
-
-
-def edge_kernel(raw_ref, wave_ref, t_ref, edge_ref, corner_ref, strip_ref):
-    gz = lax.axis_index("gz")
-    lane = lanes((BY, BZ))
-    tile_row = rows((8, BZ))
-    strips = [jnp.zeros((BY, BZ), F32) for _ in range(2)]
-    sources = (
-        (wave_ref, 0), (wave_ref, PLANES), (raw_ref, PLANES), (t_ref, 0), (raw_ref, 2 * PLANES)
-    )
-    for field, (source, first_row) in enumerate(sources):
-        group, slot = (0, field) if field < 2 else (1, field - 2)
-        for x in range(BX):
-            block = source[first_row + x * BY : first_row + x * BY + BY]
-            tile = jnp.where(tile_row < MARGIN, block[0:8], block[BY - 8 : BY])
-            index = field * BX + x
-            edge_ref[index * 8 : index * 8 + 8] = tile
+        fields = [stored[index, x] for index in range(4)] + [adj[0, x]]
+        fields += [buoyancy * adj[index, x] for index in range(1, 4)] + [labels]
+        p_ref[plane] = fields[0]
+        ql_ref[plane] = fields[4]
+        ql_ref[PLANES + x * BY : PLANES + x * BY + BY] = labels
+        for index, block in enumerate(fields):
+            tiles[index * BX + x] = edge_tile(block)
+            group, slot = divmod(index, 4)
             base = slot * BX * STRIP + x * STRIP
             rolled = pltpu.roll(block, base + MARGIN, 1)
             first = base + MARGIN * gz
             strips[group] = jnp.where(
                 (lane >= first) & (lane < first + MARGIN), rolled, strips[group]
             )
-    for group in range(2):
-        strip = strips[group]
-        strip_ref[group * BY : group * BY + BY] = strip
-        tile = jnp.where(tile_row < MARGIN, strip[0:8], strip[BY - 8 : BY])
-        index = 5 * BX + group
-        edge_ref[index * 8 : index * 8 + 8] = tile
-        corner_ref[group * 8 : group * 8 + 8] = tile
+        for kind, target in enumerate((s_ref, t_ref)):
+            vx, vy, vz = fields[4 * kind + 1 : 4 * kind + 4]
+            spread = vx if x == 0 else vx - previous[kind]
+            spread = spread + (vy - jnp.where(row == 0, 0.0, pltpu.roll(vy, 1, 0)))
+            spread = spread + (vz - jnp.where(lane == 0, 0.0, pltpu.roll(vz, 1, 1)))
+            target[plane] = spread
+            previous[kind] = vx
+            index = (kind * BX + x) * 8
+            last_y_ref[index : index + 8] = vy[BY - 8 : BY]
+    for kind in range(2):
+        last_x_ref[kind * BY : kind * BY + BY] = previous[kind]
+    for group in range(3):
+        strip_ref[group * BY : group * BY + BY] = strips[group]
+        tiles[9 * BX + group] = edge_tile(strips[group])
+
+    def joined(first, second):
+        second = first if second is None else second
+        upward = jnp.where(tile_row < MARGIN, half_turn(first), second)
+        downward = jnp.where(tile_row < MARGIN, first, half_turn(second))
+        if len(sends) == 2:
+            return (jnp.where(gy == 0, upward, downward),)
+        return upward, downward
+
+    tiles.append(None)
+    half = len(sends) // 2
+    for place in range(20):
+        for target, tile in zip(sends[:half], joined(tiles[2 * place], tiles[2 * place + 1])):
+            target[place * 8 : place * 8 + 8] = tile
+    for place in range(2):
+        first = tiles[9 * BX + 2 * place]
+        for target, tile in zip(sends[half:], joined(first, tiles[9 * BX + 2 * place + 1])):
+            target[place * 8 : place * 8 + 8] = tile
 
 
 def copy_rows(target, base, source, first, count):
@@ -168,46 +149,103 @@
 
 
 def merge_kernel(
-    up_ref, down_ref, strip_ref, other_ref, corner_up_ref, corner_down_ref, _a, _b,
-    wave_edge_ref, adj_edge_ref,
+    from_up, from_down, corner_up, corner_down, strip_ref, other_ref,
+    s_ref, t_ref, last_x_ref, last_y_ref, _a, _b,
+    wave_ref, adj_ref, token_ref,
 ):
+    token_ref[...] = jnp.zeros((8, BZ), F32)
     gy = lax.axis_index("gy")
-    row = rows((8, BZ))
-    take_up = (row < MARGIN) & (gy < lax.axis_size("gy") - 1)
-    take_down = (row >= MARGIN) & (gy > 0)
+    tile_row = rows((8, BZ))
+    row, lane = rows((BY, BZ)), lanes((BY, BZ))
+    take_up = (tile_row < MARGIN) & (gy < lax.axis_size("gy") - 1)
+    take_down = (tile_row >= MARGIN) & (gy > 0)
+    _, cut_down = cut_flags()
 
     def halo(up, down, index):
-        sl = slice(index * 8, index * 8 + 8)
-        return jnp.where(take_up, up[sl], jnp.where(take_down, down[sl], 0.0))
-
-    for index in range(5 * BX):
-        target, place = (wave_edge_ref, index) if index < 8 else (adj_edge_ref, index - 8)
-        target[place * 8 : place * 8 + 8] = halo(up_ref, down_ref, index)
-    for group, target in enumerate((wave_edge_ref, adj_edge_ref)):
-        base = target.shape[0] - EY
+        place, second = divmod(index, 2)
+        sl = slice(place * 8, place * 8 + 8)
+        above = half_turn(up[sl]) if second else up[sl]
+        below = down[sl] if second else half_turn(down[sl])
+        return jnp.where(take_up, above, jnp.where(take_down, below, 0.0))
+
+    wide = []
+    for group in range(3):
         sl = slice(group * BY, group * BY + BY)
-        target[base : base + BY] = strip_ref[sl] + other_ref[sl]
-        tile = halo(up_ref, down_ref, 5 * BX + group) + halo(corner_up_ref, corner_down_ref, group)
-        target[base + BY : base + EY] = tile
-
-
-def adjoint_join_kernel(raw_ref, t_ref, adj_edge_ref, _, even_ref, odd_ref):
+        tile = halo(from_up, from_down, 9 * BX + group) + halo(corner_up, corner_down, group)
+        wide.append(jnp.concatenate([strip_ref[sl] + other_ref[sl], tile], 0))
+    strip_lane = lanes((EY, BZ))
+
+    def strip_field(index):
+        group, slot = divmod(index, 4)
+        moved = pltpu.roll(wide[group], (BZ - slot * BX * STRIP) % BZ, 1) if slot else wide[group]
+        return jnp.where(strip_lane < BX * STRIP, moved, 0.0)
+
+    last_lanes = (BX - 1) * STRIP
+    for kind, (source, target) in enumerate(((s_ref, wave_ref), (t_ref, adj_ref))):
+        first = 4 * kind
+        planes_end, x_end, tiles_end = (WAVE_OWN, ADJ_OWN)[kind]
+        vx, vy, vz = (strip_field(first + 1 + axis) for axis in range(3))
+        spread = vx - jnp.where(strip_lane < STRIP, 0.0, pltpu.roll(vx, STRIP, 1))
+        spread = (spread + (vy - y_down(vy))) + (vz - pltpu.roll(vz, 1, 1))
+        strip = strip_field(first)
+        strip = strip + pltpu.roll(jnp.where(strip_lane < BX * STRIP, spread, 0.0), BX * STRIP, 1)
+        last_slot = 2
+        if kind == 1:
+            strip = strip + pltpu.roll(strip_field(8), 2 * BX * STRIP, 1)
+            last_slot = 3
+        last = jnp.where(strip_lane >= last_lanes, vx, 0.0)
+        strip = strip + pltpu.roll(last, last_slot * BX * STRIP - last_lanes, 1)
+        target[tiles_end : tiles_end + EY] = strip
+        target[planes_end:x_end] = last_x_ref[kind * BY : kind * BY + BY]
+
+        vx_before = None
+        for x in range(BX):
+            vx_t, vy_t, vz_t = (
+                halo(from_up, from_down, (first + 1 + axis) * BX + x) for axis in range(3)
+            )
+            below_z = pltpu.roll(vz, (BZ - (x * STRIP + MARGIN - 1)) % BZ, 1) * cut_down
+            last_y = last_y_ref[(kind * BX + x) * 8 : (kind * BX + x) * 8 + 8]
+            y_before = jnp.where(
+                tile_row == 0, pltpu.roll(last_y, 1, 0), pltpu.roll(vy_t, 1, 0)
+            )
+            z_before = jnp.where(lane[0:8] == 0, below_z[BY:EY], pltpu.roll(vz_t, 1, 1))
+            spread = vx_t if x == 0 else vx_t - vx_before
+            spread = (spread + (vy_t - y_before)) + (vz_t - z_before)
+            vx_before = vx_t
+            block = source[x * BY : x * BY + BY]
+            block = block - jnp.where(row == 0, vy_t[7:8], 0.0)
+            block = block - jnp.where(lane == 0, below_z[0:BY], 0.0)
+            target[x * BY : x * BY + BY] = block
+            base = x_end + x * 8
+            target[base : base + 8] = halo(from_up, from_down, first * BX + x)
+            target[base + 32 : base + 40] = spread
+            if kind == 1:
+                target[base + 64 : base + 72] = halo(from_up, from_down, 8 * BX + x)
+        target[tiles_end - 8 : tiles_end] = vx_before
+
+
+def adjoint_join_kernel(ql_ref, adj_ref, _, even_ref, odd_ref, token_ref):
+    token_ref[...] = jnp.zeros((8, BZ), F32)
+    planes_end, x_end, tiles_end = ADJ_OWN
     for target, first in zip((even_ref, odd_ref), pair_planes()):
-        base = copy_rows(target, 0, raw_ref, PLANES, 2 * PLANES)
-        base = copy_rows(target, base, t_ref, first * BY, 3 * BY)
-        base = copy_rows(target, base, adj_edge_ref, first * 8, 24)
-        base = copy_rows(target, base, adj_edge_ref, 32 + first * 16, 16)
-        base = copy_rows(target, base, adj_edge_ref, 64 + first * 8, 24)
-        copy_rows(target, base, adj_edge_ref, ADJ_EDGE_ROWS - EY, EY)
-
-
-def join_kernel(wave_ref, edge_ref, even_ref, odd_ref):
+        base = copy_rows(target, 0, adj_ref, first * BY, 3 * BY)
+        base = copy_rows(target, base, adj_ref, planes_end, BY)
+        base = copy_rows(target, base, adj_ref, x_end + first * 8, 24)
+        base = copy_rows(target, base, adj_ref, x_end + 32 + first * 16, 16)
+        base = copy_rows(target, base, adj_ref, x_end + 64 + first * 8, 24)
+        base = copy_rows(target, base, adj_ref, tiles_end - 8, 8 + EY)
+        copy_rows(target, base, ql_ref, 0, 2 * PLANES)
+
+
+def join_kernel(p_ref, wave_ref, _, even_ref, odd_ref):
+    planes_end, x_end, tiles_end = WAVE_OWN
     for target, first in zip((even_ref, odd_ref), pair_planes()):
-        base = copy_rows(target, 0, wave_ref, 0, PLANES)
-        base = copy_rows(target, base, wave_ref, PLANES + first * BY, 3 * BY)
-        base = copy_rows(target, base, edge_ref, first * 8, 24)
-        base = copy_rows(target, base, edge_ref, 32 + first * 16, 16)
-        copy_rows(target, base, edge_ref, WAVE_EDGE_ROWS - EY, EY)
+        base = copy_rows(target, 0, p_ref, 0, PLANES)
+        base = copy_rows(target, base, wave_ref, first * BY, 3 * BY)
+        base = copy_rows(target, base, wave_ref, planes_end, BY)
+        base = copy_rows(target, base, wave_ref, x_end + first * 8, 24)
+        base = copy_rows(target, base, wave_ref, x_end + 32 + first * 16, 16)
+        copy_rows(target, base, wave_ref, tiles_end - 8, 8 + EY)
 
 
 def split(values):
@@ -347,14 +385,14 @@
     return {plane: base + place * step for place, plane in enumerate(planes)}
 
 
-def widened(own, own_tiles, messages, x, layout, side):
+def widened(own, own_tiles, x, layout, side):
     block, plane = divmod(x, BX)
     if block == 1:
         main = own[0][own[1] + plane * BY : own[1] + plane * BY + BY]
         tile = own_tiles[0][own_tiles[1] + plane * 8 : own_tiles[1] + plane * 8 + 8]
         return jnp.concatenate([main, tile], 0)
     parts = []
-    for (base, wanted), count in zip(layout, (BY, 8)):
+    for (messages, base, wanted), count in zip(layout, (BY, 8)):
         first = side_rows(base, wanted, count, block).get(plane)
         if first is None:
             parts.append(jnp.zeros((count, BZ), F32))
@@ -363,6 +401,32 @@
     return jnp.concatenate(parts, 0)
 
 
+def less_plane_below(value, x, own_ref, own_rows, messages, side_rows_of, side):
+    if x == BX:
+        planes_end, _, tiles_end = side_rows_of
+        main = from_side(messages, planes_end, BY, 0, side)
+        tile = from_side(messages, tiles_end - 8, 8, 0, side)
+    elif x == 2 * BX:
+        planes_end, _, tiles_end = own_rows
+        high = side[1]
+        main = own_ref[planes_end : planes_end + BY] * high
+        tile = own_ref[tiles_end - 8 : tiles_end] * high
+    else:
+        return value
+    return value - jnp.concatenate([main, tile], 0)
+
+
+def strip_below(own, messages, first, slot, side):
+    lane = lanes(own.shape)
+    width = BX * STRIP
+    low = from_side(messages, first, EY, 0, side)
+    low = pltpu.roll(low, (width - slot * width) % BZ, 1)
+    own = pltpu.roll(own * side[1], (2 * width - slot * width) % BZ, 1)
+    in_own = (lane >= width) & (lane < width + STRIP)
+    in_high = (lane >= 2 * width) & (lane < 2 * width + STRIP)
+    return jnp.where(in_own, low, jnp.where(in_high, own, 0.0))
+
+
 def whole_strip(own, messages, first, slot, side):
     low = from_side(messages, first, EY, 0, side)
     high = from_side(messages, first, EY, 2, side)
@@ -370,7 +434,8 @@
 
 
 def adjoint_kernel(
-    raw_ref, t_ref, edge_ref, even, odd, adj_hbm, ra_ref, rsa_ref, rb_ref, rsb_ref, table_ref,
+    ql_ref, late_ref, even, odd, adj_hbm, ra_ref, rsa_ref, rb_ref, rsb_ref,
+    table_ref,
     out_ref, hist_ref, coef_ref, coef_strip_ref,
     field, w_sem,
 ):
@@ -381,24 +446,28 @@
     messages = (even, odd)
     r_refs = ((ra_ref, 0), (ra_ref, 1), (rb_ref, 0), (rb_ref, 1))
     rs_refs = ((rsa_ref, 0), (rsa_ref, 1), (rsb_ref, 0), (rsb_ref, 1))
-    tiles = 2 * PLANES + 3 * BY
+    tiles, own_tiles, raws = ADJ_SIDE[1], ADJ_OWN[1], ADJ_SIDE[2] + EY
 
     def initial(index, x):
-        own = ((raw_ref, PLANES), (t_ref, 0), (raw_ref, 2 * PLANES))[index]
+        own = ((ql_ref, 0), (late_ref, 0), (ql_ref, PLANES))[index]
         layout = (
-            ((0, 4), (tiles, 3)),
-            ((2 * PLANES, 3), (tiles + 24, 2)),
-            ((PLANES, 4), (tiles + 40, 3)),
+            ((messages, raws, 4), (messages, tiles, 3)),
+            ((messages, 0, 3), (messages, tiles + 24, 2)),
+            ((messages, raws + PLANES, 4), (messages, tiles + 40, 3)),
         )[index]
-        return widened(own, (edge_ref, 32 * index), messages, x, layout, side)
+        value = widened(own, (late_ref, own_tiles + 32 * index), x, layout, side)
+        if index == 1:
+            value = less_plane_below(value, x, late_ref, ADJ_OWN, messages, ADJ_SIDE, side)
+        return value
 
     for x in range(EX):
         stiff, buoy, damp = coefficients(initial(2, x), table_ref)
         coef_ref[0, x], coef_ref[1, x], coef_ref[2, x] = stiff, buoy, damp
-    own_strip = edge_ref[ADJ_EDGE_ROWS - EY : ADJ_EDGE_ROWS]
+    own_strip = late_ref[ADJ_OWN[2] : ADJ_OWN[2] + EY]
     q_s, t_s, label_s = (
-        whole_strip(own_strip, messages, ADJ_ROWS - EY, slot, side) for slot in range(3)
-    )
+        whole_strip(own_strip, messages, ADJ_SIDE[2], slot, side) for slot in range(3)
+    )
+    t_s = t_s - strip_below(own_strip, messages, ADJ_SIDE[2], 3, side)
     stiff_s, buoy_s, damp_s = coefficients(label_s, table_ref)
     coef_strip_ref[0], coef_strip_ref[1], coef_strip_ref[2] = stiff_s, buoy_s, damp_s
     w_copy.wait()
@@ -453,24 +522,31 @@
 
 
 def forward_kernel(
-    wave_ref, edge_ref, even, odd, coef_ref, coef_strip_ref, s_ref, ss_ref, hist_ref,
+    p_ref, late_ref, even, odd, coef_ref, coef_strip_ref, s_ref, ss_ref, hist_ref,
     grad_ref,
     field,
 ):
     cut_up, cut_down = cut_flags()
     side = sides()
     messages = (even, odd)
-    tiles = PLANES + 3 * BY
+    tiles, own_tiles = WAVE_SIDE[1], WAVE_OWN[1]
 
     def initial(index, x):
-        layout = (((0, 4), (tiles, 3)), ((PLANES, 3), (tiles + 24, 2)))[index]
-        own = (wave_ref, PLANES * index)
-        return widened(own, (edge_ref, 32 * index), messages, x, layout, side)
-
-    own_strip = edge_ref[WAVE_EDGE_ROWS - EY : WAVE_EDGE_ROWS]
+        layout = (
+            ((messages, 0, 4), (messages, tiles, 3)),
+            ((messages, PLANES, 3), (messages, tiles + 24, 2)),
+        )[index]
+        own = ((p_ref, 0), (late_ref, 0))[index]
+        value = widened(own, (late_ref, own_tiles + 32 * index), x, layout, side)
+        if index == 1:
+            value = less_plane_below(value, x, late_ref, WAVE_OWN, messages, WAVE_SIDE, side)
+        return value
+
+    own_strip = late_ref[WAVE_OWN[2] : WAVE_OWN[2] + EY]
     p_s, s_s = (
-        whole_strip(own_strip, messages, WAVE_ROWS - EY, slot, side) for slot in range(2)
-    )
+        whole_strip(own_strip, messages, WAVE_SIDE[2], slot, side) for slot in range(2)
+    )
+    s_s = s_s - strip_below(own_strip, messages, WAVE_SIDE[2], 2, side)
     stiff_s, buoy_s, damp_s = coef_strip_ref[0], coef_strip_ref[1], coef_strip_ref[2]
 
     for step in range(1, STEPS + 1):
@@ -522,7 +598,7 @@
     return jax.ShapeDtypeStruct(dims, F32)
 
 
-def call(kernel, outs, operands, scratch, places):
+def call(kernel, outs, operands, scratch, places, micros=0.1):
     spaces = {"h": pltpu.HBM, "a": pl.ANY, "v": pltpu.VMEM}
     operands = [
         pltpu.with_memory_space_constraint(operand, pltpu.HBM) if place == "h" else operand
@@ -535,11 +611,13 @@
         out_specs=[pl.BlockSpec(memory_space=pltpu.VMEM)] * len(outs),
         scratch_shapes=scratch,
         compiler_params=pltpu.CompilerParams(vmem_limit_bytes=VMEM_LIMIT),
-        cost_estimate=pl.CostEstimate(flops=1 << 24, bytes_accessed=1 << 20, transcendentals=0),
+        cost_estimate=pl.CostEstimate(
+            flops=0, bytes_accessed=int(3.69e6 * micros), transcendentals=0
+        ),
     )(*operands)
 
 
-def from_sides(array, axes):
+def from_sides(sends, axes):
     count = lax.axis_size("gy")
 
     def route(offset):
@@ -554,9 +632,10 @@
         return pairs
 
     if count == 2:
-        both = lax.ppermute(array, axes, route(1) + route(-1))
+        both = lax.ppermute(sends[0], axes, route(1) + route(-1))
         return both, both
-    return lax.ppermute(array, axes, route(1)), lax.ppermute(array, axes, route(-1))
+    upward, downward = sends
+    return lax.ppermute(downward, axes, route(1)), lax.ppermute(upward, axes, route(-1))
 
 
 def rotated(array, axis, offset):
@@ -582,18 +661,22 @@
         stored, adjoint_end, labels, tissue,
         receiver_cells.T, receiver_wave, source_cells.T, source_wave,
     ]
-    raw, s, t, face_x, face_y, face_z, table, receivers, receiver_wave, sources, source_wave = call(
-        face_kernel,
+    ways = 1 if lax.axis_size("gy") == 2 else 2
+    p, ql, s, t, last_x, last_y, strips, table, receivers, receiver_wave, sources, source_wave, *sends = call(
+        load_kernel,
         [
-            shape(3 * PLANES, BZ),
+            shape(PLANES, BZ),
+            shape(2 * PLANES, BZ),
             shape(PLANES, BZ),
             shape(PLANES, BZ),
             shape(2 * BY, BZ),
-            shape(8, BZ),
-            shape(BY, BZ),
+            shape(2 * BX * 8, BZ),
+            shape(3 * BY, BZ),
             shape(24, BZ),
         ]
-        + [jax.ShapeDtypeStruct(array.shape, array.dtype) for array in arguments[4:]],
+        + [jax.ShapeDtypeStruct(array.shape, array.dtype) for array in arguments[4:]]
+        + [shape(20 * 8, BZ)] * ways
+        + [shape(2 * 8, BZ)] * ways,
         arguments,
         [
             pltpu.VMEM(stored.shape, F32),
@@ -603,74 +686,63 @@
             pltpu.SemaphoreType.DMA,
         ],
         "hhhhhhhh",
-    )
+        1.4,
+    )
+    from_up, from_down = from_sides(sends[:ways], "gy")
+    other = rotated(strips, "gz", 1)
+    corner_up, corner_down = from_sides(sends[ways:], ("gy", "gz"))
+    p = rotated(p, "gx", half)
     rb, rsb = call(
         late_kernel,
         [shape(2, EX * EY, BZ), shape(2, EY, BZ)],
         [receivers, receiver_wave],
         [],
         "vv",
-    )
-    face_x = rotated(face_x, "gx", -1)
-    face_y = rotated(face_y, "gy", -1)
-    face_z = rotated(face_z, "gz", -1)
-    wave, t = call(
-        fix_kernel,
-        [shape(2 * PLANES, BZ), shape(PLANES, BZ)],
-        [raw, s, t, face_x, face_y, face_z, rsb],
+        1.2,
+    )
+    early_planes, source_planes = (last - first for first, last in (EARLY_PLANES, SOURCE_PLANES))
+    late, adj_late, token = call(
+        merge_kernel,
+        [shape(WAVE_OWN[2] + EY, BZ), shape(ADJ_OWN[2] + EY, BZ), shape(8, BZ)],
+        [from_up, from_down, corner_up, corner_down, strips, other, s, t, last_x, last_y, rsb, p],
         [],
-        "vvvvvva",
-    )
-    edges, corners, strips = call(
-        edge_kernel,
-        [shape((5 * BX + 2) * 8, BZ), shape(16, BZ), shape(2 * BY, BZ)],
-        [raw, wave, t],
-        [],
-        "vvv",
-    )
-    wave = rotated(wave, "gx", half)
-    early_planes, source_planes = (last - first for first, last in (EARLY_PLANES, SOURCE_PLANES))
+        "vvvvvvvvvvaa",
+    )
+    late = rotated(late, "gx", half)
+    token = rotated(token, "gz", 1)
     ra, rsa = call(
         early_kernel,
         [shape(2, early_planes * EY, BZ), shape(2, EY, BZ)],
-        [receivers, receiver_wave, corners],
+        [receivers, receiver_wave, adj_late],
         [],
         "vva",
+        1.0,
     )
     ra, rb = ra.reshape(2, early_planes, EY, BZ), rb.reshape(2, EX, EY, BZ)
-    other = rotated(strips, "gz", 1)
-    up, down = from_sides(edges, "gy")
-    corner_up, corner_down = from_sides(corners, ("gy", "gz"))
-    wave_edge, adj_edge = call(
-        merge_kernel,
-        [shape(WAVE_EDGE_ROWS, BZ), shape(ADJ_EDGE_ROWS, BZ)],
-        [up, down, strips, other, corner_up, corner_down, rsa, wave],
+    even, odd, second = call(
+        adjoint_join_kernel,
+        [shape(ADJ_SIDE[2] + EY + 2 * PLANES, BZ)] * 2 + [shape(8, BZ)],
+        [ql, adj_late, token],
         [],
-        "vvvvvvaa",
-    )
-    wave_edge = rotated(wave_edge, "gx", half)
+        "vva",
+    )
+    even, odd = paired(even, False), paired(odd, True)
+    second = rotated(second, "gz", 1)
     src, src_strip = call(
         source_kernel,
         [shape(STEPS - 1, source_planes * EY, BZ), shape(STEPS - 1, EY, BZ)],
-        [sources, source_wave, adj_edge],
+        [sources, source_wave, second],
         [],
         "vva",
+        0.5,
     )
     src = src.reshape(STEPS - 1, source_planes, EY, BZ)
-    even, odd = call(
-        adjoint_join_kernel,
-        [shape(ADJ_ROWS, BZ), shape(ADJ_ROWS, BZ)],
-        [raw, t, adj_edge, wave_edge],
-        [],
-        "vvva",
-    )
-    even, odd = paired(even, False), paired(odd, True)
     wave_even, wave_odd = call(
         join_kernel,
-        [shape(WAVE_ROWS, BZ), shape(WAVE_ROWS, BZ)],
-        [wave, wave_edge],
+        [shape(WAVE_SIDE[2] + EY, BZ)] * 2,
+        [p, late, second],
         [],
-        "vv",
+        "vva",
     )
     wave_even, wave_odd = paired(wave_even, False), paired(wave_odd, True)
     adjoint_start, hist, coef, coef_strip = call(
@@ -681,16 +753,18 @@
             shape(3, EX, EY, BZ),
             shape(3, EY, BZ),
         ],
-        [raw, t, adj_edge, even, odd, adjoint_end, ra, rsa, rb, rsb, table],
+        [ql, adj_late, even, odd, adjoint_end, ra, rsa, rb, rsb, table],
         [pltpu.VMEM((2, EX, EY, BZ), F32), pltpu.SemaphoreType.DMA],
-        "vvvvvhvvvvv",
+        "vvvvhvvvvv",
+        3.9,
     )
     (gradient,) = call(
         forward_kernel,
         [shape(2, BX, BY, BZ)],
-        [wave, wave_edge, wave_even, wave_odd, coef, coef_strip, src, src_strip, hist],
+        [p, late, wave_even, wave_odd, coef, coef_strip, src, src_strip, hist],
         [pltpu.VMEM((2, EX, EY, BZ), F32)],
         "vvvvvvvvv",
+        2.5,
     )
     return gradient, adjoint_start
 

time: 37.9 us -> 33.2 us (0.88)
  the two profiles are of different devices: /device:TPU:8 before, /device:TPU:0 now
where the time goes in v6:
time: 33.2 us; the launch traced here: 33 us
  starting transfers between devices  13.3 us (40%)
  Pallas kernels  11 us (33%)
  waiting for transfers between devices  7.99 us (24%)
  between operations  0.73 us (2%)
    pallas_call x9, Pallas kernels, call(): pl.pallas_call(kernel, out_shape=outs, in_specs=[pl.BlockSpec(memory_spac...  11 us
    ppermute x4, starting transfers between devices, paired(): return lax.ppermute(array, 'gx', pairs)  4.83 us
    ppermute x5, starting transfers between devices, rotated(): lax.ppermute(array, axis, [((i + offset) % count, i) for i in range(count)])  4.78 us
    ppermute x5, waiting for transfers between devices, rotated(): lax.ppermute(array, axis, [((i + offset) % count, i) for i in range(count)])  4.08 us
    ppermute x2, starting transfers between devices, from_sides(): both = lax.ppermute(sends[0], axes, route(1) + route(-1))  3.65 us
    ppermute x4, waiting for transfers between devices, paired(): return lax.ppermute(array, 'gx', pairs)  2.73 us
    ppermute x2, waiting for transfers between devices, from_sides(): both = lax.ppermute(sends[0], axes, route(1) + route(-1))  1.18 us
  transfers between devices with their start and end apart: 11, of which 5 were waited for; matrix products, arithmetic and copies ran while one was open for 0% of the time, Pallas kernels for 21%

profile of v6, /device:TPU:0, one launch (start us, length us, event | category | flops | bytes accessed | tf_op | source)
XLA Modules:
  0.0 33.0 jit_solution(14595308435470094281)
XLA Ops:
  0.6 1.3 %shard_map.95 = (f32[128,128]{1,0:T(8,128)S(1)}, f32[256,128]{1,0:T(8,128)S(1)}, f32[128,128]{1,0:T(8,128)S(1)}, f32[128,128]{1,0:T(8,128)S(1)}, f32[64,128]{1,0...) custom-call(f32[4,4,32,128]{3,2,1,0:T(8,128)} %stored_hbm.1, ...), custom_call_target="tpu_custom_call" | custom-call | bytes 5166000 | tf_op jit(solution)/shard_map/pallas_call | solution.py:607
  2.0 3.0 %collective-permute-start.1 = (f32[160,128]{1,0:T(8,128)S(1)}, f32[160,128]{1,0:T(8,128)S(1)}, u32[]{:S(2)}, u32[]{:S(2)}) collective-permute-start(f32[160,128]{1,0:T(8,128)S(1)} %get-tuple-element.35), channel_id=1, source_target_pairs={{2,0},{0,2},{3,1},{1,3},{6,4},{4,6},{7,5},{5,7},{10,8},{8,10},{11,... | collective-permute-start | bytes 245768 | tf_op jit(solution)/shard_map/ppermute | solution.py:635
  5.0 2.6 %collective-permute-start = (f32[128,128]{1,0:T(8,128)S(1)}, f32[128,128]{1,0:T(8,128)S(1)}, u32[]{:S(2)}, u32[]{:S(2)}) collective-permute-start(f32[128,128]{1,0:T(8,128)S(1)} %get-tuple-element.34), channel_id=1, source_target_pairs={{8,0},{12,4},{0,8},{4,12},{9,1},{13,5},{1,9},{5,13},{10,2},{14,6},... | collective-permute-start | bytes 196616 | tf_op jit(solution)/shard_map/ppermute | solution.py:643
  7.5 0.0 collective-permute-start.3
  7.6 0.6 %collective-permute-start.2 = (f32[16,128]{1,0:T(8,128)S(1)}, f32[16,128]{1,0:T(8,128)S(1)}, u32[]{:S(2)}, u32[]{:S(2)}) collective-permute-start(f32[16,128]{1,0:T(8,128)S(1)} %get-tuple-element.36), channel_id=1, source_target_pairs={{2,1},{3,0},{0,3},{1,2},{6,5},{7,4},{4,7},{5,6},{10,9},{11,8},{8,1... | collective-permute-start | bytes 24584 | tf_op jit(solution)/shard_map/ppermute | solution.py:635
  8.2 1.2 %shard_map.96 = (f32[2,480,128]{2,1,0:T(8,128)S(1)}, f32[2,40,128]{2,1,0:T(8,128)S(1)}) custom-call(s32[3,1024]{1,0:T(4,128)S(1)} %get-tuple-element.42.receivers, f32[4,1024]{1,0:T(4,128)S(1)} %get-tuple-element.43.receiver_wave), custom_call_target="tpu_custom_call" | custom-call | bytes 4428000 | tf_op jit(solution)/shard_map/pallas_call | solution.py:607
  9.5 1.2 %collective-permute-done.2.corner_up.corner_down = f32[16,128]{1,0:T(8,128)S(1)} collective-permute-done((f32[16,128]{1,0:T(8,128)S(1)}, f32[16,128]{1,0:T(8,128)S(1)}, u32[]{:S(2)}, u32[]{:S(2)}) %collective-permute-start.2) | collective-permute-done | bytes 8224 | tf_op jit(solution)/shard_map/ppermute | solution.py:635
  10.6 0.0 collective-permute-done.3.other_ref
  10.6 0.0 collective-permute-done._b.p_ref
  10.6 0.0 collective-permute-done.1.from_up.from_down
  10.6 0.3 shard_map.97
  10.9 2.2 %collective-permute-start.4 = (f32[272,128]{1,0:T(8,128)S(1)}, f32[272,128]{1,0:T(8,128)S(1)}, u32[]{:S(2)}, u32[]{:S(2)}) collective-permute-start(f32[272,128]{1,0:T(8,128)S(1)} %get-tuple-element.45), channel_id=1, source_target_pairs={{8,0},{12,4},{0,8},{4,12},{9,1},{13,5},{1,9},{5,13},{10,2},{14,6},... | collective-permute-start | bytes 417800 | tf_op jit(solution)/shard_map/ppermute | solution.py:643
  13.1 0.0 collective-permute-start.5
  13.1 1.2 %collective-permute-done.5._ = f32[8,128]{1,0:T(8,128)S(1)} collective-permute-done((f32[8,128]{1,0:T(8,128)S(1)}, f32[8,128]{1,0:T(8,128)S(1)}, u32[]{:S(2)}, u32[]{:S(2)}) %collective-permute-start.5) | collective-permute-done | bytes 4128 | tf_op jit(solution)/shard_map/ppermute | solution.py:643
  14.3 0.7 %collective-permute-start.10 = (f32[496,128]{1,0:T(8,128)S(1)}, f32[496,128]{1,0:T(8,128)S(1)}, u32[]{:S(2)}, u32[]{:S(2)}) collective-permute-start(f32[496,128]{1,0:T(8,128)S(1)} %get-tuple-element.53), channel_id=1, source_target_pairs={{0,0},{8,4},{4,8},{12,12},{1,1},{9,5},{5,9},{13,13},{2,2},{10,6},{... | collective-permute-start | bytes 761864 | tf_op jit(solution)/shard_map/ppermute | solution.py:652
  15.0 3.4 %collective-permute-start.9 = (f32[496,128]{1,0:T(8,128)S(1)}, f32[496,128]{1,0:T(8,128)S(1)}, u32[]{:S(2)}, u32[]{:S(2)}) collective-permute-start(f32[496,128]{1,0:T(8,128)S(1)} %get-tuple-element.52), channel_id=1, source_target_pairs={{4,0},{0,4},{12,8},{8,12},{5,1},{1,5},{13,9},{9,13},{6,2},{2,6},{1... | collective-permute-start | bytes 761864 | tf_op jit(solution)/shard_map/ppermute | solution.py:652
  18.4 0.0 collective-permute-start.6
  18.4 1.2 %collective-permute-done.6._ = f32[8,128]{1,0:T(8,128)S(1)} collective-permute-done((f32[8,128]{1,0:T(8,128)S(1)}, f32[8,128]{1,0:T(8,128)S(1)}, u32[]{:S(2)}, u32[]{:S(2)}) %collective-permute-start.6) | collective-permute-done | bytes 4128 | tf_op jit(solution)/shard_map/ppermute | solution.py:643
  19.6 1.7 %collective-permute-done.4.wave_ref.late_ref = f32[272,128]{1,0:T(8,128)S(1)} collective-permute-done((f32[272,128]{1,0:T(8,128)S(1)}, f32[272,128]{1,0:T(8,128)S(1)}, u32[]{:S(2)}, u32[]{:S(2)}) %collective-permute-start.4) | collective-permute-done | bytes 139296 | tf_op jit(solution)/shard_map/ppermute | solution.py:643
  21.3 0.1 collective-permute-start.7
  21.4 0.7 %collective-permute-start.8 = (f32[344,128]{1,0:T(8,128)S(1)}, f32[344,128]{1,0:T(8,128)S(1)}, u32[]{:S(2)}, u32[]{:S(2)}) collective-permute-start(f32[344,128]{1,0:T(8,128)S(1)} %get-tuple-element.51), channel_id=1, source_target_pairs={{0,0},{8,4},{4,8},{12,12},{1,1},{9,5},{5,9},{13,13},{2,2},{10,6},{... | collective-permute-start | bytes 528392 | tf_op jit(solution)/shard_map/ppermute | solution.py:652
  22.1 1.0 %shard_map.100 = (f32[2,320,128]{2,1,0:T(8,128)S(1)}, f32[2,40,128]{2,1,0:T(8,128)S(1)}) custom-call(s32[3,1024]{1,0:T(4,128)S(1)} %get-tuple-element.42.receivers, f32[4,1024]{1,0:T(4,128)S(1)} %get-tuple-element.43.receiver_wave, f32[304,128]{1,0:T(8,128)S(1)} %get-tuple-element.47.adj_ref._.late_ref), custom_call_target="tpu_custom_call" | custom-call | bytes 3690000 | tf_op jit(solution)/shard_map/pallas_call | solution.py:607
  23.1 0.6 %shard_map.102 = (f32[3,400,128]{2,1,0:T(8,128)S(1)}, f32[3,40,128]{2,1,0:T(8,128)S(1)}) custom-call(s32[3,64]{1,0:T(4,128)S(1)} %get-tuple-element.60.sources, f32[4,64]{1,0:T(4,128)S(1)} %get-tuple-element.61.source_wave, f32[8,128]{1,0:T(8,128)S(1)} %collective-permute-done.6._), custom_call_target="tpu_custom_call" | custom-call | bytes 1845000 | tf_op jit(solution)/shard_map/pallas_call | solution.py:607
  23.7 0.0 collective-permute-done.10.odd
  23.7 2.7 %collective-permute-done.9.even = f32[496,128]{1,0:T(8,128)S(1)} collective-permute-done((f32[496,128]{1,0:T(8,128)S(1)}, f32[496,128]{1,0:T(8,128)S(1)}, u32[]{:S(2)}, u32[]{:S(2)}) %collective-permute-start.9) | collective-permute-done | bytes 253984 | tf_op jit(solution)/shard_map/ppermute | solution.py:652
  26.4 4.0 %shard_map.101 = (f32[4,4,32,128]{3,2,1,0:T(8,128)}, f32[4,4,4,32,128]{4,3,2,1,0:T(8,128)S(1)}, f32[3,12,40,128]{3,2,1,0:T(8,128)S(1)}, f32[3,40,128]{2,1,0:T(8,128)S(1)}) custom-call(f32[256,128]{1,0:T(8,128)S(1)} %get-tuple-element.46.ql_ref, f32[304,128]{1,0:T(8,128)S(1)} %get-tuple-element.47.adj_ref._.late_ref, ...), custom_call_target="tpu_custom_call" | custom-call | bytes 14391000 | tf_op jit(solution)/shard_map/pallas_call | solution.py:607
  30.4 0.0 collective-permute-done.7.even
  30.4 0.0 collective-permute-done.8.odd
  30.4 2.6 %shard_map.103 = f32[2,4,32,128]{3,2,1,0:T(8,128)} custom-call(f32[128,128]{1,0:T(8,128)S(1)} %collective-permute-done._b.p_ref, f32[272,128]{1,0:T(8,128)S(1)} %collective-permute-done.4.wave_ref.late_ref, f32[344,128]{1,0:T(8,128)S(1)} %collective-permute-done.7.even, f32[344,128]{1,0:T(8,128)S(1)} %collective-permute-done.8.odd, ...), custom_call_target="tpu_custom_call" | custom-call | bytes 9225000 | tf_op jit(solution)/shard_map/pallas_call | solution.py:607
  (2 shorter events, 0.1 us)
Async XLA Ops:
  2.0 8.7 %collective-permute-start.1 = (f32[160,128]{1,0:T(8,128)S(1)}, f32[160,128]{1,0:T(8,128)S(1)}, u32[]{:S(2)}, u32[]{:S(2)}) collective-permute-start(f32[160,128]{1,0:T(8,128)S(1)} %get-tuple-element.35), channel_id=1, source_target_pairs={{2,0},{0,2},{3,1},{1,3},{6,4},{4,6},{7,5},{5,7},{10,8},{8,10},{11,... | collective-permute-start | bytes 245768 | tf_op jit(solution)/shard_map/ppermute | solution.py:635
  5.0 5.7 %collective-permute-start = (f32[128,128]{1,0:T(8,128)S(1)}, f32[128,128]{1,0:T(8,128)S(1)}, u32[]{:S(2)}, u32[]{:S(2)}) collective-permute-start(f32[128,128]{1,0:T(8,128)S(1)} %get-tuple-element.34), channel_id=1, source_target_pairs={{8,0},{12,4},{0,8},{4,12},{9,1},{13,5},{1,9},{5,13},{10,2},{14,6},... | collective-permute-start | bytes 196616 | tf_op jit(solution)/shard_map/ppermute | solution.py:643
  7.5 3.1 %collective-permute-start.3 = (f32[96,128]{1,0:T(8,128)S(1)}, f32[96,128]{1,0:T(8,128)S(1)}, u32[]{:S(2)}, u32[]{:S(2)}) collective-permute-start(f32[96,128]{1,0:T(8,128)S(1)} %get-tuple-element.37.strip_ref), channel_id=1, source_target_pairs={{1,0},{0,1},{3,2},{2,3},{5,4},{4,5},{7,6},{6,7},{9,8},{8,9},{11,10... | collective-permute-start | bytes 147464 | tf_op jit(solution)/shard_map/ppermute | solution.py:643
  7.6 3.1 %collective-permute-start.2 = (f32[16,128]{1,0:T(8,128)S(1)}, f32[16,128]{1,0:T(8,128)S(1)}, u32[]{:S(2)}, u32[]{:S(2)}) collective-permute-start(f32[16,128]{1,0:T(8,128)S(1)} %get-tuple-element.36), channel_id=1, source_target_pairs={{2,1},{3,0},{0,3},{1,2},{6,5},{7,4},{4,7},{5,6},{10,9},{11,8},{8,1... | collective-permute-start | bytes 24584 | tf_op jit(solution)/shard_map/ppermute | solution.py:635
  10.9 10.4 %collective-permute-start.4 = (f32[272,128]{1,0:T(8,128)S(1)}, f32[272,128]{1,0:T(8,128)S(1)}, u32[]{:S(2)}, u32[]{:S(2)}) collective-permute-start(f32[272,128]{1,0:T(8,128)S(1)} %get-tuple-element.45), channel_id=1, source_target_pairs={{8,0},{12,4},{0,8},{4,12},{9,1},{13,5},{1,9},{5,13},{10,2},{14,6},... | collective-permute-start | bytes 417800 | tf_op jit(solution)/shard_map/ppermute | solution.py:643
  13.1 1.2 %collective-permute-start.5 = (f32[8,128]{1,0:T(8,128)S(1)}, f32[8,128]{1,0:T(8,128)S(1)}, u32[]{:S(2)}, u32[]{:S(2)}) collective-permute-start(f32[8,128]{1,0:T(8,128)S(1)} %get-tuple-element.48), channel_id=1, source_target_pairs={{1,0},{0,1},{3,2},{2,3},{5,4},{4,5},{7,6},{6,7},{9,8},{8,9},{11,10... | collective-permute-start | bytes 12296 | tf_op jit(solution)/shard_map/ppermute | solution.py:643
  14.3 9.4 %collective-permute-start.10 = (f32[496,128]{1,0:T(8,128)S(1)}, f32[496,128]{1,0:T(8,128)S(1)}, u32[]{:S(2)}, u32[]{:S(2)}) collective-permute-start(f32[496,128]{1,0:T(8,128)S(1)} %get-tuple-element.53), channel_id=1, source_target_pairs={{0,0},{8,4},{4,8},{12,12},{1,1},{9,5},{5,9},{13,13},{2,2},{10,6},{... | collective-permute-start | bytes 761864 | tf_op jit(solution)/shard_map/ppermute | solution.py:652
  15.0 11.4 %collective-permute-start.9 = (f32[496,128]{1,0:T(8,128)S(1)}, f32[496,128]{1,0:T(8,128)S(1)}, u32[]{:S(2)}, u32[]{:S(2)}) collective-permute-start(f32[496,128]{1,0:T(8,128)S(1)} %get-tuple-element.52), channel_id=1, source_target_pairs={{4,0},{0,4},{12,8},{8,12},{5,1},{1,5},{13,9},{9,13},{6,2},{2,6},{1... | collective-permute-start | bytes 761864 | tf_op jit(solution)/shard_map/ppermute | solution.py:652
  18.4 1.2 %collective-permute-start.6 = (f32[8,128]{1,0:T(8,128)S(1)}, f32[8,128]{1,0:T(8,128)S(1)}, u32[]{:S(2)}, u32[]{:S(2)}) collective-permute-start(f32[8,128]{1,0:T(8,128)S(1)} %get-tuple-element.49), channel_id=1, source_target_pairs={{1,0},{0,1},{3,2},{2,3},{5,4},{4,5},{7,6},{6,7},{9,8},{8,9},{11,10... | collective-permute-start | bytes 12296 | tf_op jit(solution)/shard_map/ppermute | solution.py:643
  21.3 9.1 %collective-permute-start.7 = (f32[344,128]{1,0:T(8,128)S(1)}, f32[344,128]{1,0:T(8,128)S(1)}, u32[]{:S(2)}, u32[]{:S(2)}) collective-permute-start(f32[344,128]{1,0:T(8,128)S(1)} %get-tuple-element.50), channel_id=1, source_target_pairs={{4,0},{0,4},{12,8},{8,12},{5,1},{1,5},{13,9},{9,13},{6,2},{2,6},{1... | collective-permute-start | bytes 528392 | tf_op jit(solution)/shard_map/ppermute | solution.py:652
  21.4 9.0 %collective-permute-start.8 = (f32[344,128]{1,0:T(8,128)S(1)}, f32[344,128]{1,0:T(8,128)S(1)}, u32[]{:S(2)}, u32[]{:S(2)}) collective-permute-start(f32[344,128]{1,0:T(8,128)S(1)} %get-tuple-element.51), channel_id=1, source_target_pairs={{0,0},{8,4},{4,8},{12,12},{1,1},{9,5},{5,9},{13,13},{2,2},{10,6},{... | collective-permute-start | bytes 528392 | tf_op jit(solution)/shard_map/ppermute | solution.py:652

commit v7 on v6

--- a/solution.py
+++ b/solution.py
@@ -150,7 +150,7 @@
 
 def merge_kernel(
     from_up, from_down, corner_up, corner_down, strip_ref, other_ref,
-    s_ref, t_ref, last_x_ref, last_y_ref, _a, _b,
+    s_ref, t_ref, last_x_ref, last_y_ref, _,
     wave_ref, adj_ref, token_ref,
 ):
     token_ref[...] = jnp.zeros((8, BZ), F32)
@@ -224,7 +224,7 @@
         target[tiles_end - 8 : tiles_end] = vx_before
 
 
-def adjoint_join_kernel(ql_ref, adj_ref, _, even_ref, odd_ref, token_ref):
+def adjoint_join_kernel(ql_ref, adj_ref, _a, _b, even_ref, odd_ref, token_ref):
     token_ref[...] = jnp.zeros((8, BZ), F32)
     planes_end, x_end, tiles_end = ADJ_OWN
     for target, first in zip((even_ref, odd_ref), pair_planes()):
@@ -342,14 +342,23 @@
     return pltpu.roll(v, 1, 0)
 
 
-def z_up(v, strip, x):
-    edge = pltpu.roll(strip, (BZ - 1 - (x * STRIP + MARGIN)) % BZ, 1)
+def z_up(v, edge):
     return jnp.where(lanes(v.shape) == BZ - 1, edge, pltpu.roll(v, BZ - 1, 1))
 
 
-def z_down(v, strip, x):
-    edge = pltpu.roll(strip, (BZ - (x * STRIP + MARGIN - 1)) % BZ, 1)
+def z_down(v, edge):
     return jnp.where(lanes(v.shape) == 0, edge, pltpu.roll(v, 1, 1))
+
+
+def cut_edges(values, flux_z, cut_up, cut_down):
+    place = lax.rem(lanes(values.shape), STRIP)
+    above = jnp.where(place == MARGIN, values * cut_up, 0.0)
+    below = jnp.where(place == MARGIN - 1, flux_z * cut_down, 0.0)
+    return pltpu.roll(above, BZ - 2, 1) + below
+
+
+def plane_edge(edges, x):
+    return pltpu.roll(edges, (BZ - (x * STRIP + MARGIN - 1)) % BZ, 1)
 
 
 def strip_flux(values, buoyancy):
@@ -437,7 +446,7 @@
     ql_ref, late_ref, even, odd, adj_hbm, ra_ref, rsa_ref, rb_ref, rsb_ref,
     table_ref,
     out_ref, hist_ref, coef_ref, coef_strip_ref,
-    field, w_sem,
+    q_ref, t_ref, u_ref, scale_ref, edge_ref, flux_ref, w_sem,
 ):
     w_copy = pltpu.make_async_copy(adj_hbm.at[pl.ds(1, 3)], out_ref.at[pl.ds(1, 3)], w_sem)
     w_copy.start()
@@ -463,6 +472,7 @@
     for x in range(EX):
         stiff, buoy, damp = coefficients(initial(2, x), table_ref)
         coef_ref[0, x], coef_ref[1, x], coef_ref[2, x] = stiff, buoy, damp
+        scale_ref[x] = stiff * damp
     own_strip = late_ref[ADJ_OWN[2] : ADJ_OWN[2] + EY]
     q_s, t_s, label_s = (
         whole_strip(own_strip, messages, ADJ_SIDE[2], slot, side) for slot in range(3)
@@ -480,51 +490,49 @@
         flux_s, spread = strip_flux(u_s, buoy_s)
         t_s = t_s + spread
         q_s = damp_s * q_s + t_s
-        edge_up = u_s * cut_up
-        edge_down = flux_s * cut_down
-
-        def injected(x):
-            r_ref, place = r_refs[k]
-            value = initial(0, x) if step == 1 else field[0, x]
-            value = value + r_ref[place, x - (EARLY_PLANES if k < 2 else LATE_PLANES)[0]]
-            return value, coef_ref[0, x] * coef_ref[2, x] * value
-
-        flux_below = None
-        q_now, u_now = injected(step - 1)
+        edges = cut_edges(u_s, flux_s, cut_up, cut_down)
+        r_ref, place = r_refs[k]
+        r_first = (EARLY_PLANES if k < 2 else LATE_PLANES)[0]
+
+        for x in range(step - 1, EX - step + 1):
+            q = (initial(0, x) if step == 1 else q_ref[x]) + r_ref[place, x - r_first]
+            q_ref[x] = q
+            u_ref[x] = scale_ref[x] * q
+            if step <= x < EX - step:
+                edge_ref[x] = plane_edge(edges, x)
+
         for x in range(step - 1, EX - step):
-            q_next, u_next = injected(x + 1)
-            buoyancy = coef_ref[1, x]
-            slope_x = u_next - u_now
-            flux_x = buoyancy * slope_x
+            u, buoyancy = u_ref[x], coef_ref[1, x]
+            slopes = [u_ref[x + 1] - u]
             if x >= step:
-                slope_y = y_up(u_now) - u_now
-                slope_z = z_up(u_now, edge_up, x) - u_now
-                flux_y = buoyancy * slope_y
-                flux_z = buoyancy * slope_z
-                spread = (flux_x - flux_below) + (flux_y - y_down(flux_y))
-                spread = spread + (flux_z - z_down(flux_z, edge_down, x))
-                damped = coef_ref[2, x] * q_now
-                if BX <= x < 2 * BX:
-                    place = x - BX
-                    hist_ref[k, 0, place] = damped[0:BY]
-                    for index, slope in enumerate((slope_x, slope_y, slope_z)):
-                        w = out_ref[1 + index, place] + slope[0:BY]
-                        out_ref[1 + index, place] = w
-                        hist_ref[k, 1 + index, place] = w
-                t = (initial(1, x) if step == 1 else field[1, x]) + spread
-                if step < STEPS:
-                    field[1, x] = t
-                    field[0, x] = damped + t
-                else:
-                    out_ref[0, x - BX] = (damped + t)[0:BY]
-            flux_below = flux_x
-            q_now, u_now = q_next, u_next
+                slopes += [y_up(u) - u, z_up(u, edge_ref[x]) - u]
+            for axis, slope in enumerate(slopes):
+                flux_ref[axis, x] = buoyancy * slope
+            if BX <= x < 2 * BX:
+                for axis, slope in enumerate(slopes):
+                    w = out_ref[1 + axis, x - BX] + slope[0:BY]
+                    out_ref[1 + axis, x - BX] = w
+                    hist_ref[k, 1 + axis, x - BX] = w
+
+        for x in range(step, EX - step):
+            flux_y, flux_z = flux_ref[1, x], flux_ref[2, x]
+            spread = (flux_ref[0, x] - flux_ref[0, x - 1]) + (flux_y - y_down(flux_y))
+            spread = spread + (flux_z - z_down(flux_z, edge_ref[x]))
+            damped = coef_ref[2, x] * q_ref[x]
+            t = (initial(1, x) if step == 1 else t_ref[x]) + spread
+            if BX <= x < 2 * BX:
+                hist_ref[k, 0, x - BX] = damped[0:BY]
+            if step < STEPS:
+                t_ref[x] = t
+                q_ref[x] = damped + t
+            else:
+                out_ref[0, x - BX] = (damped + t)[0:BY]
 
 
 def forward_kernel(
-    p_ref, late_ref, even, odd, coef_ref, coef_strip_ref, s_ref, ss_ref, hist_ref,
+    own_p_ref, late_ref, even, odd, coef_ref, coef_strip_ref, s_ref, ss_ref, hist_ref,
     grad_ref,
-    field,
+    p_ref, spread_ref, edge_ref, flux_ref,
 ):
     cut_up, cut_down = cut_flags()
     side = sides()
@@ -536,7 +544,7 @@
             ((messages, 0, 4), (messages, tiles, 3)),
             ((messages, PLANES, 3), (messages, tiles + 24, 2)),
         )[index]
-        own = ((p_ref, 0), (late_ref, 0))[index]
+        own = ((own_p_ref, 0), (late_ref, 0))[index]
         value = widened(own, (late_ref, own_tiles + 32 * index), x, layout, side)
         if index == 1:
             value = less_plane_below(value, x, late_ref, WAVE_OWN, messages, WAVE_SIDE, side)
@@ -551,47 +559,47 @@
 
     for step in range(1, STEPS + 1):
         k = step - 1
-        edge_up = p_s * cut_up
         flux_s, spread = strip_flux(p_s, buoy_s)
-        edge_down = flux_s * cut_down
+        edges = cut_edges(p_s, flux_s, cut_up, cut_down)
         if step < STEPS:
             s_s = s_s - spread
             p_s = damp_s * (p_s - stiff_s * s_s) + ss_ref[k]
 
-        def pressure(x):
-            return initial(0, x) if step == 1 else field[0, x]
-
-        flux_below = None
-        p_now = pressure(step - 1)
+        for x in range(step - 1, EX - step + 1):
+            if step == 1:
+                p_ref[x] = initial(0, x)
+            if step <= x < EX - step:
+                edge_ref[x] = plane_edge(edges, x)
+
         for x in range(step - 1, EX - step):
-            p_next = pressure(x + 1)
-            buoyancy = coef_ref[1, x]
-            slope_x = p_next - p_now
-            flux_x = buoyancy * slope_x
+            p, buoyancy = p_ref[x], coef_ref[1, x]
+            slopes = [p_ref[x + 1] - p]
             if x >= step:
-                slope_y = y_up(p_now) - p_now
-                slope_z = z_up(p_now, edge_up, x) - p_now
-                flux_y = buoyancy * slope_y
-                flux_z = buoyancy * slope_z
-                spread = (flux_x - flux_below) + (flux_y - y_down(flux_y))
-                spread = spread + (flux_z - z_down(flux_z, edge_down, x))
-                spread = (initial(1, x) if step == 1 else field[1, x]) - spread
-                if step < STEPS:
-                    field[1, x] = spread
-                    field[0, x] = (
-                        coef_ref[2, x] * (p_now - coef_ref[0, x] * spread)
-                        + s_ref[k, x - SOURCE_PLANES[0]]
-                    )
-                if BX <= x < 2 * BX:
-                    place = x - BX
-                    term = hist_ref[k, 0, place] * spread[0:BY]
-                    grad_ref[0, place] = -term if k == 0 else grad_ref[0, place] - term
-                    term = hist_ref[k, 1, place] * slope_x[0:BY]
-                    term = term + hist_ref[k, 2, place] * slope_y[0:BY]
-                    term = term + hist_ref[k, 3, place] * slope_z[0:BY]
-                    grad_ref[1, place] = -term if k == 0 else grad_ref[1, place] - term
-            flux_below = flux_x
-            p_now = p_next
+                slopes += [y_up(p) - p, z_up(p, edge_ref[x]) - p]
+            for axis, slope in enumerate(slopes):
+                flux_ref[axis, x] = buoyancy * slope
+            if BX <= x < 2 * BX:
+                place = x - BX
+                term = hist_ref[k, 1, place] * slopes[0][0:BY]
+                term = term + hist_ref[k, 2, place] * slopes[1][0:BY]
+                term = term + hist_ref[k, 3, place] * slopes[2][0:BY]
+                grad_ref[1, place] = -term if k == 0 else grad_ref[1, place] - term
+
+        for x in range(step, EX - step):
+            flux_y, flux_z = flux_ref[1, x], flux_ref[2, x]
+            spread = (flux_ref[0, x] - flux_ref[0, x - 1]) + (flux_y - y_down(flux_y))
+            spread = spread + (flux_z - z_down(flux_z, edge_ref[x]))
+            spread = (initial(1, x) if step == 1 else spread_ref[x]) - spread
+            if step < STEPS:
+                spread_ref[x] = spread
+                p_ref[x] = (
+                    coef_ref[2, x] * (p_ref[x] - coef_ref[0, x] * spread)
+                    + s_ref[k, x - SOURCE_PLANES[0]]
+                )
+            if BX <= x < 2 * BX:
+                place = x - BX
+                term = hist_ref[k, 0, place] * spread[0:BY]
+                grad_ref[0, place] = -term if k == 0 else grad_ref[0, place] - term
 
 
 def shape(*dims):
@@ -704,9 +712,9 @@
     late, adj_late, token = call(
         merge_kernel,
         [shape(WAVE_OWN[2] + EY, BZ), shape(ADJ_OWN[2] + EY, BZ), shape(8, BZ)],
-        [from_up, from_down, corner_up, corner_down, strips, other, s, t, last_x, last_y, rsb, p],
+        [from_up, from_down, corner_up, corner_down, strips, other, s, t, last_x, last_y, rsb],
         [],
-        "vvvvvvvvvvaa",
+        "vvvvvvvvvva",
     )
     late = rotated(late, "gx", half)
     token = rotated(token, "gz", 1)
@@ -722,9 +730,9 @@
     even, odd, second = call(
         adjoint_join_kernel,
         [shape(ADJ_SIDE[2] + EY + 2 * PLANES, BZ)] * 2 + [shape(8, BZ)],
-        [ql, adj_late, token],
+        [ql, adj_late, token, p],
         [],
-        "vva",
+        "vvaa",
     )
     even, odd = paired(even, False), paired(odd, True)
     second = rotated(second, "gz", 1)
@@ -754,7 +762,8 @@
             shape(3, EY, BZ),
         ],
         [ql, adj_late, even, odd, adjoint_end, ra, rsa, rb, rsb, table],
-        [pltpu.VMEM((2, EX, EY, BZ), F32), pltpu.SemaphoreType.DMA],
+        [pltpu.VMEM((EX, EY, BZ), F32)] * 5
+        + [pltpu.VMEM((3, EX, EY, BZ), F32), pltpu.SemaphoreType.DMA],
         "vvvvhvvvvv",
         3.9,
     )
@@ -762,7 +771,7 @@
         forward_kernel,
         [shape(2, BX, BY, BZ)],
         [p, late, wave_even, wave_odd, coef, coef_strip, src, src_strip, hist],
-        [pltpu.VMEM((2, EX, EY, BZ), F32)],
+        [pltpu.VMEM((EX, EY, BZ), F32)] * 3 + [pltpu.VMEM((3, EX, EY, BZ), F32)],
         "vvvvvvvvv",
         2.5,
     )

time: 33.2 us -> 30.2 us (0.910)
  Pallas kernels: 11 us -> 9.22 us
  waiting for transfers between devices: 7.99 us -> 7.32 us
  starting transfers between devices: 13.3 us -> 12.7 us
    pallas_call x9, Pallas kernels: 11 us -> 9.22 us  [call(): pl.pallas_call(kernel, out_shape=outs, in_specs=[pl.BlockSpec(memory_spac...]
    ppermute x2, waiting for transfers between devices: 1.18 us -> 0.01 us  [from_sides(): both = lax.ppermute(sends[0], axes, route(1) + route(-1))]
    ppermute x2, starting transfers between devices: 3.65 us -> 3.21 us  [from_sides(): both = lax.ppermute(sends[0], axes, route(1) + route(-1))]
    ppermute x5, waiting for transfers between devices: 4.08 us -> 4.48 us  [rotated(): lax.ppermute(array, axis, [((i + offset) % count, i) for i in range(count)])]
  transfers between devices with their start and end apart: 11 -> 11, of which waited for: 5 -> 6; matrix products, arithmetic and copies ran while one was open for 0% -> 0% of each run, Pallas kernels for 21% -> 20%
where the time goes in v7:
time: 30.2 us; the launch traced here: 30 us
  starting transfers between devices  12.7 us (42%)
  Pallas kernels  9.22 us (31%)
  waiting for transfers between devices  7.32 us (24%)
  between operations  0.74 us (2%)
    pallas_call x9, Pallas kernels, call(): pl.pallas_call(kernel, out_shape=outs, in_specs=[pl.BlockSpec(memory_spac...  9.22 us
    ppermute x4, starting transfers between devices, paired(): return lax.ppermute(array, 'gx', pairs)  5.06 us
    ppermute x5, waiting for transfers between devices, rotated(): lax.ppermute(array, axis, [((i + offset) % count, i) for i in range(count)])  4.48 us
    ppermute x5, starting transfers between devices, rotated(): lax.ppermute(array, axis, [((i + offset) % count, i) for i in range(count)])  4.46 us
    ppermute x2, starting transfers between devices, from_sides(): both = lax.ppermute(sends[0], axes, route(1) + route(-1))  3.21 us
    ppermute x4, waiting for transfers between devices, paired(): return lax.ppermute(array, 'gx', pairs)  2.84 us
  transfers between devices with their start and end apart: 11, of which 6 were waited for; matrix products, arithmetic and copies ran while one was open for 0% of the time, Pallas kernels for 20%

profile of v7, /device:TPU:0, one launch (start us, length us, event | category | flops | bytes accessed | tf_op | source)
XLA Modules:
  0.0 30.0 jit_solution(5860771276102868911)
XLA Ops:
  0.6 1.3 %shard_map.95 = (f32[128,128]{1,0:T(8,128)S(1)}, f32[256,128]{1,0:T(8,128)S(1)}, f32[128,128]{1,0:T(8,128)S(1)}, f32[128,128]{1,0:T(8,128)S(1)}, f32[64,128]{1,0...) custom-call(f32[4,4,32,128]{3,2,1,0:T(8,128)} %stored_hbm.1, ...), custom_call_target="tpu_custom_call" | custom-call | bytes 5166000 | tf_op jit(solution)/shard_map/pallas_call | solution.py:615
  2.0 3.0 %collective-permute-start.1 = (f32[160,128]{1,0:T(8,128)S(1)}, f32[160,128]{1,0:T(8,128)S(1)}, u32[]{:S(2)}, u32[]{:S(2)}) collective-permute-start(f32[160,128]{1,0:T(8,128)S(1)} %get-tuple-element.35), channel_id=1, source_target_pairs={{2,0},{0,2},{3,1},{1,3},{6,4},{4,6},{7,5},{5,7},{10,8},{8,10},{11,... | collective-permute-start | bytes 245768 | tf_op jit(solution)/shard_map/ppermute | solution.py:643
  5.0 0.0 collective-permute-start.3
  5.0 0.2 collective-permute-start.2
  5.2 3.0 %collective-permute-start = (f32[128,128]{1,0:T(8,128)S(1)}, f32[128,128]{1,0:T(8,128)S(1)}, u32[]{:S(2)}, u32[]{:S(2)}) collective-permute-start(f32[128,128]{1,0:T(8,128)S(1)} %get-tuple-element.34), channel_id=1, source_target_pairs={{8,0},{12,4},{0,8},{4,12},{9,1},{13,5},{1,9},{5,13},{10,2},{14,6},... | collective-permute-start | bytes 196616 | tf_op jit(solution)/shard_map/ppermute | solution.py:651
  8.2 1.2 %shard_map.96 = (f32[2,480,128]{2,1,0:T(8,128)S(1)}, f32[2,40,128]{2,1,0:T(8,128)S(1)}) custom-call(s32[3,1024]{1,0:T(4,128)S(1)} %get-tuple-element.42.receivers, f32[4,1024]{1,0:T(4,128)S(1)} %get-tuple-element.43.receiver_wave), custom_call_target="tpu_custom_call" | custom-call | bytes 4428000 | tf_op jit(solution)/shard_map/pallas_call | solution.py:615
  9.5 0.0 collective-permute-done.2.corner_up.corner_down
  9.5 0.0 collective-permute-done.3.other_ref
  9.5 0.0 collective-permute-done.1.from_up.from_down
  9.5 0.3 shard_map.97
  9.8 1.2 %collective-permute-start.4 = (f32[272,128]{1,0:T(8,128)S(1)}, f32[272,128]{1,0:T(8,128)S(1)}, u32[]{:S(2)}, u32[]{:S(2)}) collective-permute-start(f32[272,128]{1,0:T(8,128)S(1)} %get-tuple-element.45), channel_id=1, source_target_pairs={{8,0},{12,4},{0,8},{4,12},{9,1},{13,5},{1,9},{5,13},{10,2},{14,6},... | collective-permute-start | bytes 417800 | tf_op jit(solution)/shard_map/ppermute | solution.py:651
  11.0 0.2 collective-permute-start.5
  11.2 0.7 %collective-permute-done._b.p_ref.own_p_ref = f32[128,128]{1,0:T(8,128)S(1)} collective-permute-done((f32[128,128]{1,0:T(8,128)S(1)}, f32[128,128]{1,0:T(8,128)S(1)}, u32[]{:S(2)}, u32[]{:S(2)}) %collective-permute-start) | collective-permute-done | bytes 65568 | tf_op jit(solution)/shard_map/ppermute | solution.py:651
  11.9 0.3 collective-permute-done.5._a
  12.2 0.7 %collective-permute-start.10 = (f32[496,128]{1,0:T(8,128)S(1)}, f32[496,128]{1,0:T(8,128)S(1)}, u32[]{:S(2)}, u32[]{:S(2)}) collective-permute-start(f32[496,128]{1,0:T(8,128)S(1)} %get-tuple-element.53), channel_id=1, source_target_pairs={{0,0},{8,4},{4,8},{12,12},{1,1},{9,5},{5,9},{13,13},{2,2},{10,6},{... | collective-permute-start | bytes 761864 | tf_op jit(solution)/shard_map/ppermute | solution.py:660
  12.8 3.6 %collective-permute-start.9 = (f32[496,128]{1,0:T(8,128)S(1)}, f32[496,128]{1,0:T(8,128)S(1)}, u32[]{:S(2)}, u32[]{:S(2)}) collective-permute-start(f32[496,128]{1,0:T(8,128)S(1)} %get-tuple-element.52), channel_id=1, source_target_pairs={{4,0},{0,4},{12,8},{8,12},{5,1},{1,5},{13,9},{9,13},{6,2},{2,6},{1... | collective-permute-start | bytes 761864 | tf_op jit(solution)/shard_map/ppermute | solution.py:660
  16.5 0.0 collective-permute-start.6
  16.5 1.2 %collective-permute-done.6._ = f32[8,128]{1,0:T(8,128)S(1)} collective-permute-done((f32[8,128]{1,0:T(8,128)S(1)}, f32[8,128]{1,0:T(8,128)S(1)}, u32[]{:S(2)}, u32[]{:S(2)}) %collective-permute-start.6) | collective-permute-done | bytes 4128 | tf_op jit(solution)/shard_map/ppermute | solution.py:651
  17.6 2.4 %collective-permute-done.4.wave_ref.late_ref = f32[272,128]{1,0:T(8,128)S(1)} collective-permute-done((f32[272,128]{1,0:T(8,128)S(1)}, f32[272,128]{1,0:T(8,128)S(1)}, u32[]{:S(2)}, u32[]{:S(2)}) %collective-permute-start.4) | collective-permute-done | bytes 139296 | tf_op jit(solution)/shard_map/ppermute | solution.py:651
  20.1 0.1 collective-permute-start.7
  20.1 0.7 %collective-permute-start.8 = (f32[344,128]{1,0:T(8,128)S(1)}, f32[344,128]{1,0:T(8,128)S(1)}, u32[]{:S(2)}, u32[]{:S(2)}) collective-permute-start(f32[344,128]{1,0:T(8,128)S(1)} %get-tuple-element.51), channel_id=1, source_target_pairs={{0,0},{8,4},{4,8},{12,12},{1,1},{9,5},{5,9},{13,13},{2,2},{10,6},{... | collective-permute-start | bytes 528392 | tf_op jit(solution)/shard_map/ppermute | solution.py:660
  20.8 1.0 %shard_map.100 = (f32[2,320,128]{2,1,0:T(8,128)S(1)}, f32[2,40,128]{2,1,0:T(8,128)S(1)}) custom-call(s32[3,1024]{1,0:T(4,128)S(1)} %get-tuple-element.42.receivers, f32[4,1024]{1,0:T(4,128)S(1)} %get-tuple-element.43.receiver_wave, f32[304,128]{1,0:T(8,128)S(1)} %get-tuple-element.47.adj_ref._.late_ref), custom_call_target="tpu_custom_call" | custom-call | bytes 3690000 | tf_op jit(solution)/shard_map/pallas_call | solution.py:615
  21.8 0.5 %shard_map.102 = (f32[3,400,128]{2,1,0:T(8,128)S(1)}, f32[3,40,128]{2,1,0:T(8,128)S(1)}) custom-call(s32[3,64]{1,0:T(4,128)S(1)} %get-tuple-element.60.sources, f32[4,64]{1,0:T(4,128)S(1)} %get-tuple-element.61.source_wave, f32[8,128]{1,0:T(8,128)S(1)} %collective-permute-done.6._), custom_call_target="tpu_custom_call" | custom-call | bytes 1845000 | tf_op jit(solution)/shard_map/pallas_call | solution.py:615
  22.4 0.0 collective-permute-done.10.odd
  22.4 2.1 %collective-permute-done.9.even = f32[496,128]{1,0:T(8,128)S(1)} collective-permute-done((f32[496,128]{1,0:T(8,128)S(1)}, f32[496,128]{1,0:T(8,128)S(1)}, u32[]{:S(2)}, u32[]{:S(2)}) %collective-permute-start.9) | collective-permute-done | bytes 253984 | tf_op jit(solution)/shard_map/ppermute | solution.py:660
  24.5 3.0 %shard_map.101 = (f32[4,4,32,128]{3,2,1,0:T(8,128)}, f32[4,4,4,32,128]{4,3,2,1,0:T(8,128)S(1)}, f32[3,12,40,128]{3,2,1,0:T(8,128)S(1)}, f32[3,40,128]{2,1,0:T(8,128)S(1)}) custom-call(f32[256,128]{1,0:T(8,128)S(1)} %get-tuple-element.46.ql_ref, f32[304,128]{1,0:T(8,128)S(1)} %get-tuple-element.47.adj_ref._.late_ref, ...), custom_call_target="tpu_custom_call" | custom-call | bytes 14391000 | tf_op jit(solution)/shard_map/pallas_call | solution.py:615
  27.5 0.7 %collective-permute-done.7.even = f32[344,128]{1,0:T(8,128)S(1)} collective-permute-done((f32[344,128]{1,0:T(8,128)S(1)}, f32[344,128]{1,0:T(8,128)S(1)}, u32[]{:S(2)}, u32[]{:S(2)}) %collective-permute-start.7) | collective-permute-done | bytes 176160 | tf_op jit(solution)/shard_map/ppermute | solution.py:660
  28.2 0.0 collective-permute-done.8.odd
  28.2 1.8 %shard_map.103 = f32[2,4,32,128]{3,2,1,0:T(8,128)} custom-call(f32[128,128]{1,0:T(8,128)S(1)} %collective-permute-done._b.p_ref.own_p_ref, f32[272,128]{1,0:T(8,128)S(1)} %collective-permute-done.4.wave_ref.late_ref, f32[344,128]{1,0:T(8,128)S(1)} %collective-permute-done.7.even, f32[344,128]{1,0:T(8,128)S(1)} %collective-permute-done.8.odd, ...), custom_call_target="tpu_custom_call" | custom-call | bytes 9225000 | tf_op jit(solution)/shard_map/pallas_call | solution.py:615
  (2 shorter events, 0.1 us)
Async XLA Ops:
  2.0 7.5 %collective-permute-start.1 = (f32[160,128]{1,0:T(8,128)S(1)}, f32[160,128]{1,0:T(8,128)S(1)}, u32[]{:S(2)}, u32[]{:S(2)}) collective-permute-start(f32[160,128]{1,0:T(8,128)S(1)} %get-tuple-element.35), channel_id=1, source_target_pairs={{2,0},{0,2},{3,1},{1,3},{6,4},{4,6},{7,5},{5,7},{10,8},{8,10},{11,... | collective-permute-start | bytes 245768 | tf_op jit(solution)/shard_map/ppermute | solution.py:643
  5.0 4.5 %collective-permute-start.3 = (f32[96,128]{1,0:T(8,128)S(1)}, f32[96,128]{1,0:T(8,128)S(1)}, u32[]{:S(2)}, u32[]{:S(2)}) collective-permute-start(f32[96,128]{1,0:T(8,128)S(1)} %get-tuple-element.37.strip_ref), channel_id=1, source_target_pairs={{1,0},{0,1},{3,2},{2,3},{5,4},{4,5},{7,6},{6,7},{9,8},{8,9},{11,10... | collective-permute-start | bytes 147464 | tf_op jit(solution)/shard_map/ppermute | solution.py:651
  5.0 4.5 %collective-permute-start.2 = (f32[16,128]{1,0:T(8,128)S(1)}, f32[16,128]{1,0:T(8,128)S(1)}, u32[]{:S(2)}, u32[]{:S(2)}) collective-permute-start(f32[16,128]{1,0:T(8,128)S(1)} %get-tuple-element.36), channel_id=1, source_target_pairs={{2,1},{3,0},{0,3},{1,2},{6,5},{7,4},{4,7},{5,6},{10,9},{11,8},{8,1... | collective-permute-start | bytes 24584 | tf_op jit(solution)/shard_map/ppermute | solution.py:643
  5.2 6.7 %collective-permute-start = (f32[128,128]{1,0:T(8,128)S(1)}, f32[128,128]{1,0:T(8,128)S(1)}, u32[]{:S(2)}, u32[]{:S(2)}) collective-permute-start(f32[128,128]{1,0:T(8,128)S(1)} %get-tuple-element.34), channel_id=1, source_target_pairs={{8,0},{12,4},{0,8},{4,12},{9,1},{13,5},{1,9},{5,13},{10,2},{14,6},... | collective-permute-start | bytes 196616 | tf_op jit(solution)/shard_map/ppermute | solution.py:651
  9.8 10.3 %collective-permute-start.4 = (f32[272,128]{1,0:T(8,128)S(1)}, f32[272,128]{1,0:T(8,128)S(1)}, u32[]{:S(2)}, u32[]{:S(2)}) collective-permute-start(f32[272,128]{1,0:T(8,128)S(1)} %get-tuple-element.45), channel_id=1, source_target_pairs={{8,0},{12,4},{0,8},{4,12},{9,1},{13,5},{1,9},{5,13},{10,2},{14,6},... | collective-permute-start | bytes 417800 | tf_op jit(solution)/shard_map/ppermute | solution.py:651
  11.0 1.2 %collective-permute-start.5 = (f32[8,128]{1,0:T(8,128)S(1)}, f32[8,128]{1,0:T(8,128)S(1)}, u32[]{:S(2)}, u32[]{:S(2)}) collective-permute-start(f32[8,128]{1,0:T(8,128)S(1)} %get-tuple-element.48), channel_id=1, source_target_pairs={{1,0},{0,1},{3,2},{2,3},{5,4},{4,5},{7,6},{6,7},{9,8},{8,9},{11,10... | collective-permute-start | bytes 12296 | tf_op jit(solution)/shard_map/ppermute | solution.py:651
  12.2 10.2 %collective-permute-start.10 = (f32[496,128]{1,0:T(8,128)S(1)}, f32[496,128]{1,0:T(8,128)S(1)}, u32[]{:S(2)}, u32[]{:S(2)}) collective-permute-start(f32[496,128]{1,0:T(8,128)S(1)} %get-tuple-element.53), channel_id=1, source_target_pairs={{0,0},{8,4},{4,8},{12,12},{1,1},{9,5},{5,9},{13,13},{2,2},{10,6},{... | collective-permute-start | bytes 761864 | tf_op jit(solution)/shard_map/ppermute | solution.py:660
  12.8 11.7 %collective-permute-start.9 = (f32[496,128]{1,0:T(8,128)S(1)}, f32[496,128]{1,0:T(8,128)S(1)}, u32[]{:S(2)}, u32[]{:S(2)}) collective-permute-start(f32[496,128]{1,0:T(8,128)S(1)} %get-tuple-element.52), channel_id=1, source_target_pairs={{4,0},{0,4},{12,8},{8,12},{5,1},{1,5},{13,9},{9,13},{6,2},{2,6},{1... | collective-permute-start | bytes 761864 | tf_op jit(solution)/shard_map/ppermute | solution.py:660
  16.5 1.2 %collective-permute-start.6 = (f32[8,128]{1,0:T(8,128)S(1)}, f32[8,128]{1,0:T(8,128)S(1)}, u32[]{:S(2)}, u32[]{:S(2)}) collective-permute-start(f32[8,128]{1,0:T(8,128)S(1)} %get-tuple-element.49), channel_id=1, source_target_pairs={{1,0},{0,1},{3,2},{2,3},{5,4},{4,5},{7,6},{6,7},{9,8},{8,9},{11,10... | collective-permute-start | bytes 12296 | tf_op jit(solution)/shard_map/ppermute | solution.py:651
  20.1 8.2 %collective-permute-start.7 = (f32[344,128]{1,0:T(8,128)S(1)}, f32[344,128]{1,0:T(8,128)S(1)}, u32[]{:S(2)}, u32[]{:S(2)}) collective-permute-start(f32[344,128]{1,0:T(8,128)S(1)} %get-tuple-element.50), channel_id=1, source_target_pairs={{4,0},{0,4},{12,8},{8,12},{5,1},{1,5},{13,9},{9,13},{6,2},{2,6},{1... | collective-permute-start | bytes 528392 | tf_op jit(solution)/shard_map/ppermute | solution.py:660
  20.1 8.1 %collective-permute-start.8 = (f32[344,128]{1,0:T(8,128)S(1)}, f32[344,128]{1,0:T(8,128)S(1)}, u32[]{:S(2)}, u32[]{:S(2)}) collective-permute-start(f32[344,128]{1,0:T(8,128)S(1)} %get-tuple-element.51), channel_id=1, source_target_pairs={{0,0},{8,4},{4,8},{12,12},{1,1},{9,5},{5,9},{13,13},{2,2},{10,6},{... | collective-permute-start | bytes 528392 | tf_op jit(solution)/shard_map/ppermute | solution.py:660

commit v8 on v7

--- a/solution.py
+++ b/solution.py
@@ -14,7 +14,9 @@
 BF16 = jnp.bfloat16
 VMEM_LIMIT = 16 * 1024 * 1024
 PLANES = BX * BY
-WAVE_OWN = (PLANES, PLANES + BY, PLANES + BY + 9 * 8)
+WAVE_OWN = (0, BY, BY + 9 * 8)
+WAVE_FIX = WAVE_OWN[2] + EY
+FIX_LANE = 3 * BX * STRIP
 ADJ_OWN = (PLANES, PLANES + BY, PLANES + BY + 13 * 8)
 WAVE_SIDE = (PLANES + 3 * BY, PLANES + 4 * BY, PLANES + 4 * BY + 6 * 8)
 ADJ_SIDE = (3 * BY, 4 * BY, 4 * BY + 9 * 8)
@@ -58,7 +60,7 @@
 
 def load_kernel(
     stored_hbm, adj_hbm, lab_hbm, tissue_hbm, rc_hbm, rw_hbm, sc_hbm, sw_hbm,
-    p_ref, ql_ref, s_ref, t_ref, last_x_ref, last_y_ref, strip_ref, table_ref,
+    wave_ref, ql_ref, t_ref, last_x_ref, last_y_ref, strip_ref, table_ref,
     rc_ref, rw_ref, sc_ref, sw_ref, *rest,
 ):
     *sends, stored, adj, lab, tissue, sem = rest
@@ -92,7 +94,7 @@
         plane = slice(x * BY, x * BY + BY)
         fields = [stored[index, x] for index in range(4)] + [adj[0, x]]
         fields += [buoyancy * adj[index, x] for index in range(1, 4)] + [labels]
-        p_ref[plane] = fields[0]
+        wave_ref[plane] = fields[0]
         ql_ref[plane] = fields[4]
         ql_ref[PLANES + x * BY : PLANES + x * BY + BY] = labels
         for index, block in enumerate(fields):
@@ -104,12 +106,12 @@
             strips[group] = jnp.where(
                 (lane >= first) & (lane < first + MARGIN), rolled, strips[group]
             )
-        for kind, target in enumerate((s_ref, t_ref)):
+        for kind, (target, base) in enumerate(((wave_ref, PLANES), (t_ref, 0))):
             vx, vy, vz = fields[4 * kind + 1 : 4 * kind + 4]
             spread = vx if x == 0 else vx - previous[kind]
             spread = spread + (vy - jnp.where(row == 0, 0.0, pltpu.roll(vy, 1, 0)))
             spread = spread + (vz - jnp.where(lane == 0, 0.0, pltpu.roll(vz, 1, 1)))
-            target[plane] = spread
+            target[base + x * BY : base + x * BY + BY] = spread
             previous[kind] = vx
             index = (kind * BX + x) * 8
             last_y_ref[index : index + 8] = vy[BY - 8 : BY]
@@ -150,7 +152,7 @@
 
 def merge_kernel(
     from_up, from_down, corner_up, corner_down, strip_ref, other_ref,
-    s_ref, t_ref, last_x_ref, last_y_ref, _,
+    t_ref, last_x_ref, last_y_ref, _,
     wave_ref, adj_ref, token_ref,
 ):
     token_ref[...] = jnp.zeros((8, BZ), F32)
@@ -181,7 +183,9 @@
         return jnp.where(strip_lane < BX * STRIP, moved, 0.0)
 
     last_lanes = (BX - 1) * STRIP
-    for kind, (source, target) in enumerate(((s_ref, wave_ref), (t_ref, adj_ref))):
+    fix_row = jnp.zeros((8, BZ), F32)
+    fix_lane = jnp.zeros((BY, BZ), F32)
+    for kind, target in enumerate((wave_ref, adj_ref)):
         first = 4 * kind
         planes_end, x_end, tiles_end = (WAVE_OWN, ADJ_OWN)[kind]
         vx, vy, vz = (strip_field(first + 1 + axis) for axis in range(3))
@@ -195,7 +199,6 @@
             last_slot = 3
         last = jnp.where(strip_lane >= last_lanes, vx, 0.0)
         strip = strip + pltpu.roll(last, last_slot * BX * STRIP - last_lanes, 1)
-        target[tiles_end : tiles_end + EY] = strip
         target[planes_end:x_end] = last_x_ref[kind * BY : kind * BY + BY]
 
         vx_before = None
@@ -212,16 +215,27 @@
             spread = vx_t if x == 0 else vx_t - vx_before
             spread = (spread + (vy_t - y_before)) + (vz_t - z_before)
             vx_before = vx_t
-            block = source[x * BY : x * BY + BY]
-            block = block - jnp.where(row == 0, vy_t[7:8], 0.0)
-            block = block - jnp.where(lane == 0, below_z[0:BY], 0.0)
-            target[x * BY : x * BY + BY] = block
+            if kind == 0:
+                fix_row = jnp.where(tile_row == x, vy_t[7:8], fix_row)
+                moved = pltpu.roll(below_z[0:BY], FIX_LANE + x, 1)
+                fix_lane = jnp.where(lane == FIX_LANE + x, moved, fix_lane)
+            else:
+                block = t_ref[x * BY : x * BY + BY]
+                block = block - jnp.where(row == 0, vy_t[7:8], 0.0)
+                block = block - jnp.where(lane == 0, below_z[0:BY], 0.0)
+                target[x * BY : x * BY + BY] = block
             base = x_end + x * 8
             target[base : base + 8] = halo(from_up, from_down, first * BX + x)
             target[base + 32 : base + 40] = spread
             if kind == 1:
                 target[base + 64 : base + 72] = halo(from_up, from_down, 8 * BX + x)
         target[tiles_end - 8 : tiles_end] = vx_before
+        if kind == 0:
+            target[tiles_end : tiles_end + BY] = strip[0:BY] + fix_lane
+            target[tiles_end + BY : tiles_end + EY] = strip[BY:EY]
+            target[WAVE_FIX : WAVE_FIX + 8] = fix_row
+        else:
+            target[tiles_end : tiles_end + EY] = strip
 
 
 def adjoint_join_kernel(ql_ref, adj_ref, _a, _b, even_ref, odd_ref, token_ref):
@@ -237,15 +251,23 @@
         copy_rows(target, base, ql_ref, 0, 2 * PLANES)
 
 
-def join_kernel(p_ref, wave_ref, _, even_ref, odd_ref):
+def join_kernel(wave_ref, late_ref, _, s_ref, even_ref, odd_ref):
     planes_end, x_end, tiles_end = WAVE_OWN
+    row, lane = rows((BY, BZ)), lanes((BY, BZ))
+    fix_lane = late_ref[tiles_end : tiles_end + BY]
+    for x in range(BX):
+        block = wave_ref[PLANES + x * BY : PLANES + x * BY + BY]
+        fix_row = late_ref[WAVE_FIX + x : WAVE_FIX + x + 1]
+        block = block - jnp.where(row == 0, fix_row, 0.0)
+        block = block - jnp.where(lane == 0, pltpu.roll(fix_lane, BZ - FIX_LANE - x, 1), 0.0)
+        s_ref[x * BY : x * BY + BY] = block
     for target, first in zip((even_ref, odd_ref), pair_planes()):
-        base = copy_rows(target, 0, p_ref, 0, PLANES)
-        base = copy_rows(target, base, wave_ref, first * BY, 3 * BY)
-        base = copy_rows(target, base, wave_ref, planes_end, BY)
-        base = copy_rows(target, base, wave_ref, x_end + first * 8, 24)
-        base = copy_rows(target, base, wave_ref, x_end + 32 + first * 16, 16)
-        copy_rows(target, base, wave_ref, tiles_end - 8, 8 + EY)
+        base = copy_rows(target, 0, wave_ref, 0, PLANES)
+        base = copy_rows(target, base, s_ref, first * BY, 3 * BY)
+        base = copy_rows(target, base, late_ref, planes_end, BY)
+        base = copy_rows(target, base, late_ref, x_end + first * 8, 24)
+        base = copy_rows(target, base, late_ref, x_end + 32 + first * 16, 16)
+        copy_rows(target, base, late_ref, tiles_end - 8, 8 + EY)
 
 
 def split(values):
@@ -530,7 +552,7 @@
 
 
 def forward_kernel(
-    own_p_ref, late_ref, even, odd, coef_ref, coef_strip_ref, s_ref, ss_ref, hist_ref,
+    wave_ref, own_s_ref, late_ref, even, odd, coef_ref, coef_strip_ref, s_ref, ss_ref, hist_ref,
     grad_ref,
     p_ref, spread_ref, edge_ref, flux_ref,
 ):
@@ -544,7 +566,7 @@
             ((messages, 0, 4), (messages, tiles, 3)),
             ((messages, PLANES, 3), (messages, tiles + 24, 2)),
         )[index]
-        own = ((own_p_ref, 0), (late_ref, 0))[index]
+        own = ((wave_ref, 0), (own_s_ref, 0))[index]
         value = widened(own, (late_ref, own_tiles + 32 * index), x, layout, side)
         if index == 1:
             value = less_plane_below(value, x, late_ref, WAVE_OWN, messages, WAVE_SIDE, side)
@@ -670,12 +692,11 @@
         receiver_cells.T, receiver_wave, source_cells.T, source_wave,
     ]
     ways = 1 if lax.axis_size("gy") == 2 else 2
-    p, ql, s, t, last_x, last_y, strips, table, receivers, receiver_wave, sources, source_wave, *sends = call(
+    wave, ql, t, last_x, last_y, strips, table, receivers, receiver_wave, sources, source_wave, *sends = call(
         load_kernel,
         [
-            shape(PLANES, BZ),
             shape(2 * PLANES, BZ),
-            shape(PLANES, BZ),
+            shape(2 * PLANES, BZ),
             shape(PLANES, BZ),
             shape(2 * BY, BZ),
             shape(2 * BX * 8, BZ),
@@ -699,7 +720,7 @@
     from_up, from_down = from_sides(sends[:ways], "gy")
     other = rotated(strips, "gz", 1)
     corner_up, corner_down = from_sides(sends[ways:], ("gy", "gz"))
-    p = rotated(p, "gx", half)
+    wave = rotated(wave, "gx", half)
     rb, rsb = call(
         late_kernel,
         [shape(2, EX * EY, BZ), shape(2, EY, BZ)],
@@ -711,10 +732,10 @@
     early_planes, source_planes = (last - first for first, last in (EARLY_PLANES, SOURCE_PLANES))
     late, adj_late, token = call(
         merge_kernel,
-        [shape(WAVE_OWN[2] + EY, BZ), shape(ADJ_OWN[2] + EY, BZ), shape(8, BZ)],
-        [from_up, from_down, corner_up, corner_down, strips, other, s, t, last_x, last_y, rsb],
+        [shape(WAVE_FIX + 8, BZ), shape(ADJ_OWN[2] + EY, BZ), shape(8, BZ)],
+        [from_up, from_down, corner_up, corner_down, strips, other, t, last_x, last_y, rsb],
         [],
-        "vvvvvvvvvva",
+        "vvvvvvvvva",
     )
     late = rotated(late, "gx", half)
     token = rotated(token, "gz", 1)
@@ -730,7 +751,7 @@
     even, odd, second = call(
         adjoint_join_kernel,
         [shape(ADJ_SIDE[2] + EY + 2 * PLANES, BZ)] * 2 + [shape(8, BZ)],
-        [ql, adj_late, token, p],
+        [ql, adj_late, token, wave],
         [],
         "vvaa",
     )
@@ -745,10 +766,10 @@
         0.5,
     )
     src = src.reshape(STEPS - 1, source_planes, EY, BZ)
-    wave_even, wave_odd = call(
+    own_s, wave_even, wave_odd = call(
         join_kernel,
-        [shape(WAVE_SIDE[2] + EY, BZ)] * 2,
-        [p, late, second],
+        [shape(PLANES, BZ)] + [shape(WAVE_SIDE[2] + EY, BZ)] * 2,
+        [wave, late, second],
         [],
         "vva",
     )
@@ -770,9 +791,9 @@
     (gradient,) = call(
         forward_kernel,
         [shape(2, BX, BY, BZ)],
-        [p, late, wave_even, wave_odd, coef, coef_strip, src, src_strip, hist],
+        [wave, own_s, late, wave_even, wave_odd, coef, coef_strip, src, src_strip, hist],
         [pltpu.VMEM((EX, EY, BZ), F32)] * 3 + [pltpu.VMEM((3, EX, EY, BZ), F32)],
-        "vvvvvvvvv",
+        "vvvvvvvvvv",
         2.5,
     )
     return gradient, adjoint_start

time: 30.2 us -> 37.2 us (1.23)
  the two profiles are of different devices: /device:TPU:0 before, /device:TPU:8 now
where the time goes in v8:
time: 37.2 us; the launch traced here: 37 us
  starting transfers between devices  16.5 us (44%)
  waiting for transfers between devices  10.5 us (28%)
  Pallas kernels  9.3 us (25%)
  between operations  0.74 us (2%)
    ppermute x4, starting transfers between devices, paired(): return lax.ppermute(array, 'gx', pairs)  11 us
    pallas_call x9, Pallas kernels, call(): pl.pallas_call(kernel, out_shape=outs, in_specs=[pl.BlockSpec(memory_spac...  9.3 us
    ppermute x5, waiting for transfers between devices, rotated(): lax.ppermute(array, axis, [((i + offset) % count, i) for i in range(count)])  9.27 us
    ppermute x5, starting transfers between devices, rotated(): lax.ppermute(array, axis, [((i + offset) % count, i) for i in range(count)])  3.37 us
    ppermute x2, starting transfers between devices, from_sides(): both = lax.ppermute(sends[0], axes, route(1) + route(-1))  2.14 us
    ppermute x2, waiting for transfers between devices, from_sides(): both = lax.ppermute(sends[0], axes, route(1) + route(-1))  1.17 us
  transfers between devices with their start and end apart: 11, of which 4 were waited for; matrix products, arithmetic and copies ran while one was open for 0% of the time, Pallas kernels for 17%

profile of v8, /device:TPU:8, one launch (start us, length us, event | category | flops | bytes accessed | tf_op | source)
XLA Modules:
  0.0 37.0 jit_solution(10478354201349163303)
XLA Ops:
  0.6 1.3 %shard_map.95 = (f32[256,128]{1,0:T(8,128)S(1)}, f32[256,128]{1,0:T(8,128)S(1)}, f32[128,128]{1,0:T(8,128)S(1)}, f32[64,128]{1,0:T(8,128)S(1)}, f32[64,128]{1,0:...) custom-call(f32[4,4,32,128]{3,2,1,0:T(8,128)} %stored_hbm.1, ...), custom_call_target="tpu_custom_call" | custom-call | bytes 5166000 | tf_op jit(solution)/shard_map/pallas_call | solution.py:637
  2.0 2.7 %collective-permute-start = (f32[256,128]{1,0:T(8,128)S(1)}, f32[256,128]{1,0:T(8,128)S(1)}, u32[]{:S(2)}, u32[]{:S(2)}) collective-permute-start(f32[256,128]{1,0:T(8,128)S(1)} %get-tuple-element.34), channel_id=1, source_target_pairs={{8,0},{12,4},{0,8},{4,12},{9,1},{13,5},{1,9},{5,13},{10,2},{14,6},... | collective-permute-start | bytes 393224 | tf_op jit(solution)/shard_map/ppermute | solution.py:673
  4.6 1.5 %collective-permute-start.1 = (f32[160,128]{1,0:T(8,128)S(1)}, f32[160,128]{1,0:T(8,128)S(1)}, u32[]{:S(2)}, u32[]{:S(2)}) collective-permute-start(f32[160,128]{1,0:T(8,128)S(1)} %get-tuple-element.35), channel_id=1, source_target_pairs={{2,0},{0,2},{3,1},{1,3},{6,4},{4,6},{7,5},{5,7},{10,8},{8,10},{11,... | collective-permute-start | bytes 245768 | tf_op jit(solution)/shard_map/ppermute | solution.py:665
  6.1 0.0 collective-permute-start.3
  6.1 0.6 %collective-permute-start.2 = (f32[16,128]{1,0:T(8,128)S(1)}, f32[16,128]{1,0:T(8,128)S(1)}, u32[]{:S(2)}, u32[]{:S(2)}) collective-permute-start(f32[16,128]{1,0:T(8,128)S(1)} %get-tuple-element.36), channel_id=1, source_target_pairs={{2,1},{3,0},{0,3},{1,2},{6,5},{7,4},{4,7},{5,6},{10,9},{11,8},{8,1... | collective-permute-start | bytes 24584 | tf_op jit(solution)/shard_map/ppermute | solution.py:665
  6.8 1.2 %shard_map.96 = (f32[2,480,128]{2,1,0:T(8,128)S(1)}, f32[2,40,128]{2,1,0:T(8,128)S(1)}) custom-call(s32[3,1024]{1,0:T(4,128)S(1)} %get-tuple-element.41.receivers, f32[4,1024]{1,0:T(4,128)S(1)} %get-tuple-element.42.receiver_wave), custom_call_target="tpu_custom_call" | custom-call | bytes 4428000 | tf_op jit(solution)/shard_map/pallas_call | solution.py:637
  8.0 1.2 %collective-permute-done.2.corner_up.corner_down = f32[16,128]{1,0:T(8,128)S(1)} collective-permute-done((f32[16,128]{1,0:T(8,128)S(1)}, f32[16,128]{1,0:T(8,128)S(1)}, u32[]{:S(2)}, u32[]{:S(2)}) %collective-permute-start.2) | collective-permute-done | bytes 8224 | tf_op jit(solution)/shard_map/ppermute | solution.py:665
  9.2 0.0 collective-permute-done.3.other_ref
  9.2 0.0 collective-permute-done.1.from_up.from_down
  9.2 0.3 shard_map.97
  9.5 0.6 %collective-permute-start.5 = (f32[8,128]{1,0:T(8,128)S(1)}, f32[8,128]{1,0:T(8,128)S(1)}, u32[]{:S(2)}, u32[]{:S(2)}) collective-permute-start(f32[8,128]{1,0:T(8,128)S(1)} %get-tuple-element.47), channel_id=1, source_target_pairs={{1,0},{0,1},{3,2},{2,3},{5,4},{4,5},{7,6},{6,7},{9,8},{8,9},{11,10... | collective-permute-start | bytes 12296 | tf_op jit(solution)/shard_map/ppermute | solution.py:673
  10.0 0.8 %collective-permute-done.5._a = f32[8,128]{1,0:T(8,128)S(1)} collective-permute-done((f32[8,128]{1,0:T(8,128)S(1)}, f32[8,128]{1,0:T(8,128)S(1)}, u32[]{:S(2)}, u32[]{:S(2)}) %collective-permute-start.5) | collective-permute-done | bytes 4128 | tf_op jit(solution)/shard_map/ppermute | solution.py:673
  10.9 0.0 collective-permute-done._b.wave_ref
  10.9 0.8 %collective-permute-start.9 = (f32[496,128]{1,0:T(8,128)S(1)}, f32[496,128]{1,0:T(8,128)S(1)}, u32[]{:S(2)}, u32[]{:S(2)}) collective-permute-start(f32[496,128]{1,0:T(8,128)S(1)} %get-tuple-element.52), channel_id=1, source_target_pairs={{4,0},{0,4},{12,8},{8,12},{5,1},{1,5},{13,9},{9,13},{6,2},{2,6},{1... | collective-permute-start | bytes 761864 | tf_op jit(solution)/shard_map/ppermute | solution.py:682
  11.7 4.3 %collective-permute-start.10 = (f32[496,128]{1,0:T(8,128)S(1)}, f32[496,128]{1,0:T(8,128)S(1)}, u32[]{:S(2)}, u32[]{:S(2)}) collective-permute-start(f32[496,128]{1,0:T(8,128)S(1)} %get-tuple-element.53), channel_id=1, source_target_pairs={{0,0},{8,4},{4,8},{12,12},{1,1},{9,5},{5,9},{13,13},{2,2},{10,6},{... | collective-permute-start | bytes 761864 | tf_op jit(solution)/shard_map/ppermute | solution.py:682
  16.0 0.1 collective-permute-start.4
  16.1 0.1 collective-permute-start.6
  16.2 1.2 %collective-permute-done.6._ = f32[8,128]{1,0:T(8,128)S(1)} collective-permute-done((f32[8,128]{1,0:T(8,128)S(1)}, f32[8,128]{1,0:T(8,128)S(1)}, u32[]{:S(2)}, u32[]{:S(2)}) %collective-permute-start.6) | collective-permute-done | bytes 4128 | tf_op jit(solution)/shard_map/ppermute | solution.py:673
  17.3 7.3 %collective-permute-done.4.late_ref = f32[152,128]{1,0:T(8,128)S(1)} collective-permute-done((f32[152,128]{1,0:T(8,128)S(1)}, f32[152,128]{1,0:T(8,128)S(1)}, u32[]{:S(2)}, u32[]{:S(2)}) %collective-permute-start.4) | collective-permute-done | bytes 77856 | tf_op jit(solution)/shard_map/ppermute | solution.py:673
  24.6 0.1 shard_map.99
  24.7 2.3 %collective-permute-start.7 = (f32[344,128]{1,0:T(8,128)S(1)}, f32[344,128]{1,0:T(8,128)S(1)}, u32[]{:S(2)}, u32[]{:S(2)}) collective-permute-start(f32[344,128]{1,0:T(8,128)S(1)} %get-tuple-element.50), channel_id=1, source_target_pairs={{4,0},{0,4},{12,8},{8,12},{5,1},{1,5},{13,9},{9,13},{6,2},{2,6},{1... | collective-permute-start | bytes 528392 | tf_op jit(solution)/shard_map/ppermute | solution.py:682
  27.0 3.6 %collective-permute-start.8 = (f32[344,128]{1,0:T(8,128)S(1)}, f32[344,128]{1,0:T(8,128)S(1)}, u32[]{:S(2)}, u32[]{:S(2)}) collective-permute-start(f32[344,128]{1,0:T(8,128)S(1)} %get-tuple-element.51), channel_id=1, source_target_pairs={{0,0},{8,4},{4,8},{12,12},{1,1},{9,5},{5,9},{13,13},{2,2},{10,6},{... | collective-permute-start | bytes 528392 | tf_op jit(solution)/shard_map/ppermute | solution.py:682
  30.6 1.0 %shard_map.100 = (f32[2,320,128]{2,1,0:T(8,128)S(1)}, f32[2,40,128]{2,1,0:T(8,128)S(1)}) custom-call(s32[3,1024]{1,0:T(4,128)S(1)} %get-tuple-element.41.receivers, f32[4,1024]{1,0:T(4,128)S(1)} %get-tuple-element.42.receiver_wave, f32[304,128]{1,0:T(8,128)S(1)} %get-tuple-element.46.adj_ref._.late_ref), custom_call_target="tpu_custom_call" | custom-call | bytes 3690000 | tf_op jit(solution)/shard_map/pallas_call | solution.py:637
  31.7 0.6 %shard_map.102 = (f32[3,400,128]{2,1,0:T(8,128)S(1)}, f32[3,40,128]{2,1,0:T(8,128)S(1)}) custom-call(s32[3,64]{1,0:T(4,128)S(1)} %get-tuple-element.60.sources, f32[4,64]{1,0:T(4,128)S(1)} %get-tuple-element.61.source_wave, f32[8,128]{1,0:T(8,128)S(1)} %collective-permute-done.6._), custom_call_target="tpu_custom_call" | custom-call | bytes 1845000 | tf_op jit(solution)/shard_map/pallas_call | solution.py:637
  32.2 0.0 collective-permute-done.9.even
  32.2 0.0 collective-permute-done.10.odd
  32.2 3.0 %shard_map.101 = (f32[4,4,32,128]{3,2,1,0:T(8,128)}, f32[4,4,4,32,128]{4,3,2,1,0:T(8,128)S(1)}, f32[3,12,40,128]{3,2,1,0:T(8,128)S(1)}, f32[3,40,128]{2,1,0:T(8,128)S(1)}) custom-call(f32[256,128]{1,0:T(8,128)S(1)} %get-tuple-element.45.ql_ref, f32[304,128]{1,0:T(8,128)S(1)} %get-tuple-element.46.adj_ref._.late_ref, ...), custom_call_target="tpu_custom_call" | custom-call | bytes 14391000 | tf_op jit(solution)/shard_map/pallas_call | solution.py:637
  35.2 0.0 collective-permute-done.7.even
  35.2 0.0 collective-permute-done.8.odd
  35.2 1.8 %shard_map.103 = f32[2,4,32,128]{3,2,1,0:T(8,128)} custom-call(f32[256,128]{1,0:T(8,128)S(1)} %collective-permute-done._b.wave_ref, f32[128,128]{1,0:T(8,128)S(1)} %get-tuple-element.49.own_s_ref, f32[152,128]{1,0:T(8,128)S(1)} %collective-permute-done.4.late_ref, f32[344,128]{1,0:T(8,128)S(1)} %collective-permute-done.7.even, ...), custom_call_target="tpu_custom_call" | custom-call | bytes 9225000 | tf_op jit(solution)/shard_map/pallas_call | solution.py:637
  (1 shorter events, 0.0 us)
Async XLA Ops:
  2.0 8.9 %collective-permute-start = (f32[256,128]{1,0:T(8,128)S(1)}, f32[256,128]{1,0:T(8,128)S(1)}, u32[]{:S(2)}, u32[]{:S(2)}) collective-permute-start(f32[256,128]{1,0:T(8,128)S(1)} %get-tuple-element.34), channel_id=1, source_target_pairs={{8,0},{12,4},{0,8},{4,12},{9,1},{13,5},{1,9},{5,13},{10,2},{14,6},... | collective-permute-start | bytes 393224 | tf_op jit(solution)/shard_map/ppermute | solution.py:673
  4.6 4.6 %collective-permute-start.1 = (f32[160,128]{1,0:T(8,128)S(1)}, f32[160,128]{1,0:T(8,128)S(1)}, u32[]{:S(2)}, u32[]{:S(2)}) collective-permute-start(f32[160,128]{1,0:T(8,128)S(1)} %get-tuple-element.35), channel_id=1, source_target_pairs={{2,0},{0,2},{3,1},{1,3},{6,4},{4,6},{7,5},{5,7},{10,8},{8,10},{11,... | collective-permute-start | bytes 245768 | tf_op jit(solution)/shard_map/ppermute | solution.py:665
  6.1 3.1 %collective-permute-start.3 = (f32[96,128]{1,0:T(8,128)S(1)}, f32[96,128]{1,0:T(8,128)S(1)}, u32[]{:S(2)}, u32[]{:S(2)}) collective-permute-start(f32[96,128]{1,0:T(8,128)S(1)} %get-tuple-element.37.strip_ref), channel_id=1, source_target_pairs={{1,0},{0,1},{3,2},{2,3},{5,4},{4,5},{7,6},{6,7},{9,8},{8,9},{11,10... | collective-permute-start | bytes 147464 | tf_op jit(solution)/shard_map/ppermute | solution.py:673
  6.1 3.1 %collective-permute-start.2 = (f32[16,128]{1,0:T(8,128)S(1)}, f32[16,128]{1,0:T(8,128)S(1)}, u32[]{:S(2)}, u32[]{:S(2)}) collective-permute-start(f32[16,128]{1,0:T(8,128)S(1)} %get-tuple-element.36), channel_id=1, source_target_pairs={{2,1},{3,0},{0,3},{1,2},{6,5},{7,4},{4,7},{5,6},{10,9},{11,8},{8,1... | collective-permute-start | bytes 24584 | tf_op jit(solution)/shard_map/ppermute | solution.py:665
  9.5 1.4 %collective-permute-start.5 = (f32[8,128]{1,0:T(8,128)S(1)}, f32[8,128]{1,0:T(8,128)S(1)}, u32[]{:S(2)}, u32[]{:S(2)}) collective-permute-start(f32[8,128]{1,0:T(8,128)S(1)} %get-tuple-element.47), channel_id=1, source_target_pairs={{1,0},{0,1},{3,2},{2,3},{5,4},{4,5},{7,6},{6,7},{9,8},{8,9},{11,10... | collective-permute-start | bytes 12296 | tf_op jit(solution)/shard_map/ppermute | solution.py:673
  10.9 21.3 %collective-permute-start.9 = (f32[496,128]{1,0:T(8,128)S(1)}, f32[496,128]{1,0:T(8,128)S(1)}, u32[]{:S(2)}, u32[]{:S(2)}) collective-permute-start(f32[496,128]{1,0:T(8,128)S(1)} %get-tuple-element.52), channel_id=1, source_target_pairs={{4,0},{0,4},{12,8},{8,12},{5,1},{1,5},{13,9},{9,13},{6,2},{2,6},{1... | collective-permute-start | bytes 761864 | tf_op jit(solution)/shard_map/ppermute | solution.py:682
  11.7 20.5 %collective-permute-start.10 = (f32[496,128]{1,0:T(8,128)S(1)}, f32[496,128]{1,0:T(8,128)S(1)}, u32[]{:S(2)}, u32[]{:S(2)}) collective-permute-start(f32[496,128]{1,0:T(8,128)S(1)} %get-tuple-element.53), channel_id=1, source_target_pairs={{0,0},{8,4},{4,8},{12,12},{1,1},{9,5},{5,9},{13,13},{2,2},{10,6},{... | collective-permute-start | bytes 761864 | tf_op jit(solution)/shard_map/ppermute | solution.py:682
  16.0 8.6 %collective-permute-start.4 = (f32[152,128]{1,0:T(8,128)S(1)}, f32[152,128]{1,0:T(8,128)S(1)}, u32[]{:S(2)}, u32[]{:S(2)}) collective-permute-start(f32[152,128]{1,0:T(8,128)S(1)} %get-tuple-element.44), channel_id=1, source_target_pairs={{8,0},{12,4},{0,8},{4,12},{9,1},{13,5},{1,9},{5,13},{10,2},{14,6},... | collective-permute-start | bytes 233480 | tf_op jit(solution)/shard_map/ppermute | solution.py:673
  16.1 1.2 %collective-permute-start.6 = (f32[8,128]{1,0:T(8,128)S(1)}, f32[8,128]{1,0:T(8,128)S(1)}, u32[]{:S(2)}, u32[]{:S(2)}) collective-permute-start(f32[8,128]{1,0:T(8,128)S(1)} %get-tuple-element.48), channel_id=1, source_target_pairs={{1,0},{0,1},{3,2},{2,3},{5,4},{4,5},{7,6},{6,7},{9,8},{8,9},{11,10... | collective-permute-start | bytes 12296 | tf_op jit(solution)/shard_map/ppermute | solution.py:673
  24.7 10.5 %collective-permute-start.7 = (f32[344,128]{1,0:T(8,128)S(1)}, f32[344,128]{1,0:T(8,128)S(1)}, u32[]{:S(2)}, u32[]{:S(2)}) collective-permute-start(f32[344,128]{1,0:T(8,128)S(1)} %get-tuple-element.50), channel_id=1, source_target_pairs={{4,0},{0,4},{12,8},{8,12},{5,1},{1,5},{13,9},{9,13},{6,2},{2,6},{1... | collective-permute-start | bytes 528392 | tf_op jit(solution)/shard_map/ppermute | solution.py:682
  27.0 8.2 %collective-permute-start.8 = (f32[344,128]{1,0:T(8,128)S(1)}, f32[344,128]{1,0:T(8,128)S(1)}, u32[]{:S(2)}, u32[]{:S(2)}) collective-permute-start(f32[344,128]{1,0:T(8,128)S(1)} %get-tuple-element.51), channel_id=1, source_target_pairs={{0,0},{8,4},{4,8},{12,12},{1,1},{9,5},{5,9},{13,13},{2,2},{10,6},{... | collective-permute-start | bytes 528392 | tf_op jit(solution)/shard_map/ppermute | solution.py:682

commit v9 on v8

--- a/solution.py
+++ b/solution.py
@@ -234,6 +234,7 @@
             target[tiles_end : tiles_end + BY] = strip[0:BY] + fix_lane
             target[tiles_end + BY : tiles_end + EY] = strip[BY:EY]
             target[WAVE_FIX : WAVE_FIX + 8] = fix_row
+            target[WAVE_FIX + 8 : WAVE_FIX + 24] = jnp.zeros((16, BZ), F32)
         else:
             target[tiles_end : tiles_end + EY] = strip
 
@@ -732,7 +733,7 @@
     early_planes, source_planes = (last - first for first, last in (EARLY_PLANES, SOURCE_PLANES))
     late, adj_late, token = call(
         merge_kernel,
-        [shape(WAVE_FIX + 8, BZ), shape(ADJ_OWN[2] + EY, BZ), shape(8, BZ)],
+        [shape(WAVE_FIX + 24, BZ), shape(ADJ_OWN[2] + EY, BZ), shape(8, BZ)],
         [from_up, from_down, corner_up, corner_down, strips, other, t, last_x, last_y, rsb],
         [],
         "vvvvvvvvva",

time: 37.2 us -> 29.7 us (0.80)
  the two profiles are of different devices: /device:TPU:8 before, /device:TPU:10 now
where the time goes in v9:
time: 29.7 us; the launch traced here: 29.5 us
  starting transfers between devices  14.1 us (47%)
  Pallas kernels  9.29 us (31%)
  waiting for transfers between devices  5.34 us (18%)
  between operations  0.73 us (2%)
    pallas_call x9, Pallas kernels, call(): pl.pallas_call(kernel, out_shape=outs, in_specs=[pl.BlockSpec(memory_spac...  9.29 us
    ppermute x4, starting transfers between devices, paired(): return lax.ppermute(array, 'gx', pairs)  8.86 us
    ppermute x5, starting transfers between devices, rotated(): lax.ppermute(array, axis, [((i + offset) % count, i) for i in range(count)])  3.13 us
    ppermute x5, waiting for transfers between devices, rotated(): lax.ppermute(array, axis, [((i + offset) % count, i) for i in range(count)])  2.32 us
    ppermute x2, starting transfers between devices, from_sides(): both = lax.ppermute(sends[0], axes, route(1) + route(-1))  2.14 us
    ppermute x4, waiting for transfers between devices, paired(): return lax.ppermute(array, 'gx', pairs)  1.92 us
    ppermute x2, waiting for transfers between devices, from_sides(): both = lax.ppermute(sends[0], axes, route(1) + route(-1))  1.09 us
  transfers between devices with their start and end apart: 11, of which 5 were waited for; matrix products, arithmetic and copies ran while one was open for 0% of the time, Pallas kernels for 21%

profile of v9, /device:TPU:10, one launch (start us, length us, event | category | flops | bytes accessed | tf_op | source)
XLA Modules:
  0.0 29.5 jit_solution(7434453119243703162)
XLA Ops:
  0.6 1.3 %shard_map.95 = (f32[256,128]{1,0:T(8,128)S(1)}, f32[256,128]{1,0:T(8,128)S(1)}, f32[128,128]{1,0:T(8,128)S(1)}, f32[64,128]{1,0:T(8,128)S(1)}, f32[64,128]{1,0:...) custom-call(f32[4,4,32,128]{3,2,1,0:T(8,128)} %stored_hbm.1, ...), custom_call_target="tpu_custom_call" | custom-call | bytes 5166000 | tf_op jit(solution)/shard_map/pallas_call | solution.py:638
  2.0 2.7 %collective-permute-start = (f32[256,128]{1,0:T(8,128)S(1)}, f32[256,128]{1,0:T(8,128)S(1)}, u32[]{:S(2)}, u32[]{:S(2)}) collective-permute-start(f32[256,128]{1,0:T(8,128)S(1)} %get-tuple-element.34), channel_id=1, source_target_pairs={{8,0},{12,4},{0,8},{4,12},{9,1},{13,5},{1,9},{5,13},{10,2},{14,6},... | collective-permute-start | bytes 393224 | tf_op jit(solution)/shard_map/ppermute | solution.py:674
  4.6 0.5 %collective-permute-start.1 = (f32[160,128]{1,0:T(8,128)S(1)}, f32[160,128]{1,0:T(8,128)S(1)}, u32[]{:S(2)}, u32[]{:S(2)}) collective-permute-start(f32[160,128]{1,0:T(8,128)S(1)} %get-tuple-element.35), channel_id=1, source_target_pairs={{2,0},{0,2},{3,1},{1,3},{6,4},{4,6},{7,5},{5,7},{10,8},{8,10},{11,... | collective-permute-start | bytes 245768 | tf_op jit(solution)/shard_map/ppermute | solution.py:666
  5.1 0.0 collective-permute-start.3
  5.1 1.6 %collective-permute-start.2 = (f32[16,128]{1,0:T(8,128)S(1)}, f32[16,128]{1,0:T(8,128)S(1)}, u32[]{:S(2)}, u32[]{:S(2)}) collective-permute-start(f32[16,128]{1,0:T(8,128)S(1)} %get-tuple-element.36), channel_id=1, source_target_pairs={{2,1},{3,0},{0,3},{1,2},{6,5},{7,4},{4,7},{5,6},{10,9},{11,8},{8,1... | collective-permute-start | bytes 24584 | tf_op jit(solution)/shard_map/ppermute | solution.py:666
  6.8 1.2 %shard_map.96 = (f32[2,480,128]{2,1,0:T(8,128)S(1)}, f32[2,40,128]{2,1,0:T(8,128)S(1)}) custom-call(s32[3,1024]{1,0:T(4,128)S(1)} %get-tuple-element.41.receivers, f32[4,1024]{1,0:T(4,128)S(1)} %get-tuple-element.42.receiver_wave), custom_call_target="tpu_custom_call" | custom-call | bytes 4428000 | tf_op jit(solution)/shard_map/pallas_call | solution.py:638
  8.0 0.3 collective-permute-done.2.corner_up.corner_down
  8.3 0.0 collective-permute-done.3.other_ref
  8.3 0.8 %collective-permute-done.1.from_up.from_down = f32[160,128]{1,0:T(8,128)S(1)} collective-permute-done((f32[160,128]{1,0:T(8,128)S(1)}, f32[160,128]{1,0:T(8,128)S(1)}, u32[]{:S(2)}, u32[]{:S(2)}) %collective-permute-start.1) | collective-permute-done | bytes 81952 | tf_op jit(solution)/shard_map/ppermute | solution.py:666
  9.1 0.3 shard_map.97
  9.4 0.4 %collective-permute-start.4 = (f32[168,128]{1,0:T(8,128)S(1)}, f32[168,128]{1,0:T(8,128)S(1)}, u32[]{:S(2)}, u32[]{:S(2)}) collective-permute-start(f32[168,128]{1,0:T(8,128)S(1)} %get-tuple-element.44), channel_id=1, source_target_pairs={{8,0},{12,4},{0,8},{4,12},{9,1},{13,5},{1,9},{5,13},{10,2},{14,6},... | collective-permute-start | bytes 258056 | tf_op jit(solution)/shard_map/ppermute | solution.py:674
  9.8 0.0 collective-permute-start.5
  9.8 1.2 %collective-permute-done.5._a = f32[8,128]{1,0:T(8,128)S(1)} collective-permute-done((f32[8,128]{1,0:T(8,128)S(1)}, f32[8,128]{1,0:T(8,128)S(1)}, u32[]{:S(2)}, u32[]{:S(2)}) %collective-permute-start.5) | collective-permute-done | bytes 4128 | tf_op jit(solution)/shard_map/ppermute | solution.py:674
  10.9 0.0 collective-permute-done._b.wave_ref
  11.0 0.5 %collective-permute-start.9 = (f32[496,128]{1,0:T(8,128)S(1)}, f32[496,128]{1,0:T(8,128)S(1)}, u32[]{:S(2)}, u32[]{:S(2)}) collective-permute-start(f32[496,128]{1,0:T(8,128)S(1)} %get-tuple-element.52), channel_id=1, source_target_pairs={{4,0},{0,4},{12,8},{8,12},{5,1},{1,5},{13,9},{9,13},{6,2},{2,6},{1... | collective-permute-start | bytes 761864 | tf_op jit(solution)/shard_map/ppermute | solution.py:683
  11.5 6.3 %collective-permute-start.10 = (f32[496,128]{1,0:T(8,128)S(1)}, f32[496,128]{1,0:T(8,128)S(1)}, u32[]{:S(2)}, u32[]{:S(2)}) collective-permute-start(f32[496,128]{1,0:T(8,128)S(1)} %get-tuple-element.53), channel_id=1, source_target_pairs={{0,0},{8,4},{4,8},{12,12},{1,1},{9,5},{5,9},{13,13},{2,2},{10,6},{... | collective-permute-start | bytes 761864 | tf_op jit(solution)/shard_map/ppermute | solution.py:683
  17.9 0.1 collective-permute-start.6
  17.9 1.2 %collective-permute-done.6._ = f32[8,128]{1,0:T(8,128)S(1)} collective-permute-done((f32[8,128]{1,0:T(8,128)S(1)}, f32[8,128]{1,0:T(8,128)S(1)}, u32[]{:S(2)}, u32[]{:S(2)}) %collective-permute-start.6) | collective-permute-done | bytes 4128 | tf_op jit(solution)/shard_map/ppermute | solution.py:674
  19.1 0.0 collective-permute-done.4.late_ref
  19.1 0.1 shard_map.99
  19.2 0.1 collective-permute-start.7
  19.3 1.9 %collective-permute-start.8 = (f32[344,128]{1,0:T(8,128)S(1)}, f32[344,128]{1,0:T(8,128)S(1)}, u32[]{:S(2)}, u32[]{:S(2)}) collective-permute-start(f32[344,128]{1,0:T(8,128)S(1)} %get-tuple-element.51), channel_id=1, source_target_pairs={{0,0},{8,4},{4,8},{12,12},{1,1},{9,5},{5,9},{13,13},{2,2},{10,6},{... | collective-permute-start | bytes 528392 | tf_op jit(solution)/shard_map/ppermute | solution.py:683
  21.2 1.0 %shard_map.100 = (f32[2,320,128]{2,1,0:T(8,128)S(1)}, f32[2,40,128]{2,1,0:T(8,128)S(1)}) custom-call(s32[3,1024]{1,0:T(4,128)S(1)} %get-tuple-element.41.receivers, f32[4,1024]{1,0:T(4,128)S(1)} %get-tuple-element.42.receiver_wave, f32[304,128]{1,0:T(8,128)S(1)} %get-tuple-element.46.adj_ref._.late_ref), custom_call_target="tpu_custom_call" | custom-call | bytes 3690000 | tf_op jit(solution)/shard_map/pallas_call | solution.py:638
  22.2 0.5 %shard_map.102 = (f32[3,400,128]{2,1,0:T(8,128)S(1)}, f32[3,40,128]{2,1,0:T(8,128)S(1)}) custom-call(s32[3,64]{1,0:T(4,128)S(1)} %get-tuple-element.60.sources, f32[4,64]{1,0:T(4,128)S(1)} %get-tuple-element.61.source_wave, f32[8,128]{1,0:T(8,128)S(1)} %collective-permute-done.6._), custom_call_target="tpu_custom_call" | custom-call | bytes 1845000 | tf_op jit(solution)/shard_map/pallas_call | solution.py:638
  22.8 0.0 collective-permute-done.9.even
  22.8 0.0 collective-permute-done.10.odd
  22.8 3.0 %shard_map.101 = (f32[4,4,32,128]{3,2,1,0:T(8,128)}, f32[4,4,4,32,128]{4,3,2,1,0:T(8,128)S(1)}, f32[3,12,40,128]{3,2,1,0:T(8,128)S(1)}, f32[3,40,128]{2,1,0:T(8,128)S(1)}) custom-call(f32[256,128]{1,0:T(8,128)S(1)} %get-tuple-element.45.ql_ref, f32[304,128]{1,0:T(8,128)S(1)} %get-tuple-element.46.adj_ref._.late_ref, ...), custom_call_target="tpu_custom_call" | custom-call | bytes 14391000 | tf_op jit(solution)/shard_map/pallas_call | solution.py:638
  25.8 0.0 collective-permute-done.7.even
  25.8 1.9 %collective-permute-done.8.odd = f32[344,128]{1,0:T(8,128)S(1)} collective-permute-done((f32[344,128]{1,0:T(8,128)S(1)}, f32[344,128]{1,0:T(8,128)S(1)}, u32[]{:S(2)}, u32[]{:S(2)}) %collective-permute-start.8) | collective-permute-done | bytes 176160 | tf_op jit(solution)/shard_map/ppermute | solution.py:683
  27.7 1.8 %shard_map.103 = f32[2,4,32,128]{3,2,1,0:T(8,128)} custom-call(f32[256,128]{1,0:T(8,128)S(1)} %collective-permute-done._b.wave_ref, f32[128,128]{1,0:T(8,128)S(1)} %get-tuple-element.49.own_s_ref, f32[168,128]{1,0:T(8,128)S(1)} %collective-permute-done.4.late_ref, f32[344,128]{1,0:T(8,128)S(1)} %collective-permute-done.7.even, ...), custom_call_target="tpu_custom_call" | custom-call | bytes 9225000 | tf_op jit(solution)/shard_map/pallas_call | solution.py:638
  (1 shorter events, 0.0 us)
Async XLA Ops:
  2.0 9.0 %collective-permute-start = (f32[256,128]{1,0:T(8,128)S(1)}, f32[256,128]{1,0:T(8,128)S(1)}, u32[]{:S(2)}, u32[]{:S(2)}) collective-permute-start(f32[256,128]{1,0:T(8,128)S(1)} %get-tuple-element.34), channel_id=1, source_target_pairs={{8,0},{12,4},{0,8},{4,12},{9,1},{13,5},{1,9},{5,13},{10,2},{14,6},... | collective-permute-start | bytes 393224 | tf_op jit(solution)/shard_map/ppermute | solution.py:674
  4.6 4.5 %collective-permute-start.1 = (f32[160,128]{1,0:T(8,128)S(1)}, f32[160,128]{1,0:T(8,128)S(1)}, u32[]{:S(2)}, u32[]{:S(2)}) collective-permute-start(f32[160,128]{1,0:T(8,128)S(1)} %get-tuple-element.35), channel_id=1, source_target_pairs={{2,0},{0,2},{3,1},{1,3},{6,4},{4,6},{7,5},{5,7},{10,8},{8,10},{11,... | collective-permute-start | bytes 245768 | tf_op jit(solution)/shard_map/ppermute | solution.py:666
  5.1 3.1 %collective-permute-start.3 = (f32[96,128]{1,0:T(8,128)S(1)}, f32[96,128]{1,0:T(8,128)S(1)}, u32[]{:S(2)}, u32[]{:S(2)}) collective-permute-start(f32[96,128]{1,0:T(8,128)S(1)} %get-tuple-element.37.strip_ref), channel_id=1, source_target_pairs={{1,0},{0,1},{3,2},{2,3},{5,4},{4,5},{7,6},{6,7},{9,8},{8,9},{11,10... | collective-permute-start | bytes 147464 | tf_op jit(solution)/shard_map/ppermute | solution.py:674
  5.1 3.1 %collective-permute-start.2 = (f32[16,128]{1,0:T(8,128)S(1)}, f32[16,128]{1,0:T(8,128)S(1)}, u32[]{:S(2)}, u32[]{:S(2)}) collective-permute-start(f32[16,128]{1,0:T(8,128)S(1)} %get-tuple-element.36), channel_id=1, source_target_pairs={{2,1},{3,0},{0,3},{1,2},{6,5},{7,4},{4,7},{5,6},{10,9},{11,8},{8,1... | collective-permute-start | bytes 24584 | tf_op jit(solution)/shard_map/ppermute | solution.py:666
  9.4 9.7 %collective-permute-start.4 = (f32[168,128]{1,0:T(8,128)S(1)}, f32[168,128]{1,0:T(8,128)S(1)}, u32[]{:S(2)}, u32[]{:S(2)}) collective-permute-start(f32[168,128]{1,0:T(8,128)S(1)} %get-tuple-element.44), channel_id=1, source_target_pairs={{8,0},{12,4},{0,8},{4,12},{9,1},{13,5},{1,9},{5,13},{10,2},{14,6},... | collective-permute-start | bytes 258056 | tf_op jit(solution)/shard_map/ppermute | solution.py:674
  9.8 1.2 %collective-permute-start.5 = (f32[8,128]{1,0:T(8,128)S(1)}, f32[8,128]{1,0:T(8,128)S(1)}, u32[]{:S(2)}, u32[]{:S(2)}) collective-permute-start(f32[8,128]{1,0:T(8,128)S(1)} %get-tuple-element.47), channel_id=1, source_target_pairs={{1,0},{0,1},{3,2},{2,3},{5,4},{4,5},{7,6},{6,7},{9,8},{8,9},{11,10... | collective-permute-start | bytes 12296 | tf_op jit(solution)/shard_map/ppermute | solution.py:674
  11.0 11.8 %collective-permute-start.9 = (f32[496,128]{1,0:T(8,128)S(1)}, f32[496,128]{1,0:T(8,128)S(1)}, u32[]{:S(2)}, u32[]{:S(2)}) collective-permute-start(f32[496,128]{1,0:T(8,128)S(1)} %get-tuple-element.52), channel_id=1, source_target_pairs={{4,0},{0,4},{12,8},{8,12},{5,1},{1,5},{13,9},{9,13},{6,2},{2,6},{1... | collective-permute-start | bytes 761864 | tf_op jit(solution)/shard_map/ppermute | solution.py:683
  11.5 11.3 %collective-permute-start.10 = (f32[496,128]{1,0:T(8,128)S(1)}, f32[496,128]{1,0:T(8,128)S(1)}, u32[]{:S(2)}, u32[]{:S(2)}) collective-permute-start(f32[496,128]{1,0:T(8,128)S(1)} %get-tuple-element.53), channel_id=1, source_target_pairs={{0,0},{8,4},{4,8},{12,12},{1,1},{9,5},{5,9},{13,13},{2,2},{10,6},{... | collective-permute-start | bytes 761864 | tf_op jit(solution)/shard_map/ppermute | solution.py:683
  17.9 1.2 %collective-permute-start.6 = (f32[8,128]{1,0:T(8,128)S(1)}, f32[8,128]{1,0:T(8,128)S(1)}, u32[]{:S(2)}, u32[]{:S(2)}) collective-permute-start(f32[8,128]{1,0:T(8,128)S(1)} %get-tuple-element.48), channel_id=1, source_target_pairs={{1,0},{0,1},{3,2},{2,3},{5,4},{4,5},{7,6},{6,7},{9,8},{8,9},{11,10... | collective-permute-start | bytes 12296 | tf_op jit(solution)/shard_map/ppermute | solution.py:674
  19.2 6.6 %collective-permute-start.7 = (f32[344,128]{1,0:T(8,128)S(1)}, f32[344,128]{1,0:T(8,128)S(1)}, u32[]{:S(2)}, u32[]{:S(2)}) collective-permute-start(f32[344,128]{1,0:T(8,128)S(1)} %get-tuple-element.50), channel_id=1, source_target_pairs={{4,0},{0,4},{12,8},{8,12},{5,1},{1,5},{13,9},{9,13},{6,2},{2,6},{1... | collective-permute-start | bytes 528392 | tf_op jit(solution)/shard_map/ppermute | solution.py:683
  19.3 8.4 %collective-permute-start.8 = (f32[344,128]{1,0:T(8,128)S(1)}, f32[344,128]{1,0:T(8,128)S(1)}, u32[]{:S(2)}, u32[]{:S(2)}) collective-permute-start(f32[344,128]{1,0:T(8,128)S(1)} %get-tuple-element.51), channel_id=1, source_target_pairs={{0,0},{8,4},{4,8},{12,12},{1,1},{9,5},{5,9},{13,13},{2,2},{10,6},{... | collective-permute-start | bytes 528392 | tf_op jit(solution)/shard_map/ppermute | solution.py:683

commit v10 on v9

--- a/solution.py
+++ b/solution.py
@@ -554,9 +554,20 @@
 
 def forward_kernel(
     wave_ref, own_s_ref, late_ref, even, odd, coef_ref, coef_strip_ref, s_ref, ss_ref, hist_ref,
-    grad_ref,
-    p_ref, spread_ref, edge_ref, flux_ref,
+    adjoint_ref, grad_hbm, adjoint_hbm,
+    p_ref, spread_ref, edge_ref, flux_ref, grad_ref, sems,
 ):
+    copies = [pltpu.make_async_copy(adjoint_ref, adjoint_hbm, sems.at[0])]
+    copies[0].start()
+
+    def send(index, kind, first, count):
+        planes = pl.ds(first, count)
+        copy = pltpu.make_async_copy(
+            grad_ref.at[kind, planes], grad_hbm.at[kind, planes], sems.at[index]
+        )
+        copy.start()
+        copies.append(copy)
+
     cut_up, cut_down = cut_flags()
     side = sides()
     messages = (even, odd)
@@ -607,6 +618,8 @@
                 term = term + hist_ref[k, 2, place] * slopes[1][0:BY]
                 term = term + hist_ref[k, 3, place] * slopes[2][0:BY]
                 grad_ref[1, place] = -term if k == 0 else grad_ref[1, place] - term
+        if step == STEPS:
+            send(1, 1, 0, BX)
 
         for x in range(step, EX - step):
             flux_y, flux_z = flux_ref[1, x], flux_ref[2, x]
@@ -623,13 +636,17 @@
                 place = x - BX
                 term = hist_ref[k, 0, place] * spread[0:BY]
                 grad_ref[0, place] = -term if k == 0 else grad_ref[0, place] - term
+                if step == STEPS:
+                    send(2 + place, 0, place, 1)
+    for copy in copies:
+        copy.wait()
 
 
 def shape(*dims):
     return jax.ShapeDtypeStruct(dims, F32)
 
 
-def call(kernel, outs, operands, scratch, places, micros=0.1):
+def call(kernel, outs, operands, scratch, places, micros=0.1, out_place="v"):
     spaces = {"h": pltpu.HBM, "a": pl.ANY, "v": pltpu.VMEM}
     operands = [
         pltpu.with_memory_space_constraint(operand, pltpu.HBM) if place == "h" else operand
@@ -639,7 +656,7 @@
         kernel,
         out_shape=outs,
         in_specs=[pl.BlockSpec(memory_space=spaces[place]) for place in places],
-        out_specs=[pl.BlockSpec(memory_space=pltpu.VMEM)] * len(outs),
+        out_specs=[pl.BlockSpec(memory_space=spaces[out_place])] * len(outs),
         scratch_shapes=scratch,
         compiler_params=pltpu.CompilerParams(vmem_limit_bytes=VMEM_LIMIT),
         cost_estimate=pl.CostEstimate(
@@ -775,7 +792,7 @@
         "vva",
     )
     wave_even, wave_odd = paired(wave_even, False), paired(wave_odd, True)
-    adjoint_start, hist, coef, coef_strip = call(
+    adjoint_out, hist, coef, coef_strip = call(
         adjoint_kernel,
         [
             shape(4, BX, BY, BZ),
@@ -789,15 +806,23 @@
         "vvvvhvvvvv",
         3.9,
     )
-    (gradient,) = call(
+    return call(
         forward_kernel,
-        [shape(2, BX, BY, BZ)],
-        [wave, own_s, late, wave_even, wave_odd, coef, coef_strip, src, src_strip, hist],
-        [pltpu.VMEM((EX, EY, BZ), F32)] * 3 + [pltpu.VMEM((3, EX, EY, BZ), F32)],
-        "vvvvvvvvvv",
+        [shape(2, BX, BY, BZ), shape(4, BX, BY, BZ)],
+        [
+            wave, own_s, late, wave_even, wave_odd, coef, coef_strip, src, src_strip, hist,
+            adjoint_out,
+        ],
+        [pltpu.VMEM((EX, EY, BZ), F32)] * 3
+        + [
+            pltpu.VMEM((3, EX, EY, BZ), F32),
+            pltpu.VMEM((2, BX, BY, BZ), F32),
+            pltpu.SemaphoreType.DMA((2 + BX,)),
+        ],
+        "vvvvvvvvvvv",
         2.5,
-    )
-    return gradient, adjoint_start
+        "a",
+    )
 
 
 def solution(mesh):

time: 29.7 us -> 29.7 us (level)
  waiting for transfers between devices: 5.34 us -> 5.94 us
  Pallas kernels: 9.29 us -> 8.7 us
    ppermute x4, waiting for transfers between devices: 1.92 us -> 2.52 us  [paired(): return lax.ppermute(array, 'gx', pairs)]
    pallas_call x9, Pallas kernels: 9.29 us -> 8.7 us  [call(): pl.pallas_call(kernel, out_shape=outs, in_specs=[pl.BlockSpec(memory_spac...]
  transfers between devices with their start and end apart: 11 -> 11, of which waited for: 5 -> 6; matrix products, arithmetic and copies ran while one was open for 0% -> 0% of each run, Pallas kernels for 21% -> 19%
where the time goes in v10:
time: 29.7 us; the launch traced here: 29.5 us
  starting transfers between devices  14.1 us (47%)
  Pallas kernels  8.7 us (29%)
  waiting for transfers between devices  5.94 us (20%)
  between operations  0.73 us (2%)
    ppermute x4, starting transfers between devices, paired(): return lax.ppermute(array, 'gx', pairs)  8.86 us
    pallas_call x9, Pallas kernels, call(): pl.pallas_call(kernel, out_shape=outs, in_specs=[pl.BlockSpec(memory_spac...  8.7 us
    ppermute x5, starting transfers between devices, rotated(): lax.ppermute(array, axis, [((i + offset) % count, i) for i in range(count)])  3.13 us
    ppermute x4, waiting for transfers between devices, paired(): return lax.ppermute(array, 'gx', pairs)  2.52 us
    ppermute x5, waiting for transfers between devices, rotated(): lax.ppermute(array, axis, [((i + offset) % count, i) for i in range(count)])  2.32 us
    ppermute x2, starting transfers between devices, from_sides(): both = lax.ppermute(sends[0], axes, route(1) + route(-1))  2.14 us
    ppermute x2, waiting for transfers between devices, from_sides(): both = lax.ppermute(sends[0], axes, route(1) + route(-1))  1.09 us
  transfers between devices with their start and end apart: 11, of which 6 were waited for; matrix products, arithmetic and copies ran while one was open for 0% of the time, Pallas kernels for 19%

profile of v10, /device:TPU:10, one launch (start us, length us, event | category | flops | bytes accessed | tf_op | source)
XLA Modules:
  0.0 29.5 jit_solution(14911958222370256242)
XLA Ops:
  0.6 1.3 %shard_map.95 = (f32[256,128]{1,0:T(8,128)S(1)}, f32[256,128]{1,0:T(8,128)S(1)}, f32[128,128]{1,0:T(8,128)S(1)}, f32[64,128]{1,0:T(8,128)S(1)}, f32[64,128]{1,0:...) custom-call(f32[4,4,32,128]{3,2,1,0:T(8,128)} %stored_hbm.1, ...), custom_call_target="tpu_custom_call" | custom-call | bytes 5166000 | tf_op jit(solution)/shard_map/pallas_call | solution.py:655
  2.0 2.7 %collective-permute-start = (f32[256,128]{1,0:T(8,128)S(1)}, f32[256,128]{1,0:T(8,128)S(1)}, u32[]{:S(2)}, u32[]{:S(2)}) collective-permute-start(f32[256,128]{1,0:T(8,128)S(1)} %get-tuple-element.34), channel_id=1, source_target_pairs={{8,0},{12,4},{0,8},{4,12},{9,1},{13,5},{1,9},{5,13},{10,2},{14,6},... | collective-permute-start | bytes 393224 | tf_op jit(solution)/shard_map/ppermute | solution.py:691
  4.6 0.5 %collective-permute-start.1 = (f32[160,128]{1,0:T(8,128)S(1)}, f32[160,128]{1,0:T(8,128)S(1)}, u32[]{:S(2)}, u32[]{:S(2)}) collective-permute-start(f32[160,128]{1,0:T(8,128)S(1)} %get-tuple-element.35), channel_id=1, source_target_pairs={{2,0},{0,2},{3,1},{1,3},{6,4},{4,6},{7,5},{5,7},{10,8},{8,10},{11,... | collective-permute-start | bytes 245768 | tf_op jit(solution)/shard_map/ppermute | solution.py:683
  5.1 0.0 collective-permute-start.3
  5.1 1.6 %collective-permute-start.2 = (f32[16,128]{1,0:T(8,128)S(1)}, f32[16,128]{1,0:T(8,128)S(1)}, u32[]{:S(2)}, u32[]{:S(2)}) collective-permute-start(f32[16,128]{1,0:T(8,128)S(1)} %get-tuple-element.36), channel_id=1, source_target_pairs={{2,1},{3,0},{0,3},{1,2},{6,5},{7,4},{4,7},{5,6},{10,9},{11,8},{8,1... | collective-permute-start | bytes 24584 | tf_op jit(solution)/shard_map/ppermute | solution.py:683
  6.8 1.2 %shard_map.96 = (f32[2,480,128]{2,1,0:T(8,128)S(1)}, f32[2,40,128]{2,1,0:T(8,128)S(1)}) custom-call(s32[3,1024]{1,0:T(4,128)S(1)} %get-tuple-element.41.receivers, f32[4,1024]{1,0:T(4,128)S(1)} %get-tuple-element.42.receiver_wave), custom_call_target="tpu_custom_call" | custom-call | bytes 4428000 | tf_op jit(solution)/shard_map/pallas_call | solution.py:655
  8.0 0.3 collective-permute-done.2.corner_up.corner_down
  8.3 0.0 collective-permute-done.3.other_ref
  8.3 0.8 %collective-permute-done.1.from_up.from_down = f32[160,128]{1,0:T(8,128)S(1)} collective-permute-done((f32[160,128]{1,0:T(8,128)S(1)}, f32[160,128]{1,0:T(8,128)S(1)}, u32[]{:S(2)}, u32[]{:S(2)}) %collective-permute-start.1) | collective-permute-done | bytes 81952 | tf_op jit(solution)/shard_map/ppermute | solution.py:683
  9.1 0.3 shard_map.97
  9.4 0.4 %collective-permute-start.4 = (f32[168,128]{1,0:T(8,128)S(1)}, f32[168,128]{1,0:T(8,128)S(1)}, u32[]{:S(2)}, u32[]{:S(2)}) collective-permute-start(f32[168,128]{1,0:T(8,128)S(1)} %get-tuple-element.44), channel_id=1, source_target_pairs={{8,0},{12,4},{0,8},{4,12},{9,1},{13,5},{1,9},{5,13},{10,2},{14,6},... | collective-permute-start | bytes 258056 | tf_op jit(solution)/shard_map/ppermute | solution.py:691
  9.8 0.0 collective-permute-start.5
  9.8 1.2 %collective-permute-done.5._a = f32[8,128]{1,0:T(8,128)S(1)} collective-permute-done((f32[8,128]{1,0:T(8,128)S(1)}, f32[8,128]{1,0:T(8,128)S(1)}, u32[]{:S(2)}, u32[]{:S(2)}) %collective-permute-start.5) | collective-permute-done | bytes 4128 | tf_op jit(solution)/shard_map/ppermute | solution.py:691
  10.9 0.0 collective-permute-done._b.wave_ref
  11.0 0.5 %collective-permute-start.9 = (f32[496,128]{1,0:T(8,128)S(1)}, f32[496,128]{1,0:T(8,128)S(1)}, u32[]{:S(2)}, u32[]{:S(2)}) collective-permute-start(f32[496,128]{1,0:T(8,128)S(1)} %get-tuple-element.52), channel_id=1, source_target_pairs={{4,0},{0,4},{12,8},{8,12},{5,1},{1,5},{13,9},{9,13},{6,2},{2,6},{1... | collective-permute-start | bytes 761864 | tf_op jit(solution)/shard_map/ppermute | solution.py:700
  11.5 6.3 %collective-permute-start.10 = (f32[496,128]{1,0:T(8,128)S(1)}, f32[496,128]{1,0:T(8,128)S(1)}, u32[]{:S(2)}, u32[]{:S(2)}) collective-permute-start(f32[496,128]{1,0:T(8,128)S(1)} %get-tuple-element.53), channel_id=1, source_target_pairs={{0,0},{8,4},{4,8},{12,12},{1,1},{9,5},{5,9},{13,13},{2,2},{10,6},{... | collective-permute-start | bytes 761864 | tf_op jit(solution)/shard_map/ppermute | solution.py:700
  17.9 0.1 collective-permute-start.6
  17.9 1.2 %collective-permute-done.6._ = f32[8,128]{1,0:T(8,128)S(1)} collective-permute-done((f32[8,128]{1,0:T(8,128)S(1)}, f32[8,128]{1,0:T(8,128)S(1)}, u32[]{:S(2)}, u32[]{:S(2)}) %collective-permute-start.6) | collective-permute-done | bytes 4128 | tf_op jit(solution)/shard_map/ppermute | solution.py:691
  19.1 0.0 collective-permute-done.4.late_ref
  19.1 0.1 shard_map.99
  19.2 0.1 collective-permute-start.7
  19.3 1.9 %collective-permute-start.8 = (f32[344,128]{1,0:T(8,128)S(1)}, f32[344,128]{1,0:T(8,128)S(1)}, u32[]{:S(2)}, u32[]{:S(2)}) collective-permute-start(f32[344,128]{1,0:T(8,128)S(1)} %get-tuple-element.51), channel_id=1, source_target_pairs={{0,0},{8,4},{4,8},{12,12},{1,1},{9,5},{5,9},{13,13},{2,2},{10,6},{... | collective-permute-start | bytes 528392 | tf_op jit(solution)/shard_map/ppermute | solution.py:700
  21.2 1.0 %shard_map.100 = (f32[2,320,128]{2,1,0:T(8,128)S(1)}, f32[2,40,128]{2,1,0:T(8,128)S(1)}) custom-call(s32[3,1024]{1,0:T(4,128)S(1)} %get-tuple-element.41.receivers, f32[4,1024]{1,0:T(4,128)S(1)} %get-tuple-element.42.receiver_wave, f32[304,128]{1,0:T(8,128)S(1)} %get-tuple-element.46.adj_ref._.late_ref), custom_call_target="tpu_custom_call" | custom-call | bytes 3690000 | tf_op jit(solution)/shard_map/pallas_call | solution.py:655
  22.2 0.5 %shard_map.102 = (f32[3,400,128]{2,1,0:T(8,128)S(1)}, f32[3,40,128]{2,1,0:T(8,128)S(1)}) custom-call(s32[3,64]{1,0:T(4,128)S(1)} %get-tuple-element.60.sources, f32[4,64]{1,0:T(4,128)S(1)} %get-tuple-element.61.source_wave, f32[8,128]{1,0:T(8,128)S(1)} %collective-permute-done.6._), custom_call_target="tpu_custom_call" | custom-call | bytes 1845000 | tf_op jit(solution)/shard_map/pallas_call | solution.py:655
  22.8 0.0 collective-permute-done.9.even
  22.8 0.0 collective-permute-done.10.odd
  22.8 2.4 %shard_map.101 = (f32[4,4,32,128]{3,2,1,0:T(8,128)S(1)}, f32[4,4,4,32,128]{4,3,2,1,0:T(8,128)S(1)}, f32[3,12,40,128]{3,2,1,0:T(8,128)S(1)}, f32[3,40,128]{2,1,0:T(8,128)S(1)}) custom-call(f32[256,128]{1,0:T(8,128)S(1)} %get-tuple-element.45.ql_ref, f32[304,128]{1,0:T(8,128)S(1)} %get-tuple-element.46.adj_ref._.late_ref, ...), custom_call_target="tpu_custom_call" | custom-call | bytes 14391000 | tf_op jit(solution)/shard_map/pallas_call | solution.py:655
  25.2 0.6 %collective-permute-done.7.even = f32[344,128]{1,0:T(8,128)S(1)} collective-permute-done((f32[344,128]{1,0:T(8,128)S(1)}, f32[344,128]{1,0:T(8,128)S(1)}, u32[]{:S(2)}, u32[]{:S(2)}) %collective-permute-start.7) | collective-permute-done | bytes 176160 | tf_op jit(solution)/shard_map/ppermute | solution.py:700
  25.8 1.9 %collective-permute-done.8.odd = f32[344,128]{1,0:T(8,128)S(1)} collective-permute-done((f32[344,128]{1,0:T(8,128)S(1)}, f32[344,128]{1,0:T(8,128)S(1)}, u32[]{:S(2)}, u32[]{:S(2)}) %collective-permute-start.8) | collective-permute-done | bytes 176160 | tf_op jit(solution)/shard_map/ppermute | solution.py:700
  27.7 1.8 %shard_map.103 = (f32[2,4,32,128]{3,2,1,0:T(8,128)}, f32[4,4,32,128]{3,2,1,0:T(8,128)}) custom-call(f32[256,128]{1,0:T(8,128)S(1)} %collective-permute-done._b.wave_ref, f32[128,128]{1,0:T(8,128)S(1)} %get-tuple-element.49.own_s_ref, f32[168,128]{1,0:T(8,128)S(1)} %collective-permute-done.4.late_ref, f32[344,128]{1,0:T(8,128)S(1)} %collective-permute-done.7.even, ...), custom_call_target="tpu_custom_call" | custom-call | bytes 9225000 | tf_op jit(solution)/shard_map/pallas_call | solution.py:655
  (1 shorter events, 0.0 us)
Async XLA Ops:
  2.0 9.0 %collective-permute-start = (f32[256,128]{1,0:T(8,128)S(1)}, f32[256,128]{1,0:T(8,128)S(1)}, u32[]{:S(2)}, u32[]{:S(2)}) collective-permute-start(f32[256,128]{1,0:T(8,128)S(1)} %get-tuple-element.34), channel_id=1, source_target_pairs={{8,0},{12,4},{0,8},{4,12},{9,1},{13,5},{1,9},{5,13},{10,2},{14,6},... | collective-permute-start | bytes 393224 | tf_op jit(solution)/shard_map/ppermute | solution.py:691
  4.6 4.5 %collective-permute-start.1 = (f32[160,128]{1,0:T(8,128)S(1)}, f32[160,128]{1,0:T(8,128)S(1)}, u32[]{:S(2)}, u32[]{:S(2)}) collective-permute-start(f32[160,128]{1,0:T(8,128)S(1)} %get-tuple-element.35), channel_id=1, source_target_pairs={{2,0},{0,2},{3,1},{1,3},{6,4},{4,6},{7,5},{5,7},{10,8},{8,10},{11,... | collective-permute-start | bytes 245768 | tf_op jit(solution)/shard_map/ppermute | solution.py:683
  5.1 3.1 %collective-permute-start.3 = (f32[96,128]{1,0:T(8,128)S(1)}, f32[96,128]{1,0:T(8,128)S(1)}, u32[]{:S(2)}, u32[]{:S(2)}) collective-permute-start(f32[96,128]{1,0:T(8,128)S(1)} %get-tuple-element.37.strip_ref), channel_id=1, source_target_pairs={{1,0},{0,1},{3,2},{2,3},{5,4},{4,5},{7,6},{6,7},{9,8},{8,9},{11,10... | collective-permute-start | bytes 147464 | tf_op jit(solution)/shard_map/ppermute | solution.py:691
  5.1 3.1 %collective-permute-start.2 = (f32[16,128]{1,0:T(8,128)S(1)}, f32[16,128]{1,0:T(8,128)S(1)}, u32[]{:S(2)}, u32[]{:S(2)}) collective-permute-start(f32[16,128]{1,0:T(8,128)S(1)} %get-tuple-element.36), channel_id=1, source_target_pairs={{2,1},{3,0},{0,3},{1,2},{6,5},{7,4},{4,7},{5,6},{10,9},{11,8},{8,1... | collective-permute-start | bytes 24584 | tf_op jit(solution)/shard_map/ppermute | solution.py:683
  9.4 9.7 %collective-permute-start.4 = (f32[168,128]{1,0:T(8,128)S(1)}, f32[168,128]{1,0:T(8,128)S(1)}, u32[]{:S(2)}, u32[]{:S(2)}) collective-permute-start(f32[168,128]{1,0:T(8,128)S(1)} %get-tuple-element.44), channel_id=1, source_target_pairs={{8,0},{12,4},{0,8},{4,12},{9,1},{13,5},{1,9},{5,13},{10,2},{14,6},... | collective-permute-start | bytes 258056 | tf_op jit(solution)/shard_map/ppermute | solution.py:691
  9.8 1.2 %collective-permute-start.5 = (f32[8,128]{1,0:T(8,128)S(1)}, f32[8,128]{1,0:T(8,128)S(1)}, u32[]{:S(2)}, u32[]{:S(2)}) collective-permute-start(f32[8,128]{1,0:T(8,128)S(1)} %get-tuple-element.47), channel_id=1, source_target_pairs={{1,0},{0,1},{3,2},{2,3},{5,4},{4,5},{7,6},{6,7},{9,8},{8,9},{11,10... | collective-permute-start | bytes 12296 | tf_op jit(solution)/shard_map/ppermute | solution.py:691
  11.0 11.8 %collective-permute-start.9 = (f32[496,128]{1,0:T(8,128)S(1)}, f32[496,128]{1,0:T(8,128)S(1)}, u32[]{:S(2)}, u32[]{:S(2)}) collective-permute-start(f32[496,128]{1,0:T(8,128)S(1)} %get-tuple-element.52), channel_id=1, source_target_pairs={{4,0},{0,4},{12,8},{8,12},{5,1},{1,5},{13,9},{9,13},{6,2},{2,6},{1... | collective-permute-start | bytes 761864 | tf_op jit(solution)/shard_map/ppermute | solution.py:700
  11.5 11.3 %collective-permute-start.10 = (f32[496,128]{1,0:T(8,128)S(1)}, f32[496,128]{1,0:T(8,128)S(1)}, u32[]{:S(2)}, u32[]{:S(2)}) collective-permute-start(f32[496,128]{1,0:T(8,128)S(1)} %get-tuple-element.53), channel_id=1, source_target_pairs={{0,0},{8,4},{4,8},{12,12},{1,1},{9,5},{5,9},{13,13},{2,2},{10,6},{... | collective-permute-start | bytes 761864 | tf_op jit(solution)/shard_map/ppermute | solution.py:700
  17.9 1.2 %collective-permute-start.6 = (f32[8,128]{1,0:T(8,128)S(1)}, f32[8,128]{1,0:T(8,128)S(1)}, u32[]{:S(2)}, u32[]{:S(2)}) collective-permute-start(f32[8,128]{1,0:T(8,128)S(1)} %get-tuple-element.48), channel_id=1, source_target_pairs={{1,0},{0,1},{3,2},{2,3},{5,4},{4,5},{7,6},{6,7},{9,8},{8,9},{11,10... | collective-permute-start | bytes 12296 | tf_op jit(solution)/shard_map/ppermute | solution.py:691
  19.2 6.6 %collective-permute-start.7 = (f32[344,128]{1,0:T(8,128)S(1)}, f32[344,128]{1,0:T(8,128)S(1)}, u32[]{:S(2)}, u32[]{:S(2)}) collective-permute-start(f32[344,128]{1,0:T(8,128)S(1)} %get-tuple-element.50), channel_id=1, source_target_pairs={{4,0},{0,4},{12,8},{8,12},{5,1},{1,5},{13,9},{9,13},{6,2},{2,6},{1... | collective-permute-start | bytes 528392 | tf_op jit(solution)/shard_map/ppermute | solution.py:700
  19.3 8.4 %collective-permute-start.8 = (f32[344,128]{1,0:T(8,128)S(1)}, f32[344,128]{1,0:T(8,128)S(1)}, u32[]{:S(2)}, u32[]{:S(2)}) collective-permute-start(f32[344,128]{1,0:T(8,128)S(1)} %get-tuple-element.51), channel_id=1, source_target_pairs={{0,0},{8,4},{4,8},{12,12},{1,1},{9,5},{5,9},{13,13},{2,2},{10,6},{... | collective-permute-start | bytes 528392 | tf_op jit(solution)/shard_map/ppermute | solution.py:700

commit v11 on v10

--- a/solution.py
+++ b/solution.py
@@ -60,7 +60,7 @@
 
 def load_kernel(
     stored_hbm, adj_hbm, lab_hbm, tissue_hbm, rc_hbm, rw_hbm, sc_hbm, sw_hbm,
-    wave_ref, ql_ref, t_ref, last_x_ref, last_y_ref, strip_ref, table_ref,
+    wave_ref, ql_ref, q_ref, t_ref, last_x_ref, last_y_ref, strip_ref, table_ref,
     rc_ref, rw_ref, sc_ref, sw_ref, *rest,
 ):
     *sends, stored, adj, lab, tissue, sem = rest
@@ -95,7 +95,7 @@
         fields = [stored[index, x] for index in range(4)] + [adj[0, x]]
         fields += [buoyancy * adj[index, x] for index in range(1, 4)] + [labels]
         wave_ref[plane] = fields[0]
-        ql_ref[plane] = fields[4]
+        ql_ref[plane] = q_ref[plane] = fields[4]
         ql_ref[PLANES + x * BY : PLANES + x * BY + BY] = labels
         for index, block in enumerate(fields):
             tiles[index * BX + x] = edge_tile(block)
@@ -239,7 +239,7 @@
             target[tiles_end : tiles_end + EY] = strip
 
 
-def adjoint_join_kernel(ql_ref, adj_ref, _a, _b, even_ref, odd_ref, token_ref):
+def adjoint_join_kernel(ql_ref, adj_ref, _a, _b, _c, even_ref, odd_ref, token_ref):
     token_ref[...] = jnp.zeros((8, BZ), F32)
     planes_end, x_end, tiles_end = ADJ_OWN
     for target, first in zip((even_ref, odd_ref), pair_planes()):
@@ -249,7 +249,8 @@
         base = copy_rows(target, base, adj_ref, x_end + 32 + first * 16, 16)
         base = copy_rows(target, base, adj_ref, x_end + 64 + first * 8, 24)
         base = copy_rows(target, base, adj_ref, tiles_end - 8, 8 + EY)
-        copy_rows(target, base, ql_ref, 0, 2 * PLANES)
+        base = copy_rows(target, base, ql_ref, PLANES, PLANES)
+    copy_rows(even_ref, base, ql_ref, 0, PLANES)
 
 
 def join_kernel(wave_ref, late_ref, _, s_ref, even_ref, odd_ref):
@@ -405,7 +406,7 @@
 
 
 def from_side(messages, first, count, block, side):
-    even, odd = (message[first : first + count] for message in messages)
+    even, odd = (ref[base + first : base + first + count] for ref, base in messages)
     low, high, even_above = side
     if block == 0:
         return jnp.where(even_above, odd, even) * low
@@ -466,7 +467,7 @@
 
 
 def adjoint_kernel(
-    ql_ref, late_ref, even, odd, adj_hbm, ra_ref, rsa_ref, rb_ref, rsb_ref,
+    ql_ref, q_odd, late_ref, even, odd, adj_hbm, ra_ref, rsa_ref, rb_ref, rsb_ref,
     table_ref,
     out_ref, hist_ref, coef_ref, coef_strip_ref,
     q_ref, t_ref, u_ref, scale_ref, edge_ref, flux_ref, w_sem,
@@ -475,17 +476,18 @@
     w_copy.start()
     cut_up, cut_down = cut_flags()
     side = sides()
-    messages = (even, odd)
+    messages = ((even, 0), (odd, 0))
+    q_messages = ((even, ADJ_SIDE[2] + EY + PLANES), (q_odd, 0))
     r_refs = ((ra_ref, 0), (ra_ref, 1), (rb_ref, 0), (rb_ref, 1))
     rs_refs = ((rsa_ref, 0), (rsa_ref, 1), (rsb_ref, 0), (rsb_ref, 1))
-    tiles, own_tiles, raws = ADJ_SIDE[1], ADJ_OWN[1], ADJ_SIDE[2] + EY
+    tiles, own_tiles = ADJ_SIDE[1], ADJ_OWN[1]
 
     def initial(index, x):
         own = ((ql_ref, 0), (late_ref, 0), (ql_ref, PLANES))[index]
         layout = (
-            ((messages, raws, 4), (messages, tiles, 3)),
+            ((q_messages, 0, 4), (messages, tiles, 3)),
             ((messages, 0, 3), (messages, tiles + 24, 2)),
-            ((messages, raws + PLANES, 4), (messages, tiles + 40, 3)),
+            ((messages, ADJ_SIDE[2] + EY, 4), (messages, tiles + 40, 3)),
         )[index]
         value = widened(own, (late_ref, own_tiles + 32 * index), x, layout, side)
         if index == 1:
@@ -570,7 +572,7 @@
 
     cut_up, cut_down = cut_flags()
     side = sides()
-    messages = (even, odd)
+    messages = ((even, 0), (odd, 0))
     tiles, own_tiles = WAVE_SIDE[1], WAVE_OWN[1]
 
     def initial(index, x):
@@ -710,11 +712,12 @@
         receiver_cells.T, receiver_wave, source_cells.T, source_wave,
     ]
     ways = 1 if lax.axis_size("gy") == 2 else 2
-    wave, ql, t, last_x, last_y, strips, table, receivers, receiver_wave, sources, source_wave, *sends = call(
+    wave, ql, q, t, last_x, last_y, strips, table, receivers, receiver_wave, sources, source_wave, *sends = call(
         load_kernel,
         [
             shape(2 * PLANES, BZ),
             shape(2 * PLANES, BZ),
+            shape(PLANES, BZ),
             shape(PLANES, BZ),
             shape(2 * BY, BZ),
             shape(2 * BX * 8, BZ),
@@ -739,6 +742,7 @@
     other = rotated(strips, "gz", 1)
     corner_up, corner_down = from_sides(sends[ways:], ("gy", "gz"))
     wave = rotated(wave, "gx", half)
+    q_odd = paired(q, True)
     rb, rsb = call(
         late_kernel,
         [shape(2, EX * EY, BZ), shape(2, EY, BZ)],
@@ -768,17 +772,17 @@
     ra, rb = ra.reshape(2, early_planes, EY, BZ), rb.reshape(2, EX, EY, BZ)
     even, odd, second = call(
         adjoint_join_kernel,
-        [shape(ADJ_SIDE[2] + EY + 2 * PLANES, BZ)] * 2 + [shape(8, BZ)],
-        [ql, adj_late, token, wave],
+        [shape(ADJ_SIDE[2] + EY + 2 * PLANES, BZ), shape(ADJ_SIDE[2] + EY + PLANES, BZ), shape(8, BZ)],
+        [ql, adj_late, token, wave, q_odd],
         [],
-        "vvaa",
+        "vvaaa",
     )
     even, odd = paired(even, False), paired(odd, True)
     second = rotated(second, "gz", 1)
     src, src_strip = call(
         source_kernel,
         [shape(STEPS - 1, source_planes * EY, BZ), shape(STEPS - 1, EY, BZ)],
-        [sources, source_wave, second],
+        [sources, source_wave, adj_late],
         [],
         "vva",
         0.5,
@@ -800,10 +804,10 @@
             shape(3, EX, EY, BZ),
             shape(3, EY, BZ),
         ],
-        [ql, adj_late, even, odd, adjoint_end, ra, rsa, rb, rsb, table],
+        [ql, q_odd, adj_late, even, odd, adjoint_end, ra, rsa, rb, rsb, table],
         [pltpu.VMEM((EX, EY, BZ), F32)] * 5
         + [pltpu.VMEM((3, EX, EY, BZ), F32), pltpu.SemaphoreType.DMA],
-        "vvvvhvvvvv",
+        "vvvvvhvvvvv",
         3.9,
     )
     return call(

time: 29.7 us -> 32.5 us (1.094)
  the two profiles are of different devices: /device:TPU:10 before, /device:TPU:0 now
where the time goes in v11:
time: 32.5 us; the launch traced here: 32.3 us
  starting transfers between devices  15 us (46%)
  Pallas kernels  8.68 us (27%)
  waiting for transfers between devices  7.93 us (24%)
  between operations  0.73 us (2%)
    ppermute x5, starting transfers between devices, rotated(): lax.ppermute(array, axis, [((i + offset) % count, i) for i in range(count)])  9.39 us
    pallas_call x9, Pallas kernels, call(): pl.pallas_call(kernel, out_shape=outs, in_specs=[pl.BlockSpec(memory_spac...  8.68 us
    ppermute x5, waiting for transfers between devices, rotated(): lax.ppermute(array, axis, [((i + offset) % count, i) for i in range(count)])  3.6 us
    ppermute x5, starting transfers between devices, paired(): return lax.ppermute(array, 'gx', pairs)  3.43 us
    ppermute x5, waiting for transfers between devices, paired(): return lax.ppermute(array, 'gx', pairs)  3.1 us
    ppermute x2, starting transfers between devices, from_sides(): both = lax.ppermute(sends[0], axes, route(1) + route(-1))  2.14 us
    ppermute x2, waiting for transfers between devices, from_sides(): both = lax.ppermute(sends[0], axes, route(1) + route(-1))  1.24 us
  transfers between devices with their start and end apart: 12, of which 6 were waited for; matrix products, arithmetic and copies ran while one was open for 0% of the time, Pallas kernels for 17%

profile of v11, /device:TPU:0, one launch (start us, length us, event | category | flops | bytes accessed | tf_op | source)
XLA Modules:
  0.0 32.3 jit_solution(16622735648453270565)
XLA Ops:
  0.6 1.3 %shard_map.95 = (f32[256,128]{1,0:T(8,128)S(1)}, f32[256,128]{1,0:T(8,128)S(1)}, f32[128,128]{1,0:T(8,128)S(1)}, f32[128,128]{1,0:T(8,128)S(1)}, f32[64,128]{1,0...) custom-call(f32[4,4,32,128]{3,2,1,0:T(8,128)} %stored_hbm.1, ...), custom_call_target="tpu_custom_call" | custom-call | bytes 5166000 | tf_op jit(solution)/shard_map/pallas_call | solution.py:657
  2.0 4.1 %collective-permute-start = (f32[256,128]{1,0:T(8,128)S(1)}, f32[256,128]{1,0:T(8,128)S(1)}, u32[]{:S(2)}, u32[]{:S(2)}) collective-permute-start(f32[256,128]{1,0:T(8,128)S(1)} %get-tuple-element.35), channel_id=1, source_target_pairs={{8,0},{12,4},{0,8},{4,12},{9,1},{13,5},{1,9},{5,13},{10,2},{14,6},... | collective-permute-start | bytes 393224 | tf_op jit(solution)/shard_map/ppermute | solution.py:693
  6.1 1.5 %collective-permute-start.1 = (f32[160,128]{1,0:T(8,128)S(1)}, f32[160,128]{1,0:T(8,128)S(1)}, u32[]{:S(2)}, u32[]{:S(2)}) collective-permute-start(f32[160,128]{1,0:T(8,128)S(1)} %get-tuple-element.36), channel_id=1, source_target_pairs={{2,0},{0,2},{3,1},{1,3},{6,4},{4,6},{7,5},{5,7},{10,8},{8,10},{11,... | collective-permute-start | bytes 245768 | tf_op jit(solution)/shard_map/ppermute | solution.py:685
  7.5 0.7 %collective-permute-start.6 = (f32[128,128]{1,0:T(8,128)S(1)}, f32[128,128]{1,0:T(8,128)S(1)}, u32[]{:S(2)}, u32[]{:S(2)}) collective-permute-start(f32[128,128]{1,0:T(8,128)S(1)} %get-tuple-element.49), channel_id=1, source_target_pairs={{0,0},{8,4},{4,8},{12,12},{1,1},{9,5},{5,9},{13,13},{2,2},{10,6},{... | collective-permute-start | bytes 196616 | tf_op jit(solution)/shard_map/ppermute | solution.py:702
  8.2 0.1 collective-permute-start.3
  8.3 0.7 %collective-permute-start.2 = (f32[16,128]{1,0:T(8,128)S(1)}, f32[16,128]{1,0:T(8,128)S(1)}, u32[]{:S(2)}, u32[]{:S(2)}) collective-permute-start(f32[16,128]{1,0:T(8,128)S(1)} %get-tuple-element.37), channel_id=1, source_target_pairs={{2,1},{3,0},{0,3},{1,2},{6,5},{7,4},{4,7},{5,6},{10,9},{11,8},{8,1... | collective-permute-start | bytes 24584 | tf_op jit(solution)/shard_map/ppermute | solution.py:685
  8.9 1.2 %shard_map.96 = (f32[2,480,128]{2,1,0:T(8,128)S(1)}, f32[2,40,128]{2,1,0:T(8,128)S(1)}) custom-call(s32[3,1024]{1,0:T(4,128)S(1)} %get-tuple-element.42.receivers, f32[4,1024]{1,0:T(4,128)S(1)} %get-tuple-element.43.receiver_wave), custom_call_target="tpu_custom_call" | custom-call | bytes 4428000 | tf_op jit(solution)/shard_map/pallas_call | solution.py:657
  10.2 1.2 %collective-permute-done.2.corner_up.corner_down = f32[16,128]{1,0:T(8,128)S(1)} collective-permute-done((f32[16,128]{1,0:T(8,128)S(1)}, f32[16,128]{1,0:T(8,128)S(1)}, u32[]{:S(2)}, u32[]{:S(2)}) %collective-permute-start.2) | collective-permute-done | bytes 8224 | tf_op jit(solution)/shard_map/ppermute | solution.py:685
  11.4 0.0 collective-permute-done.3.other_ref
  11.4 0.0 collective-permute-done.1.from_up.from_down
  11.4 0.3 shard_map.97
  11.7 4.3 %collective-permute-start.4 = (f32[168,128]{1,0:T(8,128)S(1)}, f32[168,128]{1,0:T(8,128)S(1)}, u32[]{:S(2)}, u32[]{:S(2)}) collective-permute-start(f32[168,128]{1,0:T(8,128)S(1)} %get-tuple-element.45), channel_id=1, source_target_pairs={{8,0},{12,4},{0,8},{4,12},{9,1},{13,5},{1,9},{5,13},{10,2},{14,6},... | collective-permute-start | bytes 258056 | tf_op jit(solution)/shard_map/ppermute | solution.py:693
  16.1 0.5 %collective-permute-start.5 = (f32[8,128]{1,0:T(8,128)S(1)}, f32[8,128]{1,0:T(8,128)S(1)}, u32[]{:S(2)}, u32[]{:S(2)}) collective-permute-start(f32[8,128]{1,0:T(8,128)S(1)} %get-tuple-element.48), channel_id=1, source_target_pairs={{1,0},{0,1},{3,2},{2,3},{5,4},{4,5},{7,6},{6,7},{9,8},{8,9},{11,10... | collective-permute-start | bytes 12296 | tf_op jit(solution)/shard_map/ppermute | solution.py:693
  16.5 0.0 collective-permute-done.6._c.q_odd
  16.5 0.8 %collective-permute-done.5._a = f32[8,128]{1,0:T(8,128)S(1)} collective-permute-done((f32[8,128]{1,0:T(8,128)S(1)}, f32[8,128]{1,0:T(8,128)S(1)}, u32[]{:S(2)}, u32[]{:S(2)}) %collective-permute-start.5) | collective-permute-done | bytes 4128 | tf_op jit(solution)/shard_map/ppermute | solution.py:693
  17.3 0.0 collective-permute-done._b.wave_ref
  17.4 0.1 collective-permute-start.10
  17.5 0.7 %collective-permute-start.11 = (f32[368,128]{1,0:T(8,128)S(1)}, f32[368,128]{1,0:T(8,128)S(1)}, u32[]{:S(2)}, u32[]{:S(2)}) collective-permute-start(f32[368,128]{1,0:T(8,128)S(1)} %get-tuple-element.55), channel_id=1, source_target_pairs={{0,0},{8,4},{4,8},{12,12},{1,1},{9,5},{5,9},{13,13},{2,2},{10,6},{... | collective-permute-start | bytes 565256 | tf_op jit(solution)/shard_map/ppermute | solution.py:702
  18.1 0.4 %collective-permute-start.7 = (f32[8,128]{1,0:T(8,128)S(1)}, f32[8,128]{1,0:T(8,128)S(1)}, u32[]{:S(2)}, u32[]{:S(2)}) collective-permute-start(f32[8,128]{1,0:T(8,128)S(1)} %get-tuple-element.50), channel_id=1, source_target_pairs={{1,0},{0,1},{3,2},{2,3},{5,4},{4,5},{7,6},{6,7},{9,8},{8,9},{11,10... | collective-permute-start | bytes 12296 | tf_op jit(solution)/shard_map/ppermute | solution.py:693
  18.5 0.8 %collective-permute-done.7._ = f32[8,128]{1,0:T(8,128)S(1)} collective-permute-done((f32[8,128]{1,0:T(8,128)S(1)}, f32[8,128]{1,0:T(8,128)S(1)}, u32[]{:S(2)}, u32[]{:S(2)}) %collective-permute-start.7) | collective-permute-done | bytes 4128 | tf_op jit(solution)/shard_map/ppermute | solution.py:693
  19.4 1.9 %collective-permute-done.4.late_ref = f32[168,128]{1,0:T(8,128)S(1)} collective-permute-done((f32[168,128]{1,0:T(8,128)S(1)}, f32[168,128]{1,0:T(8,128)S(1)}, u32[]{:S(2)}, u32[]{:S(2)}) %collective-permute-start.4) | collective-permute-done | bytes 86048 | tf_op jit(solution)/shard_map/ppermute | solution.py:693
  21.3 0.1 shard_map.99
  21.4 1.4 %collective-permute-start.8 = (f32[344,128]{1,0:T(8,128)S(1)}, f32[344,128]{1,0:T(8,128)S(1)}, u32[]{:S(2)}, u32[]{:S(2)}) collective-permute-start(f32[344,128]{1,0:T(8,128)S(1)} %get-tuple-element.52), channel_id=1, source_target_pairs={{4,0},{0,4},{12,8},{8,12},{5,1},{1,5},{13,9},{9,13},{6,2},{2,6},{1... | collective-permute-start | bytes 528392 | tf_op jit(solution)/shard_map/ppermute | solution.py:702
  22.8 0.7 %collective-permute-start.9 = (f32[344,128]{1,0:T(8,128)S(1)}, f32[344,128]{1,0:T(8,128)S(1)}, u32[]{:S(2)}, u32[]{:S(2)}) collective-permute-start(f32[344,128]{1,0:T(8,128)S(1)} %get-tuple-element.53), channel_id=1, source_target_pairs={{0,0},{8,4},{4,8},{12,12},{1,1},{9,5},{5,9},{13,13},{2,2},{10,6},{... | collective-permute-start | bytes 528392 | tf_op jit(solution)/shard_map/ppermute | solution.py:702
  23.5 1.0 %shard_map.100 = (f32[2,320,128]{2,1,0:T(8,128)S(1)}, f32[2,40,128]{2,1,0:T(8,128)S(1)}) custom-call(s32[3,1024]{1,0:T(4,128)S(1)} %get-tuple-element.42.receivers, f32[4,1024]{1,0:T(4,128)S(1)} %get-tuple-element.43.receiver_wave, f32[304,128]{1,0:T(8,128)S(1)} %get-tuple-element.47.adj_ref._.late_ref), custom_call_target="tpu_custom_call" | custom-call | bytes 3690000 | tf_op jit(solution)/shard_map/pallas_call | solution.py:657
  24.5 0.5 %shard_map.102 = (f32[3,400,128]{2,1,0:T(8,128)S(1)}, f32[3,40,128]{2,1,0:T(8,128)S(1)}) custom-call(s32[3,64]{1,0:T(4,128)S(1)} %get-tuple-element.62.sources, f32[4,64]{1,0:T(4,128)S(1)} %get-tuple-element.63.source_wave, f32[304,128]{1,0:T(8,128)S(1)} %get-tuple-element.47.adj_ref._.late_ref), custom_call_target="tpu_custom_call" | custom-call | bytes 1845000 | tf_op jit(solution)/shard_map/pallas_call | solution.py:657
  25.0 0.0 collective-permute-done.11.odd
  25.0 1.8 %collective-permute-done.10.even = f32[496,128]{1,0:T(8,128)S(1)} collective-permute-done((f32[496,128]{1,0:T(8,128)S(1)}, f32[496,128]{1,0:T(8,128)S(1)}, u32[]{:S(2)}, u32[]{:S(2)}) %collective-permute-start.10) | collective-permute-done | bytes 253984 | tf_op jit(solution)/shard_map/ppermute | solution.py:702
  26.8 2.4 %shard_map.101 = (f32[4,4,32,128]{3,2,1,0:T(8,128)S(1)}, f32[4,4,4,32,128]{4,3,2,1,0:T(8,128)S(1)}, f32[3,12,40,128]{3,2,1,0:T(8,128)S(1)}, f32[3,40,128]{2,1,0:T(8,128)S(1)}) custom-call(f32[256,128]{1,0:T(8,128)S(1)} %get-tuple-element.46.ql_ref, f32[128,128]{1,0:T(8,128)S(1)} %collective-permute-done.6._c.q_odd, ...), custom_call_target="tpu_custom_call" | custom-call | bytes 14391000 | tf_op jit(solution)/shard_map/pallas_call | solution.py:657
  29.2 1.3 %collective-permute-done.8.even = f32[344,128]{1,0:T(8,128)S(1)} collective-permute-done((f32[344,128]{1,0:T(8,128)S(1)}, f32[344,128]{1,0:T(8,128)S(1)}, u32[]{:S(2)}, u32[]{:S(2)}) %collective-permute-start.8) | collective-permute-done | bytes 176160 | tf_op jit(solution)/shard_map/ppermute | solution.py:702
  30.5 0.0 collective-permute-done.9.odd
  30.5 1.8 %shard_map.103 = (f32[2,4,32,128]{3,2,1,0:T(8,128)}, f32[4,4,32,128]{3,2,1,0:T(8,128)}) custom-call(f32[256,128]{1,0:T(8,128)S(1)} %collective-permute-done._b.wave_ref, f32[128,128]{1,0:T(8,128)S(1)} %get-tuple-element.51.own_s_ref, f32[168,128]{1,0:T(8,128)S(1)} %collective-permute-done.4.late_ref, f32[344,128]{1,0:T(8,128)S(1)} %collective-permute-done.8.even, ...), custom_call_target="tpu_custom_call" | custom-call | bytes 9225000 | tf_op jit(solution)/shard_map/pallas_call | solution.py:657
  (1 shorter events, 0.0 us)
Async XLA Ops:
  2.0 15.4 %collective-permute-start = (f32[256,128]{1,0:T(8,128)S(1)}, f32[256,128]{1,0:T(8,128)S(1)}, u32[]{:S(2)}, u32[]{:S(2)}) collective-permute-start(f32[256,128]{1,0:T(8,128)S(1)} %get-tuple-element.35), channel_id=1, source_target_pairs={{8,0},{12,4},{0,8},{4,12},{9,1},{13,5},{1,9},{5,13},{10,2},{14,6},... | collective-permute-start | bytes 393224 | tf_op jit(solution)/shard_map/ppermute | solution.py:693
  6.1 5.4 %collective-permute-start.1 = (f32[160,128]{1,0:T(8,128)S(1)}, f32[160,128]{1,0:T(8,128)S(1)}, u32[]{:S(2)}, u32[]{:S(2)}) collective-permute-start(f32[160,128]{1,0:T(8,128)S(1)} %get-tuple-element.36), channel_id=1, source_target_pairs={{2,0},{0,2},{3,1},{1,3},{6,4},{4,6},{7,5},{5,7},{10,8},{8,10},{11,... | collective-permute-start | bytes 245768 | tf_op jit(solution)/shard_map/ppermute | solution.py:685
  7.5 9.0 %collective-permute-start.6 = (f32[128,128]{1,0:T(8,128)S(1)}, f32[128,128]{1,0:T(8,128)S(1)}, u32[]{:S(2)}, u32[]{:S(2)}) collective-permute-start(f32[128,128]{1,0:T(8,128)S(1)} %get-tuple-element.49), channel_id=1, source_target_pairs={{0,0},{8,4},{4,8},{12,12},{1,1},{9,5},{5,9},{13,13},{2,2},{10,6},{... | collective-permute-start | bytes 196616 | tf_op jit(solution)/shard_map/ppermute | solution.py:702
  8.2 3.2 %collective-permute-start.3 = (f32[96,128]{1,0:T(8,128)S(1)}, f32[96,128]{1,0:T(8,128)S(1)}, u32[]{:S(2)}, u32[]{:S(2)}) collective-permute-start(f32[96,128]{1,0:T(8,128)S(1)} %get-tuple-element.38.strip_ref), channel_id=1, source_target_pairs={{1,0},{0,1},{3,2},{2,3},{5,4},{4,5},{7,6},{6,7},{9,8},{8,9},{11,10... | collective-permute-start | bytes 147464 | tf_op jit(solution)/shard_map/ppermute | solution.py:693
  8.3 3.1 %collective-permute-start.2 = (f32[16,128]{1,0:T(8,128)S(1)}, f32[16,128]{1,0:T(8,128)S(1)}, u32[]{:S(2)}, u32[]{:S(2)}) collective-permute-start(f32[16,128]{1,0:T(8,128)S(1)} %get-tuple-element.37), channel_id=1, source_target_pairs={{2,1},{3,0},{0,3},{1,2},{6,5},{7,4},{4,7},{5,6},{10,9},{11,8},{8,1... | collective-permute-start | bytes 24584 | tf_op jit(solution)/shard_map/ppermute | solution.py:685
  11.7 9.6 %collective-permute-start.4 = (f32[168,128]{1,0:T(8,128)S(1)}, f32[168,128]{1,0:T(8,128)S(1)}, u32[]{:S(2)}, u32[]{:S(2)}) collective-permute-start(f32[168,128]{1,0:T(8,128)S(1)} %get-tuple-element.45), channel_id=1, source_target_pairs={{8,0},{12,4},{0,8},{4,12},{9,1},{13,5},{1,9},{5,13},{10,2},{14,6},... | collective-permute-start | bytes 258056 | tf_op jit(solution)/shard_map/ppermute | solution.py:693
  16.1 1.3 %collective-permute-start.5 = (f32[8,128]{1,0:T(8,128)S(1)}, f32[8,128]{1,0:T(8,128)S(1)}, u32[]{:S(2)}, u32[]{:S(2)}) collective-permute-start(f32[8,128]{1,0:T(8,128)S(1)} %get-tuple-element.48), channel_id=1, source_target_pairs={{1,0},{0,1},{3,2},{2,3},{5,4},{4,5},{7,6},{6,7},{9,8},{8,9},{11,10... | collective-permute-start | bytes 12296 | tf_op jit(solution)/shard_map/ppermute | solution.py:693
  17.4 9.4 %collective-permute-start.10 = (f32[496,128]{1,0:T(8,128)S(1)}, f32[496,128]{1,0:T(8,128)S(1)}, u32[]{:S(2)}, u32[]{:S(2)}) collective-permute-start(f32[496,128]{1,0:T(8,128)S(1)} %get-tuple-element.54), channel_id=1, source_target_pairs={{4,0},{0,4},{12,8},{8,12},{5,1},{1,5},{13,9},{9,13},{6,2},{2,6},{1... | collective-permute-start | bytes 761864 | tf_op jit(solution)/shard_map/ppermute | solution.py:702
  17.5 7.6 %collective-permute-start.11 = (f32[368,128]{1,0:T(8,128)S(1)}, f32[368,128]{1,0:T(8,128)S(1)}, u32[]{:S(2)}, u32[]{:S(2)}) collective-permute-start(f32[368,128]{1,0:T(8,128)S(1)} %get-tuple-element.55), channel_id=1, source_target_pairs={{0,0},{8,4},{4,8},{12,12},{1,1},{9,5},{5,9},{13,13},{2,2},{10,6},{... | collective-permute-start | bytes 565256 | tf_op jit(solution)/shard_map/ppermute | solution.py:702
  18.1 1.2 %collective-permute-start.7 = (f32[8,128]{1,0:T(8,128)S(1)}, f32[8,128]{1,0:T(8,128)S(1)}, u32[]{:S(2)}, u32[]{:S(2)}) collective-permute-start(f32[8,128]{1,0:T(8,128)S(1)} %get-tuple-element.50), channel_id=1, source_target_pairs={{1,0},{0,1},{3,2},{2,3},{5,4},{4,5},{7,6},{6,7},{9,8},{8,9},{11,10... | collective-permute-start | bytes 12296 | tf_op jit(solution)/shard_map/ppermute | solution.py:693
  21.4 9.1 %collective-permute-start.8 = (f32[344,128]{1,0:T(8,128)S(1)}, f32[344,128]{1,0:T(8,128)S(1)}, u32[]{:S(2)}, u32[]{:S(2)}) collective-permute-start(f32[344,128]{1,0:T(8,128)S(1)} %get-tuple-element.52), channel_id=1, source_target_pairs={{4,0},{0,4},{12,8},{8,12},{5,1},{1,5},{13,9},{9,13},{6,2},{2,6},{1... | collective-permute-start | bytes 528392 | tf_op jit(solution)/shard_map/ppermute | solution.py:702
  22.8 7.7 %collective-permute-start.9 = (f32[344,128]{1,0:T(8,128)S(1)}, f32[344,128]{1,0:T(8,128)S(1)}, u32[]{:S(2)}, u32[]{:S(2)}) collective-permute-start(f32[344,128]{1,0:T(8,128)S(1)} %get-tuple-element.53), channel_id=1, source_target_pairs={{0,0},{8,4},{4,8},{12,12},{1,1},{9,5},{5,9},{13,13},{2,2},{10,6},{... | collective-permute-start | bytes 528392 | tf_op jit(solution)/shard_map/ppermute | solution.py:702

commit v12 on v10

--- a/solution.py
+++ b/solution.py
@@ -239,8 +239,7 @@
             target[tiles_end : tiles_end + EY] = strip
 
 
-def adjoint_join_kernel(ql_ref, adj_ref, _a, _b, even_ref, odd_ref, token_ref):
-    token_ref[...] = jnp.zeros((8, BZ), F32)
+def adjoint_join_kernel(ql_ref, adj_ref, _a, _b, even_ref, odd_ref):
     planes_end, x_end, tiles_end = ADJ_OWN
     for target, first in zip((even_ref, odd_ref), pair_planes()):
         base = copy_rows(target, 0, adj_ref, first * BY, 3 * BY)
@@ -252,7 +251,7 @@
         copy_rows(target, base, ql_ref, 0, 2 * PLANES)
 
 
-def join_kernel(wave_ref, late_ref, _, s_ref, even_ref, odd_ref):
+def join_kernel(wave_ref, late_ref, s_ref, even_ref, odd_ref):
     planes_end, x_end, tiles_end = WAVE_OWN
     row, lane = rows((BY, BZ)), lanes((BY, BZ))
     fix_lane = late_ref[tiles_end : tiles_end + BY]
@@ -502,18 +501,23 @@
     )
     t_s = t_s - strip_below(own_strip, messages, ADJ_SIDE[2], 3, side)
     stiff_s, buoy_s, damp_s = coefficients(label_s, table_ref)
+    scale_s = stiff_s * damp_s
     coef_strip_ref[0], coef_strip_ref[1], coef_strip_ref[2] = stiff_s, buoy_s, damp_s
     w_copy.wait()
 
     for step in range(1, STEPS + 1):
-        k = STEPS - step
-        rs_ref, place = rs_refs[k]
+        rs_ref, place = rs_refs[STEPS - step]
         q_s = q_s + rs_ref[place]
-        u_s = stiff_s * damp_s * q_s
+        u_s = scale_s * q_s
         flux_s, spread = strip_flux(u_s, buoy_s)
         t_s = t_s + spread
         q_s = damp_s * q_s + t_s
         edges = cut_edges(u_s, flux_s, cut_up, cut_down)
+        for x in range(step, EX - step):
+            edge_ref[step - 1, x] = plane_edge(edges, x)
+
+    for step in range(1, STEPS + 1):
+        k = STEPS - step
         r_ref, place = r_refs[k]
         r_first = (EARLY_PLANES if k < 2 else LATE_PLANES)[0]
 
@@ -521,14 +525,12 @@
             q = (initial(0, x) if step == 1 else q_ref[x]) + r_ref[place, x - r_first]
             q_ref[x] = q
             u_ref[x] = scale_ref[x] * q
-            if step <= x < EX - step:
-                edge_ref[x] = plane_edge(edges, x)
 
         for x in range(step - 1, EX - step):
             u, buoyancy = u_ref[x], coef_ref[1, x]
             slopes = [u_ref[x + 1] - u]
             if x >= step:
-                slopes += [y_up(u) - u, z_up(u, edge_ref[x]) - u]
+                slopes += [y_up(u) - u, z_up(u, edge_ref[step - 1, x]) - u]
             for axis, slope in enumerate(slopes):
                 flux_ref[axis, x] = buoyancy * slope
             if BX <= x < 2 * BX:
@@ -540,7 +542,7 @@
         for x in range(step, EX - step):
             flux_y, flux_z = flux_ref[1, x], flux_ref[2, x]
             spread = (flux_ref[0, x] - flux_ref[0, x - 1]) + (flux_y - y_down(flux_y))
-            spread = spread + (flux_z - z_down(flux_z, edge_ref[x]))
+            spread = spread + (flux_z - z_down(flux_z, edge_ref[step - 1, x]))
             damped = coef_ref[2, x] * q_ref[x]
             t = (initial(1, x) if step == 1 else t_ref[x]) + spread
             if BX <= x < 2 * BX:
@@ -592,24 +594,23 @@
     stiff_s, buoy_s, damp_s = coef_strip_ref[0], coef_strip_ref[1], coef_strip_ref[2]
 
     for step in range(1, STEPS + 1):
-        k = step - 1
         flux_s, spread = strip_flux(p_s, buoy_s)
         edges = cut_edges(p_s, flux_s, cut_up, cut_down)
         if step < STEPS:
             s_s = s_s - spread
-            p_s = damp_s * (p_s - stiff_s * s_s) + ss_ref[k]
-
-        for x in range(step - 1, EX - step + 1):
-            if step == 1:
-                p_ref[x] = initial(0, x)
-            if step <= x < EX - step:
-                edge_ref[x] = plane_edge(edges, x)
-
+            p_s = damp_s * (p_s - stiff_s * s_s) + ss_ref[step - 1]
+        for x in range(step, EX - step):
+            edge_ref[step - 1, x] = plane_edge(edges, x)
+    for x in range(EX):
+        p_ref[x] = initial(0, x)
+
+    for step in range(1, STEPS + 1):
+        k = step - 1
         for x in range(step - 1, EX - step):
             p, buoyancy = p_ref[x], coef_ref[1, x]
             slopes = [p_ref[x + 1] - p]
             if x >= step:
-                slopes += [y_up(p) - p, z_up(p, edge_ref[x]) - p]
+                slopes += [y_up(p) - p, z_up(p, edge_ref[step - 1, x]) - p]
             for axis, slope in enumerate(slopes):
                 flux_ref[axis, x] = buoyancy * slope
             if BX <= x < 2 * BX:
@@ -624,7 +625,7 @@
         for x in range(step, EX - step):
             flux_y, flux_z = flux_ref[1, x], flux_ref[2, x]
             spread = (flux_ref[0, x] - flux_ref[0, x - 1]) + (flux_y - y_down(flux_y))
-            spread = spread + (flux_z - z_down(flux_z, edge_ref[x]))
+            spread = spread + (flux_z - z_down(flux_z, edge_ref[step - 1, x]))
             spread = (initial(1, x) if step == 1 else spread_ref[x]) - spread
             if step < STEPS:
                 spread_ref[x] = spread
@@ -766,19 +767,18 @@
         1.0,
     )
     ra, rb = ra.reshape(2, early_planes, EY, BZ), rb.reshape(2, EX, EY, BZ)
-    even, odd, second = call(
+    even, odd = call(
         adjoint_join_kernel,
-        [shape(ADJ_SIDE[2] + EY + 2 * PLANES, BZ)] * 2 + [shape(8, BZ)],
+        [shape(ADJ_SIDE[2] + EY + 2 * PLANES, BZ)] * 2,
         [ql, adj_late, token, wave],
         [],
         "vvaa",
     )
     even, odd = paired(even, False), paired(odd, True)
-    second = rotated(second, "gz", 1)
     src, src_strip = call(
         source_kernel,
         [shape(STEPS - 1, source_planes * EY, BZ), shape(STEPS - 1, EY, BZ)],
-        [sources, source_wave, second],
+        [sources, source_wave, adj_late],
         [],
         "vva",
         0.5,
@@ -787,9 +787,9 @@
     own_s, wave_even, wave_odd = call(
         join_kernel,
         [shape(PLANES, BZ)] + [shape(WAVE_SIDE[2] + EY, BZ)] * 2,
-        [wave, late, second],
+        [wave, late],
         [],
-        "vva",
+        "vv",
     )
     wave_even, wave_odd = paired(wave_even, False), paired(wave_odd, True)
     adjoint_out, hist, coef, coef_strip = call(
@@ -801,8 +801,12 @@
             shape(3, EY, BZ),
         ],
         [ql, adj_late, even, odd, adjoint_end, ra, rsa, rb, rsb, table],
-        [pltpu.VMEM((EX, EY, BZ), F32)] * 5
-        + [pltpu.VMEM((3, EX, EY, BZ), F32), pltpu.SemaphoreType.DMA],
+        [pltpu.VMEM((EX, EY, BZ), F32)] * 4
+        + [
+            pltpu.VMEM((STEPS, EX, EY, BZ), F32),
+            pltpu.VMEM((3, EX, EY, BZ), F32),
+            pltpu.SemaphoreType.DMA,
+        ],
         "vvvvhvvvvv",
         3.9,
     )
@@ -813,8 +817,9 @@
             wave, own_s, late, wave_even, wave_odd, coef, coef_strip, src, src_strip, hist,
             adjoint_out,
         ],
-        [pltpu.VMEM((EX, EY, BZ), F32)] * 3
+        [pltpu.VMEM((EX, EY, BZ), F32)] * 2
         + [
+            pltpu.VMEM((STEPS, EX, EY, BZ), F32),
             pltpu.VMEM((3, EX, EY, BZ), F32),
             pltpu.VMEM((2, BX, BY, BZ), F32),
             pltpu.SemaphoreType.DMA((2 + BX,)),

time: 29.7 us -> 28.8 us (0.970)
  the two profiles are of different devices: /device:TPU:10 before, /device:TPU:18 now
where the time goes in v12:
time: 28.8 us; the launch traced here: 28.6 us
  starting transfers between devices  14.5 us (50%)
  Pallas kernels  8.68 us (30%)
  waiting for transfers between devices  4.63 us (16%)
  between operations  0.74 us (3%)
    ppermute x4, starting transfers between devices, paired(): return lax.ppermute(array, 'gx', pairs)  9.29 us
    pallas_call x9, Pallas kernels, call(): pl.pallas_call(kernel, out_shape=outs, in_specs=[pl.BlockSpec(memory_spac...  8.68 us
    ppermute x4, starting transfers between devices, rotated(): lax.ppermute(array, axis, [((i + offset) % count, i) for i in range(count)])  3.11 us
    ppermute x4, waiting for transfers between devices, paired(): return lax.ppermute(array, 'gx', pairs)  2.42 us
    ppermute x2, starting transfers between devices, from_sides(): both = lax.ppermute(sends[0], axes, route(1) + route(-1))  2.14 us
    ppermute x4, waiting for transfers between devices, rotated(): lax.ppermute(array, axis, [((i + offset) % count, i) for i in range(count)])  1.17 us
    ppermute x2, waiting for transfers between devices, from_sides(): both = lax.ppermute(sends[0], axes, route(1) + route(-1))  1.04 us
  transfers between devices with their start and end apart: 10, of which 4 were waited for; matrix products, arithmetic and copies ran while one was open for 0% of the time, Pallas kernels for 19%

profile of v12, /device:TPU:18, one launch (start us, length us, event | category | flops | bytes accessed | tf_op | source)
XLA Modules:
  0.0 28.6 jit_solution(4828223792175430555)
XLA Ops:
  0.6 1.3 %shard_map.95 = (f32[256,128]{1,0:T(8,128)S(1)}, f32[256,128]{1,0:T(8,128)S(1)}, f32[128,128]{1,0:T(8,128)S(1)}, f32[64,128]{1,0:T(8,128)S(1)}, f32[64,128]{1,0:...) custom-call(f32[4,4,32,128]{3,2,1,0:T(8,128)} %stored_hbm.1, ...), custom_call_target="tpu_custom_call" | custom-call | bytes 5166000 | tf_op jit(solution)/shard_map/pallas_call | solution.py:656
  2.0 0.4 %collective-permute-start = (f32[256,128]{1,0:T(8,128)S(1)}, f32[256,128]{1,0:T(8,128)S(1)}, u32[]{:S(2)}, u32[]{:S(2)}) collective-permute-start(f32[256,128]{1,0:T(8,128)S(1)} %get-tuple-element.33), channel_id=1, source_target_pairs={{8,0},{12,4},{0,8},{4,12},{9,1},{13,5},{1,9},{5,13},{10,2},{14,6},... | collective-permute-start | bytes 393224 | tf_op jit(solution)/shard_map/ppermute | solution.py:692
  2.4 0.3 collective-permute-start.1
  2.6 0.0 collective-permute-start.3
  2.6 1.9 %collective-permute-start.2 = (f32[16,128]{1,0:T(8,128)S(1)}, f32[16,128]{1,0:T(8,128)S(1)}, u32[]{:S(2)}, u32[]{:S(2)}) collective-permute-start(f32[16,128]{1,0:T(8,128)S(1)} %get-tuple-element.35), channel_id=1, source_target_pairs={{2,1},{3,0},{0,3},{1,2},{6,5},{7,4},{4,7},{5,6},{10,9},{11,8},{8,1... | collective-permute-start | bytes 24584 | tf_op jit(solution)/shard_map/ppermute | solution.py:684
  4.5 1.2 %shard_map.96 = (f32[2,480,128]{2,1,0:T(8,128)S(1)}, f32[2,40,128]{2,1,0:T(8,128)S(1)}) custom-call(s32[3,1024]{1,0:T(4,128)S(1)} %get-tuple-element.40.receivers, f32[4,1024]{1,0:T(4,128)S(1)} %get-tuple-element.41.receiver_wave), custom_call_target="tpu_custom_call" | custom-call | bytes 4428000 | tf_op jit(solution)/shard_map/pallas_call | solution.py:656
  5.8 0.1 collective-permute-done.2.corner_up.corner_down
  5.9 0.0 collective-permute-done.3.other_ref
  5.9 0.9 %collective-permute-done.1.from_up.from_down = f32[160,128]{1,0:T(8,128)S(1)} collective-permute-done((f32[160,128]{1,0:T(8,128)S(1)}, f32[160,128]{1,0:T(8,128)S(1)}, u32[]{:S(2)}, u32[]{:S(2)}) %collective-permute-start.1) | collective-permute-done | bytes 81952 | tf_op jit(solution)/shard_map/ppermute | solution.py:684
  6.8 0.3 shard_map.97
  7.1 2.7 %collective-permute-start.4 = (f32[168,128]{1,0:T(8,128)S(1)}, f32[168,128]{1,0:T(8,128)S(1)}, u32[]{:S(2)}, u32[]{:S(2)}) collective-permute-start(f32[168,128]{1,0:T(8,128)S(1)} %get-tuple-element.43), channel_id=1, source_target_pairs={{8,0},{12,4},{0,8},{4,12},{9,1},{13,5},{1,9},{5,13},{10,2},{14,6},... | collective-permute-start | bytes 258056 | tf_op jit(solution)/shard_map/ppermute | solution.py:692
  9.8 0.0 collective-permute-start.7
  9.8 1.2 %collective-permute-done.7._a = f32[8,128]{1,0:T(8,128)S(1)} collective-permute-done((f32[8,128]{1,0:T(8,128)S(1)}, f32[8,128]{1,0:T(8,128)S(1)}, u32[]{:S(2)}, u32[]{:S(2)}) %collective-permute-start.7) | collective-permute-done | bytes 4128 | tf_op jit(solution)/shard_map/ppermute | solution.py:692
  10.9 0.0 collective-permute-done.wave_ref._b
  11.0 3.4 %collective-permute-start.8 = (f32[496,128]{1,0:T(8,128)S(1)}, f32[496,128]{1,0:T(8,128)S(1)}, u32[]{:S(2)}, u32[]{:S(2)}) collective-permute-start(f32[496,128]{1,0:T(8,128)S(1)} %get-tuple-element.50), channel_id=1, source_target_pairs={{4,0},{0,4},{12,8},{8,12},{5,1},{1,5},{13,9},{9,13},{6,2},{2,6},{1... | collective-permute-start | bytes 761864 | tf_op jit(solution)/shard_map/ppermute | solution.py:701
  14.4 1.9 %collective-permute-start.9 = (f32[496,128]{1,0:T(8,128)S(1)}, f32[496,128]{1,0:T(8,128)S(1)}, u32[]{:S(2)}, u32[]{:S(2)}) collective-permute-start(f32[496,128]{1,0:T(8,128)S(1)} %get-tuple-element.51), channel_id=1, source_target_pairs={{0,0},{8,4},{4,8},{12,12},{1,1},{9,5},{5,9},{13,13},{2,2},{10,6},{... | collective-permute-start | bytes 761864 | tf_op jit(solution)/shard_map/ppermute | solution.py:701
  16.3 0.0 collective-permute-done.4.late_ref
  16.3 0.1 shard_map.98
  16.4 0.1 collective-permute-start.5
  16.5 3.9 %collective-permute-start.6 = (f32[344,128]{1,0:T(8,128)S(1)}, f32[344,128]{1,0:T(8,128)S(1)}, u32[]{:S(2)}, u32[]{:S(2)}) collective-permute-start(f32[344,128]{1,0:T(8,128)S(1)} %get-tuple-element.46), channel_id=1, source_target_pairs={{0,0},{8,4},{4,8},{12,12},{1,1},{9,5},{5,9},{13,13},{2,2},{10,6},{... | collective-permute-start | bytes 528392 | tf_op jit(solution)/shard_map/ppermute | solution.py:701
  20.4 1.0 %shard_map.100 = (f32[2,320,128]{2,1,0:T(8,128)S(1)}, f32[2,40,128]{2,1,0:T(8,128)S(1)}) custom-call(s32[3,1024]{1,0:T(4,128)S(1)} %get-tuple-element.40.receivers, f32[4,1024]{1,0:T(4,128)S(1)} %get-tuple-element.41.receiver_wave, f32[304,128]{1,0:T(8,128)S(1)} %get-tuple-element.48.adj_ref._.late_ref), custom_call_target="tpu_custom_call" | custom-call | bytes 3690000 | tf_op jit(solution)/shard_map/pallas_call | solution.py:656
  21.4 0.6 %shard_map.102 = (f32[3,400,128]{2,1,0:T(8,128)S(1)}, f32[3,40,128]{2,1,0:T(8,128)S(1)}) custom-call(s32[3,64]{1,0:T(4,128)S(1)} %get-tuple-element.58.sources, f32[4,64]{1,0:T(4,128)S(1)} %get-tuple-element.59.source_wave, f32[304,128]{1,0:T(8,128)S(1)} %get-tuple-element.48.adj_ref._.late_ref), custom_call_target="tpu_custom_call" | custom-call | bytes 1845000 | tf_op jit(solution)/shard_map/pallas_call | solution.py:656
  22.0 0.0 collective-permute-done.8.even
  22.0 2.4 %collective-permute-done.9.odd = f32[496,128]{1,0:T(8,128)S(1)} collective-permute-done((f32[496,128]{1,0:T(8,128)S(1)}, f32[496,128]{1,0:T(8,128)S(1)}, u32[]{:S(2)}, u32[]{:S(2)}) %collective-permute-start.9) | collective-permute-done | bytes 253984 | tf_op jit(solution)/shard_map/ppermute | solution.py:701
  24.4 2.3 %shard_map.101 = (f32[4,4,32,128]{3,2,1,0:T(8,128)S(1)}, f32[4,4,4,32,128]{4,3,2,1,0:T(8,128)S(1)}, f32[3,12,40,128]{3,2,1,0:T(8,128)S(1)}, f32[3,40,128]{2,1,0:T(8,128)S(1)}) custom-call(f32[256,128]{1,0:T(8,128)S(1)} %get-tuple-element.47.ql_ref, f32[304,128]{1,0:T(8,128)S(1)} %get-tuple-element.48.adj_ref._.late_ref, ...), custom_call_target="tpu_custom_call" | custom-call | bytes 14391000 | tf_op jit(solution)/shard_map/pallas_call | solution.py:656
  26.8 0.0 collective-permute-done.5.even
  26.8 0.0 collective-permute-done.6.odd
  26.8 1.8 %shard_map.103 = (f32[2,4,32,128]{3,2,1,0:T(8,128)}, f32[4,4,32,128]{3,2,1,0:T(8,128)}) custom-call(f32[256,128]{1,0:T(8,128)S(1)} %collective-permute-done.wave_ref._b, f32[128,128]{1,0:T(8,128)S(1)} %get-tuple-element.44.own_s_ref, f32[168,128]{1,0:T(8,128)S(1)} %collective-permute-done.4.late_ref, f32[344,128]{1,0:T(8,128)S(1)} %collective-permute-done.5.even, ...), custom_call_target="tpu_custom_call" | custom-call | bytes 9225000 | tf_op jit(solution)/shard_map/pallas_call | solution.py:656
  (1 shorter events, 0.0 us)
Async XLA Ops:
  2.0 9.0 %collective-permute-start = (f32[256,128]{1,0:T(8,128)S(1)}, f32[256,128]{1,0:T(8,128)S(1)}, u32[]{:S(2)}, u32[]{:S(2)}) collective-permute-start(f32[256,128]{1,0:T(8,128)S(1)} %get-tuple-element.33), channel_id=1, source_target_pairs={{8,0},{12,4},{0,8},{4,12},{9,1},{13,5},{1,9},{5,13},{10,2},{14,6},... | collective-permute-start | bytes 393224 | tf_op jit(solution)/shard_map/ppermute | solution.py:692
  2.4 4.4 %collective-permute-start.1 = (f32[160,128]{1,0:T(8,128)S(1)}, f32[160,128]{1,0:T(8,128)S(1)}, u32[]{:S(2)}, u32[]{:S(2)}) collective-permute-start(f32[160,128]{1,0:T(8,128)S(1)} %get-tuple-element.34), channel_id=1, source_target_pairs={{2,0},{0,2},{3,1},{1,3},{6,4},{4,6},{7,5},{5,7},{10,8},{8,10},{11,... | collective-permute-start | bytes 245768 | tf_op jit(solution)/shard_map/ppermute | solution.py:684
  2.6 3.2 %collective-permute-start.3 = (f32[96,128]{1,0:T(8,128)S(1)}, f32[96,128]{1,0:T(8,128)S(1)}, u32[]{:S(2)}, u32[]{:S(2)}) collective-permute-start(f32[96,128]{1,0:T(8,128)S(1)} %get-tuple-element.36.strip_ref), channel_id=1, source_target_pairs={{1,0},{0,1},{3,2},{2,3},{5,4},{4,5},{7,6},{6,7},{9,8},{8,9},{11,10... | collective-permute-start | bytes 147464 | tf_op jit(solution)/shard_map/ppermute | solution.py:692
  2.6 3.2 %collective-permute-start.2 = (f32[16,128]{1,0:T(8,128)S(1)}, f32[16,128]{1,0:T(8,128)S(1)}, u32[]{:S(2)}, u32[]{:S(2)}) collective-permute-start(f32[16,128]{1,0:T(8,128)S(1)} %get-tuple-element.35), channel_id=1, source_target_pairs={{2,1},{3,0},{0,3},{1,2},{6,5},{7,4},{4,7},{5,6},{10,9},{11,8},{8,1... | collective-permute-start | bytes 24584 | tf_op jit(solution)/shard_map/ppermute | solution.py:684
  7.1 9.2 %collective-permute-start.4 = (f32[168,128]{1,0:T(8,128)S(1)}, f32[168,128]{1,0:T(8,128)S(1)}, u32[]{:S(2)}, u32[]{:S(2)}) collective-permute-start(f32[168,128]{1,0:T(8,128)S(1)} %get-tuple-element.43), channel_id=1, source_target_pairs={{8,0},{12,4},{0,8},{4,12},{9,1},{13,5},{1,9},{5,13},{10,2},{14,6},... | collective-permute-start | bytes 258056 | tf_op jit(solution)/shard_map/ppermute | solution.py:692
  9.8 1.2 %collective-permute-start.7 = (f32[8,128]{1,0:T(8,128)S(1)}, f32[8,128]{1,0:T(8,128)S(1)}, u32[]{:S(2)}, u32[]{:S(2)}) collective-permute-start(f32[8,128]{1,0:T(8,128)S(1)} %get-tuple-element.49), channel_id=1, source_target_pairs={{1,0},{0,1},{3,2},{2,3},{5,4},{4,5},{7,6},{6,7},{9,8},{8,9},{11,10... | collective-permute-start | bytes 12296 | tf_op jit(solution)/shard_map/ppermute | solution.py:692
  11.0 11.0 %collective-permute-start.8 = (f32[496,128]{1,0:T(8,128)S(1)}, f32[496,128]{1,0:T(8,128)S(1)}, u32[]{:S(2)}, u32[]{:S(2)}) collective-permute-start(f32[496,128]{1,0:T(8,128)S(1)} %get-tuple-element.50), channel_id=1, source_target_pairs={{4,0},{0,4},{12,8},{8,12},{5,1},{1,5},{13,9},{9,13},{6,2},{2,6},{1... | collective-permute-start | bytes 761864 | tf_op jit(solution)/shard_map/ppermute | solution.py:701
  14.4 10.1 %collective-permute-start.9 = (f32[496,128]{1,0:T(8,128)S(1)}, f32[496,128]{1,0:T(8,128)S(1)}, u32[]{:S(2)}, u32[]{:S(2)}) collective-permute-start(f32[496,128]{1,0:T(8,128)S(1)} %get-tuple-element.51), channel_id=1, source_target_pairs={{0,0},{8,4},{4,8},{12,12},{1,1},{9,5},{5,9},{13,13},{2,2},{10,6},{... | collective-permute-start | bytes 761864 | tf_op jit(solution)/shard_map/ppermute | solution.py:701
  16.4 10.4 %collective-permute-start.5 = (f32[344,128]{1,0:T(8,128)S(1)}, f32[344,128]{1,0:T(8,128)S(1)}, u32[]{:S(2)}, u32[]{:S(2)}) collective-permute-start(f32[344,128]{1,0:T(8,128)S(1)} %get-tuple-element.45), channel_id=1, source_target_pairs={{4,0},{0,4},{12,8},{8,12},{5,1},{1,5},{13,9},{9,13},{6,2},{2,6},{1... | collective-permute-start | bytes 528392 | tf_op jit(solution)/shard_map/ppermute | solution.py:701
  16.5 10.3 %collective-permute-start.6 = (f32[344,128]{1,0:T(8,128)S(1)}, f32[344,128]{1,0:T(8,128)S(1)}, u32[]{:S(2)}, u32[]{:S(2)}) collective-permute-start(f32[344,128]{1,0:T(8,128)S(1)} %get-tuple-element.46), channel_id=1, source_target_pairs={{0,0},{8,4},{4,8},{12,12},{1,1},{9,5},{5,9},{13,13},{2,2},{10,6},{... | collective-permute-start | bytes 528392 | tf_op jit(solution)/shard_map/ppermute | solution.py:701

commit v13 on v12

--- a/solution.py
+++ b/solution.py
@@ -153,9 +153,8 @@
 def merge_kernel(
     from_up, from_down, corner_up, corner_down, strip_ref, other_ref,
     t_ref, last_x_ref, last_y_ref, _,
-    wave_ref, adj_ref, token_ref,
+    wave_ref, adj_ref,
 ):
-    token_ref[...] = jnp.zeros((8, BZ), F32)
     gy = lax.axis_index("gy")
     tile_row = rows((8, BZ))
     row, lane = rows((BY, BZ)), lanes((BY, BZ))
@@ -239,7 +238,7 @@
             target[tiles_end : tiles_end + EY] = strip
 
 
-def adjoint_join_kernel(ql_ref, adj_ref, _a, _b, even_ref, odd_ref):
+def adjoint_join_kernel(ql_ref, adj_ref, _, even_ref, odd_ref):
     planes_end, x_end, tiles_end = ADJ_OWN
     for target, first in zip((even_ref, odd_ref), pair_planes()):
         base = copy_rows(target, 0, adj_ref, first * BY, 3 * BY)
@@ -749,15 +748,14 @@
         1.2,
     )
     early_planes, source_planes = (last - first for first, last in (EARLY_PLANES, SOURCE_PLANES))
-    late, adj_late, token = call(
+    late, adj_late = call(
         merge_kernel,
-        [shape(WAVE_FIX + 24, BZ), shape(ADJ_OWN[2] + EY, BZ), shape(8, BZ)],
+        [shape(WAVE_FIX + 24, BZ), shape(ADJ_OWN[2] + EY, BZ)],
         [from_up, from_down, corner_up, corner_down, strips, other, t, last_x, last_y, rsb],
         [],
         "vvvvvvvvva",
     )
     late = rotated(late, "gx", half)
-    token = rotated(token, "gz", 1)
     ra, rsa = call(
         early_kernel,
         [shape(2, early_planes * EY, BZ), shape(2, EY, BZ)],
@@ -770,9 +768,9 @@
     even, odd = call(
         adjoint_join_kernel,
         [shape(ADJ_SIDE[2] + EY + 2 * PLANES, BZ)] * 2,
-        [ql, adj_late, token, wave],
+        [ql, adj_late, wave],
         [],
-        "vvaa",
+        "vva",
     )
     even, odd = paired(even, False), paired(odd, True)
     src, src_strip = call(

time: 28.8 us -> 28.8 us (level)
  starting transfers between devices: 14.5 us -> 15.7 us
  waiting for transfers between devices: 4.63 us -> 3.47 us
    ppermute x4, starting transfers between devices: 9.29 us -> 10.5 us  [paired(): return lax.ppermute(array, 'gx', pairs)]
    ppermute x4 -> x3, waiting for transfers between devices: 1.17 us -> 0.01 us  [rotated(): lax.ppermute(array, axis, [((i + offset) % count, i) for i in range(count)])]
    ppermute x4 -> x3, starting transfers between devices: 3.11 us -> 3.11 us  [rotated(): lax.ppermute(array, axis, [((i + offset) % count, i) for i in range(count)])]
  transfers between devices with their start and end apart: 10 -> 9, of which waited for: 4 -> 3; matrix products, arithmetic and copies ran while one was open for 0% -> 0% of each run, Pallas kernels for 19% -> 19%
where the time goes in v13:
time: 28.8 us; the launch traced here: 28.6 us
  starting transfers between devices  15.7 us (55%)
  Pallas kernels  8.68 us (30%)
  waiting for transfers between devices  3.47 us (12%)
  between operations  0.73 us (3%)
    ppermute x4, starting transfers between devices, paired(): return lax.ppermute(array, 'gx', pairs)  10.5 us
    pallas_call x9, Pallas kernels, call(): pl.pallas_call(kernel, out_shape=outs, in_specs=[pl.BlockSpec(memory_spac...  8.68 us
    ppermute x3, starting transfers between devices, rotated(): lax.ppermute(array, axis, [((i + offset) % count, i) for i in range(count)])  3.11 us
    ppermute x4, waiting for transfers between devices, paired(): return lax.ppermute(array, 'gx', pairs)  2.42 us
    ppermute x2, starting transfers between devices, from_sides(): both = lax.ppermute(sends[0], axes, route(1) + route(-1))  2.14 us
    ppermute x2, waiting for transfers between devices, from_sides(): both = lax.ppermute(sends[0], axes, route(1) + route(-1))  1.04 us
  transfers between devices with their start and end apart: 9, of which 3 were waited for; matrix products, arithmetic and copies ran while one was open for 0% of the time, Pallas kernels for 19%

profile of v13, /device:TPU:18, one launch (start us, length us, event | category | flops | bytes accessed | tf_op | source)
XLA Modules:
  0.0 28.6 jit_solution(8861859038154933174)
XLA Ops:
  0.6 1.3 %shard_map.95 = (f32[256,128]{1,0:T(8,128)S(1)}, f32[256,128]{1,0:T(8,128)S(1)}, f32[128,128]{1,0:T(8,128)S(1)}, f32[64,128]{1,0:T(8,128)S(1)}, f32[64,128]{1,0:...) custom-call(f32[4,4,32,128]{3,2,1,0:T(8,128)} %stored_hbm.1, ...), custom_call_target="tpu_custom_call" | custom-call | bytes 5166000 | tf_op jit(solution)/shard_map/pallas_call | solution.py:655
  2.0 0.4 %collective-permute-start = (f32[256,128]{1,0:T(8,128)S(1)}, f32[256,128]{1,0:T(8,128)S(1)}, u32[]{:S(2)}, u32[]{:S(2)}) collective-permute-start(f32[256,128]{1,0:T(8,128)S(1)} %get-tuple-element.32), channel_id=1, source_target_pairs={{8,0},{12,4},{0,8},{4,12},{9,1},{13,5},{1,9},{5,13},{10,2},{14,6},... | collective-permute-start | bytes 393224 | tf_op jit(solution)/shard_map/ppermute | solution.py:691
  2.4 0.3 collective-permute-start.1
  2.6 0.0 collective-permute-start.3
  2.6 1.9 %collective-permute-start.2 = (f32[16,128]{1,0:T(8,128)S(1)}, f32[16,128]{1,0:T(8,128)S(1)}, u32[]{:S(2)}, u32[]{:S(2)}) collective-permute-start(f32[16,128]{1,0:T(8,128)S(1)} %get-tuple-element.34), channel_id=1, source_target_pairs={{2,1},{3,0},{0,3},{1,2},{6,5},{7,4},{4,7},{5,6},{10,9},{11,8},{8,1... | collective-permute-start | bytes 24584 | tf_op jit(solution)/shard_map/ppermute | solution.py:683
  4.5 1.2 %shard_map.96 = (f32[2,480,128]{2,1,0:T(8,128)S(1)}, f32[2,40,128]{2,1,0:T(8,128)S(1)}) custom-call(s32[3,1024]{1,0:T(4,128)S(1)} %get-tuple-element.39.receivers, f32[4,1024]{1,0:T(4,128)S(1)} %get-tuple-element.40.receiver_wave), custom_call_target="tpu_custom_call" | custom-call | bytes 4428000 | tf_op jit(solution)/shard_map/pallas_call | solution.py:655
  5.8 0.1 collective-permute-done.2.corner_up.corner_down
  5.9 0.0 collective-permute-done.3.other_ref
  5.9 0.9 %collective-permute-done.1.from_up.from_down = f32[160,128]{1,0:T(8,128)S(1)} collective-permute-done((f32[160,128]{1,0:T(8,128)S(1)}, f32[160,128]{1,0:T(8,128)S(1)}, u32[]{:S(2)}, u32[]{:S(2)}) %collective-permute-start.1) | collective-permute-done | bytes 81952 | tf_op jit(solution)/shard_map/ppermute | solution.py:683
  6.8 0.3 shard_map.97
  7.1 2.7 %collective-permute-start.4 = (f32[168,128]{1,0:T(8,128)S(1)}, f32[168,128]{1,0:T(8,128)S(1)}, u32[]{:S(2)}, u32[]{:S(2)}) collective-permute-start(f32[168,128]{1,0:T(8,128)S(1)} %get-tuple-element.42), channel_id=1, source_target_pairs={{8,0},{12,4},{0,8},{4,12},{9,1},{13,5},{1,9},{5,13},{10,2},{14,6},... | collective-permute-start | bytes 258056 | tf_op jit(solution)/shard_map/ppermute | solution.py:691
  9.8 0.0 collective-permute-done.wave_ref._
  9.8 4.6 %collective-permute-start.7 = (f32[496,128]{1,0:T(8,128)S(1)}, f32[496,128]{1,0:T(8,128)S(1)}, u32[]{:S(2)}, u32[]{:S(2)}) collective-permute-start(f32[496,128]{1,0:T(8,128)S(1)} %get-tuple-element.48), channel_id=1, source_target_pairs={{4,0},{0,4},{12,8},{8,12},{5,1},{1,5},{13,9},{9,13},{6,2},{2,6},{1... | collective-permute-start | bytes 761864 | tf_op jit(solution)/shard_map/ppermute | solution.py:700
  14.4 1.9 %collective-permute-start.8 = (f32[496,128]{1,0:T(8,128)S(1)}, f32[496,128]{1,0:T(8,128)S(1)}, u32[]{:S(2)}, u32[]{:S(2)}) collective-permute-start(f32[496,128]{1,0:T(8,128)S(1)} %get-tuple-element.49), channel_id=1, source_target_pairs={{0,0},{8,4},{4,8},{12,12},{1,1},{9,5},{5,9},{13,13},{2,2},{10,6},{... | collective-permute-start | bytes 761864 | tf_op jit(solution)/shard_map/ppermute | solution.py:700
  16.3 0.0 collective-permute-done.4.late_ref
  16.3 0.1 shard_map.98
  16.4 0.1 collective-permute-start.5
  16.5 3.9 %collective-permute-start.6 = (f32[344,128]{1,0:T(8,128)S(1)}, f32[344,128]{1,0:T(8,128)S(1)}, u32[]{:S(2)}, u32[]{:S(2)}) collective-permute-start(f32[344,128]{1,0:T(8,128)S(1)} %get-tuple-element.45), channel_id=1, source_target_pairs={{0,0},{8,4},{4,8},{12,12},{1,1},{9,5},{5,9},{13,13},{2,2},{10,6},{... | collective-permute-start | bytes 528392 | tf_op jit(solution)/shard_map/ppermute | solution.py:700
  20.4 1.0 %shard_map.100 = (f32[2,320,128]{2,1,0:T(8,128)S(1)}, f32[2,40,128]{2,1,0:T(8,128)S(1)}) custom-call(s32[3,1024]{1,0:T(4,128)S(1)} %get-tuple-element.39.receivers, f32[4,1024]{1,0:T(4,128)S(1)} %get-tuple-element.40.receiver_wave, f32[304,128]{1,0:T(8,128)S(1)} %get-tuple-element.47.adj_ref._.late_ref), custom_call_target="tpu_custom_call" | custom-call | bytes 3690000 | tf_op jit(solution)/shard_map/pallas_call | solution.py:655
  21.4 0.6 %shard_map.102 = (f32[3,400,128]{2,1,0:T(8,128)S(1)}, f32[3,40,128]{2,1,0:T(8,128)S(1)}) custom-call(s32[3,64]{1,0:T(4,128)S(1)} %get-tuple-element.56.sources, f32[4,64]{1,0:T(4,128)S(1)} %get-tuple-element.57.source_wave, f32[304,128]{1,0:T(8,128)S(1)} %get-tuple-element.47.adj_ref._.late_ref), custom_call_target="tpu_custom_call" | custom-call | bytes 1845000 | tf_op jit(solution)/shard_map/pallas_call | solution.py:655
  22.0 0.0 collective-permute-done.7.even
  22.0 2.4 %collective-permute-done.8.odd = f32[496,128]{1,0:T(8,128)S(1)} collective-permute-done((f32[496,128]{1,0:T(8,128)S(1)}, f32[496,128]{1,0:T(8,128)S(1)}, u32[]{:S(2)}, u32[]{:S(2)}) %collective-permute-start.8) | collective-permute-done | bytes 253984 | tf_op jit(solution)/shard_map/ppermute | solution.py:700
  24.4 2.3 %shard_map.101 = (f32[4,4,32,128]{3,2,1,0:T(8,128)S(1)}, f32[4,4,4,32,128]{4,3,2,1,0:T(8,128)S(1)}, f32[3,12,40,128]{3,2,1,0:T(8,128)S(1)}, f32[3,40,128]{2,1,0:T(8,128)S(1)}) custom-call(f32[256,128]{1,0:T(8,128)S(1)} %get-tuple-element.46.ql_ref, f32[304,128]{1,0:T(8,128)S(1)} %get-tuple-element.47.adj_ref._.late_ref, ...), custom_call_target="tpu_custom_call" | custom-call | bytes 14391000 | tf_op jit(solution)/shard_map/pallas_call | solution.py:655
  26.8 0.0 collective-permute-done.5.even
  26.8 0.0 collective-permute-done.6.odd
  26.8 1.8 %shard_map.103 = (f32[2,4,32,128]{3,2,1,0:T(8,128)}, f32[4,4,32,128]{3,2,1,0:T(8,128)}) custom-call(f32[256,128]{1,0:T(8,128)S(1)} %collective-permute-done.wave_ref._, f32[128,128]{1,0:T(8,128)S(1)} %get-tuple-element.43.own_s_ref, f32[168,128]{1,0:T(8,128)S(1)} %collective-permute-done.4.late_ref, f32[344,128]{1,0:T(8,128)S(1)} %collective-permute-done.5.even, ...), custom_call_target="tpu_custom_call" | custom-call | bytes 9225000 | tf_op jit(solution)/shard_map/pallas_call | solution.py:655
  (1 shorter events, 0.0 us)
Async XLA Ops:
  2.0 7.8 %collective-permute-start = (f32[256,128]{1,0:T(8,128)S(1)}, f32[256,128]{1,0:T(8,128)S(1)}, u32[]{:S(2)}, u32[]{:S(2)}) collective-permute-start(f32[256,128]{1,0:T(8,128)S(1)} %get-tuple-element.32), channel_id=1, source_target_pairs={{8,0},{12,4},{0,8},{4,12},{9,1},{13,5},{1,9},{5,13},{10,2},{14,6},... | collective-permute-start | bytes 393224 | tf_op jit(solution)/shard_map/ppermute | solution.py:691
  2.4 4.4 %collective-permute-start.1 = (f32[160,128]{1,0:T(8,128)S(1)}, f32[160,128]{1,0:T(8,128)S(1)}, u32[]{:S(2)}, u32[]{:S(2)}) collective-permute-start(f32[160,128]{1,0:T(8,128)S(1)} %get-tuple-element.33), channel_id=1, source_target_pairs={{2,0},{0,2},{3,1},{1,3},{6,4},{4,6},{7,5},{5,7},{10,8},{8,10},{11,... | collective-permute-start | bytes 245768 | tf_op jit(solution)/shard_map/ppermute | solution.py:683
  2.6 3.2 %collective-permute-start.3 = (f32[96,128]{1,0:T(8,128)S(1)}, f32[96,128]{1,0:T(8,128)S(1)}, u32[]{:S(2)}, u32[]{:S(2)}) collective-permute-start(f32[96,128]{1,0:T(8,128)S(1)} %get-tuple-element.35.strip_ref), channel_id=1, source_target_pairs={{1,0},{0,1},{3,2},{2,3},{5,4},{4,5},{7,6},{6,7},{9,8},{8,9},{11,10... | collective-permute-start | bytes 147464 | tf_op jit(solution)/shard_map/ppermute | solution.py:691
  2.6 3.2 %collective-permute-start.2 = (f32[16,128]{1,0:T(8,128)S(1)}, f32[16,128]{1,0:T(8,128)S(1)}, u32[]{:S(2)}, u32[]{:S(2)}) collective-permute-start(f32[16,128]{1,0:T(8,128)S(1)} %get-tuple-element.34), channel_id=1, source_target_pairs={{2,1},{3,0},{0,3},{1,2},{6,5},{7,4},{4,7},{5,6},{10,9},{11,8},{8,1... | collective-permute-start | bytes 24584 | tf_op jit(solution)/shard_map/ppermute | solution.py:683
  7.1 9.2 %collective-permute-start.4 = (f32[168,128]{1,0:T(8,128)S(1)}, f32[168,128]{1,0:T(8,128)S(1)}, u32[]{:S(2)}, u32[]{:S(2)}) collective-permute-start(f32[168,128]{1,0:T(8,128)S(1)} %get-tuple-element.42), channel_id=1, source_target_pairs={{8,0},{12,4},{0,8},{4,12},{9,1},{13,5},{1,9},{5,13},{10,2},{14,6},... | collective-permute-start | bytes 258056 | tf_op jit(solution)/shard_map/ppermute | solution.py:691
  9.8 12.2 %collective-permute-start.7 = (f32[496,128]{1,0:T(8,128)S(1)}, f32[496,128]{1,0:T(8,128)S(1)}, u32[]{:S(2)}, u32[]{:S(2)}) collective-permute-start(f32[496,128]{1,0:T(8,128)S(1)} %get-tuple-element.48), channel_id=1, source_target_pairs={{4,0},{0,4},{12,8},{8,12},{5,1},{1,5},{13,9},{9,13},{6,2},{2,6},{1... | collective-permute-start | bytes 761864 | tf_op jit(solution)/shard_map/ppermute | solution.py:700
  14.4 10.1 %collective-permute-start.8 = (f32[496,128]{1,0:T(8,128)S(1)}, f32[496,128]{1,0:T(8,128)S(1)}, u32[]{:S(2)}, u32[]{:S(2)}) collective-permute-start(f32[496,128]{1,0:T(8,128)S(1)} %get-tuple-element.49), channel_id=1, source_target_pairs={{0,0},{8,4},{4,8},{12,12},{1,1},{9,5},{5,9},{13,13},{2,2},{10,6},{... | collective-permute-start | bytes 761864 | tf_op jit(solution)/shard_map/ppermute | solution.py:700
  16.4 10.4 %collective-permute-start.5 = (f32[344,128]{1,0:T(8,128)S(1)}, f32[344,128]{1,0:T(8,128)S(1)}, u32[]{:S(2)}, u32[]{:S(2)}) collective-permute-start(f32[344,128]{1,0:T(8,128)S(1)} %get-tuple-element.44), channel_id=1, source_target_pairs={{4,0},{0,4},{12,8},{8,12},{5,1},{1,5},{13,9},{9,13},{6,2},{2,6},{1... | collective-permute-start | bytes 528392 | tf_op jit(solution)/shard_map/ppermute | solution.py:700
  16.5 10.3 %collective-permute-start.6 = (f32[344,128]{1,0:T(8,128)S(1)}, f32[344,128]{1,0:T(8,128)S(1)}, u32[]{:S(2)}, u32[]{:S(2)}) collective-permute-start(f32[344,128]{1,0:T(8,128)S(1)} %get-tuple-element.45), channel_id=1, source_target_pairs={{0,0},{8,4},{4,8},{12,12},{1,1},{9,5},{5,9},{13,13},{2,2},{10,6},{... | collective-permute-start | bytes 528392 | tf_op jit(solution)/shard_map/ppermute | solution.py:700

commit v14 on v13

--- a/solution.py
+++ b/solution.py
@@ -238,7 +238,7 @@
             target[tiles_end : tiles_end + EY] = strip
 
 
-def adjoint_join_kernel(ql_ref, adj_ref, _, even_ref, odd_ref):
+def adjoint_join_kernel(ql_ref, adj_ref, even_ref, odd_ref):
     planes_end, x_end, tiles_end = ADJ_OWN
     for target, first in zip((even_ref, odd_ref), pair_planes()):
         base = copy_rows(target, 0, adj_ref, first * BY, 3 * BY)
@@ -768,9 +768,9 @@
     even, odd = call(
         adjoint_join_kernel,
         [shape(ADJ_SIDE[2] + EY + 2 * PLANES, BZ)] * 2,
-        [ql, adj_late, wave],
+        [ql, adj_late],
         [],
-        "vva",
+        "vv",
     )
     even, odd = paired(even, False), paired(odd, True)
     src, src_strip = call(

time: 28.8 us -> 28.5 us (0.990)
  the two profiles are of different devices: /device:TPU:18 before, /device:TPU:8 now
where the time goes in v14:
time: 28.5 us; the launch traced here: 28.2 us
  starting transfers between devices  16 us (56%)
  Pallas kernels  8.66 us (30%)
  waiting for transfers between devices  2.83 us (10%)
  between operations  0.72 us (3%)
    ppermute x4, starting transfers between devices, paired(): return lax.ppermute(array, 'gx', pairs)  11 us
    pallas_call x9, Pallas kernels, call(): pl.pallas_call(kernel, out_shape=outs, in_specs=[pl.BlockSpec(memory_spac...  8.66 us
    ppermute x3, starting transfers between devices, rotated(): lax.ppermute(array, axis, [((i + offset) % count, i) for i in range(count)])  2.99 us
    ppermute x2, starting transfers between devices, from_sides(): both = lax.ppermute(sends[0], axes, route(1) + route(-1))  1.92 us
    ppermute x2, waiting for transfers between devices, from_sides(): both = lax.ppermute(sends[0], axes, route(1) + route(-1))  1.45 us
    ppermute x3, waiting for transfers between devices, rotated(): lax.ppermute(array, axis, [((i + offset) % count, i) for i in range(count)])  0.97 us
  transfers between devices with their start and end apart: 9, of which 3 were waited for; matrix products, arithmetic and copies ran while one was open for 0% of the time, Pallas kernels for 20%

profile of v14, /device:TPU:8, one launch (start us, length us, event | category | flops | bytes accessed | tf_op | source)
XLA Modules:
  0.0 28.2 jit_solution(2079244729743305421)
XLA Ops:
  0.6 1.3 %shard_map.95 = (f32[256,128]{1,0:T(8,128)S(1)}, f32[256,128]{1,0:T(8,128)S(1)}, f32[128,128]{1,0:T(8,128)S(1)}, f32[64,128]{1,0:T(8,128)S(1)}, f32[64,128]{1,0:...) custom-call(f32[4,4,32,128]{3,2,1,0:T(8,128)} %stored_hbm.1, ...), custom_call_target="tpu_custom_call" | custom-call | bytes 5166000 | tf_op jit(solution)/shard_map/pallas_call | solution.py:655
  2.0 1.6 %collective-permute-start.1 = (f32[160,128]{1,0:T(8,128)S(1)}, f32[160,128]{1,0:T(8,128)S(1)}, u32[]{:S(2)}, u32[]{:S(2)}) collective-permute-start(f32[160,128]{1,0:T(8,128)S(1)} %get-tuple-element.33), channel_id=1, source_target_pairs={{2,0},{0,2},{3,1},{1,3},{6,4},{4,6},{7,5},{5,7},{10,8},{8,10},{11,... | collective-permute-start | bytes 245768 | tf_op jit(solution)/shard_map/ppermute | solution.py:683
  3.5 0.0 collective-permute-start.3
  3.5 2.6 %collective-permute-start = (f32[256,128]{1,0:T(8,128)S(1)}, f32[256,128]{1,0:T(8,128)S(1)}, u32[]{:S(2)}, u32[]{:S(2)}) collective-permute-start(f32[256,128]{1,0:T(8,128)S(1)} %get-tuple-element.32), channel_id=1, source_target_pairs={{8,0},{12,4},{0,8},{4,12},{9,1},{13,5},{1,9},{5,13},{10,2},{14,6},... | collective-permute-start | bytes 393224 | tf_op jit(solution)/shard_map/ppermute | solution.py:691
  6.1 0.4 %collective-permute-start.2 = (f32[16,128]{1,0:T(8,128)S(1)}, f32[16,128]{1,0:T(8,128)S(1)}, u32[]{:S(2)}, u32[]{:S(2)}) collective-permute-start(f32[16,128]{1,0:T(8,128)S(1)} %get-tuple-element.34), channel_id=1, source_target_pairs={{2,1},{3,0},{0,3},{1,2},{6,5},{7,4},{4,7},{5,6},{10,9},{11,8},{8,1... | collective-permute-start | bytes 24584 | tf_op jit(solution)/shard_map/ppermute | solution.py:683
  6.5 1.2 %shard_map.96 = (f32[2,480,128]{2,1,0:T(8,128)S(1)}, f32[2,40,128]{2,1,0:T(8,128)S(1)}) custom-call(s32[3,1024]{1,0:T(4,128)S(1)} %get-tuple-element.39.receivers, f32[4,1024]{1,0:T(4,128)S(1)} %get-tuple-element.40.receiver_wave), custom_call_target="tpu_custom_call" | custom-call | bytes 4428000 | tf_op jit(solution)/shard_map/pallas_call | solution.py:655
  7.7 1.5 %collective-permute-done.2.corner_up.corner_down = f32[16,128]{1,0:T(8,128)S(1)} collective-permute-done((f32[16,128]{1,0:T(8,128)S(1)}, f32[16,128]{1,0:T(8,128)S(1)}, u32[]{:S(2)}, u32[]{:S(2)}) %collective-permute-start.2) | collective-permute-done | bytes 8224 | tf_op jit(solution)/shard_map/ppermute | solution.py:683
  9.2 0.0 collective-permute-done.3.other_ref
  9.2 0.0 collective-permute-done.1.from_up.from_down
  9.2 0.3 shard_map.97
  9.5 0.4 %collective-permute-start.4 = (f32[168,128]{1,0:T(8,128)S(1)}, f32[168,128]{1,0:T(8,128)S(1)}, u32[]{:S(2)}, u32[]{:S(2)}) collective-permute-start(f32[168,128]{1,0:T(8,128)S(1)} %get-tuple-element.42), channel_id=1, source_target_pairs={{8,0},{12,4},{0,8},{4,12},{9,1},{13,5},{1,9},{5,13},{10,2},{14,6},... | collective-permute-start | bytes 258056 | tf_op jit(solution)/shard_map/ppermute | solution.py:691
  9.9 0.5 %collective-permute-start.7 = (f32[496,128]{1,0:T(8,128)S(1)}, f32[496,128]{1,0:T(8,128)S(1)}, u32[]{:S(2)}, u32[]{:S(2)}) collective-permute-start(f32[496,128]{1,0:T(8,128)S(1)} %get-tuple-element.48), channel_id=1, source_target_pairs={{4,0},{0,4},{12,8},{8,12},{5,1},{1,5},{13,9},{9,13},{6,2},{2,6},{1... | collective-permute-start | bytes 761864 | tf_op jit(solution)/shard_map/ppermute | solution.py:700
  10.4 4.6 %collective-permute-start.8 = (f32[496,128]{1,0:T(8,128)S(1)}, f32[496,128]{1,0:T(8,128)S(1)}, u32[]{:S(2)}, u32[]{:S(2)}) collective-permute-start(f32[496,128]{1,0:T(8,128)S(1)} %get-tuple-element.49), channel_id=1, source_target_pairs={{0,0},{8,4},{4,8},{12,12},{1,1},{9,5},{5,9},{13,13},{2,2},{10,6},{... | collective-permute-start | bytes 761864 | tf_op jit(solution)/shard_map/ppermute | solution.py:700
  15.0 0.0 collective-permute-done.wave_ref
  15.0 1.0 %collective-permute-done.4.late_ref = f32[168,128]{1,0:T(8,128)S(1)} collective-permute-done((f32[168,128]{1,0:T(8,128)S(1)}, f32[168,128]{1,0:T(8,128)S(1)}, u32[]{:S(2)}, u32[]{:S(2)}) %collective-permute-start.4) | collective-permute-done | bytes 86048 | tf_op jit(solution)/shard_map/ppermute | solution.py:691
  16.0 0.1 shard_map.98
  16.1 2.1 %collective-permute-start.5 = (f32[344,128]{1,0:T(8,128)S(1)}, f32[344,128]{1,0:T(8,128)S(1)}, u32[]{:S(2)}, u32[]{:S(2)}) collective-permute-start(f32[344,128]{1,0:T(8,128)S(1)} %get-tuple-element.44), channel_id=1, source_target_pairs={{4,0},{0,4},{12,8},{8,12},{5,1},{1,5},{13,9},{9,13},{6,2},{2,6},{1... | collective-permute-start | bytes 528392 | tf_op jit(solution)/shard_map/ppermute | solution.py:700
  18.2 3.8 %collective-permute-start.6 = (f32[344,128]{1,0:T(8,128)S(1)}, f32[344,128]{1,0:T(8,128)S(1)}, u32[]{:S(2)}, u32[]{:S(2)}) collective-permute-start(f32[344,128]{1,0:T(8,128)S(1)} %get-tuple-element.45), channel_id=1, source_target_pairs={{0,0},{8,4},{4,8},{12,12},{1,1},{9,5},{5,9},{13,13},{2,2},{10,6},{... | collective-permute-start | bytes 528392 | tf_op jit(solution)/shard_map/ppermute | solution.py:700
  22.0 1.0 %shard_map.100 = (f32[2,320,128]{2,1,0:T(8,128)S(1)}, f32[2,40,128]{2,1,0:T(8,128)S(1)}) custom-call(s32[3,1024]{1,0:T(4,128)S(1)} %get-tuple-element.39.receivers, f32[4,1024]{1,0:T(4,128)S(1)} %get-tuple-element.40.receiver_wave, f32[304,128]{1,0:T(8,128)S(1)} %get-tuple-element.47.adj_ref._.late_ref), custom_call_target="tpu_custom_call" | custom-call | bytes 3690000 | tf_op jit(solution)/shard_map/pallas_call | solution.py:655
  23.1 0.5 %shard_map.102 = (f32[3,400,128]{2,1,0:T(8,128)S(1)}, f32[3,40,128]{2,1,0:T(8,128)S(1)}) custom-call(s32[3,64]{1,0:T(4,128)S(1)} %get-tuple-element.56.sources, f32[4,64]{1,0:T(4,128)S(1)} %get-tuple-element.57.source_wave, f32[304,128]{1,0:T(8,128)S(1)} %get-tuple-element.47.adj_ref._.late_ref), custom_call_target="tpu_custom_call" | custom-call | bytes 1845000 | tf_op jit(solution)/shard_map/pallas_call | solution.py:655
  23.6 0.0 collective-permute-done.7.even
  23.6 0.0 collective-permute-done.8.odd
  23.6 2.3 %shard_map.101 = (f32[4,4,32,128]{3,2,1,0:T(8,128)S(1)}, f32[4,4,4,32,128]{4,3,2,1,0:T(8,128)S(1)}, f32[3,12,40,128]{3,2,1,0:T(8,128)S(1)}, f32[3,40,128]{2,1,0:T(8,128)S(1)}) custom-call(f32[256,128]{1,0:T(8,128)S(1)} %get-tuple-element.46.ql_ref, f32[304,128]{1,0:T(8,128)S(1)} %get-tuple-element.47.adj_ref._.late_ref, ...), custom_call_target="tpu_custom_call" | custom-call | bytes 14391000 | tf_op jit(solution)/shard_map/pallas_call | solution.py:655
  26.0 0.0 collective-permute-done.5.even
  26.0 0.4 %collective-permute-done.6.odd = f32[344,128]{1,0:T(8,128)S(1)} collective-permute-done((f32[344,128]{1,0:T(8,128)S(1)}, f32[344,128]{1,0:T(8,128)S(1)}, u32[]{:S(2)}, u32[]{:S(2)}) %collective-permute-start.6) | collective-permute-done | bytes 176160 | tf_op jit(solution)/shard_map/ppermute | solution.py:700
  26.4 1.8 %shard_map.103 = (f32[2,4,32,128]{3,2,1,0:T(8,128)}, f32[4,4,32,128]{3,2,1,0:T(8,128)}) custom-call(f32[256,128]{1,0:T(8,128)S(1)} %collective-permute-done.wave_ref, f32[128,128]{1,0:T(8,128)S(1)} %get-tuple-element.43.own_s_ref, f32[168,128]{1,0:T(8,128)S(1)} %collective-permute-done.4.late_ref, f32[344,128]{1,0:T(8,128)S(1)} %collective-permute-done.5.even, ...), custom_call_target="tpu_custom_call" | custom-call | bytes 9225000 | tf_op jit(solution)/shard_map/pallas_call | solution.py:655
  (1 shorter events, 0.0 us)
Async XLA Ops:
  2.0 7.2 %collective-permute-start.1 = (f32[160,128]{1,0:T(8,128)S(1)}, f32[160,128]{1,0:T(8,128)S(1)}, u32[]{:S(2)}, u32[]{:S(2)}) collective-permute-start(f32[160,128]{1,0:T(8,128)S(1)} %get-tuple-element.33), channel_id=1, source_target_pairs={{2,0},{0,2},{3,1},{1,3},{6,4},{4,6},{7,5},{5,7},{10,8},{8,10},{11,... | collective-permute-start | bytes 245768 | tf_op jit(solution)/shard_map/ppermute | solution.py:683
  3.5 5.7 %collective-permute-start.3 = (f32[96,128]{1,0:T(8,128)S(1)}, f32[96,128]{1,0:T(8,128)S(1)}, u32[]{:S(2)}, u32[]{:S(2)}) collective-permute-start(f32[96,128]{1,0:T(8,128)S(1)} %get-tuple-element.35.strip_ref), channel_id=1, source_target_pairs={{1,0},{0,1},{3,2},{2,3},{5,4},{4,5},{7,6},{6,7},{9,8},{8,9},{11,10... | collective-permute-start | bytes 147464 | tf_op jit(solution)/shard_map/ppermute | solution.py:691
  3.5 11.5 %collective-permute-start = (f32[256,128]{1,0:T(8,128)S(1)}, f32[256,128]{1,0:T(8,128)S(1)}, u32[]{:S(2)}, u32[]{:S(2)}) collective-permute-start(f32[256,128]{1,0:T(8,128)S(1)} %get-tuple-element.32), channel_id=1, source_target_pairs={{8,0},{12,4},{0,8},{4,12},{9,1},{13,5},{1,9},{5,13},{10,2},{14,6},... | collective-permute-start | bytes 393224 | tf_op jit(solution)/shard_map/ppermute | solution.py:691
  6.1 3.1 %collective-permute-start.2 = (f32[16,128]{1,0:T(8,128)S(1)}, f32[16,128]{1,0:T(8,128)S(1)}, u32[]{:S(2)}, u32[]{:S(2)}) collective-permute-start(f32[16,128]{1,0:T(8,128)S(1)} %get-tuple-element.34), channel_id=1, source_target_pairs={{2,1},{3,0},{0,3},{1,2},{6,5},{7,4},{4,7},{5,6},{10,9},{11,8},{8,1... | collective-permute-start | bytes 24584 | tf_op jit(solution)/shard_map/ppermute | solution.py:683
  9.5 6.5 %collective-permute-start.4 = (f32[168,128]{1,0:T(8,128)S(1)}, f32[168,128]{1,0:T(8,128)S(1)}, u32[]{:S(2)}, u32[]{:S(2)}) collective-permute-start(f32[168,128]{1,0:T(8,128)S(1)} %get-tuple-element.42), channel_id=1, source_target_pairs={{8,0},{12,4},{0,8},{4,12},{9,1},{13,5},{1,9},{5,13},{10,2},{14,6},... | collective-permute-start | bytes 258056 | tf_op jit(solution)/shard_map/ppermute | solution.py:691
  9.9 13.7 %collective-permute-start.7 = (f32[496,128]{1,0:T(8,128)S(1)}, f32[496,128]{1,0:T(8,128)S(1)}, u32[]{:S(2)}, u32[]{:S(2)}) collective-permute-start(f32[496,128]{1,0:T(8,128)S(1)} %get-tuple-element.48), channel_id=1, source_target_pairs={{4,0},{0,4},{12,8},{8,12},{5,1},{1,5},{13,9},{9,13},{6,2},{2,6},{1... | collective-permute-start | bytes 761864 | tf_op jit(solution)/shard_map/ppermute | solution.py:700
  10.4 13.2 %collective-permute-start.8 = (f32[496,128]{1,0:T(8,128)S(1)}, f32[496,128]{1,0:T(8,128)S(1)}, u32[]{:S(2)}, u32[]{:S(2)}) collective-permute-start(f32[496,128]{1,0:T(8,128)S(1)} %get-tuple-element.49), channel_id=1, source_target_pairs={{0,0},{8,4},{4,8},{12,12},{1,1},{9,5},{5,9},{13,13},{2,2},{10,6},{... | collective-permute-start | bytes 761864 | tf_op jit(solution)/shard_map/ppermute | solution.py:700
  16.1 9.9 %collective-permute-start.5 = (f32[344,128]{1,0:T(8,128)S(1)}, f32[344,128]{1,0:T(8,128)S(1)}, u32[]{:S(2)}, u32[]{:S(2)}) collective-permute-start(f32[344,128]{1,0:T(8,128)S(1)} %get-tuple-element.44), channel_id=1, source_target_pairs={{4,0},{0,4},{12,8},{8,12},{5,1},{1,5},{13,9},{9,13},{6,2},{2,6},{1... | collective-permute-start | bytes 528392 | tf_op jit(solution)/shard_map/ppermute | solution.py:700
  18.2 8.2 %collective-permute-start.6 = (f32[344,128]{1,0:T(8,128)S(1)}, f32[344,128]{1,0:T(8,128)S(1)}, u32[]{:S(2)}, u32[]{:S(2)}) collective-permute-start(f32[344,128]{1,0:T(8,128)S(1)} %get-tuple-element.45), channel_id=1, source_target_pairs={{0,0},{8,4},{4,8},{12,12},{1,1},{9,5},{5,9},{13,13},{2,2},{10,6},{... | collective-permute-start | bytes 528392 | tf_op jit(solution)/shard_map/ppermute | solution.py:700

commit v15 on v13

--- a/solution.py
+++ b/solution.py
@@ -467,7 +467,7 @@
     ql_ref, late_ref, even, odd, adj_hbm, ra_ref, rsa_ref, rb_ref, rsb_ref,
     table_ref,
     out_ref, hist_ref, coef_ref, coef_strip_ref,
-    q_ref, t_ref, u_ref, scale_ref, edge_ref, flux_ref, w_sem,
+    q_ref, t_ref, u_ref, scale_ref, edge_ref, w_sem,
 ):
     w_copy = pltpu.make_async_copy(adj_hbm.at[pl.ds(1, 3)], out_ref.at[pl.ds(1, 3)], w_sem)
     w_copy.start()
@@ -525,22 +525,9 @@
             q_ref[x] = q
             u_ref[x] = scale_ref[x] * q
 
-        for x in range(step - 1, EX - step):
-            u, buoyancy = u_ref[x], coef_ref[1, x]
-            slopes = [u_ref[x + 1] - u]
-            if x >= step:
-                slopes += [y_up(u) - u, z_up(u, edge_ref[step - 1, x]) - u]
-            for axis, slope in enumerate(slopes):
-                flux_ref[axis, x] = buoyancy * slope
-            if BX <= x < 2 * BX:
-                for axis, slope in enumerate(slopes):
-                    w = out_ref[1 + axis, x - BX] + slope[0:BY]
-                    out_ref[1 + axis, x - BX] = w
-                    hist_ref[k, 1 + axis, x - BX] = w
-
-        for x in range(step, EX - step):
-            flux_y, flux_z = flux_ref[1, x], flux_ref[2, x]
-            spread = (flux_ref[0, x] - flux_ref[0, x - 1]) + (flux_y - y_down(flux_y))
+        def close(x, flux_below, fluxes):
+            flux_x, flux_y, flux_z = fluxes
+            spread = (flux_x - flux_below) + (flux_y - y_down(flux_y))
             spread = spread + (flux_z - z_down(flux_z, edge_ref[step - 1, x]))
             damped = coef_ref[2, x] * q_ref[x]
             t = (initial(1, x) if step == 1 else t_ref[x]) + spread
@@ -552,22 +539,32 @@
             else:
                 out_ref[0, x - BX] = (damped + t)[0:BY]
 
+        waiting = flux_below = None
+        for x in range(step - 1, EX - step):
+            u, buoyancy = u_ref[x], coef_ref[1, x]
+            slopes = [u_ref[x + 1] - u]
+            if x >= step:
+                slopes += [y_up(u) - u, z_up(u, edge_ref[step - 1, x]) - u]
+            fluxes = [buoyancy * slope for slope in slopes]
+            if BX <= x < 2 * BX:
+                for axis, slope in enumerate(slopes):
+                    w = out_ref[1 + axis, x - BX] + slope[0:BY]
+                    out_ref[1 + axis, x - BX] = w
+                    hist_ref[k, 1 + axis, x - BX] = w
+            if waiting is not None:
+                close(*waiting)
+            waiting = (x, flux_below, fluxes) if x >= step else None
+            flux_below = fluxes[0]
+        close(*waiting)
+
 
 def forward_kernel(
     wave_ref, own_s_ref, late_ref, even, odd, coef_ref, coef_strip_ref, s_ref, ss_ref, hist_ref,
     adjoint_ref, grad_hbm, adjoint_hbm,
-    p_ref, spread_ref, edge_ref, flux_ref, grad_ref, sems,
+    p_ref, spread_ref, edge_ref, grad_ref, sems,
 ):
     copies = [pltpu.make_async_copy(adjoint_ref, adjoint_hbm, sems.at[0])]
     copies[0].start()
-
-    def send(index, kind, first, count):
-        planes = pl.ds(first, count)
-        copy = pltpu.make_async_copy(
-            grad_ref.at[kind, planes], grad_hbm.at[kind, planes], sems.at[index]
-        )
-        copy.start()
-        copies.append(copy)
 
     cut_up, cut_down = cut_flags()
     side = sides()
@@ -605,25 +602,9 @@
 
     for step in range(1, STEPS + 1):
         k = step - 1
-        for x in range(step - 1, EX - step):
-            p, buoyancy = p_ref[x], coef_ref[1, x]
-            slopes = [p_ref[x + 1] - p]
-            if x >= step:
-                slopes += [y_up(p) - p, z_up(p, edge_ref[step - 1, x]) - p]
-            for axis, slope in enumerate(slopes):
-                flux_ref[axis, x] = buoyancy * slope
-            if BX <= x < 2 * BX:
-                place = x - BX
-                term = hist_ref[k, 1, place] * slopes[0][0:BY]
-                term = term + hist_ref[k, 2, place] * slopes[1][0:BY]
-                term = term + hist_ref[k, 3, place] * slopes[2][0:BY]
-                grad_ref[1, place] = -term if k == 0 else grad_ref[1, place] - term
-        if step == STEPS:
-            send(1, 1, 0, BX)
-
-        for x in range(step, EX - step):
-            flux_y, flux_z = flux_ref[1, x], flux_ref[2, x]
-            spread = (flux_ref[0, x] - flux_ref[0, x - 1]) + (flux_y - y_down(flux_y))
+        def close(x, flux_below, fluxes):
+            flux_x, flux_y, flux_z = fluxes
+            spread = (flux_x - flux_below) + (flux_y - y_down(flux_y))
             spread = spread + (flux_z - z_down(flux_z, edge_ref[step - 1, x]))
             spread = (initial(1, x) if step == 1 else spread_ref[x]) - spread
             if step < STEPS:
@@ -636,8 +617,30 @@
                 place = x - BX
                 term = hist_ref[k, 0, place] * spread[0:BY]
                 grad_ref[0, place] = -term if k == 0 else grad_ref[0, place] - term
-                if step == STEPS:
-                    send(2 + place, 0, place, 1)
+
+        waiting = flux_below = None
+        for x in range(step - 1, EX - step):
+            p, buoyancy = p_ref[x], coef_ref[1, x]
+            slopes = [p_ref[x + 1] - p]
+            if x >= step:
+                slopes += [y_up(p) - p, z_up(p, edge_ref[step - 1, x]) - p]
+            fluxes = [buoyancy * slope for slope in slopes]
+            if BX <= x < 2 * BX:
+                place = x - BX
+                term = hist_ref[k, 1, place] * slopes[0][0:BY]
+                term = term + hist_ref[k, 2, place] * slopes[1][0:BY]
+                term = term + hist_ref[k, 3, place] * slopes[2][0:BY]
+                grad_ref[1, place] = -term if k == 0 else grad_ref[1, place] - term
+            if waiting is not None:
+                close(*waiting)
+            waiting = (x, flux_below, fluxes) if x >= step else None
+            flux_below = fluxes[0]
+        close(*waiting)
+
+    for kind in range(2):
+        copy = pltpu.make_async_copy(grad_ref.at[kind], grad_hbm.at[kind], sems.at[1 + kind])
+        copy.start()
+        copies.append(copy)
     for copy in copies:
         copy.wait()
 
@@ -802,7 +805,6 @@
         [pltpu.VMEM((EX, EY, BZ), F32)] * 4
         + [
             pltpu.VMEM((STEPS, EX, EY, BZ), F32),
-            pltpu.VMEM((3, EX, EY, BZ), F32),
             pltpu.SemaphoreType.DMA,
         ],
         "vvvvhvvvvv",
@@ -818,9 +820,8 @@
         [pltpu.VMEM((EX, EY, BZ), F32)] * 2
         + [
             pltpu.VMEM((STEPS, EX, EY, BZ), F32),
-            pltpu.VMEM((3, EX, EY, BZ), F32),
             pltpu.VMEM((2, BX, BY, BZ), F32),
-            pltpu.SemaphoreType.DMA((2 + BX,)),
+            pltpu.SemaphoreType.DMA((3,)),
         ],
         "vvvvvvvvvvv",
         2.5,

time: 28.8 us -> 28.8 us (level)
  no operation moved by 1% of the time
where the time goes in v15:
time: 28.8 us; the launch traced here: 28.6 us
  starting transfers between devices  15.7 us (55%)
  Pallas kernels  8.69 us (30%)
  waiting for transfers between devices  3.47 us (12%)
  between operations  0.73 us (3%)
    ppermute x4, starting transfers between devices, paired(): return lax.ppermute(array, 'gx', pairs)  10.5 us
    pallas_call x9, Pallas kernels, call(): pl.pallas_call(kernel, out_shape=outs, in_specs=[pl.BlockSpec(memory_spac...  8.69 us
    ppermute x3, starting transfers between devices, rotated(): lax.ppermute(array, axis, [((i + offset) % count, i) for i in range(count)])  3.11 us
    ppermute x4, waiting for transfers between devices, paired(): return lax.ppermute(array, 'gx', pairs)  2.42 us
    ppermute x2, starting transfers between devices, from_sides(): both = lax.ppermute(sends[0], axes, route(1) + route(-1))  2.14 us
    ppermute x2, waiting for transfers between devices, from_sides(): both = lax.ppermute(sends[0], axes, route(1) + route(-1))  1.04 us
  transfers between devices with their start and end apart: 9, of which 3 were waited for; matrix products, arithmetic and copies ran while one was open for 0% of the time, Pallas kernels for 19%

profile of v15, /device:TPU:18, one launch (start us, length us, event | category | flops | bytes accessed | tf_op | source)
XLA Modules:
  0.0 28.6 jit_solution(13970410197085823189)
XLA Ops:
  0.6 1.3 %shard_map.95 = (f32[256,128]{1,0:T(8,128)S(1)}, f32[256,128]{1,0:T(8,128)S(1)}, f32[128,128]{1,0:T(8,128)S(1)}, f32[64,128]{1,0:T(8,128)S(1)}, f32[64,128]{1,0:...) custom-call(f32[4,4,32,128]{3,2,1,0:T(8,128)} %stored_hbm.1, ...), custom_call_target="tpu_custom_call" | custom-call | bytes 5166000 | tf_op jit(solution)/shard_map/pallas_call | solution.py:658
  2.0 0.4 %collective-permute-start = (f32[256,128]{1,0:T(8,128)S(1)}, f32[256,128]{1,0:T(8,128)S(1)}, u32[]{:S(2)}, u32[]{:S(2)}) collective-permute-start(f32[256,128]{1,0:T(8,128)S(1)} %get-tuple-element.32), channel_id=1, source_target_pairs={{8,0},{12,4},{0,8},{4,12},{9,1},{13,5},{1,9},{5,13},{10,2},{14,6},... | collective-permute-start | bytes 393224 | tf_op jit(solution)/shard_map/ppermute | solution.py:694
  2.4 0.3 collective-permute-start.1
  2.6 0.0 collective-permute-start.3
  2.6 1.9 %collective-permute-start.2 = (f32[16,128]{1,0:T(8,128)S(1)}, f32[16,128]{1,0:T(8,128)S(1)}, u32[]{:S(2)}, u32[]{:S(2)}) collective-permute-start(f32[16,128]{1,0:T(8,128)S(1)} %get-tuple-element.34), channel_id=1, source_target_pairs={{2,1},{3,0},{0,3},{1,2},{6,5},{7,4},{4,7},{5,6},{10,9},{11,8},{8,1... | collective-permute-start | bytes 24584 | tf_op jit(solution)/shard_map/ppermute | solution.py:686
  4.5 1.2 %shard_map.96 = (f32[2,480,128]{2,1,0:T(8,128)S(1)}, f32[2,40,128]{2,1,0:T(8,128)S(1)}) custom-call(s32[3,1024]{1,0:T(4,128)S(1)} %get-tuple-element.39.receivers, f32[4,1024]{1,0:T(4,128)S(1)} %get-tuple-element.40.receiver_wave), custom_call_target="tpu_custom_call" | custom-call | bytes 4428000 | tf_op jit(solution)/shard_map/pallas_call | solution.py:658
  5.8 0.1 collective-permute-done.2.corner_up.corner_down
  5.9 0.0 collective-permute-done.3.other_ref
  5.9 0.9 %collective-permute-done.1.from_up.from_down = f32[160,128]{1,0:T(8,128)S(1)} collective-permute-done((f32[160,128]{1,0:T(8,128)S(1)}, f32[160,128]{1,0:T(8,128)S(1)}, u32[]{:S(2)}, u32[]{:S(2)}) %collective-permute-start.1) | collective-permute-done | bytes 81952 | tf_op jit(solution)/shard_map/ppermute | solution.py:686
  6.8 0.3 shard_map.97
  7.1 2.7 %collective-permute-start.4 = (f32[168,128]{1,0:T(8,128)S(1)}, f32[168,128]{1,0:T(8,128)S(1)}, u32[]{:S(2)}, u32[]{:S(2)}) collective-permute-start(f32[168,128]{1,0:T(8,128)S(1)} %get-tuple-element.42), channel_id=1, source_target_pairs={{8,0},{12,4},{0,8},{4,12},{9,1},{13,5},{1,9},{5,13},{10,2},{14,6},... | collective-permute-start | bytes 258056 | tf_op jit(solution)/shard_map/ppermute | solution.py:694
  9.8 0.0 collective-permute-done.wave_ref._
  9.8 4.6 %collective-permute-start.7 = (f32[496,128]{1,0:T(8,128)S(1)}, f32[496,128]{1,0:T(8,128)S(1)}, u32[]{:S(2)}, u32[]{:S(2)}) collective-permute-start(f32[496,128]{1,0:T(8,128)S(1)} %get-tuple-element.48), channel_id=1, source_target_pairs={{4,0},{0,4},{12,8},{8,12},{5,1},{1,5},{13,9},{9,13},{6,2},{2,6},{1... | collective-permute-start | bytes 761864 | tf_op jit(solution)/shard_map/ppermute | solution.py:703
  14.4 1.9 %collective-permute-start.8 = (f32[496,128]{1,0:T(8,128)S(1)}, f32[496,128]{1,0:T(8,128)S(1)}, u32[]{:S(2)}, u32[]{:S(2)}) collective-permute-start(f32[496,128]{1,0:T(8,128)S(1)} %get-tuple-element.49), channel_id=1, source_target_pairs={{0,0},{8,4},{4,8},{12,12},{1,1},{9,5},{5,9},{13,13},{2,2},{10,6},{... | collective-permute-start | bytes 761864 | tf_op jit(solution)/shard_map/ppermute | solution.py:703
  16.3 0.0 collective-permute-done.4.late_ref
  16.3 0.1 shard_map.98
  16.4 0.1 collective-permute-start.5
  16.5 3.9 %collective-permute-start.6 = (f32[344,128]{1,0:T(8,128)S(1)}, f32[344,128]{1,0:T(8,128)S(1)}, u32[]{:S(2)}, u32[]{:S(2)}) collective-permute-start(f32[344,128]{1,0:T(8,128)S(1)} %get-tuple-element.45), channel_id=1, source_target_pairs={{0,0},{8,4},{4,8},{12,12},{1,1},{9,5},{5,9},{13,13},{2,2},{10,6},{... | collective-permute-start | bytes 528392 | tf_op jit(solution)/shard_map/ppermute | solution.py:703
  20.4 1.0 %shard_map.100 = (f32[2,320,128]{2,1,0:T(8,128)S(1)}, f32[2,40,128]{2,1,0:T(8,128)S(1)}) custom-call(s32[3,1024]{1,0:T(4,128)S(1)} %get-tuple-element.39.receivers, f32[4,1024]{1,0:T(4,128)S(1)} %get-tuple-element.40.receiver_wave, f32[304,128]{1,0:T(8,128)S(1)} %get-tuple-element.47.adj_ref._.late_ref), custom_call_target="tpu_custom_call" | custom-call | bytes 3690000 | tf_op jit(solution)/shard_map/pallas_call | solution.py:658
  21.4 0.6 %shard_map.102 = (f32[3,400,128]{2,1,0:T(8,128)S(1)}, f32[3,40,128]{2,1,0:T(8,128)S(1)}) custom-call(s32[3,64]{1,0:T(4,128)S(1)} %get-tuple-element.56.sources, f32[4,64]{1,0:T(4,128)S(1)} %get-tuple-element.57.source_wave, f32[304,128]{1,0:T(8,128)S(1)} %get-tuple-element.47.adj_ref._.late_ref), custom_call_target="tpu_custom_call" | custom-call | bytes 1845000 | tf_op jit(solution)/shard_map/pallas_call | solution.py:658
  22.0 0.0 collective-permute-done.7.even
  22.0 2.4 %collective-permute-done.8.odd = f32[496,128]{1,0:T(8,128)S(1)} collective-permute-done((f32[496,128]{1,0:T(8,128)S(1)}, f32[496,128]{1,0:T(8,128)S(1)}, u32[]{:S(2)}, u32[]{:S(2)}) %collective-permute-start.8) | collective-permute-done | bytes 253984 | tf_op jit(solution)/shard_map/ppermute | solution.py:703
  24.4 2.3 %shard_map.101 = (f32[4,4,32,128]{3,2,1,0:T(8,128)S(1)}, f32[4,4,4,32,128]{4,3,2,1,0:T(8,128)S(1)}, f32[3,12,40,128]{3,2,1,0:T(8,128)S(1)}, f32[3,40,128]{2,1,0:T(8,128)S(1)}) custom-call(f32[256,128]{1,0:T(8,128)S(1)} %get-tuple-element.46.ql_ref, f32[304,128]{1,0:T(8,128)S(1)} %get-tuple-element.47.adj_ref._.late_ref, ...), custom_call_target="tpu_custom_call" | custom-call | bytes 14391000 | tf_op jit(solution)/shard_map/pallas_call | solution.py:658
  26.8 0.0 collective-permute-done.5.even
  26.8 0.0 collective-permute-done.6.odd
  26.8 1.8 %shard_map.103 = (f32[2,4,32,128]{3,2,1,0:T(8,128)}, f32[4,4,32,128]{3,2,1,0:T(8,128)}) custom-call(f32[256,128]{1,0:T(8,128)S(1)} %collective-permute-done.wave_ref._, f32[128,128]{1,0:T(8,128)S(1)} %get-tuple-element.43.own_s_ref, f32[168,128]{1,0:T(8,128)S(1)} %collective-permute-done.4.late_ref, f32[344,128]{1,0:T(8,128)S(1)} %collective-permute-done.5.even, ...), custom_call_target="tpu_custom_call" | custom-call | bytes 9225000 | tf_op jit(solution)/shard_map/pallas_call | solution.py:658
  (1 shorter events, 0.0 us)
Async XLA Ops:
  2.0 7.8 %collective-permute-start = (f32[256,128]{1,0:T(8,128)S(1)}, f32[256,128]{1,0:T(8,128)S(1)}, u32[]{:S(2)}, u32[]{:S(2)}) collective-permute-start(f32[256,128]{1,0:T(8,128)S(1)} %get-tuple-element.32), channel_id=1, source_target_pairs={{8,0},{12,4},{0,8},{4,12},{9,1},{13,5},{1,9},{5,13},{10,2},{14,6},... | collective-permute-start | bytes 393224 | tf_op jit(solution)/shard_map/ppermute | solution.py:694
  2.4 4.4 %collective-permute-start.1 = (f32[160,128]{1,0:T(8,128)S(1)}, f32[160,128]{1,0:T(8,128)S(1)}, u32[]{:S(2)}, u32[]{:S(2)}) collective-permute-start(f32[160,128]{1,0:T(8,128)S(1)} %get-tuple-element.33), channel_id=1, source_target_pairs={{2,0},{0,2},{3,1},{1,3},{6,4},{4,6},{7,5},{5,7},{10,8},{8,10},{11,... | collective-permute-start | bytes 245768 | tf_op jit(solution)/shard_map/ppermute | solution.py:686
  2.6 3.2 %collective-permute-start.3 = (f32[96,128]{1,0:T(8,128)S(1)}, f32[96,128]{1,0:T(8,128)S(1)}, u32[]{:S(2)}, u32[]{:S(2)}) collective-permute-start(f32[96,128]{1,0:T(8,128)S(1)} %get-tuple-element.35.strip_ref), channel_id=1, source_target_pairs={{1,0},{0,1},{3,2},{2,3},{5,4},{4,5},{7,6},{6,7},{9,8},{8,9},{11,10... | collective-permute-start | bytes 147464 | tf_op jit(solution)/shard_map/ppermute | solution.py:694
  2.6 3.2 %collective-permute-start.2 = (f32[16,128]{1,0:T(8,128)S(1)}, f32[16,128]{1,0:T(8,128)S(1)}, u32[]{:S(2)}, u32[]{:S(2)}) collective-permute-start(f32[16,128]{1,0:T(8,128)S(1)} %get-tuple-element.34), channel_id=1, source_target_pairs={{2,1},{3,0},{0,3},{1,2},{6,5},{7,4},{4,7},{5,6},{10,9},{11,8},{8,1... | collective-permute-start | bytes 24584 | tf_op jit(solution)/shard_map/ppermute | solution.py:686
  7.1 9.2 %collective-permute-start.4 = (f32[168,128]{1,0:T(8,128)S(1)}, f32[168,128]{1,0:T(8,128)S(1)}, u32[]{:S(2)}, u32[]{:S(2)}) collective-permute-start(f32[168,128]{1,0:T(8,128)S(1)} %get-tuple-element.42), channel_id=1, source_target_pairs={{8,0},{12,4},{0,8},{4,12},{9,1},{13,5},{1,9},{5,13},{10,2},{14,6},... | collective-permute-start | bytes 258056 | tf_op jit(solution)/shard_map/ppermute | solution.py:694
  9.8 12.2 %collective-permute-start.7 = (f32[496,128]{1,0:T(8,128)S(1)}, f32[496,128]{1,0:T(8,128)S(1)}, u32[]{:S(2)}, u32[]{:S(2)}) collective-permute-start(f32[496,128]{1,0:T(8,128)S(1)} %get-tuple-element.48), channel_id=1, source_target_pairs={{4,0},{0,4},{12,8},{8,12},{5,1},{1,5},{13,9},{9,13},{6,2},{2,6},{1... | collective-permute-start | bytes 761864 | tf_op jit(solution)/shard_map/ppermute | solution.py:703
  14.4 10.1 %collective-permute-start.8 = (f32[496,128]{1,0:T(8,128)S(1)}, f32[496,128]{1,0:T(8,128)S(1)}, u32[]{:S(2)}, u32[]{:S(2)}) collective-permute-start(f32[496,128]{1,0:T(8,128)S(1)} %get-tuple-element.49), channel_id=1, source_target_pairs={{0,0},{8,4},{4,8},{12,12},{1,1},{9,5},{5,9},{13,13},{2,2},{10,6},{... | collective-permute-start | bytes 761864 | tf_op jit(solution)/shard_map/ppermute | solution.py:703
  16.4 10.4 %collective-permute-start.5 = (f32[344,128]{1,0:T(8,128)S(1)}, f32[344,128]{1,0:T(8,128)S(1)}, u32[]{:S(2)}, u32[]{:S(2)}) collective-permute-start(f32[344,128]{1,0:T(8,128)S(1)} %get-tuple-element.44), channel_id=1, source_target_pairs={{4,0},{0,4},{12,8},{8,12},{5,1},{1,5},{13,9},{9,13},{6,2},{2,6},{1... | collective-permute-start | bytes 528392 | tf_op jit(solution)/shard_map/ppermute | solution.py:703
  16.5 10.3 %collective-permute-start.6 = (f32[344,128]{1,0:T(8,128)S(1)}, f32[344,128]{1,0:T(8,128)S(1)}, u32[]{:S(2)}, u32[]{:S(2)}) collective-permute-start(f32[344,128]{1,0:T(8,128)S(1)} %get-tuple-element.45), channel_id=1, source_target_pairs={{0,0},{8,4},{4,8},{12,12},{1,1},{9,5},{5,9},{13,13},{2,2},{10,6},{... | collective-permute-start | bytes 528392 | tf_op jit(solution)/shard_map/ppermute | solution.py:703

commit v16 on v15

--- a/solution.py
+++ b/solution.py
@@ -363,6 +363,16 @@
     return pltpu.roll(v, 1, 0)
 
 
+def put_with_next(ref, x, value):
+    ref[x, 0:EY] = value
+    ref[x, EY : EY + 1] = value[0:1]
+
+
+def put_with_last(ref, x, value):
+    ref[x, 8 : EY + 8] = value
+    ref[x, 7:8] = value[EY - 1 : EY]
+
+
 def z_up(v, edge):
     return jnp.where(lanes(v.shape) == BZ - 1, edge, pltpu.roll(v, BZ - 1, 1))
 
@@ -467,7 +477,7 @@
     ql_ref, late_ref, even, odd, adj_hbm, ra_ref, rsa_ref, rb_ref, rsb_ref,
     table_ref,
     out_ref, hist_ref, coef_ref, coef_strip_ref,
-    q_ref, t_ref, u_ref, scale_ref, edge_ref, w_sem,
+    u_ref, flux_ref, q_ref, t_ref, scale_ref, edge_ref, w_sem,
 ):
     w_copy = pltpu.make_async_copy(adj_hbm.at[pl.ds(1, 3)], out_ref.at[pl.ds(1, 3)], w_sem)
     w_copy.start()
@@ -523,11 +533,11 @@
         for x in range(step - 1, EX - step + 1):
             q = (initial(0, x) if step == 1 else q_ref[x]) + r_ref[place, x - r_first]
             q_ref[x] = q
-            u_ref[x] = scale_ref[x] * q
+            put_with_next(u_ref, x, scale_ref[x] * q)
 
         def close(x, flux_below, fluxes):
             flux_x, flux_y, flux_z = fluxes
-            spread = (flux_x - flux_below) + (flux_y - y_down(flux_y))
+            spread = (flux_x - flux_below) + (flux_y - flux_ref[x, 7 : EY + 7])
             spread = spread + (flux_z - z_down(flux_z, edge_ref[step - 1, x]))
             damped = coef_ref[2, x] * q_ref[x]
             t = (initial(1, x) if step == 1 else t_ref[x]) + spread
@@ -541,11 +551,13 @@
 
         waiting = flux_below = None
         for x in range(step - 1, EX - step):
-            u, buoyancy = u_ref[x], coef_ref[1, x]
-            slopes = [u_ref[x + 1] - u]
+            u, buoyancy = u_ref[x, 0:EY], coef_ref[1, x]
+            slopes = [u_ref[x + 1, 0:EY] - u]
             if x >= step:
-                slopes += [y_up(u) - u, z_up(u, edge_ref[step - 1, x]) - u]
+                slopes += [u_ref[x, 1 : EY + 1] - u, z_up(u, edge_ref[step - 1, x]) - u]
             fluxes = [buoyancy * slope for slope in slopes]
+            if x >= step:
+                put_with_last(flux_ref, x, fluxes[1])
             if BX <= x < 2 * BX:
                 for axis, slope in enumerate(slopes):
                     w = out_ref[1 + axis, x - BX] + slope[0:BY]
@@ -561,7 +573,7 @@
 def forward_kernel(
     wave_ref, own_s_ref, late_ref, even, odd, coef_ref, coef_strip_ref, s_ref, ss_ref, hist_ref,
     adjoint_ref, grad_hbm, adjoint_hbm,
-    p_ref, spread_ref, edge_ref, grad_ref, sems,
+    p_ref, flux_ref, spread_ref, edge_ref, grad_ref, sems,
 ):
     copies = [pltpu.make_async_copy(adjoint_ref, adjoint_hbm, sems.at[0])]
     copies[0].start()
@@ -598,21 +610,19 @@
         for x in range(step, EX - step):
             edge_ref[step - 1, x] = plane_edge(edges, x)
     for x in range(EX):
-        p_ref[x] = initial(0, x)
+        put_with_next(p_ref, x, initial(0, x))
 
     for step in range(1, STEPS + 1):
         k = step - 1
         def close(x, flux_below, fluxes):
             flux_x, flux_y, flux_z = fluxes
-            spread = (flux_x - flux_below) + (flux_y - y_down(flux_y))
+            spread = (flux_x - flux_below) + (flux_y - flux_ref[x, 7 : EY + 7])
             spread = spread + (flux_z - z_down(flux_z, edge_ref[step - 1, x]))
             spread = (initial(1, x) if step == 1 else spread_ref[x]) - spread
             if step < STEPS:
                 spread_ref[x] = spread
-                p_ref[x] = (
-                    coef_ref[2, x] * (p_ref[x] - coef_ref[0, x] * spread)
-                    + s_ref[k, x - SOURCE_PLANES[0]]
-                )
+                p = coef_ref[2, x] * (p_ref[x, 0:EY] - coef_ref[0, x] * spread)
+                put_with_next(p_ref, x, p + s_ref[k, x - SOURCE_PLANES[0]])
             if BX <= x < 2 * BX:
                 place = x - BX
                 term = hist_ref[k, 0, place] * spread[0:BY]
@@ -620,11 +630,13 @@
 
         waiting = flux_below = None
         for x in range(step - 1, EX - step):
-            p, buoyancy = p_ref[x], coef_ref[1, x]
-            slopes = [p_ref[x + 1] - p]
+            p, buoyancy = p_ref[x, 0:EY], coef_ref[1, x]
+            slopes = [p_ref[x + 1, 0:EY] - p]
             if x >= step:
-                slopes += [y_up(p) - p, z_up(p, edge_ref[step - 1, x]) - p]
+                slopes += [p_ref[x, 1 : EY + 1] - p, z_up(p, edge_ref[step - 1, x]) - p]
             fluxes = [buoyancy * slope for slope in slopes]
+            if x >= step:
+                put_with_last(flux_ref, x, fluxes[1])
             if BX <= x < 2 * BX:
                 place = x - BX
                 term = hist_ref[k, 1, place] * slopes[0][0:BY]
@@ -802,7 +814,8 @@
             shape(3, EY, BZ),
         ],
         [ql, adj_late, even, odd, adjoint_end, ra, rsa, rb, rsb, table],
-        [pltpu.VMEM((EX, EY, BZ), F32)] * 4
+        [pltpu.VMEM((EX, EY + 8, BZ), F32)] * 2
+        + [pltpu.VMEM((EX, EY, BZ), F32)] * 3
         + [
             pltpu.VMEM((STEPS, EX, EY, BZ), F32),
             pltpu.SemaphoreType.DMA,
@@ -817,8 +830,9 @@
             wave, own_s, late, wave_even, wave_odd, coef, coef_strip, src, src_strip, hist,
             adjoint_out,
         ],
-        [pltpu.VMEM((EX, EY, BZ), F32)] * 2
+        [pltpu.VMEM((EX, EY + 8, BZ), F32)] * 2
         + [
+            pltpu.VMEM((EX, EY, BZ), F32),
             pltpu.VMEM((STEPS, EX, EY, BZ), F32),
             pltpu.VMEM((2, BX, BY, BZ), F32),
             pltpu.SemaphoreType.DMA((3,)),

time: 28.8 us -> 28.9 us (level)
  transfers between devices with their start and end apart: 9 -> 9, of which waited for: 3 -> 3; matrix products, arithmetic and copies ran while one was open for 0% -> 0% of each run, Pallas kernels for 19% -> 20%
where the time goes in v16:
time: 28.9 us; the launch traced here: 28.7 us
  starting transfers between devices  15.7 us (54%)
  Pallas kernels  8.79 us (30%)
  waiting for transfers between devices  3.47 us (12%)
  between operations  0.73 us (3%)
    ppermute x4, starting transfers between devices, paired(): return lax.ppermute(array, 'gx', pairs)  10.5 us
    pallas_call x9, Pallas kernels, call(): pl.pallas_call(kernel, out_shape=outs, in_specs=[pl.BlockSpec(memory_spac...  8.79 us
    ppermute x3, starting transfers between devices, rotated(): lax.ppermute(array, axis, [((i + offset) % count, i) for i in range(count)])  3.11 us
    ppermute x4, waiting for transfers between devices, paired(): return lax.ppermute(array, 'gx', pairs)  2.42 us
    ppermute x2, starting transfers between devices, from_sides(): both = lax.ppermute(sends[0], axes, route(1) + route(-1))  2.14 us
    ppermute x2, waiting for transfers between devices, from_sides(): both = lax.ppermute(sends[0], axes, route(1) + route(-1))  1.04 us
  transfers between devices with their start and end apart: 9, of which 3 were waited for; matrix products, arithmetic and copies ran while one was open for 0% of the time, Pallas kernels for 20%

profile of v16, /device:TPU:18, one launch (start us, length us, event | category | flops | bytes accessed | tf_op | source)
XLA Modules:
  0.0 28.7 jit_solution(12689187313082652020)
XLA Ops:
  0.6 1.3 %shard_map.95 = (f32[256,128]{1,0:T(8,128)S(1)}, f32[256,128]{1,0:T(8,128)S(1)}, f32[128,128]{1,0:T(8,128)S(1)}, f32[64,128]{1,0:T(8,128)S(1)}, f32[64,128]{1,0:...) custom-call(f32[4,4,32,128]{3,2,1,0:T(8,128)} %stored_hbm.1, ...), custom_call_target="tpu_custom_call" | custom-call | bytes 5166000 | tf_op jit(solution)/shard_map/pallas_call | solution.py:670
  2.0 0.4 %collective-permute-start = (f32[256,128]{1,0:T(8,128)S(1)}, f32[256,128]{1,0:T(8,128)S(1)}, u32[]{:S(2)}, u32[]{:S(2)}) collective-permute-start(f32[256,128]{1,0:T(8,128)S(1)} %get-tuple-element.32), channel_id=1, source_target_pairs={{8,0},{12,4},{0,8},{4,12},{9,1},{13,5},{1,9},{5,13},{10,2},{14,6},... | collective-permute-start | bytes 393224 | tf_op jit(solution)/shard_map/ppermute | solution.py:706
  2.4 0.3 collective-permute-start.1
  2.6 0.0 collective-permute-start.3
  2.6 1.9 %collective-permute-start.2 = (f32[16,128]{1,0:T(8,128)S(1)}, f32[16,128]{1,0:T(8,128)S(1)}, u32[]{:S(2)}, u32[]{:S(2)}) collective-permute-start(f32[16,128]{1,0:T(8,128)S(1)} %get-tuple-element.34), channel_id=1, source_target_pairs={{2,1},{3,0},{0,3},{1,2},{6,5},{7,4},{4,7},{5,6},{10,9},{11,8},{8,1... | collective-permute-start | bytes 24584 | tf_op jit(solution)/shard_map/ppermute | solution.py:698
  4.5 1.2 %shard_map.96 = (f32[2,480,128]{2,1,0:T(8,128)S(1)}, f32[2,40,128]{2,1,0:T(8,128)S(1)}) custom-call(s32[3,1024]{1,0:T(4,128)S(1)} %get-tuple-element.39.receivers, f32[4,1024]{1,0:T(4,128)S(1)} %get-tuple-element.40.receiver_wave), custom_call_target="tpu_custom_call" | custom-call | bytes 4428000 | tf_op jit(solution)/shard_map/pallas_call | solution.py:670
  5.8 0.1 collective-permute-done.2.corner_up.corner_down
  5.9 0.0 collective-permute-done.3.other_ref
  5.9 0.9 %collective-permute-done.1.from_up.from_down = f32[160,128]{1,0:T(8,128)S(1)} collective-permute-done((f32[160,128]{1,0:T(8,128)S(1)}, f32[160,128]{1,0:T(8,128)S(1)}, u32[]{:S(2)}, u32[]{:S(2)}) %collective-permute-start.1) | collective-permute-done | bytes 81952 | tf_op jit(solution)/shard_map/ppermute | solution.py:698
  6.8 0.3 shard_map.97
  7.1 2.7 %collective-permute-start.4 = (f32[168,128]{1,0:T(8,128)S(1)}, f32[168,128]{1,0:T(8,128)S(1)}, u32[]{:S(2)}, u32[]{:S(2)}) collective-permute-start(f32[168,128]{1,0:T(8,128)S(1)} %get-tuple-element.42), channel_id=1, source_target_pairs={{8,0},{12,4},{0,8},{4,12},{9,1},{13,5},{1,9},{5,13},{10,2},{14,6},... | collective-permute-start | bytes 258056 | tf_op jit(solution)/shard_map/ppermute | solution.py:706
  9.8 0.0 collective-permute-done.wave_ref._
  9.8 4.6 %collective-permute-start.7 = (f32[496,128]{1,0:T(8,128)S(1)}, f32[496,128]{1,0:T(8,128)S(1)}, u32[]{:S(2)}, u32[]{:S(2)}) collective-permute-start(f32[496,128]{1,0:T(8,128)S(1)} %get-tuple-element.48), channel_id=1, source_target_pairs={{4,0},{0,4},{12,8},{8,12},{5,1},{1,5},{13,9},{9,13},{6,2},{2,6},{1... | collective-permute-start | bytes 761864 | tf_op jit(solution)/shard_map/ppermute | solution.py:715
  14.4 1.9 %collective-permute-start.8 = (f32[496,128]{1,0:T(8,128)S(1)}, f32[496,128]{1,0:T(8,128)S(1)}, u32[]{:S(2)}, u32[]{:S(2)}) collective-permute-start(f32[496,128]{1,0:T(8,128)S(1)} %get-tuple-element.49), channel_id=1, source_target_pairs={{0,0},{8,4},{4,8},{12,12},{1,1},{9,5},{5,9},{13,13},{2,2},{10,6},{... | collective-permute-start | bytes 761864 | tf_op jit(solution)/shard_map/ppermute | solution.py:715
  16.3 0.0 collective-permute-done.4.late_ref
  16.3 0.1 shard_map.98
  16.4 0.1 collective-permute-start.5
  16.5 3.9 %collective-permute-start.6 = (f32[344,128]{1,0:T(8,128)S(1)}, f32[344,128]{1,0:T(8,128)S(1)}, u32[]{:S(2)}, u32[]{:S(2)}) collective-permute-start(f32[344,128]{1,0:T(8,128)S(1)} %get-tuple-element.45), channel_id=1, source_target_pairs={{0,0},{8,4},{4,8},{12,12},{1,1},{9,5},{5,9},{13,13},{2,2},{10,6},{... | collective-permute-start | bytes 528392 | tf_op jit(solution)/shard_map/ppermute | solution.py:715
  20.4 1.0 %shard_map.100 = (f32[2,320,128]{2,1,0:T(8,128)S(1)}, f32[2,40,128]{2,1,0:T(8,128)S(1)}) custom-call(s32[3,1024]{1,0:T(4,128)S(1)} %get-tuple-element.39.receivers, f32[4,1024]{1,0:T(4,128)S(1)} %get-tuple-element.40.receiver_wave, f32[304,128]{1,0:T(8,128)S(1)} %get-tuple-element.47.adj_ref._.late_ref), custom_call_target="tpu_custom_call" | custom-call | bytes 3690000 | tf_op jit(solution)/shard_map/pallas_call | solution.py:670
  21.4 0.6 %shard_map.102 = (f32[3,400,128]{2,1,0:T(8,128)S(1)}, f32[3,40,128]{2,1,0:T(8,128)S(1)}) custom-call(s32[3,64]{1,0:T(4,128)S(1)} %get-tuple-element.56.sources, f32[4,64]{1,0:T(4,128)S(1)} %get-tuple-element.57.source_wave, f32[304,128]{1,0:T(8,128)S(1)} %get-tuple-element.47.adj_ref._.late_ref), custom_call_target="tpu_custom_call" | custom-call | bytes 1845000 | tf_op jit(solution)/shard_map/pallas_call | solution.py:670
  22.0 0.0 collective-permute-done.7.even
  22.0 2.4 %collective-permute-done.8.odd = f32[496,128]{1,0:T(8,128)S(1)} collective-permute-done((f32[496,128]{1,0:T(8,128)S(1)}, f32[496,128]{1,0:T(8,128)S(1)}, u32[]{:S(2)}, u32[]{:S(2)}) %collective-permute-start.8) | collective-permute-done | bytes 253984 | tf_op jit(solution)/shard_map/ppermute | solution.py:715
  24.4 2.4 %shard_map.101 = (f32[4,4,32,128]{3,2,1,0:T(8,128)S(1)}, f32[4,4,4,32,128]{4,3,2,1,0:T(8,128)S(1)}, f32[3,12,40,128]{3,2,1,0:T(8,128)S(1)}, f32[3,40,128]{2,1,0:T(8,128)S(1)}) custom-call(f32[256,128]{1,0:T(8,128)S(1)} %get-tuple-element.46.ql_ref, f32[304,128]{1,0:T(8,128)S(1)} %get-tuple-element.47.adj_ref._.late_ref, ...), custom_call_target="tpu_custom_call" | custom-call | bytes 14391000 | tf_op jit(solution)/shard_map/pallas_call | solution.py:670
  26.8 0.0 collective-permute-done.5.even
  26.8 0.0 collective-permute-done.6.odd
  26.8 1.9 %shard_map.103 = (f32[2,4,32,128]{3,2,1,0:T(8,128)}, f32[4,4,32,128]{3,2,1,0:T(8,128)}) custom-call(f32[256,128]{1,0:T(8,128)S(1)} %collective-permute-done.wave_ref._, f32[128,128]{1,0:T(8,128)S(1)} %get-tuple-element.43.own_s_ref, f32[168,128]{1,0:T(8,128)S(1)} %collective-permute-done.4.late_ref, f32[344,128]{1,0:T(8,128)S(1)} %collective-permute-done.5.even, ...), custom_call_target="tpu_custom_call" | custom-call | bytes 9225000 | tf_op jit(solution)/shard_map/pallas_call | solution.py:670
  (1 shorter events, 0.0 us)
Async XLA Ops:
  2.0 7.8 %collective-permute-start = (f32[256,128]{1,0:T(8,128)S(1)}, f32[256,128]{1,0:T(8,128)S(1)}, u32[]{:S(2)}, u32[]{:S(2)}) collective-permute-start(f32[256,128]{1,0:T(8,128)S(1)} %get-tuple-element.32), channel_id=1, source_target_pairs={{8,0},{12,4},{0,8},{4,12},{9,1},{13,5},{1,9},{5,13},{10,2},{14,6},... | collective-permute-start | bytes 393224 | tf_op jit(solution)/shard_map/ppermute | solution.py:706
  2.4 4.4 %collective-permute-start.1 = (f32[160,128]{1,0:T(8,128)S(1)}, f32[160,128]{1,0:T(8,128)S(1)}, u32[]{:S(2)}, u32[]{:S(2)}) collective-permute-start(f32[160,128]{1,0:T(8,128)S(1)} %get-tuple-element.33), channel_id=1, source_target_pairs={{2,0},{0,2},{3,1},{1,3},{6,4},{4,6},{7,5},{5,7},{10,8},{8,10},{11,... | collective-permute-start | bytes 245768 | tf_op jit(solution)/shard_map/ppermute | solution.py:698
  2.6 3.2 %collective-permute-start.3 = (f32[96,128]{1,0:T(8,128)S(1)}, f32[96,128]{1,0:T(8,128)S(1)}, u32[]{:S(2)}, u32[]{:S(2)}) collective-permute-start(f32[96,128]{1,0:T(8,128)S(1)} %get-tuple-element.35.strip_ref), channel_id=1, source_target_pairs={{1,0},{0,1},{3,2},{2,3},{5,4},{4,5},{7,6},{6,7},{9,8},{8,9},{11,10... | collective-permute-start | bytes 147464 | tf_op jit(solution)/shard_map/ppermute | solution.py:706
  2.6 3.2 %collective-permute-start.2 = (f32[16,128]{1,0:T(8,128)S(1)}, f32[16,128]{1,0:T(8,128)S(1)}, u32[]{:S(2)}, u32[]{:S(2)}) collective-permute-start(f32[16,128]{1,0:T(8,128)S(1)} %get-tuple-element.34), channel_id=1, source_target_pairs={{2,1},{3,0},{0,3},{1,2},{6,5},{7,4},{4,7},{5,6},{10,9},{11,8},{8,1... | collective-permute-start | bytes 24584 | tf_op jit(solution)/shard_map/ppermute | solution.py:698
  7.1 9.2 %collective-permute-start.4 = (f32[168,128]{1,0:T(8,128)S(1)}, f32[168,128]{1,0:T(8,128)S(1)}, u32[]{:S(2)}, u32[]{:S(2)}) collective-permute-start(f32[168,128]{1,0:T(8,128)S(1)} %get-tuple-element.42), channel_id=1, source_target_pairs={{8,0},{12,4},{0,8},{4,12},{9,1},{13,5},{1,9},{5,13},{10,2},{14,6},... | collective-permute-start | bytes 258056 | tf_op jit(solution)/shard_map/ppermute | solution.py:706
  9.8 12.2 %collective-permute-start.7 = (f32[496,128]{1,0:T(8,128)S(1)}, f32[496,128]{1,0:T(8,128)S(1)}, u32[]{:S(2)}, u32[]{:S(2)}) collective-permute-start(f32[496,128]{1,0:T(8,128)S(1)} %get-tuple-element.48), channel_id=1, source_target_pairs={{4,0},{0,4},{12,8},{8,12},{5,1},{1,5},{13,9},{9,13},{6,2},{2,6},{1... | collective-permute-start | bytes 761864 | tf_op jit(solution)/shard_map/ppermute | solution.py:715
  14.4 10.1 %collective-permute-start.8 = (f32[496,128]{1,0:T(8,128)S(1)}, f32[496,128]{1,0:T(8,128)S(1)}, u32[]{:S(2)}, u32[]{:S(2)}) collective-permute-start(f32[496,128]{1,0:T(8,128)S(1)} %get-tuple-element.49), channel_id=1, source_target_pairs={{0,0},{8,4},{4,8},{12,12},{1,1},{9,5},{5,9},{13,13},{2,2},{10,6},{... | collective-permute-start | bytes 761864 | tf_op jit(solution)/shard_map/ppermute | solution.py:715
  16.4 10.4 %collective-permute-start.5 = (f32[344,128]{1,0:T(8,128)S(1)}, f32[344,128]{1,0:T(8,128)S(1)}, u32[]{:S(2)}, u32[]{:S(2)}) collective-permute-start(f32[344,128]{1,0:T(8,128)S(1)} %get-tuple-element.44), channel_id=1, source_target_pairs={{4,0},{0,4},{12,8},{8,12},{5,1},{1,5},{13,9},{9,13},{6,2},{2,6},{1... | collective-permute-start | bytes 528392 | tf_op jit(solution)/shard_map/ppermute | solution.py:715
  16.5 10.4 %collective-permute-start.6 = (f32[344,128]{1,0:T(8,128)S(1)}, f32[344,128]{1,0:T(8,128)S(1)}, u32[]{:S(2)}, u32[]{:S(2)}) collective-permute-start(f32[344,128]{1,0:T(8,128)S(1)} %get-tuple-element.45), channel_id=1, source_target_pairs={{0,0},{8,4},{4,8},{12,12},{1,1},{9,5},{5,9},{13,13},{2,2},{10,6},{... | collective-permute-start | bytes 528392 | tf_op jit(solution)/shard_map/ppermute | solution.py:715

commit v17 on v13

--- a/solution.py
+++ b/solution.py
@@ -18,8 +18,9 @@
 WAVE_FIX = WAVE_OWN[2] + EY
 FIX_LANE = 3 * BX * STRIP
 ADJ_OWN = (PLANES, PLANES + BY, PLANES + BY + 13 * 8)
-WAVE_SIDE = (PLANES + 3 * BY, PLANES + 4 * BY, PLANES + 4 * BY + 6 * 8)
-ADJ_SIDE = (3 * BY, 4 * BY, 4 * BY + 9 * 8)
+WAVE_SIDE = (PLANES + 3 * BY, PLANES + 4 * BY)
+ADJ_SIDE = (3 * BY, 4 * BY)
+WAVE_TILES, ADJ_TILES = 6, 9
 
 
 def lanes(shape):
@@ -143,6 +144,33 @@
 def copy_rows(target, base, source, first, count):
     target[base : base + count] = source[pl.ds(pl.multiple_of(first, 8), count)]
     return base + count
+
+
+def halved():
+    return lax.axis_size("gy") == 2
+
+
+def tile_rows(count):
+    return (count + 1) // 2 * 8 if halved() else count * 8
+
+
+def put_tiles(target, base, source, firsts):
+    tiles = [source[pl.ds(pl.multiple_of(first, 8), 8)] for first in firsts]
+    if halved():
+        upper = lax.axis_index("gy") == 0
+        row = rows((8, BZ))
+        pairs = [(tiles[i], tiles[min(i + 1, len(tiles) - 1)]) for i in range(0, len(tiles), 2)]
+        tiles = [
+            jnp.where(
+                row < MARGIN,
+                jnp.where(upper, first, half_turn(first)),
+                jnp.where(upper, half_turn(second), second),
+            )
+            for first, second in pairs
+        ]
+    for place, tile in enumerate(tiles):
+        target[base + place * 8 : base + place * 8 + 8] = tile
+    return base + 8 * len(tiles)
 
 
 def pair_planes():
@@ -243,10 +271,11 @@
     for target, first in zip((even_ref, odd_ref), pair_planes()):
         base = copy_rows(target, 0, adj_ref, first * BY, 3 * BY)
         base = copy_rows(target, base, adj_ref, planes_end, BY)
-        base = copy_rows(target, base, adj_ref, x_end + first * 8, 24)
-        base = copy_rows(target, base, adj_ref, x_end + 32 + first * 16, 16)
-        base = copy_rows(target, base, adj_ref, x_end + 64 + first * 8, 24)
-        base = copy_rows(target, base, adj_ref, tiles_end - 8, 8 + EY)
+        near = [x_end + (first + plane) * 8 for plane in range(3)]
+        nearest = [x_end + 32 + first * 16 + plane * 8 for plane in range(2)]
+        firsts = near + nearest + [start + 64 for start in near] + [tiles_end - 8]
+        base = put_tiles(target, base, adj_ref, firsts)
+        base = copy_rows(target, base, adj_ref, tiles_end, EY)
         copy_rows(target, base, ql_ref, 0, 2 * PLANES)
 
 
@@ -264,9 +293,10 @@
         base = copy_rows(target, 0, wave_ref, 0, PLANES)
         base = copy_rows(target, base, s_ref, first * BY, 3 * BY)
         base = copy_rows(target, base, late_ref, planes_end, BY)
-        base = copy_rows(target, base, late_ref, x_end + first * 8, 24)
-        base = copy_rows(target, base, late_ref, x_end + 32 + first * 16, 16)
-        copy_rows(target, base, late_ref, tiles_end - 8, 8 + EY)
+        near = [x_end + (first + plane) * 8 for plane in range(3)]
+        nearest = [x_end + 32 + first * 16 + plane * 8 for plane in range(2)]
+        base = put_tiles(target, base, late_ref, near + nearest + [tiles_end - 8])
+        copy_rows(target, base, late_ref, tiles_end, EY)
 
 
 def split(values):
@@ -410,9 +440,19 @@
     return jnp.where(even_above, even, odd) * high
 
 
-def side_rows(base, wanted, step, block):
+def side_tile(messages, base, place, block, side):
+    if not halved():
+        return from_side(messages, base + place * 8, 8, block, side)
+    tile = from_side(messages, base + place // 2 * 8, 8, block, side)
+    upper = lax.axis_index("gy") == 0
+    turned = half_turn(tile)
+    tile = jnp.where(upper, turned, tile) if place % 2 else jnp.where(upper, tile, turned)
+    return jnp.where((rows((8, BZ)) < MARGIN) == upper, tile, 0.0)
+
+
+def side_place(wanted, plane, block):
     planes = range(BX - wanted, BX) if block == 0 else range(wanted)
-    return {plane: base + place * step for place, plane in enumerate(planes)}
+    return planes.index(plane) if plane in planes else None
 
 
 def widened(own, own_tiles, x, layout, side):
@@ -421,21 +461,22 @@
         main = own[0][own[1] + plane * BY : own[1] + plane * BY + BY]
         tile = own_tiles[0][own_tiles[1] + plane * 8 : own_tiles[1] + plane * 8 + 8]
         return jnp.concatenate([main, tile], 0)
-    parts = []
-    for (messages, base, wanted), count in zip(layout, (BY, 8)):
-        first = side_rows(base, wanted, count, block).get(plane)
-        if first is None:
-            parts.append(jnp.zeros((count, BZ), F32))
-        else:
-            parts.append(from_side(messages, first, count, block, side))
-    return jnp.concatenate(parts, 0)
-
-
-def less_plane_below(value, x, own_ref, own_rows, messages, side_rows_of, side):
+    (messages, base, wanted), (tile_messages, tile_base, tile_place, tile_wanted) = layout
+    main, tile = jnp.zeros((BY, BZ), F32), jnp.zeros((8, BZ), F32)
+    place = side_place(wanted, plane, block)
+    if place is not None:
+        main = from_side(messages, base + place * BY, BY, block, side)
+    place = side_place(tile_wanted, plane, block)
+    if place is not None:
+        tile = side_tile(tile_messages, tile_base, tile_place + place, block, side)
+    return jnp.concatenate([main, tile], 0)
+
+
+def less_plane_below(value, x, own_ref, own_rows, messages, side_layout, side):
     if x == BX:
-        planes_end, _, tiles_end = side_rows_of
+        (planes_end, x_end), count = side_layout
         main = from_side(messages, planes_end, BY, 0, side)
-        tile = from_side(messages, tiles_end - 8, 8, 0, side)
+        tile = side_tile(messages, x_end, count - 1, 0, side)
     elif x == 2 * BX:
         planes_end, _, tiles_end = own_rows
         high = side[1]
@@ -476,18 +517,22 @@
     messages = (even, odd)
     r_refs = ((ra_ref, 0), (ra_ref, 1), (rb_ref, 0), (rb_ref, 1))
     rs_refs = ((rsa_ref, 0), (rsa_ref, 1), (rsb_ref, 0), (rsb_ref, 1))
-    tiles, own_tiles, raws = ADJ_SIDE[1], ADJ_OWN[1], ADJ_SIDE[2] + EY
+    tiles, own_tiles = ADJ_SIDE[1], ADJ_OWN[1]
+    side_strip = tiles + tile_rows(ADJ_TILES)
+    raws = side_strip + EY
 
     def initial(index, x):
         own = ((ql_ref, 0), (late_ref, 0), (ql_ref, PLANES))[index]
         layout = (
-            ((messages, raws, 4), (messages, tiles, 3)),
-            ((messages, 0, 3), (messages, tiles + 24, 2)),
-            ((messages, raws + PLANES, 4), (messages, tiles + 40, 3)),
+            ((messages, raws, 4), (messages, tiles, 0, 3)),
+            ((messages, 0, 3), (messages, tiles, 3, 2)),
+            ((messages, raws + PLANES, 4), (messages, tiles, 5, 3)),
         )[index]
         value = widened(own, (late_ref, own_tiles + 32 * index), x, layout, side)
         if index == 1:
-            value = less_plane_below(value, x, late_ref, ADJ_OWN, messages, ADJ_SIDE, side)
+            value = less_plane_below(
+                value, x, late_ref, ADJ_OWN, messages, (ADJ_SIDE, ADJ_TILES), side
+            )
         return value
 
     for x in range(EX):
@@ -496,9 +541,9 @@
         scale_ref[x] = stiff * damp
     own_strip = late_ref[ADJ_OWN[2] : ADJ_OWN[2] + EY]
     q_s, t_s, label_s = (
-        whole_strip(own_strip, messages, ADJ_SIDE[2], slot, side) for slot in range(3)
-    )
-    t_s = t_s - strip_below(own_strip, messages, ADJ_SIDE[2], 3, side)
+        whole_strip(own_strip, messages, side_strip, slot, side) for slot in range(3)
+    )
+    t_s = t_s - strip_below(own_strip, messages, side_strip, 3, side)
     stiff_s, buoy_s, damp_s = coefficients(label_s, table_ref)
     scale_s = stiff_s * damp_s
     coef_strip_ref[0], coef_strip_ref[1], coef_strip_ref[2] = stiff_s, buoy_s, damp_s
@@ -573,23 +618,26 @@
     side = sides()
     messages = (even, odd)
     tiles, own_tiles = WAVE_SIDE[1], WAVE_OWN[1]
+    side_strip = tiles + tile_rows(WAVE_TILES)
 
     def initial(index, x):
         layout = (
-            ((messages, 0, 4), (messages, tiles, 3)),
-            ((messages, PLANES, 3), (messages, tiles + 24, 2)),
+            ((messages, 0, 4), (messages, tiles, 0, 3)),
+            ((messages, PLANES, 3), (messages, tiles, 3, 2)),
         )[index]
         own = ((wave_ref, 0), (own_s_ref, 0))[index]
         value = widened(own, (late_ref, own_tiles + 32 * index), x, layout, side)
         if index == 1:
-            value = less_plane_below(value, x, late_ref, WAVE_OWN, messages, WAVE_SIDE, side)
+            value = less_plane_below(
+                value, x, late_ref, WAVE_OWN, messages, (WAVE_SIDE, WAVE_TILES), side
+            )
         return value
 
     own_strip = late_ref[WAVE_OWN[2] : WAVE_OWN[2] + EY]
     p_s, s_s = (
-        whole_strip(own_strip, messages, WAVE_SIDE[2], slot, side) for slot in range(2)
-    )
-    s_s = s_s - strip_below(own_strip, messages, WAVE_SIDE[2], 2, side)
+        whole_strip(own_strip, messages, side_strip, slot, side) for slot in range(2)
+    )
+    s_s = s_s - strip_below(own_strip, messages, side_strip, 2, side)
     stiff_s, buoy_s, damp_s = coef_strip_ref[0], coef_strip_ref[1], coef_strip_ref[2]
 
     for step in range(1, STEPS + 1):
@@ -767,7 +815,7 @@
     ra, rb = ra.reshape(2, early_planes, EY, BZ), rb.reshape(2, EX, EY, BZ)
     even, odd = call(
         adjoint_join_kernel,
-        [shape(ADJ_SIDE[2] + EY + 2 * PLANES, BZ)] * 2,
+        [shape(ADJ_SIDE[1] + tile_rows(ADJ_TILES) + EY + 2 * PLANES, BZ)] * 2,
         [ql, adj_late, wave],
         [],
         "vva",
@@ -784,7 +832,7 @@
     src = src.reshape(STEPS - 1, source_planes, EY, BZ)
     own_s, wave_even, wave_odd = call(
         join_kernel,
-        [shape(PLANES, BZ)] + [shape(WAVE_SIDE[2] + EY, BZ)] * 2,
+        [shape(PLANES, BZ)] + [shape(WAVE_SIDE[1] + tile_rows(WAVE_TILES) + EY, BZ)] * 2,
         [wave, late],
         [],
         "vv",

time: 28.8 us -> 28.3 us (0.983)
  waiting for transfers between devices: 3.47 us -> 3.18 us
    ppermute x4, waiting for transfers between devices: 2.42 us -> 2.13 us  [paired(): return lax.ppermute(array, 'gx', pairs)]
where the time goes in v17:
time: 28.3 us; the launch traced here: 28.2 us
  starting transfers between devices  15.7 us (55%)
  Pallas kernels  8.53 us (30%)
  waiting for transfers between devices  3.18 us (11%)
  between operations  0.73 us (3%)
    ppermute x4, starting transfers between devices, paired(): return lax.ppermute(array, 'gx', pairs)  10.5 us
    pallas_call x9, Pallas kernels, call(): pl.pallas_call(kernel, out_shape=outs, in_specs=[pl.BlockSpec(memory_spac...  8.53 us
    ppermute x3, starting transfers between devices, rotated(): lax.ppermute(array, axis, [((i + offset) % count, i) for i in range(count)])  3.11 us
    ppermute x2, starting transfers between devices, from_sides(): both = lax.ppermute(sends[0], axes, route(1) + route(-1))  2.14 us
    ppermute x4, waiting for transfers between devices, paired(): return lax.ppermute(array, 'gx', pairs)  2.13 us
    ppermute x2, waiting for transfers between devices, from_sides(): both = lax.ppermute(sends[0], axes, route(1) + route(-1))  1.04 us
  transfers between devices with their start and end apart: 9, of which 3 were waited for; matrix products, arithmetic and copies ran while one was open for 0% of the time, Pallas kernels for 19%

profile of v17, /device:TPU:18, one launch (start us, length us, event | category | flops | bytes accessed | tf_op | source)
XLA Modules:
  0.0 28.2 jit_solution(13278015236207411426)
XLA Ops:
  0.6 1.3 %shard_map.95 = (f32[256,128]{1,0:T(8,128)S(1)}, f32[256,128]{1,0:T(8,128)S(1)}, f32[128,128]{1,0:T(8,128)S(1)}, f32[64,128]{1,0:T(8,128)S(1)}, f32[64,128]{1,0:...) custom-call(f32[4,4,32,128]{3,2,1,0:T(8,128)} %stored_hbm.1, ...), custom_call_target="tpu_custom_call" | custom-call | bytes 5166000 | tf_op jit(solution)/shard_map/pallas_call | solution.py:703
  2.0 0.4 %collective-permute-start = (f32[256,128]{1,0:T(8,128)S(1)}, f32[256,128]{1,0:T(8,128)S(1)}, u32[]{:S(2)}, u32[]{:S(2)}) collective-permute-start(f32[256,128]{1,0:T(8,128)S(1)} %get-tuple-element.32), channel_id=1, source_target_pairs={{8,0},{12,4},{0,8},{4,12},{9,1},{13,5},{1,9},{5,13},{10,2},{14,6},... | collective-permute-start | bytes 393224 | tf_op jit(solution)/shard_map/ppermute | solution.py:739
  2.4 0.3 collective-permute-start.1
  2.6 0.0 collective-permute-start.3
  2.6 1.9 %collective-permute-start.2 = (f32[16,128]{1,0:T(8,128)S(1)}, f32[16,128]{1,0:T(8,128)S(1)}, u32[]{:S(2)}, u32[]{:S(2)}) collective-permute-start(f32[16,128]{1,0:T(8,128)S(1)} %get-tuple-element.34), channel_id=1, source_target_pairs={{2,1},{3,0},{0,3},{1,2},{6,5},{7,4},{4,7},{5,6},{10,9},{11,8},{8,1... | collective-permute-start | bytes 24584 | tf_op jit(solution)/shard_map/ppermute | solution.py:731
  4.5 1.2 %shard_map.96 = (f32[2,480,128]{2,1,0:T(8,128)S(1)}, f32[2,40,128]{2,1,0:T(8,128)S(1)}) custom-call(s32[3,1024]{1,0:T(4,128)S(1)} %get-tuple-element.39.receivers, f32[4,1024]{1,0:T(4,128)S(1)} %get-tuple-element.40.receiver_wave), custom_call_target="tpu_custom_call" | custom-call | bytes 4428000 | tf_op jit(solution)/shard_map/pallas_call | solution.py:703
  5.8 0.1 collective-permute-done.2.corner_up.corner_down
  5.9 0.0 collective-permute-done.3.other_ref
  5.9 0.9 %collective-permute-done.1.from_up.from_down = f32[160,128]{1,0:T(8,128)S(1)} collective-permute-done((f32[160,128]{1,0:T(8,128)S(1)}, f32[160,128]{1,0:T(8,128)S(1)}, u32[]{:S(2)}, u32[]{:S(2)}) %collective-permute-start.1) | collective-permute-done | bytes 81952 | tf_op jit(solution)/shard_map/ppermute | solution.py:731
  6.8 0.3 shard_map.97
  7.1 2.7 %collective-permute-start.4 = (f32[168,128]{1,0:T(8,128)S(1)}, f32[168,128]{1,0:T(8,128)S(1)}, u32[]{:S(2)}, u32[]{:S(2)}) collective-permute-start(f32[168,128]{1,0:T(8,128)S(1)} %get-tuple-element.42), channel_id=1, source_target_pairs={{8,0},{12,4},{0,8},{4,12},{9,1},{13,5},{1,9},{5,13},{10,2},{14,6},... | collective-permute-start | bytes 258056 | tf_op jit(solution)/shard_map/ppermute | solution.py:739
  9.8 0.0 collective-permute-done.wave_ref._
  9.8 4.6 %collective-permute-start.7 = (f32[464,128]{1,0:T(8,128)S(1)}, f32[464,128]{1,0:T(8,128)S(1)}, u32[]{:S(2)}, u32[]{:S(2)}) collective-permute-start(f32[464,128]{1,0:T(8,128)S(1)} %get-tuple-element.48), channel_id=1, source_target_pairs={{4,0},{0,4},{12,8},{8,12},{5,1},{1,5},{13,9},{9,13},{6,2},{2,6},{1... | collective-permute-start | bytes 712712 | tf_op jit(solution)/shard_map/ppermute | solution.py:748
  14.4 1.9 %collective-permute-start.8 = (f32[464,128]{1,0:T(8,128)S(1)}, f32[464,128]{1,0:T(8,128)S(1)}, u32[]{:S(2)}, u32[]{:S(2)}) collective-permute-start(f32[464,128]{1,0:T(8,128)S(1)} %get-tuple-element.49), channel_id=1, source_target_pairs={{0,0},{8,4},{4,8},{12,12},{1,1},{9,5},{5,9},{13,13},{2,2},{10,6},{... | collective-permute-start | bytes 712712 | tf_op jit(solution)/shard_map/ppermute | solution.py:748
  16.3 0.0 collective-permute-done.4.late_ref
  16.3 0.1 shard_map.98
  16.4 0.1 collective-permute-start.5
  16.5 3.9 %collective-permute-start.6 = (f32[320,128]{1,0:T(8,128)S(1)}, f32[320,128]{1,0:T(8,128)S(1)}, u32[]{:S(2)}, u32[]{:S(2)}) collective-permute-start(f32[320,128]{1,0:T(8,128)S(1)} %get-tuple-element.45), channel_id=1, source_target_pairs={{0,0},{8,4},{4,8},{12,12},{1,1},{9,5},{5,9},{13,13},{2,2},{10,6},{... | collective-permute-start | bytes 491528 | tf_op jit(solution)/shard_map/ppermute | solution.py:748
  20.4 1.0 %shard_map.100 = (f32[2,320,128]{2,1,0:T(8,128)S(1)}, f32[2,40,128]{2,1,0:T(8,128)S(1)}) custom-call(s32[3,1024]{1,0:T(4,128)S(1)} %get-tuple-element.39.receivers, f32[4,1024]{1,0:T(4,128)S(1)} %get-tuple-element.40.receiver_wave, f32[304,128]{1,0:T(8,128)S(1)} %get-tuple-element.47.adj_ref._.late_ref), custom_call_target="tpu_custom_call" | custom-call | bytes 3690000 | tf_op jit(solution)/shard_map/pallas_call | solution.py:703
  21.4 0.5 %shard_map.102 = (f32[3,400,128]{2,1,0:T(8,128)S(1)}, f32[3,40,128]{2,1,0:T(8,128)S(1)}) custom-call(s32[3,64]{1,0:T(4,128)S(1)} %get-tuple-element.56.sources, f32[4,64]{1,0:T(4,128)S(1)} %get-tuple-element.57.source_wave, f32[304,128]{1,0:T(8,128)S(1)} %get-tuple-element.47.adj_ref._.late_ref), custom_call_target="tpu_custom_call" | custom-call | bytes 1845000 | tf_op jit(solution)/shard_map/pallas_call | solution.py:703
  22.0 0.0 collective-permute-done.7.even
  22.0 2.1 %collective-permute-done.8.odd = f32[464,128]{1,0:T(8,128)S(1)} collective-permute-done((f32[464,128]{1,0:T(8,128)S(1)}, f32[464,128]{1,0:T(8,128)S(1)}, u32[]{:S(2)}, u32[]{:S(2)}) %collective-permute-start.8) | collective-permute-done | bytes 237600 | tf_op jit(solution)/shard_map/ppermute | solution.py:748
  24.1 2.2 %shard_map.101 = (f32[4,4,32,128]{3,2,1,0:T(8,128)S(1)}, f32[4,4,4,32,128]{4,3,2,1,0:T(8,128)S(1)}, f32[3,12,40,128]{3,2,1,0:T(8,128)S(1)}, f32[3,40,128]{2,1,0:T(8,128)S(1)}) custom-call(f32[256,128]{1,0:T(8,128)S(1)} %get-tuple-element.46.ql_ref, f32[304,128]{1,0:T(8,128)S(1)} %get-tuple-element.47.adj_ref._.late_ref, ...), custom_call_target="tpu_custom_call" | custom-call | bytes 14391000 | tf_op jit(solution)/shard_map/pallas_call | solution.py:703
  26.3 0.0 collective-permute-done.5.even
  26.3 0.0 collective-permute-done.6.odd
  26.4 1.8 %shard_map.103 = (f32[2,4,32,128]{3,2,1,0:T(8,128)}, f32[4,4,32,128]{3,2,1,0:T(8,128)}) custom-call(f32[256,128]{1,0:T(8,128)S(1)} %collective-permute-done.wave_ref._, f32[128,128]{1,0:T(8,128)S(1)} %get-tuple-element.43.own_s_ref, f32[168,128]{1,0:T(8,128)S(1)} %collective-permute-done.4.late_ref, f32[320,128]{1,0:T(8,128)S(1)} %collective-permute-done.5.even, ...), custom_call_target="tpu_custom_call" | custom-call | bytes 9225000 | tf_op jit(solution)/shard_map/pallas_call | solution.py:703
  (1 shorter events, 0.0 us)
Async XLA Ops:
  2.0 7.8 %collective-permute-start = (f32[256,128]{1,0:T(8,128)S(1)}, f32[256,128]{1,0:T(8,128)S(1)}, u32[]{:S(2)}, u32[]{:S(2)}) collective-permute-start(f32[256,128]{1,0:T(8,128)S(1)} %get-tuple-element.32), channel_id=1, source_target_pairs={{8,0},{12,4},{0,8},{4,12},{9,1},{13,5},{1,9},{5,13},{10,2},{14,6},... | collective-permute-start | bytes 393224 | tf_op jit(solution)/shard_map/ppermute | solution.py:739
  2.4 4.4 %collective-permute-start.1 = (f32[160,128]{1,0:T(8,128)S(1)}, f32[160,128]{1,0:T(8,128)S(1)}, u32[]{:S(2)}, u32[]{:S(2)}) collective-permute-start(f32[160,128]{1,0:T(8,128)S(1)} %get-tuple-element.33), channel_id=1, source_target_pairs={{2,0},{0,2},{3,1},{1,3},{6,4},{4,6},{7,5},{5,7},{10,8},{8,10},{11,... | collective-permute-start | bytes 245768 | tf_op jit(solution)/shard_map/ppermute | solution.py:731
  2.6 3.2 %collective-permute-start.3 = (f32[96,128]{1,0:T(8,128)S(1)}, f32[96,128]{1,0:T(8,128)S(1)}, u32[]{:S(2)}, u32[]{:S(2)}) collective-permute-start(f32[96,128]{1,0:T(8,128)S(1)} %get-tuple-element.35.strip_ref), channel_id=1, source_target_pairs={{1,0},{0,1},{3,2},{2,3},{5,4},{4,5},{7,6},{6,7},{9,8},{8,9},{11,10... | collective-permute-start | bytes 147464 | tf_op jit(solution)/shard_map/ppermute | solution.py:739
  2.6 3.2 %collective-permute-start.2 = (f32[16,128]{1,0:T(8,128)S(1)}, f32[16,128]{1,0:T(8,128)S(1)}, u32[]{:S(2)}, u32[]{:S(2)}) collective-permute-start(f32[16,128]{1,0:T(8,128)S(1)} %get-tuple-element.34), channel_id=1, source_target_pairs={{2,1},{3,0},{0,3},{1,2},{6,5},{7,4},{4,7},{5,6},{10,9},{11,8},{8,1... | collective-permute-start | bytes 24584 | tf_op jit(solution)/shard_map/ppermute | solution.py:731
  7.1 9.2 %collective-permute-start.4 = (f32[168,128]{1,0:T(8,128)S(1)}, f32[168,128]{1,0:T(8,128)S(1)}, u32[]{:S(2)}, u32[]{:S(2)}) collective-permute-start(f32[168,128]{1,0:T(8,128)S(1)} %get-tuple-element.42), channel_id=1, source_target_pairs={{8,0},{12,4},{0,8},{4,12},{9,1},{13,5},{1,9},{5,13},{10,2},{14,6},... | collective-permute-start | bytes 258056 | tf_op jit(solution)/shard_map/ppermute | solution.py:739
  9.8 12.2 %collective-permute-start.7 = (f32[464,128]{1,0:T(8,128)S(1)}, f32[464,128]{1,0:T(8,128)S(1)}, u32[]{:S(2)}, u32[]{:S(2)}) collective-permute-start(f32[464,128]{1,0:T(8,128)S(1)} %get-tuple-element.48), channel_id=1, source_target_pairs={{4,0},{0,4},{12,8},{8,12},{5,1},{1,5},{13,9},{9,13},{6,2},{2,6},{1... | collective-permute-start | bytes 712712 | tf_op jit(solution)/shard_map/ppermute | solution.py:748
  14.4 9.7 %collective-permute-start.8 = (f32[464,128]{1,0:T(8,128)S(1)}, f32[464,128]{1,0:T(8,128)S(1)}, u32[]{:S(2)}, u32[]{:S(2)}) collective-permute-start(f32[464,128]{1,0:T(8,128)S(1)} %get-tuple-element.49), channel_id=1, source_target_pairs={{0,0},{8,4},{4,8},{12,12},{1,1},{9,5},{5,9},{13,13},{2,2},{10,6},{... | collective-permute-start | bytes 712712 | tf_op jit(solution)/shard_map/ppermute | solution.py:748
  16.4 9.9 %collective-permute-start.5 = (f32[320,128]{1,0:T(8,128)S(1)}, f32[320,128]{1,0:T(8,128)S(1)}, u32[]{:S(2)}, u32[]{:S(2)}) collective-permute-start(f32[320,128]{1,0:T(8,128)S(1)} %get-tuple-element.44), channel_id=1, source_target_pairs={{4,0},{0,4},{12,8},{8,12},{5,1},{1,5},{13,9},{9,13},{6,2},{2,6},{1... | collective-permute-start | bytes 491528 | tf_op jit(solution)/shard_map/ppermute | solution.py:748
  16.5 9.9 %collective-permute-start.6 = (f32[320,128]{1,0:T(8,128)S(1)}, f32[320,128]{1,0:T(8,128)S(1)}, u32[]{:S(2)}, u32[]{:S(2)}) collective-permute-start(f32[320,128]{1,0:T(8,128)S(1)} %get-tuple-element.45), channel_id=1, source_target_pairs={{0,0},{8,4},{4,8},{12,12},{1,1},{9,5},{5,9},{13,13},{2,2},{10,6},{... | collective-permute-start | bytes 491528 | tf_op jit(solution)/shard_map/ppermute | solution.py:748

commit v18 on v17

--- a/solution.py
+++ b/solution.py
@@ -118,6 +118,7 @@
             last_y_ref[index : index + 8] = vy[BY - 8 : BY]
     for kind in range(2):
         last_x_ref[kind * BY : kind * BY + BY] = previous[kind]
+    wave_ref[2 * PLANES : 2 * PLANES + BY] = jnp.zeros((BY, BZ), F32)
     for group in range(3):
         strip_ref[group * BY : group * BY + BY] = strips[group]
         tiles[9 * BX + group] = edge_tile(strips[group])
@@ -266,7 +267,7 @@
             target[tiles_end : tiles_end + EY] = strip
 
 
-def adjoint_join_kernel(ql_ref, adj_ref, _, even_ref, odd_ref):
+def adjoint_join_kernel(ql_ref, adj_ref, even_ref, odd_ref):
     planes_end, x_end, tiles_end = ADJ_OWN
     for target, first in zip((even_ref, odd_ref), pair_planes()):
         base = copy_rows(target, 0, adj_ref, first * BY, 3 * BY)
@@ -761,7 +762,7 @@
     wave, ql, t, last_x, last_y, strips, table, receivers, receiver_wave, sources, source_wave, *sends = call(
         load_kernel,
         [
-            shape(2 * PLANES, BZ),
+            shape(2 * PLANES + 32, BZ),
             shape(2 * PLANES, BZ),
             shape(PLANES, BZ),
             shape(2 * BY, BZ),
@@ -816,9 +817,9 @@
     even, odd = call(
         adjoint_join_kernel,
         [shape(ADJ_SIDE[1] + tile_rows(ADJ_TILES) + EY + 2 * PLANES, BZ)] * 2,
-        [ql, adj_late, wave],
+        [ql, adj_late],
         [],
-        "vva",
+        "vv",
     )
     even, odd = paired(even, False), paired(odd, True)
     src, src_strip = call(

time: 28.3 us -> 27.9 us (0.986)
  the two profiles are of different devices: /device:TPU:18 before, /device:TPU:8 now
where the time goes in v18:
time: 27.9 us; the launch traced here: 27.6 us
  starting transfers between devices  16.1 us (58%)
  Pallas kernels  8.55 us (31%)
  waiting for transfers between devices  2.19 us (8%)
  between operations  0.72 us (3%)
    ppermute x4, starting transfers between devices, paired(): return lax.ppermute(array, 'gx', pairs)  10.9 us
    pallas_call x9, Pallas kernels, call(): pl.pallas_call(kernel, out_shape=outs, in_specs=[pl.BlockSpec(memory_spac...  8.55 us
    ppermute x3, starting transfers between devices, rotated(): lax.ppermute(array, axis, [((i + offset) % count, i) for i in range(count)])  2.99 us
    ppermute x2, starting transfers between devices, from_sides(): both = lax.ppermute(sends[0], axes, route(1) + route(-1))  2.2 us
    ppermute x2, waiting for transfers between devices, from_sides(): both = lax.ppermute(sends[0], axes, route(1) + route(-1))  1.18 us
    ppermute x3, waiting for transfers between devices, rotated(): lax.ppermute(array, axis, [((i + offset) % count, i) for i in range(count)])  0.85 us
  transfers between devices with their start and end apart: 9, of which 3 were waited for; matrix products, arithmetic and copies ran while one was open for 0% of the time, Pallas kernels for 20%

profile of v18, /device:TPU:8, one launch (start us, length us, event | category | flops | bytes accessed | tf_op | source)
XLA Modules:
  0.0 27.6 jit_solution(5314263953538908934)
XLA Ops:
  0.6 1.3 %shard_map.95 = (f32[288,128]{1,0:T(8,128)S(1)}, f32[256,128]{1,0:T(8,128)S(1)}, f32[128,128]{1,0:T(8,128)S(1)}, f32[64,128]{1,0:T(8,128)S(1)}, f32[64,128]{1,0:...) custom-call(f32[4,4,32,128]{3,2,1,0:T(8,128)} %stored_hbm.1, ...), custom_call_target="tpu_custom_call" | custom-call | bytes 5166000 | tf_op jit(solution)/shard_map/pallas_call | solution.py:704
  2.0 1.6 %collective-permute-start.1 = (f32[160,128]{1,0:T(8,128)S(1)}, f32[160,128]{1,0:T(8,128)S(1)}, u32[]{:S(2)}, u32[]{:S(2)}) collective-permute-start(f32[160,128]{1,0:T(8,128)S(1)} %get-tuple-element.33), channel_id=1, source_target_pairs={{2,0},{0,2},{3,1},{1,3},{6,4},{4,6},{7,5},{5,7},{10,8},{8,10},{11,... | collective-permute-start | bytes 245768 | tf_op jit(solution)/shard_map/ppermute | solution.py:732
  3.5 2.6 %collective-permute-start = (f32[288,128]{1,0:T(8,128)S(1)}, f32[288,128]{1,0:T(8,128)S(1)}, u32[]{:S(2)}, u32[]{:S(2)}) collective-permute-start(f32[288,128]{1,0:T(8,128)S(1)} %get-tuple-element.32), channel_id=1, source_target_pairs={{8,0},{12,4},{0,8},{4,12},{9,1},{13,5},{1,9},{5,13},{10,2},{14,6},... | collective-permute-start | bytes 442376 | tf_op jit(solution)/shard_map/ppermute | solution.py:740
  6.1 0.0 collective-permute-start.3
  6.1 0.6 %collective-permute-start.2 = (f32[16,128]{1,0:T(8,128)S(1)}, f32[16,128]{1,0:T(8,128)S(1)}, u32[]{:S(2)}, u32[]{:S(2)}) collective-permute-start(f32[16,128]{1,0:T(8,128)S(1)} %get-tuple-element.34), channel_id=1, source_target_pairs={{2,1},{3,0},{0,3},{1,2},{6,5},{7,4},{4,7},{5,6},{10,9},{11,8},{8,1... | collective-permute-start | bytes 24584 | tf_op jit(solution)/shard_map/ppermute | solution.py:732
  6.8 1.2 %shard_map.96 = (f32[2,480,128]{2,1,0:T(8,128)S(1)}, f32[2,40,128]{2,1,0:T(8,128)S(1)}) custom-call(s32[3,1024]{1,0:T(4,128)S(1)} %get-tuple-element.39.receivers, f32[4,1024]{1,0:T(4,128)S(1)} %get-tuple-element.40.receiver_wave), custom_call_target="tpu_custom_call" | custom-call | bytes 4428000 | tf_op jit(solution)/shard_map/pallas_call | solution.py:704
  8.0 1.2 %collective-permute-done.2.corner_up.corner_down = f32[16,128]{1,0:T(8,128)S(1)} collective-permute-done((f32[16,128]{1,0:T(8,128)S(1)}, f32[16,128]{1,0:T(8,128)S(1)}, u32[]{:S(2)}, u32[]{:S(2)}) %collective-permute-start.2) | collective-permute-done | bytes 8224 | tf_op jit(solution)/shard_map/ppermute | solution.py:732
  9.2 0.0 collective-permute-done.3.other_ref
  9.2 0.0 collective-permute-done.1.from_up.from_down
  9.2 0.3 shard_map.97
  9.5 0.4 %collective-permute-start.4 = (f32[168,128]{1,0:T(8,128)S(1)}, f32[168,128]{1,0:T(8,128)S(1)}, u32[]{:S(2)}, u32[]{:S(2)}) collective-permute-start(f32[168,128]{1,0:T(8,128)S(1)} %get-tuple-element.42), channel_id=1, source_target_pairs={{8,0},{12,4},{0,8},{4,12},{9,1},{13,5},{1,9},{5,13},{10,2},{14,6},... | collective-permute-start | bytes 258056 | tf_op jit(solution)/shard_map/ppermute | solution.py:740
  9.9 0.5 %collective-permute-start.7 = (f32[464,128]{1,0:T(8,128)S(1)}, f32[464,128]{1,0:T(8,128)S(1)}, u32[]{:S(2)}, u32[]{:S(2)}) collective-permute-start(f32[464,128]{1,0:T(8,128)S(1)} %get-tuple-element.48), channel_id=1, source_target_pairs={{4,0},{0,4},{12,8},{8,12},{5,1},{1,5},{13,9},{9,13},{6,2},{2,6},{1... | collective-permute-start | bytes 712712 | tf_op jit(solution)/shard_map/ppermute | solution.py:749
  10.4 4.6 %collective-permute-start.8 = (f32[464,128]{1,0:T(8,128)S(1)}, f32[464,128]{1,0:T(8,128)S(1)}, u32[]{:S(2)}, u32[]{:S(2)}) collective-permute-start(f32[464,128]{1,0:T(8,128)S(1)} %get-tuple-element.49), channel_id=1, source_target_pairs={{0,0},{8,4},{4,8},{12,12},{1,1},{9,5},{5,9},{13,13},{2,2},{10,6},{... | collective-permute-start | bytes 712712 | tf_op jit(solution)/shard_map/ppermute | solution.py:749
  15.0 0.0 collective-permute-done.wave_ref
  15.0 0.8 %collective-permute-done.4.late_ref = f32[168,128]{1,0:T(8,128)S(1)} collective-permute-done((f32[168,128]{1,0:T(8,128)S(1)}, f32[168,128]{1,0:T(8,128)S(1)}, u32[]{:S(2)}, u32[]{:S(2)}) %collective-permute-start.4) | collective-permute-done | bytes 86048 | tf_op jit(solution)/shard_map/ppermute | solution.py:740
  15.9 0.1 shard_map.98
  16.0 2.1 %collective-permute-start.5 = (f32[320,128]{1,0:T(8,128)S(1)}, f32[320,128]{1,0:T(8,128)S(1)}, u32[]{:S(2)}, u32[]{:S(2)}) collective-permute-start(f32[320,128]{1,0:T(8,128)S(1)} %get-tuple-element.44), channel_id=1, source_target_pairs={{4,0},{0,4},{12,8},{8,12},{5,1},{1,5},{13,9},{9,13},{6,2},{2,6},{1... | collective-permute-start | bytes 491528 | tf_op jit(solution)/shard_map/ppermute | solution.py:749
  18.0 3.8 %collective-permute-start.6 = (f32[320,128]{1,0:T(8,128)S(1)}, f32[320,128]{1,0:T(8,128)S(1)}, u32[]{:S(2)}, u32[]{:S(2)}) collective-permute-start(f32[320,128]{1,0:T(8,128)S(1)} %get-tuple-element.45), channel_id=1, source_target_pairs={{0,0},{8,4},{4,8},{12,12},{1,1},{9,5},{5,9},{13,13},{2,2},{10,6},{... | collective-permute-start | bytes 491528 | tf_op jit(solution)/shard_map/ppermute | solution.py:749
  21.8 1.0 %shard_map.100 = (f32[2,320,128]{2,1,0:T(8,128)S(1)}, f32[2,40,128]{2,1,0:T(8,128)S(1)}) custom-call(s32[3,1024]{1,0:T(4,128)S(1)} %get-tuple-element.39.receivers, f32[4,1024]{1,0:T(4,128)S(1)} %get-tuple-element.40.receiver_wave, f32[304,128]{1,0:T(8,128)S(1)} %get-tuple-element.47.adj_ref._.late_ref), custom_call_target="tpu_custom_call" | custom-call | bytes 3690000 | tf_op jit(solution)/shard_map/pallas_call | solution.py:704
  22.8 0.6 %shard_map.102 = (f32[3,400,128]{2,1,0:T(8,128)S(1)}, f32[3,40,128]{2,1,0:T(8,128)S(1)}) custom-call(s32[3,64]{1,0:T(4,128)S(1)} %get-tuple-element.56.sources, f32[4,64]{1,0:T(4,128)S(1)} %get-tuple-element.57.source_wave, f32[304,128]{1,0:T(8,128)S(1)} %get-tuple-element.47.adj_ref._.late_ref), custom_call_target="tpu_custom_call" | custom-call | bytes 1845000 | tf_op jit(solution)/shard_map/pallas_call | solution.py:704
  23.4 0.0 collective-permute-done.7.even
  23.4 0.0 collective-permute-done.8.odd
  23.4 2.2 %shard_map.101 = (f32[4,4,32,128]{3,2,1,0:T(8,128)S(1)}, f32[4,4,4,32,128]{4,3,2,1,0:T(8,128)S(1)}, f32[3,12,40,128]{3,2,1,0:T(8,128)S(1)}, f32[3,40,128]{2,1,0:T(8,128)S(1)}) custom-call(f32[256,128]{1,0:T(8,128)S(1)} %get-tuple-element.46.ql_ref, f32[304,128]{1,0:T(8,128)S(1)} %get-tuple-element.47.adj_ref._.late_ref, ...), custom_call_target="tpu_custom_call" | custom-call | bytes 14391000 | tf_op jit(solution)/shard_map/pallas_call | solution.py:704
  25.6 0.0 collective-permute-done.5.even
  25.6 0.2 collective-permute-done.6.odd
  25.8 1.8 %shard_map.103 = (f32[2,4,32,128]{3,2,1,0:T(8,128)}, f32[4,4,32,128]{3,2,1,0:T(8,128)}) custom-call(f32[288,128]{1,0:T(8,128)S(1)} %collective-permute-done.wave_ref, f32[128,128]{1,0:T(8,128)S(1)} %get-tuple-element.43.own_s_ref, f32[168,128]{1,0:T(8,128)S(1)} %collective-permute-done.4.late_ref, f32[320,128]{1,0:T(8,128)S(1)} %collective-permute-done.5.even, ...), custom_call_target="tpu_custom_call" | custom-call | bytes 9225000 | tf_op jit(solution)/shard_map/pallas_call | solution.py:704
  (1 shorter events, 0.0 us)
Async XLA Ops:
  2.0 7.2 %collective-permute-start.1 = (f32[160,128]{1,0:T(8,128)S(1)}, f32[160,128]{1,0:T(8,128)S(1)}, u32[]{:S(2)}, u32[]{:S(2)}) collective-permute-start(f32[160,128]{1,0:T(8,128)S(1)} %get-tuple-element.33), channel_id=1, source_target_pairs={{2,0},{0,2},{3,1},{1,3},{6,4},{4,6},{7,5},{5,7},{10,8},{8,10},{11,... | collective-permute-start | bytes 245768 | tf_op jit(solution)/shard_map/ppermute | solution.py:732
  3.5 11.5 %collective-permute-start = (f32[288,128]{1,0:T(8,128)S(1)}, f32[288,128]{1,0:T(8,128)S(1)}, u32[]{:S(2)}, u32[]{:S(2)}) collective-permute-start(f32[288,128]{1,0:T(8,128)S(1)} %get-tuple-element.32), channel_id=1, source_target_pairs={{8,0},{12,4},{0,8},{4,12},{9,1},{13,5},{1,9},{5,13},{10,2},{14,6},... | collective-permute-start | bytes 442376 | tf_op jit(solution)/shard_map/ppermute | solution.py:740
  6.1 3.1 %collective-permute-start.3 = (f32[96,128]{1,0:T(8,128)S(1)}, f32[96,128]{1,0:T(8,128)S(1)}, u32[]{:S(2)}, u32[]{:S(2)}) collective-permute-start(f32[96,128]{1,0:T(8,128)S(1)} %get-tuple-element.35.strip_ref), channel_id=1, source_target_pairs={{1,0},{0,1},{3,2},{2,3},{5,4},{4,5},{7,6},{6,7},{9,8},{8,9},{11,10... | collective-permute-start | bytes 147464 | tf_op jit(solution)/shard_map/ppermute | solution.py:740
  6.1 3.1 %collective-permute-start.2 = (f32[16,128]{1,0:T(8,128)S(1)}, f32[16,128]{1,0:T(8,128)S(1)}, u32[]{:S(2)}, u32[]{:S(2)}) collective-permute-start(f32[16,128]{1,0:T(8,128)S(1)} %get-tuple-element.34), channel_id=1, source_target_pairs={{2,1},{3,0},{0,3},{1,2},{6,5},{7,4},{4,7},{5,6},{10,9},{11,8},{8,1... | collective-permute-start | bytes 24584 | tf_op jit(solution)/shard_map/ppermute | solution.py:732
  9.5 6.4 %collective-permute-start.4 = (f32[168,128]{1,0:T(8,128)S(1)}, f32[168,128]{1,0:T(8,128)S(1)}, u32[]{:S(2)}, u32[]{:S(2)}) collective-permute-start(f32[168,128]{1,0:T(8,128)S(1)} %get-tuple-element.42), channel_id=1, source_target_pairs={{8,0},{12,4},{0,8},{4,12},{9,1},{13,5},{1,9},{5,13},{10,2},{14,6},... | collective-permute-start | bytes 258056 | tf_op jit(solution)/shard_map/ppermute | solution.py:740
  9.9 13.5 %collective-permute-start.7 = (f32[464,128]{1,0:T(8,128)S(1)}, f32[464,128]{1,0:T(8,128)S(1)}, u32[]{:S(2)}, u32[]{:S(2)}) collective-permute-start(f32[464,128]{1,0:T(8,128)S(1)} %get-tuple-element.48), channel_id=1, source_target_pairs={{4,0},{0,4},{12,8},{8,12},{5,1},{1,5},{13,9},{9,13},{6,2},{2,6},{1... | collective-permute-start | bytes 712712 | tf_op jit(solution)/shard_map/ppermute | solution.py:749
  10.4 13.0 %collective-permute-start.8 = (f32[464,128]{1,0:T(8,128)S(1)}, f32[464,128]{1,0:T(8,128)S(1)}, u32[]{:S(2)}, u32[]{:S(2)}) collective-permute-start(f32[464,128]{1,0:T(8,128)S(1)} %get-tuple-element.49), channel_id=1, source_target_pairs={{0,0},{8,4},{4,8},{12,12},{1,1},{9,5},{5,9},{13,13},{2,2},{10,6},{... | collective-permute-start | bytes 712712 | tf_op jit(solution)/shard_map/ppermute | solution.py:749
  16.0 9.7 %collective-permute-start.5 = (f32[320,128]{1,0:T(8,128)S(1)}, f32[320,128]{1,0:T(8,128)S(1)}, u32[]{:S(2)}, u32[]{:S(2)}) collective-permute-start(f32[320,128]{1,0:T(8,128)S(1)} %get-tuple-element.44), channel_id=1, source_target_pairs={{4,0},{0,4},{12,8},{8,12},{5,1},{1,5},{13,9},{9,13},{6,2},{2,6},{1... | collective-permute-start | bytes 491528 | tf_op jit(solution)/shard_map/ppermute | solution.py:749
  18.0 7.8 %collective-permute-start.6 = (f32[320,128]{1,0:T(8,128)S(1)}, f32[320,128]{1,0:T(8,128)S(1)}, u32[]{:S(2)}, u32[]{:S(2)}) collective-permute-start(f32[320,128]{1,0:T(8,128)S(1)} %get-tuple-element.45), channel_id=1, source_target_pairs={{0,0},{8,4},{4,8},{12,12},{1,1},{9,5},{5,9},{13,13},{2,2},{10,6},{... | collective-permute-start | bytes 491528 | tf_op jit(solution)/shard_map/ppermute | solution.py:749

commit v19 on v18

--- a/solution.py
+++ b/solution.py
@@ -506,7 +506,7 @@
 
 
 def adjoint_kernel(
-    ql_ref, late_ref, even, odd, adj_hbm, ra_ref, rsa_ref, rb_ref, rsb_ref,
+    ql_ref, late_ref, odd, even, adj_hbm, ra_ref, rsa_ref, rb_ref, rsb_ref,
     table_ref,
     out_ref, hist_ref, coef_ref, coef_strip_ref,
     q_ref, t_ref, u_ref, scale_ref, edge_ref, flux_ref, w_sem,
@@ -600,7 +600,7 @@
 
 
 def forward_kernel(
-    wave_ref, own_s_ref, late_ref, even, odd, coef_ref, coef_strip_ref, s_ref, ss_ref, hist_ref,
+    wave_ref, own_s_ref, late_ref, odd, even, coef_ref, coef_strip_ref, s_ref, ss_ref, hist_ref,
     adjoint_ref, grad_hbm, adjoint_hbm,
     p_ref, spread_ref, edge_ref, flux_ref, grad_ref, sems,
 ):
@@ -847,7 +847,7 @@
             shape(3, EX, EY, BZ),
             shape(3, EY, BZ),
         ],
-        [ql, adj_late, even, odd, adjoint_end, ra, rsa, rb, rsb, table],
+        [ql, adj_late, odd, even, adjoint_end, ra, rsa, rb, rsb, table],
         [pltpu.VMEM((EX, EY, BZ), F32)] * 4
         + [
             pltpu.VMEM((STEPS, EX, EY, BZ), F32),
@@ -861,7 +861,7 @@
         forward_kernel,
         [shape(2, BX, BY, BZ), shape(4, BX, BY, BZ)],
         [
-            wave, own_s, late, wave_even, wave_odd, coef, coef_strip, src, src_strip, hist,
+            wave, own_s, late, wave_odd, wave_even, coef, coef_strip, src, src_strip, hist,
             adjoint_out,
         ],
         [pltpu.VMEM((EX, EY, BZ), F32)] * 2

time: 27.9 us -> 28.4 us (1.018)
  the two profiles are of different devices: /device:TPU:8 before, /device:TPU:0 now
where the time goes in v19:
time: 28.4 us; the launch traced here: 28.2 us
  starting transfers between devices  13.8 us (49%)
  Pallas kernels  8.53 us (30%)
  waiting for transfers between devices  5.12 us (18%)
  between operations  0.71 us (2%)
    pallas_call x9, Pallas kernels, call(): pl.pallas_call(kernel, out_shape=outs, in_specs=[pl.BlockSpec(memory_spac...  8.53 us
    ppermute x4, starting transfers between devices, paired(): return lax.ppermute(array, 'gx', pairs)  7.2 us
    ppermute x2, starting transfers between devices, from_sides(): both = lax.ppermute(sends[0], axes, route(1) + route(-1))  3.65 us
    ppermute x3, starting transfers between devices, rotated(): lax.ppermute(array, axis, [((i + offset) % count, i) for i in range(count)])  2.99 us
    ppermute x3, waiting for transfers between devices, rotated(): lax.ppermute(array, axis, [((i + offset) % count, i) for i in range(count)])  2.57 us
    ppermute x4, waiting for transfers between devices, paired(): return lax.ppermute(array, 'gx', pairs)  1.38 us
    ppermute x2, waiting for transfers between devices, from_sides(): both = lax.ppermute(sends[0], axes, route(1) + route(-1))  1.18 us
  transfers between devices with their start and end apart: 9, of which 4 were waited for; matrix products, arithmetic and copies ran while one was open for 0% of the time, Pallas kernels for 19%

profile of v19, /device:TPU:0, one launch (start us, length us, event | category | flops | bytes accessed | tf_op | source)
XLA Modules:
  0.0 28.2 jit_solution(15417728292888674975)
XLA Ops:
  0.6 1.3 %shard_map.95 = (f32[288,128]{1,0:T(8,128)S(1)}, f32[256,128]{1,0:T(8,128)S(1)}, f32[128,128]{1,0:T(8,128)S(1)}, f32[64,128]{1,0:T(8,128)S(1)}, f32[64,128]{1,0:...) custom-call(f32[4,4,32,128]{3,2,1,0:T(8,128)} %stored_hbm.1, ...), custom_call_target="tpu_custom_call" | custom-call | bytes 5166000 | tf_op jit(solution)/shard_map/pallas_call | solution.py:704
  2.0 3.0 %collective-permute-start.1 = (f32[160,128]{1,0:T(8,128)S(1)}, f32[160,128]{1,0:T(8,128)S(1)}, u32[]{:S(2)}, u32[]{:S(2)}) collective-permute-start(f32[160,128]{1,0:T(8,128)S(1)} %get-tuple-element.33), channel_id=1, source_target_pairs={{2,0},{0,2},{3,1},{1,3},{6,4},{4,6},{7,5},{5,7},{10,8},{8,10},{11,... | collective-permute-start | bytes 245768 | tf_op jit(solution)/shard_map/ppermute | solution.py:732
  5.0 2.6 %collective-permute-start = (f32[288,128]{1,0:T(8,128)S(1)}, f32[288,128]{1,0:T(8,128)S(1)}, u32[]{:S(2)}, u32[]{:S(2)}) collective-permute-start(f32[288,128]{1,0:T(8,128)S(1)} %get-tuple-element.32), channel_id=1, source_target_pairs={{8,0},{12,4},{0,8},{4,12},{9,1},{13,5},{1,9},{5,13},{10,2},{14,6},... | collective-permute-start | bytes 442376 | tf_op jit(solution)/shard_map/ppermute | solution.py:740
  7.5 0.0 collective-permute-start.3
  7.6 0.6 %collective-permute-start.2 = (f32[16,128]{1,0:T(8,128)S(1)}, f32[16,128]{1,0:T(8,128)S(1)}, u32[]{:S(2)}, u32[]{:S(2)}) collective-permute-start(f32[16,128]{1,0:T(8,128)S(1)} %get-tuple-element.34), channel_id=1, source_target_pairs={{2,1},{3,0},{0,3},{1,2},{6,5},{7,4},{4,7},{5,6},{10,9},{11,8},{8,1... | collective-permute-start | bytes 24584 | tf_op jit(solution)/shard_map/ppermute | solution.py:732
  8.2 1.2 %shard_map.96 = (f32[2,480,128]{2,1,0:T(8,128)S(1)}, f32[2,40,128]{2,1,0:T(8,128)S(1)}) custom-call(s32[3,1024]{1,0:T(4,128)S(1)} %get-tuple-element.39.receivers, f32[4,1024]{1,0:T(4,128)S(1)} %get-tuple-element.40.receiver_wave), custom_call_target="tpu_custom_call" | custom-call | bytes 4428000 | tf_op jit(solution)/shard_map/pallas_call | solution.py:704
  9.5 1.2 %collective-permute-done.2.corner_up.corner_down = f32[16,128]{1,0:T(8,128)S(1)} collective-permute-done((f32[16,128]{1,0:T(8,128)S(1)}, f32[16,128]{1,0:T(8,128)S(1)}, u32[]{:S(2)}, u32[]{:S(2)}) %collective-permute-start.2) | collective-permute-done | bytes 8224 | tf_op jit(solution)/shard_map/ppermute | solution.py:732
  10.6 0.0 collective-permute-done.3.other_ref
  10.6 0.0 collective-permute-done.1.from_up.from_down
  10.6 0.3 shard_map.97
  10.9 0.4 %collective-permute-start.4 = (f32[168,128]{1,0:T(8,128)S(1)}, f32[168,128]{1,0:T(8,128)S(1)}, u32[]{:S(2)}, u32[]{:S(2)}) collective-permute-start(f32[168,128]{1,0:T(8,128)S(1)} %get-tuple-element.42), channel_id=1, source_target_pairs={{8,0},{12,4},{0,8},{4,12},{9,1},{13,5},{1,9},{5,13},{10,2},{14,6},... | collective-permute-start | bytes 258056 | tf_op jit(solution)/shard_map/ppermute | solution.py:740
  11.3 0.7 %collective-permute-start.7 = (f32[464,128]{1,0:T(8,128)S(1)}, f32[464,128]{1,0:T(8,128)S(1)}, u32[]{:S(2)}, u32[]{:S(2)}) collective-permute-start(f32[464,128]{1,0:T(8,128)S(1)} %get-tuple-element.48), channel_id=1, source_target_pairs={{0,0},{8,4},{4,8},{12,12},{1,1},{9,5},{5,9},{13,13},{2,2},{10,6},{... | collective-permute-start | bytes 712712 | tf_op jit(solution)/shard_map/ppermute | solution.py:749
  12.0 4.5 %collective-permute-start.8 = (f32[464,128]{1,0:T(8,128)S(1)}, f32[464,128]{1,0:T(8,128)S(1)}, u32[]{:S(2)}, u32[]{:S(2)}) collective-permute-start(f32[464,128]{1,0:T(8,128)S(1)} %get-tuple-element.49), channel_id=1, source_target_pairs={{4,0},{0,4},{12,8},{8,12},{5,1},{1,5},{13,9},{9,13},{6,2},{2,6},{1... | collective-permute-start | bytes 712712 | tf_op jit(solution)/shard_map/ppermute | solution.py:749
  16.5 0.0 collective-permute-done.wave_ref
  16.5 2.6 %collective-permute-done.4.late_ref = f32[168,128]{1,0:T(8,128)S(1)} collective-permute-done((f32[168,128]{1,0:T(8,128)S(1)}, f32[168,128]{1,0:T(8,128)S(1)}, u32[]{:S(2)}, u32[]{:S(2)}) %collective-permute-start.4) | collective-permute-done | bytes 86048 | tf_op jit(solution)/shard_map/ppermute | solution.py:740
  19.0 0.1 shard_map.98
  19.1 0.7 %collective-permute-start.5 = (f32[320,128]{1,0:T(8,128)S(1)}, f32[320,128]{1,0:T(8,128)S(1)}, u32[]{:S(2)}, u32[]{:S(2)}) collective-permute-start(f32[320,128]{1,0:T(8,128)S(1)} %get-tuple-element.44), channel_id=1, source_target_pairs={{0,0},{8,4},{4,8},{12,12},{1,1},{9,5},{5,9},{13,13},{2,2},{10,6},{... | collective-permute-start | bytes 491528 | tf_op jit(solution)/shard_map/ppermute | solution.py:749
  19.8 1.4 %collective-permute-start.6 = (f32[320,128]{1,0:T(8,128)S(1)}, f32[320,128]{1,0:T(8,128)S(1)}, u32[]{:S(2)}, u32[]{:S(2)}) collective-permute-start(f32[320,128]{1,0:T(8,128)S(1)} %get-tuple-element.45), channel_id=1, source_target_pairs={{4,0},{0,4},{12,8},{8,12},{5,1},{1,5},{13,9},{9,13},{6,2},{2,6},{1... | collective-permute-start | bytes 491528 | tf_op jit(solution)/shard_map/ppermute | solution.py:749
  21.2 1.0 %shard_map.100 = (f32[2,320,128]{2,1,0:T(8,128)S(1)}, f32[2,40,128]{2,1,0:T(8,128)S(1)}) custom-call(s32[3,1024]{1,0:T(4,128)S(1)} %get-tuple-element.39.receivers, f32[4,1024]{1,0:T(4,128)S(1)} %get-tuple-element.40.receiver_wave, f32[304,128]{1,0:T(8,128)S(1)} %get-tuple-element.47.adj_ref._.late_ref), custom_call_target="tpu_custom_call" | custom-call | bytes 3690000 | tf_op jit(solution)/shard_map/pallas_call | solution.py:704
  22.2 0.6 %shard_map.102 = (f32[3,400,128]{2,1,0:T(8,128)S(1)}, f32[3,40,128]{2,1,0:T(8,128)S(1)}) custom-call(s32[3,64]{1,0:T(4,128)S(1)} %get-tuple-element.56.sources, f32[4,64]{1,0:T(4,128)S(1)} %get-tuple-element.57.source_wave, f32[304,128]{1,0:T(8,128)S(1)} %get-tuple-element.47.adj_ref._.late_ref), custom_call_target="tpu_custom_call" | custom-call | bytes 1845000 | tf_op jit(solution)/shard_map/pallas_call | solution.py:704
  22.8 0.0 collective-permute-done.7.odd
  22.8 0.8 %collective-permute-done.8.even = f32[464,128]{1,0:T(8,128)S(1)} collective-permute-done((f32[464,128]{1,0:T(8,128)S(1)}, f32[464,128]{1,0:T(8,128)S(1)}, u32[]{:S(2)}, u32[]{:S(2)}) %collective-permute-start.8) | collective-permute-done | bytes 237600 | tf_op jit(solution)/shard_map/ppermute | solution.py:749
  23.6 2.2 %shard_map.101 = (f32[4,4,32,128]{3,2,1,0:T(8,128)S(1)}, f32[4,4,4,32,128]{4,3,2,1,0:T(8,128)S(1)}, f32[3,12,40,128]{3,2,1,0:T(8,128)S(1)}, f32[3,40,128]{2,1,0:T(8,128)S(1)}) custom-call(f32[256,128]{1,0:T(8,128)S(1)} %get-tuple-element.46.ql_ref, f32[304,128]{1,0:T(8,128)S(1)} %get-tuple-element.47.adj_ref._.late_ref, ...), custom_call_target="tpu_custom_call" | custom-call | bytes 14391000 | tf_op jit(solution)/shard_map/pallas_call | solution.py:704
  25.8 0.0 collective-permute-done.5.odd
  25.8 0.6 %collective-permute-done.6.even = f32[320,128]{1,0:T(8,128)S(1)} collective-permute-done((f32[320,128]{1,0:T(8,128)S(1)}, f32[320,128]{1,0:T(8,128)S(1)}, u32[]{:S(2)}, u32[]{:S(2)}) %collective-permute-start.6) | collective-permute-done | bytes 163872 | tf_op jit(solution)/shard_map/ppermute | solution.py:749
  26.4 1.8 %shard_map.103 = (f32[2,4,32,128]{3,2,1,0:T(8,128)}, f32[4,4,32,128]{3,2,1,0:T(8,128)}) custom-call(f32[288,128]{1,0:T(8,128)S(1)} %collective-permute-done.wave_ref, f32[128,128]{1,0:T(8,128)S(1)} %get-tuple-element.43.own_s_ref, f32[168,128]{1,0:T(8,128)S(1)} %collective-permute-done.4.late_ref, f32[320,128]{1,0:T(8,128)S(1)} %collective-permute-done.5.odd, ...), custom_call_target="tpu_custom_call" | custom-call | bytes 9225000 | tf_op jit(solution)/shard_map/pallas_call | solution.py:704
  (1 shorter events, 0.0 us)
Async XLA Ops:
  2.0 8.7 %collective-permute-start.1 = (f32[160,128]{1,0:T(8,128)S(1)}, f32[160,128]{1,0:T(8,128)S(1)}, u32[]{:S(2)}, u32[]{:S(2)}) collective-permute-start(f32[160,128]{1,0:T(8,128)S(1)} %get-tuple-element.33), channel_id=1, source_target_pairs={{2,0},{0,2},{3,1},{1,3},{6,4},{4,6},{7,5},{5,7},{10,8},{8,10},{11,... | collective-permute-start | bytes 245768 | tf_op jit(solution)/shard_map/ppermute | solution.py:732
  5.0 11.5 %collective-permute-start = (f32[288,128]{1,0:T(8,128)S(1)}, f32[288,128]{1,0:T(8,128)S(1)}, u32[]{:S(2)}, u32[]{:S(2)}) collective-permute-start(f32[288,128]{1,0:T(8,128)S(1)} %get-tuple-element.32), channel_id=1, source_target_pairs={{8,0},{12,4},{0,8},{4,12},{9,1},{13,5},{1,9},{5,13},{10,2},{14,6},... | collective-permute-start | bytes 442376 | tf_op jit(solution)/shard_map/ppermute | solution.py:740
  7.5 3.1 %collective-permute-start.3 = (f32[96,128]{1,0:T(8,128)S(1)}, f32[96,128]{1,0:T(8,128)S(1)}, u32[]{:S(2)}, u32[]{:S(2)}) collective-permute-start(f32[96,128]{1,0:T(8,128)S(1)} %get-tuple-element.35.strip_ref), channel_id=1, source_target_pairs={{1,0},{0,1},{3,2},{2,3},{5,4},{4,5},{7,6},{6,7},{9,8},{8,9},{11,10... | collective-permute-start | bytes 147464 | tf_op jit(solution)/shard_map/ppermute | solution.py:740
  7.6 3.1 %collective-permute-start.2 = (f32[16,128]{1,0:T(8,128)S(1)}, f32[16,128]{1,0:T(8,128)S(1)}, u32[]{:S(2)}, u32[]{:S(2)}) collective-permute-start(f32[16,128]{1,0:T(8,128)S(1)} %get-tuple-element.34), channel_id=1, source_target_pairs={{2,1},{3,0},{0,3},{1,2},{6,5},{7,4},{4,7},{5,6},{10,9},{11,8},{8,1... | collective-permute-start | bytes 24584 | tf_op jit(solution)/shard_map/ppermute | solution.py:732
  10.9 8.1 %collective-permute-start.4 = (f32[168,128]{1,0:T(8,128)S(1)}, f32[168,128]{1,0:T(8,128)S(1)}, u32[]{:S(2)}, u32[]{:S(2)}) collective-permute-start(f32[168,128]{1,0:T(8,128)S(1)} %get-tuple-element.42), channel_id=1, source_target_pairs={{8,0},{12,4},{0,8},{4,12},{9,1},{13,5},{1,9},{5,13},{10,2},{14,6},... | collective-permute-start | bytes 258056 | tf_op jit(solution)/shard_map/ppermute | solution.py:740
  11.3 11.5 %collective-permute-start.7 = (f32[464,128]{1,0:T(8,128)S(1)}, f32[464,128]{1,0:T(8,128)S(1)}, u32[]{:S(2)}, u32[]{:S(2)}) collective-permute-start(f32[464,128]{1,0:T(8,128)S(1)} %get-tuple-element.48), channel_id=1, source_target_pairs={{0,0},{8,4},{4,8},{12,12},{1,1},{9,5},{5,9},{13,13},{2,2},{10,6},{... | collective-permute-start | bytes 712712 | tf_op jit(solution)/shard_map/ppermute | solution.py:749
  12.0 11.6 %collective-permute-start.8 = (f32[464,128]{1,0:T(8,128)S(1)}, f32[464,128]{1,0:T(8,128)S(1)}, u32[]{:S(2)}, u32[]{:S(2)}) collective-permute-start(f32[464,128]{1,0:T(8,128)S(1)} %get-tuple-element.49), channel_id=1, source_target_pairs={{4,0},{0,4},{12,8},{8,12},{5,1},{1,5},{13,9},{9,13},{6,2},{2,6},{1... | collective-permute-start | bytes 712712 | tf_op jit(solution)/shard_map/ppermute | solution.py:749
  19.1 6.7 %collective-permute-start.5 = (f32[320,128]{1,0:T(8,128)S(1)}, f32[320,128]{1,0:T(8,128)S(1)}, u32[]{:S(2)}, u32[]{:S(2)}) collective-permute-start(f32[320,128]{1,0:T(8,128)S(1)} %get-tuple-element.44), channel_id=1, source_target_pairs={{0,0},{8,4},{4,8},{12,12},{1,1},{9,5},{5,9},{13,13},{2,2},{10,6},{... | collective-permute-start | bytes 491528 | tf_op jit(solution)/shard_map/ppermute | solution.py:749
  19.8 6.6 %collective-permute-start.6 = (f32[320,128]{1,0:T(8,128)S(1)}, f32[320,128]{1,0:T(8,128)S(1)}, u32[]{:S(2)}, u32[]{:S(2)}) collective-permute-start(f32[320,128]{1,0:T(8,128)S(1)} %get-tuple-element.45), channel_id=1, source_target_pairs={{4,0},{0,4},{12,8},{8,12},{5,1},{1,5},{13,9},{9,13},{6,2},{2,6},{1... | collective-permute-start | bytes 491528 | tf_op jit(solution)/shard_map/ppermute | solution.py:749

commit v20 on v18

--- a/solution.py
+++ b/solution.py
@@ -15,8 +15,8 @@
 VMEM_LIMIT = 16 * 1024 * 1024
 PLANES = BX * BY
 WAVE_OWN = (0, BY, BY + 9 * 8)
-WAVE_FIX = WAVE_OWN[2] + EY
 FIX_LANE = 3 * BX * STRIP
+SPARE = 64
 ADJ_OWN = (PLANES, PLANES + BY, PLANES + BY + 13 * 8)
 WAVE_SIDE = (PLANES + 3 * BY, PLANES + 4 * BY)
 ADJ_SIDE = (3 * BY, 4 * BY)
@@ -116,9 +116,8 @@
             previous[kind] = vx
             index = (kind * BX + x) * 8
             last_y_ref[index : index + 8] = vy[BY - 8 : BY]
-    for kind in range(2):
-        last_x_ref[kind * BY : kind * BY + BY] = previous[kind]
-    wave_ref[2 * PLANES : 2 * PLANES + BY] = jnp.zeros((BY, BZ), F32)
+    wave_ref[2 * PLANES : 2 * PLANES + BY] = previous[0]
+    last_x_ref[...] = previous[1]
     for group in range(3):
         strip_ref[group * BY : group * BY + BY] = strips[group]
         tiles[9 * BX + group] = edge_tile(strips[group])
@@ -182,7 +181,8 @@
 def merge_kernel(
     from_up, from_down, corner_up, corner_down, strip_ref, other_ref,
     t_ref, last_x_ref, last_y_ref, _,
-    wave_ref, adj_ref,
+    late_ref, adj_ref,
+    wave_ref,
 ):
     gy = lax.axis_index("gy")
     tile_row = rows((8, BZ))
@@ -227,7 +227,6 @@
             last_slot = 3
         last = jnp.where(strip_lane >= last_lanes, vx, 0.0)
         strip = strip + pltpu.roll(last, last_slot * BX * STRIP - last_lanes, 1)
-        target[planes_end:x_end] = last_x_ref[kind * BY : kind * BY + BY]
 
         vx_before = None
         for x in range(BX):
@@ -259,11 +258,13 @@
                 target[base + 64 : base + 72] = halo(from_up, from_down, 8 * BX + x)
         target[tiles_end - 8 : tiles_end] = vx_before
         if kind == 0:
-            target[tiles_end : tiles_end + BY] = strip[0:BY] + fix_lane
-            target[tiles_end + BY : tiles_end + EY] = strip[BY:EY]
-            target[WAVE_FIX : WAVE_FIX + 8] = fix_row
-            target[WAVE_FIX + 8 : WAVE_FIX + 24] = jnp.zeros((16, BZ), F32)
+            base = put_tiles(late_ref, 0, wave_ref, range(x_end, tiles_end, 8))
+            late_ref[base : base + BY] = strip[0:BY] + fix_lane
+            late_ref[base + BY : base + EY] = strip[BY:EY]
+            late_ref[base + EY : base + EY + 8] = fix_row
+            late_ref[base + EY + 8 : base + EY + 8 + SPARE] = jnp.zeros((SPARE, BZ), F32)
         else:
+            target[planes_end:x_end] = last_x_ref[...]
             target[tiles_end : tiles_end + EY] = strip
 
 
@@ -280,24 +281,40 @@
         copy_rows(target, base, ql_ref, 0, 2 * PLANES)
 
 
-def join_kernel(wave_ref, late_ref, s_ref, even_ref, odd_ref):
+def unpacked(tile, place):
+    upper = lax.axis_index("gy") == 0
+    turned = half_turn(tile)
+    tile = jnp.where(upper, turned, tile) if place % 2 else jnp.where(upper, tile, turned)
+    return jnp.where((rows((8, BZ)) < MARGIN) == upper, tile, 0.0)
+
+
+def join_kernel(wave_ref, late_ref, s_ref, own_ref, even_ref, odd_ref):
     planes_end, x_end, tiles_end = WAVE_OWN
+    own_ref[planes_end:x_end] = wave_ref[2 * PLANES : 2 * PLANES + BY]
+    for place in range((tiles_end - x_end) // 8):
+        if halved():
+            tile = unpacked(late_ref[place // 2 * 8 : place // 2 * 8 + 8], place)
+        else:
+            tile = late_ref[place * 8 : place * 8 + 8]
+        own_ref[x_end + place * 8 : x_end + place * 8 + 8] = tile
+    strip = tile_rows((tiles_end - x_end) // 8)
+    own_ref[tiles_end : tiles_end + EY] = late_ref[strip : strip + EY]
     row, lane = rows((BY, BZ)), lanes((BY, BZ))
-    fix_lane = late_ref[tiles_end : tiles_end + BY]
+    fix_lane = late_ref[strip : strip + BY]
     for x in range(BX):
         block = wave_ref[PLANES + x * BY : PLANES + x * BY + BY]
-        fix_row = late_ref[WAVE_FIX + x : WAVE_FIX + x + 1]
+        fix_row = late_ref[strip + EY + x : strip + EY + x + 1]
         block = block - jnp.where(row == 0, fix_row, 0.0)
         block = block - jnp.where(lane == 0, pltpu.roll(fix_lane, BZ - FIX_LANE - x, 1), 0.0)
         s_ref[x * BY : x * BY + BY] = block
     for target, first in zip((even_ref, odd_ref), pair_planes()):
         base = copy_rows(target, 0, wave_ref, 0, PLANES)
         base = copy_rows(target, base, s_ref, first * BY, 3 * BY)
-        base = copy_rows(target, base, late_ref, planes_end, BY)
+        base = copy_rows(target, base, own_ref, planes_end, BY)
         near = [x_end + (first + plane) * 8 for plane in range(3)]
         nearest = [x_end + 32 + first * 16 + plane * 8 for plane in range(2)]
-        base = put_tiles(target, base, late_ref, near + nearest + [tiles_end - 8])
-        copy_rows(target, base, late_ref, tiles_end, EY)
+        base = put_tiles(target, base, own_ref, near + nearest + [tiles_end - 8])
+        copy_rows(target, base, own_ref, tiles_end, EY)
 
 
 def split(values):
@@ -445,10 +462,7 @@
     if not halved():
         return from_side(messages, base + place * 8, 8, block, side)
     tile = from_side(messages, base + place // 2 * 8, 8, block, side)
-    upper = lax.axis_index("gy") == 0
-    turned = half_turn(tile)
-    tile = jnp.where(upper, turned, tile) if place % 2 else jnp.where(upper, tile, turned)
-    return jnp.where((rows((8, BZ)) < MARGIN) == upper, tile, 0.0)
+    return unpacked(tile, place)
 
 
 def side_place(wanted, plane, block):
@@ -762,10 +776,10 @@
     wave, ql, t, last_x, last_y, strips, table, receivers, receiver_wave, sources, source_wave, *sends = call(
         load_kernel,
         [
-            shape(2 * PLANES + 32, BZ),
+            shape(2 * PLANES + BY, BZ),
             shape(2 * PLANES, BZ),
             shape(PLANES, BZ),
-            shape(2 * BY, BZ),
+            shape(BY, BZ),
             shape(2 * BX * 8, BZ),
             shape(3 * BY, BZ),
             shape(24, BZ),
@@ -799,9 +813,9 @@
     early_planes, source_planes = (last - first for first, last in (EARLY_PLANES, SOURCE_PLANES))
     late, adj_late = call(
         merge_kernel,
-        [shape(WAVE_FIX + 24, BZ), shape(ADJ_OWN[2] + EY, BZ)],
+        [shape(tile_rows(9) + EY + 8 + SPARE, BZ), shape(ADJ_OWN[2] + EY, BZ)],
         [from_up, from_down, corner_up, corner_down, strips, other, t, last_x, last_y, rsb],
-        [],
+        [pltpu.VMEM((WAVE_OWN[2], BZ), F32)],
         "vvvvvvvvva",
     )
     late = rotated(late, "gx", half)
@@ -831,9 +845,10 @@
         0.5,
     )
     src = src.reshape(STEPS - 1, source_planes, EY, BZ)
-    own_s, wave_even, wave_odd = call(
+    own_s, own_late, wave_even, wave_odd = call(
         join_kernel,
-        [shape(PLANES, BZ)] + [shape(WAVE_SIDE[1] + tile_rows(WAVE_TILES) + EY, BZ)] * 2,
+        [shape(PLANES, BZ), shape(WAVE_OWN[2] + EY, BZ)]
+        + [shape(WAVE_SIDE[1] + tile_rows(WAVE_TILES) + EY, BZ)] * 2,
         [wave, late],
         [],
         "vv",
@@ -861,7 +876,7 @@
         forward_kernel,
         [shape(2, BX, BY, BZ), shape(4, BX, BY, BZ)],
         [
-            wave, own_s, late, wave_even, wave_odd, coef, coef_strip, src, src_strip, hist,
+            wave, own_s, own_late, wave_even, wave_odd, coef, coef_strip, src, src_strip, hist,
             adjoint_out,
         ],
         [pltpu.VMEM((EX, EY, BZ), F32)] * 2

time: 27.9 us -> 27.6 us (0.989)
  no operation moved by 1% of the time
where the time goes in v20:
time: 27.6 us; the launch traced here: 27.3 us
  starting transfers between devices  15.9 us (58%)
  Pallas kernels  8.56 us (31%)
  waiting for transfers between devices  2.05 us (7%)
  between operations  0.73 us (3%)
    ppermute x4, starting transfers between devices, paired(): return lax.ppermute(array, 'gx', pairs)  10.7 us
    pallas_call x9, Pallas kernels, call(): pl.pallas_call(kernel, out_shape=outs, in_specs=[pl.BlockSpec(memory_spac...  8.56 us
    ppermute x3, starting transfers between devices, rotated(): lax.ppermute(array, axis, [((i + offset) % count, i) for i in range(count)])  2.99 us
    ppermute x2, starting transfers between devices, from_sides(): both = lax.ppermute(sends[0], axes, route(1) + route(-1))  2.2 us
    ppermute x2, waiting for transfers between devices, from_sides(): both = lax.ppermute(sends[0], axes, route(1) + route(-1))  1.17 us
    ppermute x3, waiting for transfers between devices, rotated(): lax.ppermute(array, axis, [((i + offset) % count, i) for i in range(count)])  0.67 us
  transfers between devices with their start and end apart: 9, of which 3 were waited for; matrix products, arithmetic and copies ran while one was open for 0% of the time, Pallas kernels for 20%

profile of v20, /device:TPU:8, one launch (start us, length us, event | category | flops | bytes accessed | tf_op | source)
XLA Modules:
  0.0 27.3 jit_solution(13504509322989389872)
XLA Ops:
  0.6 1.3 %shard_map.95 = (f32[288,128]{1,0:T(8,128)S(1)}, f32[256,128]{1,0:T(8,128)S(1)}, f32[128,128]{1,0:T(8,128)S(1)}, f32[32,128]{1,0:T(8,128)S(1)}, f32[64,128]{1,0:...) custom-call(f32[4,4,32,128]{3,2,1,0:T(8,128)} %stored_hbm.1, ...), custom_call_target="tpu_custom_call" | custom-call | bytes 5166000 | tf_op jit(solution)/shard_map/pallas_call | solution.py:718
  2.0 1.6 %collective-permute-start.1 = (f32[160,128]{1,0:T(8,128)S(1)}, f32[160,128]{1,0:T(8,128)S(1)}, u32[]{:S(2)}, u32[]{:S(2)}) collective-permute-start(f32[160,128]{1,0:T(8,128)S(1)} %get-tuple-element.34), channel_id=1, source_target_pairs={{2,0},{0,2},{3,1},{1,3},{6,4},{4,6},{7,5},{5,7},{10,8},{8,10},{11,... | collective-permute-start | bytes 245768 | tf_op jit(solution)/shard_map/ppermute | solution.py:746
  3.5 2.6 %collective-permute-start = (f32[288,128]{1,0:T(8,128)S(1)}, f32[288,128]{1,0:T(8,128)S(1)}, u32[]{:S(2)}, u32[]{:S(2)}) collective-permute-start(f32[288,128]{1,0:T(8,128)S(1)} %get-tuple-element.33), channel_id=1, source_target_pairs={{8,0},{12,4},{0,8},{4,12},{9,1},{13,5},{1,9},{5,13},{10,2},{14,6},... | collective-permute-start | bytes 442376 | tf_op jit(solution)/shard_map/ppermute | solution.py:754
  6.1 0.0 collective-permute-start.3
  6.1 0.6 %collective-permute-start.2 = (f32[16,128]{1,0:T(8,128)S(1)}, f32[16,128]{1,0:T(8,128)S(1)}, u32[]{:S(2)}, u32[]{:S(2)}) collective-permute-start(f32[16,128]{1,0:T(8,128)S(1)} %get-tuple-element.35), channel_id=1, source_target_pairs={{2,1},{3,0},{0,3},{1,2},{6,5},{7,4},{4,7},{5,6},{10,9},{11,8},{8,1... | collective-permute-start | bytes 24584 | tf_op jit(solution)/shard_map/ppermute | solution.py:746
  6.8 1.2 %shard_map.96 = (f32[2,480,128]{2,1,0:T(8,128)S(1)}, f32[2,40,128]{2,1,0:T(8,128)S(1)}) custom-call(s32[3,1024]{1,0:T(4,128)S(1)} %get-tuple-element.40.receivers, f32[4,1024]{1,0:T(4,128)S(1)} %get-tuple-element.41.receiver_wave), custom_call_target="tpu_custom_call" | custom-call | bytes 4428000 | tf_op jit(solution)/shard_map/pallas_call | solution.py:718
  8.0 1.2 %collective-permute-done.2.corner_up.corner_down = f32[16,128]{1,0:T(8,128)S(1)} collective-permute-done((f32[16,128]{1,0:T(8,128)S(1)}, f32[16,128]{1,0:T(8,128)S(1)}, u32[]{:S(2)}, u32[]{:S(2)}) %collective-permute-start.2) | collective-permute-done | bytes 8224 | tf_op jit(solution)/shard_map/ppermute | solution.py:746
  9.2 0.0 collective-permute-done.3.other_ref
  9.2 0.0 collective-permute-done.1.from_up.from_down
  9.2 0.3 shard_map.97
  9.5 0.4 %collective-permute-start.4 = (f32[152,128]{1,0:T(8,128)S(1)}, f32[152,128]{1,0:T(8,128)S(1)}, u32[]{:S(2)}, u32[]{:S(2)}) collective-permute-start(f32[152,128]{1,0:T(8,128)S(1)} %get-tuple-element.43), channel_id=1, source_target_pairs={{8,0},{12,4},{0,8},{4,12},{9,1},{13,5},{1,9},{5,13},{10,2},{14,6},... | collective-permute-start | bytes 233480 | tf_op jit(solution)/shard_map/ppermute | solution.py:754
  9.9 0.5 %collective-permute-start.7 = (f32[464,128]{1,0:T(8,128)S(1)}, f32[464,128]{1,0:T(8,128)S(1)}, u32[]{:S(2)}, u32[]{:S(2)}) collective-permute-start(f32[464,128]{1,0:T(8,128)S(1)} %get-tuple-element.50), channel_id=1, source_target_pairs={{4,0},{0,4},{12,8},{8,12},{5,1},{1,5},{13,9},{9,13},{6,2},{2,6},{1... | collective-permute-start | bytes 712712 | tf_op jit(solution)/shard_map/ppermute | solution.py:763
  10.4 4.6 %collective-permute-start.8 = (f32[464,128]{1,0:T(8,128)S(1)}, f32[464,128]{1,0:T(8,128)S(1)}, u32[]{:S(2)}, u32[]{:S(2)}) collective-permute-start(f32[464,128]{1,0:T(8,128)S(1)} %get-tuple-element.51), channel_id=1, source_target_pairs={{0,0},{8,4},{4,8},{12,12},{1,1},{9,5},{5,9},{13,13},{2,2},{10,6},{... | collective-permute-start | bytes 712712 | tf_op jit(solution)/shard_map/ppermute | solution.py:763
  15.0 0.0 collective-permute-done.wave_ref
  15.0 0.7 %collective-permute-done.4.late_ref = f32[152,128]{1,0:T(8,128)S(1)} collective-permute-done((f32[152,128]{1,0:T(8,128)S(1)}, f32[152,128]{1,0:T(8,128)S(1)}, u32[]{:S(2)}, u32[]{:S(2)}) %collective-permute-start.4) | collective-permute-done | bytes 77856 | tf_op jit(solution)/shard_map/ppermute | solution.py:754
  15.7 0.1 shard_map.98
  15.8 1.8 %collective-permute-start.5 = (f32[320,128]{1,0:T(8,128)S(1)}, f32[320,128]{1,0:T(8,128)S(1)}, u32[]{:S(2)}, u32[]{:S(2)}) collective-permute-start(f32[320,128]{1,0:T(8,128)S(1)} %get-tuple-element.46), channel_id=1, source_target_pairs={{4,0},{0,4},{12,8},{8,12},{5,1},{1,5},{13,9},{9,13},{6,2},{2,6},{1... | collective-permute-start | bytes 491528 | tf_op jit(solution)/shard_map/ppermute | solution.py:763
  17.6 3.8 %collective-permute-start.6 = (f32[320,128]{1,0:T(8,128)S(1)}, f32[320,128]{1,0:T(8,128)S(1)}, u32[]{:S(2)}, u32[]{:S(2)}) collective-permute-start(f32[320,128]{1,0:T(8,128)S(1)} %get-tuple-element.47), channel_id=1, source_target_pairs={{0,0},{8,4},{4,8},{12,12},{1,1},{9,5},{5,9},{13,13},{2,2},{10,6},{... | collective-permute-start | bytes 491528 | tf_op jit(solution)/shard_map/ppermute | solution.py:763
  21.4 1.0 %shard_map.100 = (f32[2,320,128]{2,1,0:T(8,128)S(1)}, f32[2,40,128]{2,1,0:T(8,128)S(1)}) custom-call(s32[3,1024]{1,0:T(4,128)S(1)} %get-tuple-element.40.receivers, f32[4,1024]{1,0:T(4,128)S(1)} %get-tuple-element.41.receiver_wave, f32[304,128]{1,0:T(8,128)S(1)} %get-tuple-element.49.adj_ref._.late_ref), custom_call_target="tpu_custom_call" | custom-call | bytes 3690000 | tf_op jit(solution)/shard_map/pallas_call | solution.py:718
  22.4 0.5 %shard_map.102 = (f32[3,400,128]{2,1,0:T(8,128)S(1)}, f32[3,40,128]{2,1,0:T(8,128)S(1)}) custom-call(s32[3,64]{1,0:T(4,128)S(1)} %get-tuple-element.58.sources, f32[4,64]{1,0:T(4,128)S(1)} %get-tuple-element.59.source_wave, f32[304,128]{1,0:T(8,128)S(1)} %get-tuple-element.49.adj_ref._.late_ref), custom_call_target="tpu_custom_call" | custom-call | bytes 1845000 | tf_op jit(solution)/shard_map/pallas_call | solution.py:718
  23.0 0.0 collective-permute-done.7.even
  23.0 0.0 collective-permute-done.8.odd
  23.0 2.2 %shard_map.101 = (f32[4,4,32,128]{3,2,1,0:T(8,128)S(1)}, f32[4,4,4,32,128]{4,3,2,1,0:T(8,128)S(1)}, f32[3,12,40,128]{3,2,1,0:T(8,128)S(1)}, f32[3,40,128]{2,1,0:T(8,128)S(1)}) custom-call(f32[256,128]{1,0:T(8,128)S(1)} %get-tuple-element.48.ql_ref, f32[304,128]{1,0:T(8,128)S(1)} %get-tuple-element.49.adj_ref._.late_ref, ...), custom_call_target="tpu_custom_call" | custom-call | bytes 14391000 | tf_op jit(solution)/shard_map/pallas_call | solution.py:718
  25.2 0.0 collective-permute-done.5.even
  25.3 0.2 collective-permute-done.6.odd
  25.5 1.8 %shard_map.103 = (f32[2,4,32,128]{3,2,1,0:T(8,128)}, f32[4,4,32,128]{3,2,1,0:T(8,128)}) custom-call(f32[288,128]{1,0:T(8,128)S(1)} %collective-permute-done.wave_ref, f32[128,128]{1,0:T(8,128)S(1)} %get-tuple-element.44.own_s_ref, f32[144,128]{1,0:T(8,128)S(1)} %get-tuple-element.45.late_ref, f32[320,128]{1,0:T(8,128)S(1)} %collective-permute-done.5.even, ...), custom_call_target="tpu_custom_call" | custom-call | bytes 9225000 | tf_op jit(solution)/shard_map/pallas_call | solution.py:718
  (1 shorter events, 0.0 us)
Async XLA Ops:
  2.0 7.2 %collective-permute-start.1 = (f32[160,128]{1,0:T(8,128)S(1)}, f32[160,128]{1,0:T(8,128)S(1)}, u32[]{:S(2)}, u32[]{:S(2)}) collective-permute-start(f32[160,128]{1,0:T(8,128)S(1)} %get-tuple-element.34), channel_id=1, source_target_pairs={{2,0},{0,2},{3,1},{1,3},{6,4},{4,6},{7,5},{5,7},{10,8},{8,10},{11,... | collective-permute-start | bytes 245768 | tf_op jit(solution)/shard_map/ppermute | solution.py:746
  3.5 11.5 %collective-permute-start = (f32[288,128]{1,0:T(8,128)S(1)}, f32[288,128]{1,0:T(8,128)S(1)}, u32[]{:S(2)}, u32[]{:S(2)}) collective-permute-start(f32[288,128]{1,0:T(8,128)S(1)} %get-tuple-element.33), channel_id=1, source_target_pairs={{8,0},{12,4},{0,8},{4,12},{9,1},{13,5},{1,9},{5,13},{10,2},{14,6},... | collective-permute-start | bytes 442376 | tf_op jit(solution)/shard_map/ppermute | solution.py:754
  6.1 3.1 %collective-permute-start.3 = (f32[96,128]{1,0:T(8,128)S(1)}, f32[96,128]{1,0:T(8,128)S(1)}, u32[]{:S(2)}, u32[]{:S(2)}) collective-permute-start(f32[96,128]{1,0:T(8,128)S(1)} %get-tuple-element.36.strip_ref), channel_id=1, source_target_pairs={{1,0},{0,1},{3,2},{2,3},{5,4},{4,5},{7,6},{6,7},{9,8},{8,9},{11,10... | collective-permute-start | bytes 147464 | tf_op jit(solution)/shard_map/ppermute | solution.py:754
  6.1 3.1 %collective-permute-start.2 = (f32[16,128]{1,0:T(8,128)S(1)}, f32[16,128]{1,0:T(8,128)S(1)}, u32[]{:S(2)}, u32[]{:S(2)}) collective-permute-start(f32[16,128]{1,0:T(8,128)S(1)} %get-tuple-element.35), channel_id=1, source_target_pairs={{2,1},{3,0},{0,3},{1,2},{6,5},{7,4},{4,7},{5,6},{10,9},{11,8},{8,1... | collective-permute-start | bytes 24584 | tf_op jit(solution)/shard_map/ppermute | solution.py:746
  9.5 6.2 %collective-permute-start.4 = (f32[152,128]{1,0:T(8,128)S(1)}, f32[152,128]{1,0:T(8,128)S(1)}, u32[]{:S(2)}, u32[]{:S(2)}) collective-permute-start(f32[152,128]{1,0:T(8,128)S(1)} %get-tuple-element.43), channel_id=1, source_target_pairs={{8,0},{12,4},{0,8},{4,12},{9,1},{13,5},{1,9},{5,13},{10,2},{14,6},... | collective-permute-start | bytes 233480 | tf_op jit(solution)/shard_map/ppermute | solution.py:754
  9.9 13.1 %collective-permute-start.7 = (f32[464,128]{1,0:T(8,128)S(1)}, f32[464,128]{1,0:T(8,128)S(1)}, u32[]{:S(2)}, u32[]{:S(2)}) collective-permute-start(f32[464,128]{1,0:T(8,128)S(1)} %get-tuple-element.50), channel_id=1, source_target_pairs={{4,0},{0,4},{12,8},{8,12},{5,1},{1,5},{13,9},{9,13},{6,2},{2,6},{1... | collective-permute-start | bytes 712712 | tf_op jit(solution)/shard_map/ppermute | solution.py:763
  10.4 12.6 %collective-permute-start.8 = (f32[464,128]{1,0:T(8,128)S(1)}, f32[464,128]{1,0:T(8,128)S(1)}, u32[]{:S(2)}, u32[]{:S(2)}) collective-permute-start(f32[464,128]{1,0:T(8,128)S(1)} %get-tuple-element.51), channel_id=1, source_target_pairs={{0,0},{8,4},{4,8},{12,12},{1,1},{9,5},{5,9},{13,13},{2,2},{10,6},{... | collective-permute-start | bytes 712712 | tf_op jit(solution)/shard_map/ppermute | solution.py:763
  15.8 9.4 %collective-permute-start.5 = (f32[320,128]{1,0:T(8,128)S(1)}, f32[320,128]{1,0:T(8,128)S(1)}, u32[]{:S(2)}, u32[]{:S(2)}) collective-permute-start(f32[320,128]{1,0:T(8,128)S(1)} %get-tuple-element.46), channel_id=1, source_target_pairs={{4,0},{0,4},{12,8},{8,12},{5,1},{1,5},{13,9},{9,13},{6,2},{2,6},{1... | collective-permute-start | bytes 491528 | tf_op jit(solution)/shard_map/ppermute | solution.py:763
  17.6 7.8 %collective-permute-start.6 = (f32[320,128]{1,0:T(8,128)S(1)}, f32[320,128]{1,0:T(8,128)S(1)}, u32[]{:S(2)}, u32[]{:S(2)}) collective-permute-start(f32[320,128]{1,0:T(8,128)S(1)} %get-tuple-element.47), channel_id=1, source_target_pairs={{0,0},{8,4},{4,8},{12,12},{1,1},{9,5},{5,9},{13,13},{2,2},{10,6},{... | collective-permute-start | bytes 491528 | tf_op jit(solution)/shard_map/ppermute | solution.py:763

commit v21 on v20

--- a/solution.py
+++ b/solution.py
@@ -117,6 +117,7 @@
             index = (kind * BX + x) * 8
             last_y_ref[index : index + 8] = vy[BY - 8 : BY]
     wave_ref[2 * PLANES : 2 * PLANES + BY] = previous[0]
+    wave_ref[2 * PLANES + BY :] = jnp.zeros((SPARE // 2, BZ), F32)
     last_x_ref[...] = previous[1]
     for group in range(3):
         strip_ref[group * BY : group * BY + BY] = strips[group]
@@ -776,7 +777,7 @@
     wave, ql, t, last_x, last_y, strips, table, receivers, receiver_wave, sources, source_wave, *sends = call(
         load_kernel,
         [
-            shape(2 * PLANES + BY, BZ),
+            shape(2 * PLANES + BY + SPARE // 2, BZ),
             shape(2 * PLANES, BZ),
             shape(PLANES, BZ),
             shape(BY, BZ),

time: 27.6 us -> 27.4 us (level)
  waiting for transfers between devices: 2.05 us -> 2.47 us
  starting transfers between devices: 15.9 us -> 15.5 us
    ppermute x4, waiting for transfers between devices: 0.21 us -> 0.69 us  [paired(): return lax.ppermute(array, 'gx', pairs)]
    ppermute x4, starting transfers between devices: 10.7 us -> 10.3 us  [paired(): return lax.ppermute(array, 'gx', pairs)]
where the time goes in v21:
time: 27.4 us; the launch traced here: 27.2 us
  starting transfers between devices  15.5 us (57%)
  Pallas kernels  8.55 us (31%)
  waiting for transfers between devices  2.47 us (9%)
  between operations  0.72 us (3%)
    ppermute x4, starting transfers between devices, paired(): return lax.ppermute(array, 'gx', pairs)  10.3 us
    pallas_call x9, Pallas kernels, call(): pl.pallas_call(kernel, out_shape=outs, in_specs=[pl.BlockSpec(memory_spac...  8.55 us
    ppermute x3, starting transfers between devices, rotated(): lax.ppermute(array, axis, [((i + offset) % count, i) for i in range(count)])  3.06 us
    ppermute x2, starting transfers between devices, from_sides(): both = lax.ppermute(sends[0], axes, route(1) + route(-1))  2.14 us
    ppermute x2, waiting for transfers between devices, from_sides(): both = lax.ppermute(sends[0], axes, route(1) + route(-1))  1.17 us
    ppermute x4, waiting for transfers between devices, paired(): return lax.ppermute(array, 'gx', pairs)  0.69 us
    ppermute x3, waiting for transfers between devices, rotated(): lax.ppermute(array, axis, [((i + offset) % count, i) for i in range(count)])  0.61 us
  transfers between devices with their start and end apart: 9, of which 3 were waited for; matrix products, arithmetic and copies ran while one was open for 0% of the time, Pallas kernels for 20%

profile of v21, /device:TPU:8, one launch (start us, length us, event | category | flops | bytes accessed | tf_op | source)
XLA Modules:
  0.0 27.2 jit_solution(7618053085538501431)
XLA Ops:
  0.6 1.3 %shard_map.95 = (f32[320,128]{1,0:T(8,128)S(1)}, f32[256,128]{1,0:T(8,128)S(1)}, f32[128,128]{1,0:T(8,128)S(1)}, f32[32,128]{1,0:T(8,128)S(1)}, f32[64,128]{1,0:...) custom-call(f32[4,4,32,128]{3,2,1,0:T(8,128)} %stored_hbm.1, ...), custom_call_target="tpu_custom_call" | custom-call | bytes 5166000 | tf_op jit(solution)/shard_map/pallas_call | solution.py:719
  2.0 2.7 %collective-permute-start = (f32[320,128]{1,0:T(8,128)S(1)}, f32[320,128]{1,0:T(8,128)S(1)}, u32[]{:S(2)}, u32[]{:S(2)}) collective-permute-start(f32[320,128]{1,0:T(8,128)S(1)} %get-tuple-element.33), channel_id=1, source_target_pairs={{8,0},{12,4},{0,8},{4,12},{9,1},{13,5},{1,9},{5,13},{10,2},{14,6},... | collective-permute-start | bytes 491528 | tf_op jit(solution)/shard_map/ppermute | solution.py:755
  4.6 1.5 %collective-permute-start.1 = (f32[160,128]{1,0:T(8,128)S(1)}, f32[160,128]{1,0:T(8,128)S(1)}, u32[]{:S(2)}, u32[]{:S(2)}) collective-permute-start(f32[160,128]{1,0:T(8,128)S(1)} %get-tuple-element.34), channel_id=1, source_target_pairs={{2,0},{0,2},{3,1},{1,3},{6,4},{4,6},{7,5},{5,7},{10,8},{8,10},{11,... | collective-permute-start | bytes 245768 | tf_op jit(solution)/shard_map/ppermute | solution.py:747
  6.1 0.0 collective-permute-start.3
  6.1 0.6 %collective-permute-start.2 = (f32[16,128]{1,0:T(8,128)S(1)}, f32[16,128]{1,0:T(8,128)S(1)}, u32[]{:S(2)}, u32[]{:S(2)}) collective-permute-start(f32[16,128]{1,0:T(8,128)S(1)} %get-tuple-element.35), channel_id=1, source_target_pairs={{2,1},{3,0},{0,3},{1,2},{6,5},{7,4},{4,7},{5,6},{10,9},{11,8},{8,1... | collective-permute-start | bytes 24584 | tf_op jit(solution)/shard_map/ppermute | solution.py:747
  6.8 1.2 %shard_map.96 = (f32[2,480,128]{2,1,0:T(8,128)S(1)}, f32[2,40,128]{2,1,0:T(8,128)S(1)}) custom-call(s32[3,1024]{1,0:T(4,128)S(1)} %get-tuple-element.40.receivers, f32[4,1024]{1,0:T(4,128)S(1)} %get-tuple-element.41.receiver_wave), custom_call_target="tpu_custom_call" | custom-call | bytes 4428000 | tf_op jit(solution)/shard_map/pallas_call | solution.py:719
  8.0 1.2 %collective-permute-done.2.corner_up.corner_down = f32[16,128]{1,0:T(8,128)S(1)} collective-permute-done((f32[16,128]{1,0:T(8,128)S(1)}, f32[16,128]{1,0:T(8,128)S(1)}, u32[]{:S(2)}, u32[]{:S(2)}) %collective-permute-start.2) | collective-permute-done | bytes 8224 | tf_op jit(solution)/shard_map/ppermute | solution.py:747
  9.2 0.0 collective-permute-done.3.other_ref
  9.2 0.0 collective-permute-done.1.from_up.from_down
  9.2 0.3 shard_map.97
  9.5 0.4 %collective-permute-start.4 = (f32[152,128]{1,0:T(8,128)S(1)}, f32[152,128]{1,0:T(8,128)S(1)}, u32[]{:S(2)}, u32[]{:S(2)}) collective-permute-start(f32[152,128]{1,0:T(8,128)S(1)} %get-tuple-element.43), channel_id=1, source_target_pairs={{8,0},{12,4},{0,8},{4,12},{9,1},{13,5},{1,9},{5,13},{10,2},{14,6},... | collective-permute-start | bytes 233480 | tf_op jit(solution)/shard_map/ppermute | solution.py:755
  9.9 0.5 %collective-permute-start.7 = (f32[464,128]{1,0:T(8,128)S(1)}, f32[464,128]{1,0:T(8,128)S(1)}, u32[]{:S(2)}, u32[]{:S(2)}) collective-permute-start(f32[464,128]{1,0:T(8,128)S(1)} %get-tuple-element.50), channel_id=1, source_target_pairs={{4,0},{0,4},{12,8},{8,12},{5,1},{1,5},{13,9},{9,13},{6,2},{2,6},{1... | collective-permute-start | bytes 712712 | tf_op jit(solution)/shard_map/ppermute | solution.py:764
  10.4 4.6 %collective-permute-start.8 = (f32[464,128]{1,0:T(8,128)S(1)}, f32[464,128]{1,0:T(8,128)S(1)}, u32[]{:S(2)}, u32[]{:S(2)}) collective-permute-start(f32[464,128]{1,0:T(8,128)S(1)} %get-tuple-element.51), channel_id=1, source_target_pairs={{0,0},{8,4},{4,8},{12,12},{1,1},{9,5},{5,9},{13,13},{2,2},{10,6},{... | collective-permute-start | bytes 712712 | tf_op jit(solution)/shard_map/ppermute | solution.py:764
  15.0 0.6 %collective-permute-done.4.late_ref = f32[152,128]{1,0:T(8,128)S(1)} collective-permute-done((f32[152,128]{1,0:T(8,128)S(1)}, f32[152,128]{1,0:T(8,128)S(1)}, u32[]{:S(2)}, u32[]{:S(2)}) %collective-permute-start.4) | collective-permute-done | bytes 77856 | tf_op jit(solution)/shard_map/ppermute | solution.py:755
  15.6 0.0 collective-permute-done.wave_ref
  15.6 0.1 shard_map.98
  15.7 2.2 %collective-permute-start.5 = (f32[320,128]{1,0:T(8,128)S(1)}, f32[320,128]{1,0:T(8,128)S(1)}, u32[]{:S(2)}, u32[]{:S(2)}) collective-permute-start(f32[320,128]{1,0:T(8,128)S(1)} %get-tuple-element.46), channel_id=1, source_target_pairs={{4,0},{0,4},{12,8},{8,12},{5,1},{1,5},{13,9},{9,13},{6,2},{2,6},{1... | collective-permute-start | bytes 491528 | tf_op jit(solution)/shard_map/ppermute | solution.py:764
  17.9 3.0 %collective-permute-start.6 = (f32[320,128]{1,0:T(8,128)S(1)}, f32[320,128]{1,0:T(8,128)S(1)}, u32[]{:S(2)}, u32[]{:S(2)}) collective-permute-start(f32[320,128]{1,0:T(8,128)S(1)} %get-tuple-element.47), channel_id=1, source_target_pairs={{0,0},{8,4},{4,8},{12,12},{1,1},{9,5},{5,9},{13,13},{2,2},{10,6},{... | collective-permute-start | bytes 491528 | tf_op jit(solution)/shard_map/ppermute | solution.py:764
  20.9 1.0 %shard_map.100 = (f32[2,320,128]{2,1,0:T(8,128)S(1)}, f32[2,40,128]{2,1,0:T(8,128)S(1)}) custom-call(s32[3,1024]{1,0:T(4,128)S(1)} %get-tuple-element.40.receivers, f32[4,1024]{1,0:T(4,128)S(1)} %get-tuple-element.41.receiver_wave, f32[304,128]{1,0:T(8,128)S(1)} %get-tuple-element.49.adj_ref._.late_ref), custom_call_target="tpu_custom_call" | custom-call | bytes 3690000 | tf_op jit(solution)/shard_map/pallas_call | solution.py:719
  21.9 0.5 %shard_map.102 = (f32[3,400,128]{2,1,0:T(8,128)S(1)}, f32[3,40,128]{2,1,0:T(8,128)S(1)}) custom-call(s32[3,64]{1,0:T(4,128)S(1)} %get-tuple-element.58.sources, f32[4,64]{1,0:T(4,128)S(1)} %get-tuple-element.59.source_wave, f32[304,128]{1,0:T(8,128)S(1)} %get-tuple-element.49.adj_ref._.late_ref), custom_call_target="tpu_custom_call" | custom-call | bytes 1845000 | tf_op jit(solution)/shard_map/pallas_call | solution.py:719
  22.5 0.0 collective-permute-done.7.even
  22.5 0.0 collective-permute-done.8.odd
  22.5 2.2 %shard_map.101 = (f32[4,4,32,128]{3,2,1,0:T(8,128)S(1)}, f32[4,4,4,32,128]{4,3,2,1,0:T(8,128)S(1)}, f32[3,12,40,128]{3,2,1,0:T(8,128)S(1)}, f32[3,40,128]{2,1,0:T(8,128)S(1)}) custom-call(f32[256,128]{1,0:T(8,128)S(1)} %get-tuple-element.48.ql_ref, f32[304,128]{1,0:T(8,128)S(1)} %get-tuple-element.49.adj_ref._.late_ref, ...), custom_call_target="tpu_custom_call" | custom-call | bytes 14391000 | tf_op jit(solution)/shard_map/pallas_call | solution.py:719
  24.7 0.0 collective-permute-done.5.even
  24.7 0.7 %collective-permute-done.6.odd = f32[320,128]{1,0:T(8,128)S(1)} collective-permute-done((f32[320,128]{1,0:T(8,128)S(1)}, f32[320,128]{1,0:T(8,128)S(1)}, u32[]{:S(2)}, u32[]{:S(2)}) %collective-permute-start.6) | collective-permute-done | bytes 163872 | tf_op jit(solution)/shard_map/ppermute | solution.py:764
  25.4 1.8 %shard_map.103 = (f32[2,4,32,128]{3,2,1,0:T(8,128)}, f32[4,4,32,128]{3,2,1,0:T(8,128)}) custom-call(f32[320,128]{1,0:T(8,128)S(1)} %collective-permute-done.wave_ref, f32[128,128]{1,0:T(8,128)S(1)} %get-tuple-element.44.own_s_ref, f32[144,128]{1,0:T(8,128)S(1)} %get-tuple-element.45.late_ref, f32[320,128]{1,0:T(8,128)S(1)} %collective-permute-done.5.even, ...), custom_call_target="tpu_custom_call" | custom-call | bytes 9225000 | tf_op jit(solution)/shard_map/pallas_call | solution.py:719
  (1 shorter events, 0.0 us)
Async XLA Ops:
  2.0 13.7 %collective-permute-start = (f32[320,128]{1,0:T(8,128)S(1)}, f32[320,128]{1,0:T(8,128)S(1)}, u32[]{:S(2)}, u32[]{:S(2)}) collective-permute-start(f32[320,128]{1,0:T(8,128)S(1)} %get-tuple-element.33), channel_id=1, source_target_pairs={{8,0},{12,4},{0,8},{4,12},{9,1},{13,5},{1,9},{5,13},{10,2},{14,6},... | collective-permute-start | bytes 491528 | tf_op jit(solution)/shard_map/ppermute | solution.py:755
  4.6 4.6 %collective-permute-start.1 = (f32[160,128]{1,0:T(8,128)S(1)}, f32[160,128]{1,0:T(8,128)S(1)}, u32[]{:S(2)}, u32[]{:S(2)}) collective-permute-start(f32[160,128]{1,0:T(8,128)S(1)} %get-tuple-element.34), channel_id=1, source_target_pairs={{2,0},{0,2},{3,1},{1,3},{6,4},{4,6},{7,5},{5,7},{10,8},{8,10},{11,... | collective-permute-start | bytes 245768 | tf_op jit(solution)/shard_map/ppermute | solution.py:747
  6.1 3.1 %collective-permute-start.3 = (f32[96,128]{1,0:T(8,128)S(1)}, f32[96,128]{1,0:T(8,128)S(1)}, u32[]{:S(2)}, u32[]{:S(2)}) collective-permute-start(f32[96,128]{1,0:T(8,128)S(1)} %get-tuple-element.36.strip_ref), channel_id=1, source_target_pairs={{1,0},{0,1},{3,2},{2,3},{5,4},{4,5},{7,6},{6,7},{9,8},{8,9},{11,10... | collective-permute-start | bytes 147464 | tf_op jit(solution)/shard_map/ppermute | solution.py:755
  6.1 3.1 %collective-permute-start.2 = (f32[16,128]{1,0:T(8,128)S(1)}, f32[16,128]{1,0:T(8,128)S(1)}, u32[]{:S(2)}, u32[]{:S(2)}) collective-permute-start(f32[16,128]{1,0:T(8,128)S(1)} %get-tuple-element.35), channel_id=1, source_target_pairs={{2,1},{3,0},{0,3},{1,2},{6,5},{7,4},{4,7},{5,6},{10,9},{11,8},{8,1... | collective-permute-start | bytes 24584 | tf_op jit(solution)/shard_map/ppermute | solution.py:747
  9.5 6.2 %collective-permute-start.4 = (f32[152,128]{1,0:T(8,128)S(1)}, f32[152,128]{1,0:T(8,128)S(1)}, u32[]{:S(2)}, u32[]{:S(2)}) collective-permute-start(f32[152,128]{1,0:T(8,128)S(1)} %get-tuple-element.43), channel_id=1, source_target_pairs={{8,0},{12,4},{0,8},{4,12},{9,1},{13,5},{1,9},{5,13},{10,2},{14,6},... | collective-permute-start | bytes 233480 | tf_op jit(solution)/shard_map/ppermute | solution.py:755
  9.9 12.6 %collective-permute-start.7 = (f32[464,128]{1,0:T(8,128)S(1)}, f32[464,128]{1,0:T(8,128)S(1)}, u32[]{:S(2)}, u32[]{:S(2)}) collective-permute-start(f32[464,128]{1,0:T(8,128)S(1)} %get-tuple-element.50), channel_id=1, source_target_pairs={{4,0},{0,4},{12,8},{8,12},{5,1},{1,5},{13,9},{9,13},{6,2},{2,6},{1... | collective-permute-start | bytes 712712 | tf_op jit(solution)/shard_map/ppermute | solution.py:764
  10.4 12.1 %collective-permute-start.8 = (f32[464,128]{1,0:T(8,128)S(1)}, f32[464,128]{1,0:T(8,128)S(1)}, u32[]{:S(2)}, u32[]{:S(2)}) collective-permute-start(f32[464,128]{1,0:T(8,128)S(1)} %get-tuple-element.51), channel_id=1, source_target_pairs={{0,0},{8,4},{4,8},{12,12},{1,1},{9,5},{5,9},{13,13},{2,2},{10,6},{... | collective-permute-start | bytes 712712 | tf_op jit(solution)/shard_map/ppermute | solution.py:764
  15.7 9.0 %collective-permute-start.5 = (f32[320,128]{1,0:T(8,128)S(1)}, f32[320,128]{1,0:T(8,128)S(1)}, u32[]{:S(2)}, u32[]{:S(2)}) collective-permute-start(f32[320,128]{1,0:T(8,128)S(1)} %get-tuple-element.46), channel_id=1, source_target_pairs={{4,0},{0,4},{12,8},{8,12},{5,1},{1,5},{13,9},{9,13},{6,2},{2,6},{1... | collective-permute-start | bytes 491528 | tf_op jit(solution)/shard_map/ppermute | solution.py:764
  17.9 7.5 %collective-permute-start.6 = (f32[320,128]{1,0:T(8,128)S(1)}, f32[320,128]{1,0:T(8,128)S(1)}, u32[]{:S(2)}, u32[]{:S(2)}) collective-permute-start(f32[320,128]{1,0:T(8,128)S(1)} %get-tuple-element.47), channel_id=1, source_target_pairs={{0,0},{8,4},{4,8},{12,12},{1,1},{9,5},{5,9},{13,13},{2,2},{10,6},{... | collective-permute-start | bytes 491528 | tf_op jit(solution)/shard_map/ppermute | solution.py:764

commit v22 on v21

--- a/solution.py
+++ b/solution.py
@@ -269,7 +269,7 @@
             target[tiles_end : tiles_end + EY] = strip
 
 
-def adjoint_join_kernel(ql_ref, adj_ref, even_ref, odd_ref):
+def adjoint_join_kernel(ql_ref, adj_ref, _, even_ref, odd_ref):
     planes_end, x_end, tiles_end = ADJ_OWN
     for target, first in zip((even_ref, odd_ref), pair_planes()):
         base = copy_rows(target, 0, adj_ref, first * BY, 3 * BY)
@@ -829,14 +829,6 @@
         1.0,
     )
     ra, rb = ra.reshape(2, early_planes, EY, BZ), rb.reshape(2, EX, EY, BZ)
-    even, odd = call(
-        adjoint_join_kernel,
-        [shape(ADJ_SIDE[1] + tile_rows(ADJ_TILES) + EY + 2 * PLANES, BZ)] * 2,
-        [ql, adj_late],
-        [],
-        "vv",
-    )
-    even, odd = paired(even, False), paired(odd, True)
     src, src_strip = call(
         source_kernel,
         [shape(STEPS - 1, source_planes * EY, BZ), shape(STEPS - 1, EY, BZ)],
@@ -845,6 +837,14 @@
         "vva",
         0.5,
     )
+    even, odd = call(
+        adjoint_join_kernel,
+        [shape(ADJ_SIDE[1] + tile_rows(ADJ_TILES) + EY + 2 * PLANES, BZ)] * 2,
+        [ql, adj_late, src_strip],
+        [],
+        "vva",
+    )
+    even, odd = paired(even, False), paired(odd, True)
     src = src.reshape(STEPS - 1, source_planes, EY, BZ)
     own_s, own_late, wave_even, wave_odd = call(
         join_kernel,

time: 27.4 us -> 27.4 us (level)
    ppermute x4, waiting for transfers between devices: 0.69 us -> 1.25 us  [paired(): return lax.ppermute(array, 'gx', pairs)]
    ppermute x3, waiting for transfers between devices: 0.61 us -> 0.06 us  [rotated(): lax.ppermute(array, axis, [((i + offset) % count, i) for i in range(count)])]
where the time goes in v22:
time: 27.4 us; the launch traced here: 27.2 us
  starting transfers between devices  15.5 us (57%)
  Pallas kernels  8.53 us (31%)
  waiting for transfers between devices  2.49 us (9%)
  between operations  0.72 us (3%)
    ppermute x4, starting transfers between devices, paired(): return lax.ppermute(array, 'gx', pairs)  10.3 us
    pallas_call x9, Pallas kernels, call(): pl.pallas_call(kernel, out_shape=outs, in_specs=[pl.BlockSpec(memory_spac...  8.53 us
    ppermute x3, starting transfers between devices, rotated(): lax.ppermute(array, axis, [((i + offset) % count, i) for i in range(count)])  3.06 us
    ppermute x2, starting transfers between devices, from_sides(): both = lax.ppermute(sends[0], axes, route(1) + route(-1))  2.14 us
    ppermute x4, waiting for transfers between devices, paired(): return lax.ppermute(array, 'gx', pairs)  1.25 us
    ppermute x2, waiting for transfers between devices, from_sides(): both = lax.ppermute(sends[0], axes, route(1) + route(-1))  1.17 us
  transfers between devices with their start and end apart: 9, of which 3 were waited for; matrix products, arithmetic and copies ran while one was open for 0% of the time, Pallas kernels for 20%

profile of v22, /device:TPU:8, one launch (start us, length us, event | category | flops | bytes accessed | tf_op | source)
XLA Modules:
  0.0 27.2 jit_solution(17647987843782860054)
XLA Ops:
  0.6 1.3 %shard_map.95 = (f32[320,128]{1,0:T(8,128)S(1)}, f32[256,128]{1,0:T(8,128)S(1)}, f32[128,128]{1,0:T(8,128)S(1)}, f32[32,128]{1,0:T(8,128)S(1)}, f32[64,128]{1,0:...) custom-call(f32[4,4,32,128]{3,2,1,0:T(8,128)} %stored_hbm.1, ...), custom_call_target="tpu_custom_call" | custom-call | bytes 5166000 | tf_op jit(solution)/shard_map/pallas_call | solution.py:719
  2.0 2.7 %collective-permute-start = (f32[320,128]{1,0:T(8,128)S(1)}, f32[320,128]{1,0:T(8,128)S(1)}, u32[]{:S(2)}, u32[]{:S(2)}) collective-permute-start(f32[320,128]{1,0:T(8,128)S(1)} %get-tuple-element.33), channel_id=1, source_target_pairs={{8,0},{12,4},{0,8},{4,12},{9,1},{13,5},{1,9},{5,13},{10,2},{14,6},... | collective-permute-start | bytes 491528 | tf_op jit(solution)/shard_map/ppermute | solution.py:755
  4.6 1.5 %collective-permute-start.1 = (f32[160,128]{1,0:T(8,128)S(1)}, f32[160,128]{1,0:T(8,128)S(1)}, u32[]{:S(2)}, u32[]{:S(2)}) collective-permute-start(f32[160,128]{1,0:T(8,128)S(1)} %get-tuple-element.34), channel_id=1, source_target_pairs={{2,0},{0,2},{3,1},{1,3},{6,4},{4,6},{7,5},{5,7},{10,8},{8,10},{11,... | collective-permute-start | bytes 245768 | tf_op jit(solution)/shard_map/ppermute | solution.py:747
  6.1 0.0 collective-permute-start.3
  6.1 0.6 %collective-permute-start.2 = (f32[16,128]{1,0:T(8,128)S(1)}, f32[16,128]{1,0:T(8,128)S(1)}, u32[]{:S(2)}, u32[]{:S(2)}) collective-permute-start(f32[16,128]{1,0:T(8,128)S(1)} %get-tuple-element.35), channel_id=1, source_target_pairs={{2,1},{3,0},{0,3},{1,2},{6,5},{7,4},{4,7},{5,6},{10,9},{11,8},{8,1... | collective-permute-start | bytes 24584 | tf_op jit(solution)/shard_map/ppermute | solution.py:747
  6.8 1.2 %shard_map.96 = (f32[2,480,128]{2,1,0:T(8,128)S(1)}, f32[2,40,128]{2,1,0:T(8,128)S(1)}) custom-call(s32[3,1024]{1,0:T(4,128)S(1)} %get-tuple-element.40.receivers, f32[4,1024]{1,0:T(4,128)S(1)} %get-tuple-element.41.receiver_wave), custom_call_target="tpu_custom_call" | custom-call | bytes 4428000 | tf_op jit(solution)/shard_map/pallas_call | solution.py:719
  8.0 1.2 %collective-permute-done.2.corner_up.corner_down = f32[16,128]{1,0:T(8,128)S(1)} collective-permute-done((f32[16,128]{1,0:T(8,128)S(1)}, f32[16,128]{1,0:T(8,128)S(1)}, u32[]{:S(2)}, u32[]{:S(2)}) %collective-permute-start.2) | collective-permute-done | bytes 8224 | tf_op jit(solution)/shard_map/ppermute | solution.py:747
  9.2 0.0 collective-permute-done.3.other_ref
  9.2 0.0 collective-permute-done.1.from_up.from_down
  9.2 0.3 shard_map.97
  9.5 0.4 %collective-permute-start.4 = (f32[152,128]{1,0:T(8,128)S(1)}, f32[152,128]{1,0:T(8,128)S(1)}, u32[]{:S(2)}, u32[]{:S(2)}) collective-permute-start(f32[152,128]{1,0:T(8,128)S(1)} %get-tuple-element.43), channel_id=1, source_target_pairs={{8,0},{12,4},{0,8},{4,12},{9,1},{13,5},{1,9},{5,13},{10,2},{14,6},... | collective-permute-start | bytes 233480 | tf_op jit(solution)/shard_map/ppermute | solution.py:755
  9.9 0.5 %shard_map.99 = (f32[3,400,128]{2,1,0:T(8,128)S(1)}, f32[3,40,128]{2,1,0:T(8,128)S(1)}) custom-call(s32[3,64]{1,0:T(4,128)S(1)} %get-tuple-element.50.sources, f32[4,64]{1,0:T(4,128)S(1)} %get-tuple-element.51.source_wave, f32[304,128]{1,0:T(8,128)S(1)} %get-tuple-element.49._.adj_ref.late_ref), custom_call_target="tpu_custom_call" | custom-call | bytes 1845000 | tf_op jit(solution)/shard_map/pallas_call | solution.py:719
  10.4 0.5 %collective-permute-start.7 = (f32[464,128]{1,0:T(8,128)S(1)}, f32[464,128]{1,0:T(8,128)S(1)}, u32[]{:S(2)}, u32[]{:S(2)}) collective-permute-start(f32[464,128]{1,0:T(8,128)S(1)} %get-tuple-element.53), channel_id=1, source_target_pairs={{4,0},{0,4},{12,8},{8,12},{5,1},{1,5},{13,9},{9,13},{6,2},{2,6},{1... | collective-permute-start | bytes 712712 | tf_op jit(solution)/shard_map/ppermute | solution.py:764
  11.0 4.6 %collective-permute-start.8 = (f32[464,128]{1,0:T(8,128)S(1)}, f32[464,128]{1,0:T(8,128)S(1)}, u32[]{:S(2)}, u32[]{:S(2)}) collective-permute-start(f32[464,128]{1,0:T(8,128)S(1)} %get-tuple-element.54), channel_id=1, source_target_pairs={{0,0},{8,4},{4,8},{12,12},{1,1},{9,5},{5,9},{13,13},{2,2},{10,6},{... | collective-permute-start | bytes 712712 | tf_op jit(solution)/shard_map/ppermute | solution.py:764
  15.6 0.1 collective-permute-done.4.late_ref
  15.6 0.0 collective-permute-done.wave_ref
  15.6 0.1 shard_map.98
  15.7 2.2 %collective-permute-start.5 = (f32[320,128]{1,0:T(8,128)S(1)}, f32[320,128]{1,0:T(8,128)S(1)}, u32[]{:S(2)}, u32[]{:S(2)}) collective-permute-start(f32[320,128]{1,0:T(8,128)S(1)} %get-tuple-element.46), channel_id=1, source_target_pairs={{4,0},{0,4},{12,8},{8,12},{5,1},{1,5},{13,9},{9,13},{6,2},{2,6},{1... | collective-permute-start | bytes 491528 | tf_op jit(solution)/shard_map/ppermute | solution.py:764
  17.9 3.0 %collective-permute-start.6 = (f32[320,128]{1,0:T(8,128)S(1)}, f32[320,128]{1,0:T(8,128)S(1)}, u32[]{:S(2)}, u32[]{:S(2)}) collective-permute-start(f32[320,128]{1,0:T(8,128)S(1)} %get-tuple-element.47), channel_id=1, source_target_pairs={{0,0},{8,4},{4,8},{12,12},{1,1},{9,5},{5,9},{13,13},{2,2},{10,6},{... | collective-permute-start | bytes 491528 | tf_op jit(solution)/shard_map/ppermute | solution.py:764
  20.9 1.0 %shard_map.101 = (f32[2,320,128]{2,1,0:T(8,128)S(1)}, f32[2,40,128]{2,1,0:T(8,128)S(1)}) custom-call(s32[3,1024]{1,0:T(4,128)S(1)} %get-tuple-element.40.receivers, f32[4,1024]{1,0:T(4,128)S(1)} %get-tuple-element.41.receiver_wave, f32[304,128]{1,0:T(8,128)S(1)} %get-tuple-element.49._.adj_ref.late_ref), custom_call_target="tpu_custom_call" | custom-call | bytes 3690000 | tf_op jit(solution)/shard_map/pallas_call | solution.py:719
  21.9 0.0 collective-permute-done.7.even
  22.0 0.0 collective-permute-done.8.odd
  22.0 2.2 %shard_map.102 = (f32[4,4,32,128]{3,2,1,0:T(8,128)S(1)}, f32[4,4,4,32,128]{4,3,2,1,0:T(8,128)S(1)}, f32[3,12,40,128]{3,2,1,0:T(8,128)S(1)}, f32[3,40,128]{2,1,0:T(8,128)S(1)}) custom-call(f32[256,128]{1,0:T(8,128)S(1)} %get-tuple-element.48.ql_ref, f32[304,128]{1,0:T(8,128)S(1)} %get-tuple-element.49._.adj_ref.late_ref, ...), custom_call_target="tpu_custom_call" | custom-call | bytes 14391000 | tf_op jit(solution)/shard_map/pallas_call | solution.py:719
  24.2 0.0 collective-permute-done.5.even
  24.2 1.2 %collective-permute-done.6.odd = f32[320,128]{1,0:T(8,128)S(1)} collective-permute-done((f32[320,128]{1,0:T(8,128)S(1)}, f32[320,128]{1,0:T(8,128)S(1)}, u32[]{:S(2)}, u32[]{:S(2)}) %collective-permute-start.6) | collective-permute-done | bytes 163872 | tf_op jit(solution)/shard_map/ppermute | solution.py:764
  25.4 1.8 %shard_map.103 = (f32[2,4,32,128]{3,2,1,0:T(8,128)}, f32[4,4,32,128]{3,2,1,0:T(8,128)}) custom-call(f32[320,128]{1,0:T(8,128)S(1)} %collective-permute-done.wave_ref, f32[128,128]{1,0:T(8,128)S(1)} %get-tuple-element.44.own_s_ref, f32[144,128]{1,0:T(8,128)S(1)} %get-tuple-element.45.late_ref, f32[320,128]{1,0:T(8,128)S(1)} %collective-permute-done.5.even, ...), custom_call_target="tpu_custom_call" | custom-call | bytes 9225000 | tf_op jit(solution)/shard_map/pallas_call | solution.py:719
  (1 shorter events, 0.0 us)
Async XLA Ops:
  2.0 13.7 %collective-permute-start = (f32[320,128]{1,0:T(8,128)S(1)}, f32[320,128]{1,0:T(8,128)S(1)}, u32[]{:S(2)}, u32[]{:S(2)}) collective-permute-start(f32[320,128]{1,0:T(8,128)S(1)} %get-tuple-element.33), channel_id=1, source_target_pairs={{8,0},{12,4},{0,8},{4,12},{9,1},{13,5},{1,9},{5,13},{10,2},{14,6},... | collective-permute-start | bytes 491528 | tf_op jit(solution)/shard_map/ppermute | solution.py:755
  4.6 4.6 %collective-permute-start.1 = (f32[160,128]{1,0:T(8,128)S(1)}, f32[160,128]{1,0:T(8,128)S(1)}, u32[]{:S(2)}, u32[]{:S(2)}) collective-permute-start(f32[160,128]{1,0:T(8,128)S(1)} %get-tuple-element.34), channel_id=1, source_target_pairs={{2,0},{0,2},{3,1},{1,3},{6,4},{4,6},{7,5},{5,7},{10,8},{8,10},{11,... | collective-permute-start | bytes 245768 | tf_op jit(solution)/shard_map/ppermute | solution.py:747
  6.1 3.1 %collective-permute-start.3 = (f32[96,128]{1,0:T(8,128)S(1)}, f32[96,128]{1,0:T(8,128)S(1)}, u32[]{:S(2)}, u32[]{:S(2)}) collective-permute-start(f32[96,128]{1,0:T(8,128)S(1)} %get-tuple-element.36.strip_ref), channel_id=1, source_target_pairs={{1,0},{0,1},{3,2},{2,3},{5,4},{4,5},{7,6},{6,7},{9,8},{8,9},{11,10... | collective-permute-start | bytes 147464 | tf_op jit(solution)/shard_map/ppermute | solution.py:755
  6.1 3.1 %collective-permute-start.2 = (f32[16,128]{1,0:T(8,128)S(1)}, f32[16,128]{1,0:T(8,128)S(1)}, u32[]{:S(2)}, u32[]{:S(2)}) collective-permute-start(f32[16,128]{1,0:T(8,128)S(1)} %get-tuple-element.35), channel_id=1, source_target_pairs={{2,1},{3,0},{0,3},{1,2},{6,5},{7,4},{4,7},{5,6},{10,9},{11,8},{8,1... | collective-permute-start | bytes 24584 | tf_op jit(solution)/shard_map/ppermute | solution.py:747
  9.5 6.2 %collective-permute-start.4 = (f32[152,128]{1,0:T(8,128)S(1)}, f32[152,128]{1,0:T(8,128)S(1)}, u32[]{:S(2)}, u32[]{:S(2)}) collective-permute-start(f32[152,128]{1,0:T(8,128)S(1)} %get-tuple-element.43), channel_id=1, source_target_pairs={{8,0},{12,4},{0,8},{4,12},{9,1},{13,5},{1,9},{5,13},{10,2},{14,6},... | collective-permute-start | bytes 233480 | tf_op jit(solution)/shard_map/ppermute | solution.py:755
  10.4 11.5 %collective-permute-start.7 = (f32[464,128]{1,0:T(8,128)S(1)}, f32[464,128]{1,0:T(8,128)S(1)}, u32[]{:S(2)}, u32[]{:S(2)}) collective-permute-start(f32[464,128]{1,0:T(8,128)S(1)} %get-tuple-element.53), channel_id=1, source_target_pairs={{4,0},{0,4},{12,8},{8,12},{5,1},{1,5},{13,9},{9,13},{6,2},{2,6},{1... | collective-permute-start | bytes 712712 | tf_op jit(solution)/shard_map/ppermute | solution.py:764
  11.0 11.0 %collective-permute-start.8 = (f32[464,128]{1,0:T(8,128)S(1)}, f32[464,128]{1,0:T(8,128)S(1)}, u32[]{:S(2)}, u32[]{:S(2)}) collective-permute-start(f32[464,128]{1,0:T(8,128)S(1)} %get-tuple-element.54), channel_id=1, source_target_pairs={{0,0},{8,4},{4,8},{12,12},{1,1},{9,5},{5,9},{13,13},{2,2},{10,6},{... | collective-permute-start | bytes 712712 | tf_op jit(solution)/shard_map/ppermute | solution.py:764
  15.7 8.4 %collective-permute-start.5 = (f32[320,128]{1,0:T(8,128)S(1)}, f32[320,128]{1,0:T(8,128)S(1)}, u32[]{:S(2)}, u32[]{:S(2)}) collective-permute-start(f32[320,128]{1,0:T(8,128)S(1)} %get-tuple-element.46), channel_id=1, source_target_pairs={{4,0},{0,4},{12,8},{8,12},{5,1},{1,5},{13,9},{9,13},{6,2},{2,6},{1... | collective-permute-start | bytes 491528 | tf_op jit(solution)/shard_map/ppermute | solution.py:764
  17.9 7.5 %collective-permute-start.6 = (f32[320,128]{1,0:T(8,128)S(1)}, f32[320,128]{1,0:T(8,128)S(1)}, u32[]{:S(2)}, u32[]{:S(2)}) collective-permute-start(f32[320,128]{1,0:T(8,128)S(1)} %get-tuple-element.47), channel_id=1, source_target_pairs={{0,0},{8,4},{4,8},{12,12},{1,1},{9,5},{5,9},{13,13},{2,2},{10,6},{... | collective-permute-start | bytes 491528 | tf_op jit(solution)/shard_map/ppermute | solution.py:764

commit v23 on v21

--- a/solution.py
+++ b/solution.py
@@ -1,3 +1,5 @@
+import functools
+
 import jax
 import jax.numpy as jnp
 from jax import lax
@@ -180,10 +182,10 @@
 
 
 def merge_kernel(
+    kinds,
     from_up, from_down, corner_up, corner_down, strip_ref, other_ref,
     t_ref, last_x_ref, last_y_ref, _,
-    late_ref, adj_ref,
-    wave_ref,
+    out_ref, wave_ref,
 ):
     gy = lax.axis_index("gy")
     tile_row = rows((8, BZ))
@@ -214,7 +216,9 @@
     last_lanes = (BX - 1) * STRIP
     fix_row = jnp.zeros((8, BZ), F32)
     fix_lane = jnp.zeros((BY, BZ), F32)
-    for kind, target in enumerate((wave_ref, adj_ref)):
+    late_ref = out_ref
+    for kind in kinds:
+        target = (wave_ref, out_ref)[kind]
         first = 4 * kind
         planes_end, x_end, tiles_end = (WAVE_OWN, ADJ_OWN)[kind]
         vx, vy, vz = (strip_field(first + 1 + axis) for axis in range(3))
@@ -812,10 +816,18 @@
         1.2,
     )
     early_planes, source_planes = (last - first for first, last in (EARLY_PLANES, SOURCE_PLANES))
-    late, adj_late = call(
-        merge_kernel,
-        [shape(tile_rows(9) + EY + 8 + SPARE, BZ), shape(ADJ_OWN[2] + EY, BZ)],
-        [from_up, from_down, corner_up, corner_down, strips, other, t, last_x, last_y, rsb],
+    ends = [from_up, from_down, corner_up, corner_down, strips, other, t, last_x, last_y]
+    (late,) = call(
+        functools.partial(merge_kernel, (0,)),
+        [shape(tile_rows(9) + EY + 8 + SPARE, BZ)],
+        ends + [rsb],
+        [pltpu.VMEM((WAVE_OWN[2], BZ), F32)],
+        "vvvvvvvvva",
+    )
+    (adj_late,) = call(
+        functools.partial(merge_kernel, (1,)),
+        [shape(ADJ_OWN[2] + EY, BZ)],
+        ends + [late],
         [pltpu.VMEM((WAVE_OWN[2], BZ), F32)],
         "vvvvvvvvva",
     )

time: 27.4 us -> 27.4 us (level)
  waiting for transfers between devices: 2.47 us -> 2.19 us
    pallas_call x9 -> x10, Pallas kernels: 8.55 us -> 8.77 us  [call(): pl.pallas_call(kernel, out_shape=outs, in_specs=[pl.BlockSpec(memory_spac...]
  transfers between devices with their start and end apart: 9 -> 9, of which waited for: 3 -> 3; matrix products, arithmetic and copies ran while one was open for 0% -> 0% of each run, Pallas kernels for 20% -> 21%
where the time goes in v23:
time: 27.4 us; the launch traced here: 27.2 us
  starting transfers between devices  15.5 us (57%)
  Pallas kernels  8.77 us (32%)
  waiting for transfers between devices  2.19 us (8%)
  between operations  0.73 us (3%)
    ppermute x4, starting transfers between devices, paired(): return lax.ppermute(array, 'gx', pairs)  10.3 us
    pallas_call x10, Pallas kernels, call(): pl.pallas_call(kernel, out_shape=outs, in_specs=[pl.BlockSpec(memory_spac...  8.77 us
    ppermute x3, starting transfers between devices, rotated(): lax.ppermute(array, axis, [((i + offset) % count, i) for i in range(count)])  3.06 us
    ppermute x2, starting transfers between devices, from_sides(): both = lax.ppermute(sends[0], axes, route(1) + route(-1))  2.14 us
    ppermute x2, waiting for transfers between devices, from_sides(): both = lax.ppermute(sends[0], axes, route(1) + route(-1))  1.17 us
    ppermute x4, waiting for transfers between devices, paired(): return lax.ppermute(array, 'gx', pairs)  0.65 us
  transfers between devices with their start and end apart: 9, of which 3 were waited for; matrix products, arithmetic and copies ran while one was open for 0% of the time, Pallas kernels for 21%

profile of v23, /device:TPU:8, one launch (start us, length us, event | category | flops | bytes accessed | tf_op | source)
XLA Modules:
  0.0 27.2 jit_solution(1759664322720498567)
XLA Ops:
  0.6 1.3 %shard_map.95 = (f32[320,128]{1,0:T(8,128)S(1)}, f32[256,128]{1,0:T(8,128)S(1)}, f32[128,128]{1,0:T(8,128)S(1)}, f32[32,128]{1,0:T(8,128)S(1)}, f32[64,128]{1,0:...) custom-call(f32[4,4,32,128]{3,2,1,0:T(8,128)} %stored_hbm.1, ...), custom_call_target="tpu_custom_call" | custom-call | bytes 5166000 | tf_op jit(solution)/shard_map/pallas_call | solution.py:723
  2.0 2.7 %collective-permute-start = (f32[320,128]{1,0:T(8,128)S(1)}, f32[320,128]{1,0:T(8,128)S(1)}, u32[]{:S(2)}, u32[]{:S(2)}) collective-permute-start(f32[320,128]{1,0:T(8,128)S(1)} %get-tuple-element.31), channel_id=1, source_target_pairs={{8,0},{12,4},{0,8},{4,12},{9,1},{13,5},{1,9},{5,13},{10,2},{14,6},... | collective-permute-start | bytes 491528 | tf_op jit(solution)/shard_map/ppermute | solution.py:759
  4.6 1.5 %collective-permute-start.1 = (f32[160,128]{1,0:T(8,128)S(1)}, f32[160,128]{1,0:T(8,128)S(1)}, u32[]{:S(2)}, u32[]{:S(2)}) collective-permute-start(f32[160,128]{1,0:T(8,128)S(1)} %get-tuple-element.32), channel_id=1, source_target_pairs={{2,0},{0,2},{3,1},{1,3},{6,4},{4,6},{7,5},{5,7},{10,8},{8,10},{11,... | collective-permute-start | bytes 245768 | tf_op jit(solution)/shard_map/ppermute | solution.py:751
  6.1 0.0 collective-permute-start.3
  6.1 0.6 %collective-permute-start.2 = (f32[16,128]{1,0:T(8,128)S(1)}, f32[16,128]{1,0:T(8,128)S(1)}, u32[]{:S(2)}, u32[]{:S(2)}) collective-permute-start(f32[16,128]{1,0:T(8,128)S(1)} %get-tuple-element.33), channel_id=1, source_target_pairs={{2,1},{3,0},{0,3},{1,2},{6,5},{7,4},{4,7},{5,6},{10,9},{11,8},{8,1... | collective-permute-start | bytes 24584 | tf_op jit(solution)/shard_map/ppermute | solution.py:751
  6.8 1.2 %shard_map.96 = (f32[2,480,128]{2,1,0:T(8,128)S(1)}, f32[2,40,128]{2,1,0:T(8,128)S(1)}) custom-call(s32[3,1024]{1,0:T(4,128)S(1)} %get-tuple-element.38.receivers, f32[4,1024]{1,0:T(4,128)S(1)} %get-tuple-element.39.receiver_wave), custom_call_target="tpu_custom_call" | custom-call | bytes 4428000 | tf_op jit(solution)/shard_map/pallas_call | solution.py:723
  8.0 1.2 %collective-permute-done.2.corner_up.corner_down = f32[16,128]{1,0:T(8,128)S(1)} collective-permute-done((f32[16,128]{1,0:T(8,128)S(1)}, f32[16,128]{1,0:T(8,128)S(1)}, u32[]{:S(2)}, u32[]{:S(2)}) %collective-permute-start.2) | collective-permute-done | bytes 8224 | tf_op jit(solution)/shard_map/ppermute | solution.py:751
  9.2 0.0 collective-permute-done.3.other_ref
  9.2 0.0 collective-permute-done.1.from_up.from_down
  9.2 0.2 shard_map.97._
  9.4 0.4 %collective-permute-start.4 = (f32[152,128]{1,0:T(8,128)S(1)}, f32[152,128]{1,0:T(8,128)S(1)}, u32[]{:S(2)}, u32[]{:S(2)}) collective-permute-start(f32[152,128]{1,0:T(8,128)S(1)} %shard_map.97._), channel_id=1, source_target_pairs={{8,0},{12,4},{0,8},{4,12},{9,1},{13,5},{1,9},{5,13},{10,2},{14,6},... | collective-permute-start | bytes 233480 | tf_op jit(solution)/shard_map/ppermute | solution.py:759
  9.8 0.2 shard_map.99.adj_ref._.late_ref
  10.1 0.5 %collective-permute-start.7 = (f32[464,128]{1,0:T(8,128)S(1)}, f32[464,128]{1,0:T(8,128)S(1)}, u32[]{:S(2)}, u32[]{:S(2)}) collective-permute-start(f32[464,128]{1,0:T(8,128)S(1)} %get-tuple-element.46), channel_id=1, source_target_pairs={{4,0},{0,4},{12,8},{8,12},{5,1},{1,5},{13,9},{9,13},{6,2},{2,6},{1... | collective-permute-start | bytes 712712 | tf_op jit(solution)/shard_map/ppermute | solution.py:768
  10.6 4.6 %collective-permute-start.8 = (f32[464,128]{1,0:T(8,128)S(1)}, f32[464,128]{1,0:T(8,128)S(1)}, u32[]{:S(2)}, u32[]{:S(2)}) collective-permute-start(f32[464,128]{1,0:T(8,128)S(1)} %get-tuple-element.47), channel_id=1, source_target_pairs={{0,0},{8,4},{4,8},{12,12},{1,1},{9,5},{5,9},{13,13},{2,2},{10,6},{... | collective-permute-start | bytes 712712 | tf_op jit(solution)/shard_map/ppermute | solution.py:768
  15.2 0.4 %collective-permute-done.4.late_ref = f32[152,128]{1,0:T(8,128)S(1)} collective-permute-done((f32[152,128]{1,0:T(8,128)S(1)}, f32[152,128]{1,0:T(8,128)S(1)}, u32[]{:S(2)}, u32[]{:S(2)}) %collective-permute-start.4) | collective-permute-done | bytes 77856 | tf_op jit(solution)/shard_map/ppermute | solution.py:759
  15.6 0.0 collective-permute-done.wave_ref
  15.6 0.1 shard_map.98
  15.7 2.2 %collective-permute-start.5 = (f32[320,128]{1,0:T(8,128)S(1)}, f32[320,128]{1,0:T(8,128)S(1)}, u32[]{:S(2)}, u32[]{:S(2)}) collective-permute-start(f32[320,128]{1,0:T(8,128)S(1)} %get-tuple-element.43), channel_id=1, source_target_pairs={{4,0},{0,4},{12,8},{8,12},{5,1},{1,5},{13,9},{9,13},{6,2},{2,6},{1... | collective-permute-start | bytes 491528 | tf_op jit(solution)/shard_map/ppermute | solution.py:768
  17.9 3.1 %collective-permute-start.6 = (f32[320,128]{1,0:T(8,128)S(1)}, f32[320,128]{1,0:T(8,128)S(1)}, u32[]{:S(2)}, u32[]{:S(2)}) collective-permute-start(f32[320,128]{1,0:T(8,128)S(1)} %get-tuple-element.44), channel_id=1, source_target_pairs={{0,0},{8,4},{4,8},{12,12},{1,1},{9,5},{5,9},{13,13},{2,2},{10,6},{... | collective-permute-start | bytes 491528 | tf_op jit(solution)/shard_map/ppermute | solution.py:768
  20.9 1.0 %shard_map.101 = (f32[2,320,128]{2,1,0:T(8,128)S(1)}, f32[2,40,128]{2,1,0:T(8,128)S(1)}) custom-call(s32[3,1024]{1,0:T(4,128)S(1)} %get-tuple-element.38.receivers, f32[4,1024]{1,0:T(4,128)S(1)} %get-tuple-element.39.receiver_wave, f32[304,128]{1,0:T(8,128)S(1)} %shard_map.99.adj_ref._.late_ref), custom_call_target="tpu_custom_call" | custom-call | bytes 3690000 | tf_op jit(solution)/shard_map/pallas_call | solution.py:723
  21.9 0.6 %shard_map.103 = (f32[3,400,128]{2,1,0:T(8,128)S(1)}, f32[3,40,128]{2,1,0:T(8,128)S(1)}) custom-call(s32[3,64]{1,0:T(4,128)S(1)} %get-tuple-element.54.sources, f32[4,64]{1,0:T(4,128)S(1)} %get-tuple-element.55.source_wave, f32[304,128]{1,0:T(8,128)S(1)} %shard_map.99.adj_ref._.late_ref), custom_call_target="tpu_custom_call" | custom-call | bytes 1845000 | tf_op jit(solution)/shard_map/pallas_call | solution.py:723
  22.5 0.0 collective-permute-done.7.even
  22.5 0.0 collective-permute-done.8.odd
  22.5 2.2 %shard_map.102 = (f32[4,4,32,128]{3,2,1,0:T(8,128)S(1)}, f32[4,4,4,32,128]{4,3,2,1,0:T(8,128)S(1)}, f32[3,12,40,128]{3,2,1,0:T(8,128)S(1)}, f32[3,40,128]{2,1,0:T(8,128)S(1)}) custom-call(f32[256,128]{1,0:T(8,128)S(1)} %get-tuple-element.45.ql_ref, f32[304,128]{1,0:T(8,128)S(1)} %shard_map.99.adj_ref._.late_ref, f32[464,128]{1,0:T(8,128)S(1)} %collective-permute-done.7.even, ...), custom_call_target="tpu_custom_call" | custom-call | bytes 14391000 | tf_op jit(solution)/shard_map/pallas_call | solution.py:723
  24.8 0.0 collective-permute-done.5.even
  24.8 0.6 %collective-permute-done.6.odd = f32[320,128]{1,0:T(8,128)S(1)} collective-permute-done((f32[320,128]{1,0:T(8,128)S(1)}, f32[320,128]{1,0:T(8,128)S(1)}, u32[]{:S(2)}, u32[]{:S(2)}) %collective-permute-start.6) | collective-permute-done | bytes 163872 | tf_op jit(solution)/shard_map/ppermute | solution.py:768
  25.4 1.8 %shard_map.104 = (f32[2,4,32,128]{3,2,1,0:T(8,128)}, f32[4,4,32,128]{3,2,1,0:T(8,128)}) custom-call(f32[320,128]{1,0:T(8,128)S(1)} %collective-permute-done.wave_ref, f32[128,128]{1,0:T(8,128)S(1)} %get-tuple-element.41.own_s_ref, f32[144,128]{1,0:T(8,128)S(1)} %get-tuple-element.42.late_ref, f32[320,128]{1,0:T(8,128)S(1)} %collective-permute-done.5.even, ...), custom_call_target="tpu_custom_call" | custom-call | bytes 9225000 | tf_op jit(solution)/shard_map/pallas_call | solution.py:723
  (1 shorter events, 0.0 us)
Async XLA Ops:
  2.0 13.6 %collective-permute-start = (f32[320,128]{1,0:T(8,128)S(1)}, f32[320,128]{1,0:T(8,128)S(1)}, u32[]{:S(2)}, u32[]{:S(2)}) collective-permute-start(f32[320,128]{1,0:T(8,128)S(1)} %get-tuple-element.31), channel_id=1, source_target_pairs={{8,0},{12,4},{0,8},{4,12},{9,1},{13,5},{1,9},{5,13},{10,2},{14,6},... | collective-permute-start | bytes 491528 | tf_op jit(solution)/shard_map/ppermute | solution.py:759
  4.6 4.6 %collective-permute-start.1 = (f32[160,128]{1,0:T(8,128)S(1)}, f32[160,128]{1,0:T(8,128)S(1)}, u32[]{:S(2)}, u32[]{:S(2)}) collective-permute-start(f32[160,128]{1,0:T(8,128)S(1)} %get-tuple-element.32), channel_id=1, source_target_pairs={{2,0},{0,2},{3,1},{1,3},{6,4},{4,6},{7,5},{5,7},{10,8},{8,10},{11,... | collective-permute-start | bytes 245768 | tf_op jit(solution)/shard_map/ppermute | solution.py:751
  6.1 3.1 %collective-permute-start.3 = (f32[96,128]{1,0:T(8,128)S(1)}, f32[96,128]{1,0:T(8,128)S(1)}, u32[]{:S(2)}, u32[]{:S(2)}) collective-permute-start(f32[96,128]{1,0:T(8,128)S(1)} %get-tuple-element.34.strip_ref), channel_id=1, source_target_pairs={{1,0},{0,1},{3,2},{2,3},{5,4},{4,5},{7,6},{6,7},{9,8},{8,9},{11,10... | collective-permute-start | bytes 147464 | tf_op jit(solution)/shard_map/ppermute | solution.py:759
  6.1 3.1 %collective-permute-start.2 = (f32[16,128]{1,0:T(8,128)S(1)}, f32[16,128]{1,0:T(8,128)S(1)}, u32[]{:S(2)}, u32[]{:S(2)}) collective-permute-start(f32[16,128]{1,0:T(8,128)S(1)} %get-tuple-element.33), channel_id=1, source_target_pairs={{2,1},{3,0},{0,3},{1,2},{6,5},{7,4},{4,7},{5,6},{10,9},{11,8},{8,1... | collective-permute-start | bytes 24584 | tf_op jit(solution)/shard_map/ppermute | solution.py:751
  9.4 6.2 %collective-permute-start.4 = (f32[152,128]{1,0:T(8,128)S(1)}, f32[152,128]{1,0:T(8,128)S(1)}, u32[]{:S(2)}, u32[]{:S(2)}) collective-permute-start(f32[152,128]{1,0:T(8,128)S(1)} %shard_map.97._), channel_id=1, source_target_pairs={{8,0},{12,4},{0,8},{4,12},{9,1},{13,5},{1,9},{5,13},{10,2},{14,6},... | collective-permute-start | bytes 233480 | tf_op jit(solution)/shard_map/ppermute | solution.py:759
  10.1 12.4 %collective-permute-start.7 = (f32[464,128]{1,0:T(8,128)S(1)}, f32[464,128]{1,0:T(8,128)S(1)}, u32[]{:S(2)}, u32[]{:S(2)}) collective-permute-start(f32[464,128]{1,0:T(8,128)S(1)} %get-tuple-element.46), channel_id=1, source_target_pairs={{4,0},{0,4},{12,8},{8,12},{5,1},{1,5},{13,9},{9,13},{6,2},{2,6},{1... | collective-permute-start | bytes 712712 | tf_op jit(solution)/shard_map/ppermute | solution.py:768
  10.6 11.9 %collective-permute-start.8 = (f32[464,128]{1,0:T(8,128)S(1)}, f32[464,128]{1,0:T(8,128)S(1)}, u32[]{:S(2)}, u32[]{:S(2)}) collective-permute-start(f32[464,128]{1,0:T(8,128)S(1)} %get-tuple-element.47), channel_id=1, source_target_pairs={{0,0},{8,4},{4,8},{12,12},{1,1},{9,5},{5,9},{13,13},{2,2},{10,6},{... | collective-permute-start | bytes 712712 | tf_op jit(solution)/shard_map/ppermute | solution.py:768
  15.7 9.1 %collective-permute-start.5 = (f32[320,128]{1,0:T(8,128)S(1)}, f32[320,128]{1,0:T(8,128)S(1)}, u32[]{:S(2)}, u32[]{:S(2)}) collective-permute-start(f32[320,128]{1,0:T(8,128)S(1)} %get-tuple-element.43), channel_id=1, source_target_pairs={{4,0},{0,4},{12,8},{8,12},{5,1},{1,5},{13,9},{9,13},{6,2},{2,6},{1... | collective-permute-start | bytes 491528 | tf_op jit(solution)/shard_map/ppermute | solution.py:768
  17.9 7.5 %collective-permute-start.6 = (f32[320,128]{1,0:T(8,128)S(1)}, f32[320,128]{1,0:T(8,128)S(1)}, u32[]{:S(2)}, u32[]{:S(2)}) collective-permute-start(f32[320,128]{1,0:T(8,128)S(1)} %get-tuple-element.44), channel_id=1, source_target_pairs={{0,0},{8,4},{4,8},{12,12},{1,1},{9,5},{5,9},{13,13},{2,2},{10,6},{... | collective-permute-start | bytes 491528 | tf_op jit(solution)/shard_map/ppermute | solution.py:768

commit v24 on v21

--- a/solution.py
+++ b/solution.py
@@ -615,7 +615,7 @@
 
 
 def forward_kernel(
-    wave_ref, own_s_ref, late_ref, even, odd, coef_ref, coef_strip_ref, s_ref, ss_ref, hist_ref,
+    wave_ref, own_s_ref, late_ref, odd, even, coef_ref, coef_strip_ref, s_ref, ss_ref, hist_ref,
     adjoint_ref, grad_hbm, adjoint_hbm,
     p_ref, spread_ref, edge_ref, flux_ref, grad_ref, sems,
 ):
@@ -877,7 +877,7 @@
         forward_kernel,
         [shape(2, BX, BY, BZ), shape(4, BX, BY, BZ)],
         [
-            wave, own_s, own_late, wave_even, wave_odd, coef, coef_strip, src, src_strip, hist,
+            wave, own_s, own_late, wave_odd, wave_even, coef, coef_strip, src, src_strip, hist,
             adjoint_out,
         ],
         [pltpu.VMEM((EX, EY, BZ), F32)] * 2

time: 27.4 us -> 27.5 us (level)
  the two profiles are of different devices: /device:TPU:8 before, /device:TPU:0 now
where the time goes in v24:
time: 27.5 us; the launch traced here: 27.3 us
  starting transfers between devices  10.9 us (40%)
  Pallas kernels  8.55 us (31%)
  waiting for transfers between devices  7.15 us (26%)
  between operations  0.72 us (3%)
    pallas_call x9, Pallas kernels, call(): pl.pallas_call(kernel, out_shape=outs, in_specs=[pl.BlockSpec(memory_spac...  8.55 us
    ppermute x3, waiting for transfers between devices, rotated(): lax.ppermute(array, axis, [((i + offset) % count, i) for i in range(count)])  5.12 us
    ppermute x3, starting transfers between devices, rotated(): lax.ppermute(array, axis, [((i + offset) % count, i) for i in range(count)])  4.51 us
    ppermute x4, starting transfers between devices, paired(): return lax.ppermute(array, 'gx', pairs)  4.25 us
    ppermute x2, starting transfers between devices, from_sides(): both = lax.ppermute(sends[0], axes, route(1) + route(-1))  2.14 us
    ppermute x2, waiting for transfers between devices, from_sides(): both = lax.ppermute(sends[0], axes, route(1) + route(-1))  1.18 us
    ppermute x4, waiting for transfers between devices, paired(): return lax.ppermute(array, 'gx', pairs)  0.86 us
  transfers between devices with their start and end apart: 9, of which 3 were waited for; matrix products, arithmetic and copies ran while one was open for 0% of the time, Pallas kernels for 20%

profile of v24, /device:TPU:0, one launch (start us, length us, event | category | flops | bytes accessed | tf_op | source)
XLA Modules:
  0.0 27.3 jit_solution(8692686583001629115)
XLA Ops:
  0.6 1.3 %shard_map.95 = (f32[320,128]{1,0:T(8,128)S(1)}, f32[256,128]{1,0:T(8,128)S(1)}, f32[128,128]{1,0:T(8,128)S(1)}, f32[32,128]{1,0:T(8,128)S(1)}, f32[64,128]{1,0:...) custom-call(f32[4,4,32,128]{3,2,1,0:T(8,128)} %stored_hbm.1, ...), custom_call_target="tpu_custom_call" | custom-call | bytes 5166000 | tf_op jit(solution)/shard_map/pallas_call | solution.py:719
  2.0 4.1 %collective-permute-start = (f32[320,128]{1,0:T(8,128)S(1)}, f32[320,128]{1,0:T(8,128)S(1)}, u32[]{:S(2)}, u32[]{:S(2)}) collective-permute-start(f32[320,128]{1,0:T(8,128)S(1)} %get-tuple-element.33), channel_id=1, source_target_pairs={{8,0},{12,4},{0,8},{4,12},{9,1},{13,5},{1,9},{5,13},{10,2},{14,6},... | collective-permute-start | bytes 491528 | tf_op jit(solution)/shard_map/ppermute | solution.py:755
  6.1 1.5 %collective-permute-start.1 = (f32[160,128]{1,0:T(8,128)S(1)}, f32[160,128]{1,0:T(8,128)S(1)}, u32[]{:S(2)}, u32[]{:S(2)}) collective-permute-start(f32[160,128]{1,0:T(8,128)S(1)} %get-tuple-element.34), channel_id=1, source_target_pairs={{2,0},{0,2},{3,1},{1,3},{6,4},{4,6},{7,5},{5,7},{10,8},{8,10},{11,... | collective-permute-start | bytes 245768 | tf_op jit(solution)/shard_map/ppermute | solution.py:747
  7.5 0.0 collective-permute-start.3
  7.6 0.6 %collective-permute-start.2 = (f32[16,128]{1,0:T(8,128)S(1)}, f32[16,128]{1,0:T(8,128)S(1)}, u32[]{:S(2)}, u32[]{:S(2)}) collective-permute-start(f32[16,128]{1,0:T(8,128)S(1)} %get-tuple-element.35), channel_id=1, source_target_pairs={{2,1},{3,0},{0,3},{1,2},{6,5},{7,4},{4,7},{5,6},{10,9},{11,8},{8,1... | collective-permute-start | bytes 24584 | tf_op jit(solution)/shard_map/ppermute | solution.py:747
  8.2 1.2 %shard_map.96 = (f32[2,480,128]{2,1,0:T(8,128)S(1)}, f32[2,40,128]{2,1,0:T(8,128)S(1)}) custom-call(s32[3,1024]{1,0:T(4,128)S(1)} %get-tuple-element.40.receivers, f32[4,1024]{1,0:T(4,128)S(1)} %get-tuple-element.41.receiver_wave), custom_call_target="tpu_custom_call" | custom-call | bytes 4428000 | tf_op jit(solution)/shard_map/pallas_call | solution.py:719
  9.5 1.2 %collective-permute-done.2.corner_up.corner_down = f32[16,128]{1,0:T(8,128)S(1)} collective-permute-done((f32[16,128]{1,0:T(8,128)S(1)}, f32[16,128]{1,0:T(8,128)S(1)}, u32[]{:S(2)}, u32[]{:S(2)}) %collective-permute-start.2) | collective-permute-done | bytes 8224 | tf_op jit(solution)/shard_map/ppermute | solution.py:747
  10.6 0.0 collective-permute-done.3.other_ref
  10.6 0.0 collective-permute-done.1.from_up.from_down
  10.6 0.3 shard_map.97
  10.9 0.4 %collective-permute-start.4 = (f32[152,128]{1,0:T(8,128)S(1)}, f32[152,128]{1,0:T(8,128)S(1)}, u32[]{:S(2)}, u32[]{:S(2)}) collective-permute-start(f32[152,128]{1,0:T(8,128)S(1)} %get-tuple-element.43), channel_id=1, source_target_pairs={{8,0},{12,4},{0,8},{4,12},{9,1},{13,5},{1,9},{5,13},{10,2},{14,6},... | collective-permute-start | bytes 233480 | tf_op jit(solution)/shard_map/ppermute | solution.py:755
  11.3 1.6 %collective-permute-start.7 = (f32[464,128]{1,0:T(8,128)S(1)}, f32[464,128]{1,0:T(8,128)S(1)}, u32[]{:S(2)}, u32[]{:S(2)}) collective-permute-start(f32[464,128]{1,0:T(8,128)S(1)} %get-tuple-element.50), channel_id=1, source_target_pairs={{4,0},{0,4},{12,8},{8,12},{5,1},{1,5},{13,9},{9,13},{6,2},{2,6},{1... | collective-permute-start | bytes 712712 | tf_op jit(solution)/shard_map/ppermute | solution.py:764
  13.0 0.7 %collective-permute-start.8 = (f32[464,128]{1,0:T(8,128)S(1)}, f32[464,128]{1,0:T(8,128)S(1)}, u32[]{:S(2)}, u32[]{:S(2)}) collective-permute-start(f32[464,128]{1,0:T(8,128)S(1)} %get-tuple-element.51), channel_id=1, source_target_pairs={{0,0},{8,4},{4,8},{12,12},{1,1},{9,5},{5,9},{13,13},{2,2},{10,6},{... | collective-permute-start | bytes 712712 | tf_op jit(solution)/shard_map/ppermute | solution.py:764
  13.7 5.1 %collective-permute-done.4.late_ref = f32[152,128]{1,0:T(8,128)S(1)} collective-permute-done((f32[152,128]{1,0:T(8,128)S(1)}, f32[152,128]{1,0:T(8,128)S(1)}, u32[]{:S(2)}, u32[]{:S(2)}) %collective-permute-start.4) | collective-permute-done | bytes 77856 | tf_op jit(solution)/shard_map/ppermute | solution.py:755
  18.8 0.0 collective-permute-done.wave_ref
  18.8 0.1 shard_map.98
  18.9 0.7 %collective-permute-start.5 = (f32[320,128]{1,0:T(8,128)S(1)}, f32[320,128]{1,0:T(8,128)S(1)}, u32[]{:S(2)}, u32[]{:S(2)}) collective-permute-start(f32[320,128]{1,0:T(8,128)S(1)} %get-tuple-element.46), channel_id=1, source_target_pairs={{0,0},{8,4},{4,8},{12,12},{1,1},{9,5},{5,9},{13,13},{2,2},{10,6},{... | collective-permute-start | bytes 491528 | tf_op jit(solution)/shard_map/ppermute | solution.py:764
  19.6 1.3 %collective-permute-start.6 = (f32[320,128]{1,0:T(8,128)S(1)}, f32[320,128]{1,0:T(8,128)S(1)}, u32[]{:S(2)}, u32[]{:S(2)}) collective-permute-start(f32[320,128]{1,0:T(8,128)S(1)} %get-tuple-element.47), channel_id=1, source_target_pairs={{4,0},{0,4},{12,8},{8,12},{5,1},{1,5},{13,9},{9,13},{6,2},{2,6},{1... | collective-permute-start | bytes 491528 | tf_op jit(solution)/shard_map/ppermute | solution.py:764
  20.8 1.0 %shard_map.100 = (f32[2,320,128]{2,1,0:T(8,128)S(1)}, f32[2,40,128]{2,1,0:T(8,128)S(1)}) custom-call(s32[3,1024]{1,0:T(4,128)S(1)} %get-tuple-element.40.receivers, f32[4,1024]{1,0:T(4,128)S(1)} %get-tuple-element.41.receiver_wave, f32[304,128]{1,0:T(8,128)S(1)} %get-tuple-element.49.adj_ref._.late_ref), custom_call_target="tpu_custom_call" | custom-call | bytes 3690000 | tf_op jit(solution)/shard_map/pallas_call | solution.py:719
  21.9 0.5 %shard_map.102 = (f32[3,400,128]{2,1,0:T(8,128)S(1)}, f32[3,40,128]{2,1,0:T(8,128)S(1)}) custom-call(s32[3,64]{1,0:T(4,128)S(1)} %get-tuple-element.58.sources, f32[4,64]{1,0:T(4,128)S(1)} %get-tuple-element.59.source_wave, f32[304,128]{1,0:T(8,128)S(1)} %get-tuple-element.49.adj_ref._.late_ref), custom_call_target="tpu_custom_call" | custom-call | bytes 1845000 | tf_op jit(solution)/shard_map/pallas_call | solution.py:719
  22.4 0.0 collective-permute-done.7.even
  22.4 0.0 collective-permute-done.8.odd
  22.4 2.2 %shard_map.101 = (f32[4,4,32,128]{3,2,1,0:T(8,128)S(1)}, f32[4,4,4,32,128]{4,3,2,1,0:T(8,128)S(1)}, f32[3,12,40,128]{3,2,1,0:T(8,128)S(1)}, f32[3,40,128]{2,1,0:T(8,128)S(1)}) custom-call(f32[256,128]{1,0:T(8,128)S(1)} %get-tuple-element.48.ql_ref, f32[304,128]{1,0:T(8,128)S(1)} %get-tuple-element.49.adj_ref._.late_ref, ...), custom_call_target="tpu_custom_call" | custom-call | bytes 14391000 | tf_op jit(solution)/shard_map/pallas_call | solution.py:719
  24.6 0.0 collective-permute-done.5.odd
  24.7 0.8 %collective-permute-done.6.even = f32[320,128]{1,0:T(8,128)S(1)} collective-permute-done((f32[320,128]{1,0:T(8,128)S(1)}, f32[320,128]{1,0:T(8,128)S(1)}, u32[]{:S(2)}, u32[]{:S(2)}) %collective-permute-start.6) | collective-permute-done | bytes 163872 | tf_op jit(solution)/shard_map/ppermute | solution.py:764
  25.5 1.8 %shard_map.103 = (f32[2,4,32,128]{3,2,1,0:T(8,128)}, f32[4,4,32,128]{3,2,1,0:T(8,128)}) custom-call(f32[320,128]{1,0:T(8,128)S(1)} %collective-permute-done.wave_ref, f32[128,128]{1,0:T(8,128)S(1)} %get-tuple-element.44.own_s_ref, f32[144,128]{1,0:T(8,128)S(1)} %get-tuple-element.45.late_ref, f32[320,128]{1,0:T(8,128)S(1)} %collective-permute-done.5.odd, ...), custom_call_target="tpu_custom_call" | custom-call | bytes 9225000 | tf_op jit(solution)/shard_map/pallas_call | solution.py:719
  (1 shorter events, 0.0 us)
Async XLA Ops:
  2.0 16.8 %collective-permute-start = (f32[320,128]{1,0:T(8,128)S(1)}, f32[320,128]{1,0:T(8,128)S(1)}, u32[]{:S(2)}, u32[]{:S(2)}) collective-permute-start(f32[320,128]{1,0:T(8,128)S(1)} %get-tuple-element.33), channel_id=1, source_target_pairs={{8,0},{12,4},{0,8},{4,12},{9,1},{13,5},{1,9},{5,13},{10,2},{14,6},... | collective-permute-start | bytes 491528 | tf_op jit(solution)/shard_map/ppermute | solution.py:755
  6.1 4.6 %collective-permute-start.1 = (f32[160,128]{1,0:T(8,128)S(1)}, f32[160,128]{1,0:T(8,128)S(1)}, u32[]{:S(2)}, u32[]{:S(2)}) collective-permute-start(f32[160,128]{1,0:T(8,128)S(1)} %get-tuple-element.34), channel_id=1, source_target_pairs={{2,0},{0,2},{3,1},{1,3},{6,4},{4,6},{7,5},{5,7},{10,8},{8,10},{11,... | collective-permute-start | bytes 245768 | tf_op jit(solution)/shard_map/ppermute | solution.py:747
  7.5 3.1 %collective-permute-start.3 = (f32[96,128]{1,0:T(8,128)S(1)}, f32[96,128]{1,0:T(8,128)S(1)}, u32[]{:S(2)}, u32[]{:S(2)}) collective-permute-start(f32[96,128]{1,0:T(8,128)S(1)} %get-tuple-element.36.strip_ref), channel_id=1, source_target_pairs={{1,0},{0,1},{3,2},{2,3},{5,4},{4,5},{7,6},{6,7},{9,8},{8,9},{11,10... | collective-permute-start | bytes 147464 | tf_op jit(solution)/shard_map/ppermute | solution.py:755
  7.6 3.1 %collective-permute-start.2 = (f32[16,128]{1,0:T(8,128)S(1)}, f32[16,128]{1,0:T(8,128)S(1)}, u32[]{:S(2)}, u32[]{:S(2)}) collective-permute-start(f32[16,128]{1,0:T(8,128)S(1)} %get-tuple-element.35), channel_id=1, source_target_pairs={{2,1},{3,0},{0,3},{1,2},{6,5},{7,4},{4,7},{5,6},{10,9},{11,8},{8,1... | collective-permute-start | bytes 24584 | tf_op jit(solution)/shard_map/ppermute | solution.py:747
  10.9 7.9 %collective-permute-start.4 = (f32[152,128]{1,0:T(8,128)S(1)}, f32[152,128]{1,0:T(8,128)S(1)}, u32[]{:S(2)}, u32[]{:S(2)}) collective-permute-start(f32[152,128]{1,0:T(8,128)S(1)} %get-tuple-element.43), channel_id=1, source_target_pairs={{8,0},{12,4},{0,8},{4,12},{9,1},{13,5},{1,9},{5,13},{10,2},{14,6},... | collective-permute-start | bytes 233480 | tf_op jit(solution)/shard_map/ppermute | solution.py:755
  11.3 11.1 %collective-permute-start.7 = (f32[464,128]{1,0:T(8,128)S(1)}, f32[464,128]{1,0:T(8,128)S(1)}, u32[]{:S(2)}, u32[]{:S(2)}) collective-permute-start(f32[464,128]{1,0:T(8,128)S(1)} %get-tuple-element.50), channel_id=1, source_target_pairs={{4,0},{0,4},{12,8},{8,12},{5,1},{1,5},{13,9},{9,13},{6,2},{2,6},{1... | collective-permute-start | bytes 712712 | tf_op jit(solution)/shard_map/ppermute | solution.py:764
  13.0 9.4 %collective-permute-start.8 = (f32[464,128]{1,0:T(8,128)S(1)}, f32[464,128]{1,0:T(8,128)S(1)}, u32[]{:S(2)}, u32[]{:S(2)}) collective-permute-start(f32[464,128]{1,0:T(8,128)S(1)} %get-tuple-element.51), channel_id=1, source_target_pairs={{0,0},{8,4},{4,8},{12,12},{1,1},{9,5},{5,9},{13,13},{2,2},{10,6},{... | collective-permute-start | bytes 712712 | tf_op jit(solution)/shard_map/ppermute | solution.py:764
  18.9 5.8 %collective-permute-start.5 = (f32[320,128]{1,0:T(8,128)S(1)}, f32[320,128]{1,0:T(8,128)S(1)}, u32[]{:S(2)}, u32[]{:S(2)}) collective-permute-start(f32[320,128]{1,0:T(8,128)S(1)} %get-tuple-element.46), channel_id=1, source_target_pairs={{0,0},{8,4},{4,8},{12,12},{1,1},{9,5},{5,9},{13,13},{2,2},{10,6},{... | collective-permute-start | bytes 491528 | tf_op jit(solution)/shard_map/ppermute | solution.py:764
  19.6 5.9 %collective-permute-start.6 = (f32[320,128]{1,0:T(8,128)S(1)}, f32[320,128]{1,0:T(8,128)S(1)}, u32[]{:S(2)}, u32[]{:S(2)}) collective-permute-start(f32[320,128]{1,0:T(8,128)S(1)} %get-tuple-element.47), channel_id=1, source_target_pairs={{4,0},{0,4},{12,8},{8,12},{5,1},{1,5},{13,9},{9,13},{6,2},{2,6},{1... | collective-permute-start | bytes 491528 | tf_op jit(solution)/shard_map/ppermute | solution.py:764

commit v25 on v21

--- a/solution.py
+++ b/solution.py
@@ -289,7 +289,7 @@
     return jnp.where((rows((8, BZ)) < MARGIN) == upper, tile, 0.0)
 
 
-def join_kernel(wave_ref, late_ref, s_ref, own_ref, even_ref, odd_ref):
+def join_kernel(wave_ref, late_ref, _, s_ref, own_ref, even_ref, odd_ref):
     planes_end, x_end, tiles_end = WAVE_OWN
     own_ref[planes_end:x_end] = wave_ref[2 * PLANES : 2 * PLANES + BY]
     for place in range((tiles_end - x_end) // 8):
@@ -850,9 +850,9 @@
         join_kernel,
         [shape(PLANES, BZ), shape(WAVE_OWN[2] + EY, BZ)]
         + [shape(WAVE_SIDE[1] + tile_rows(WAVE_TILES) + EY, BZ)] * 2,
-        [wave, late],
+        [wave, late, rsa],
         [],
-        "vv",
+        "vva",
     )
     wave_even, wave_odd = paired(wave_even, False), paired(wave_odd, True)
     adjoint_out, hist, coef, coef_strip = call(

time: 27.4 us -> 27.4 us (level)
  waiting for transfers between devices: 2.47 us -> 2.9 us
  starting transfers between devices: 15.5 us -> 15.1 us
    ppermute x4, waiting for transfers between devices: 0.69 us -> 1.72 us  [paired(): return lax.ppermute(array, 'gx', pairs)]
    ppermute x3, waiting for transfers between devices: 0.61 us -> 0.01 us  [rotated(): lax.ppermute(array, axis, [((i + offset) % count, i) for i in range(count)])]
    ppermute x4, starting transfers between devices: 10.3 us -> 9.86 us  [paired(): return lax.ppermute(array, 'gx', pairs)]
  transfers between devices with their start and end apart: 9 -> 9, of which waited for: 3 -> 2; matrix products, arithmetic and copies ran while one was open for 0% -> 0% of each run, Pallas kernels for 20% -> 20%
where the time goes in v25:
time: 27.4 us; the launch traced here: 27.2 us
  starting transfers between devices  15.1 us (55%)
  Pallas kernels  8.55 us (31%)
  waiting for transfers between devices  2.9 us (11%)
  between operations  0.73 us (3%)
    ppermute x4, starting transfers between devices, paired(): return lax.ppermute(array, 'gx', pairs)  9.86 us
    pallas_call x9, Pallas kernels, call(): pl.pallas_call(kernel, out_shape=outs, in_specs=[pl.BlockSpec(memory_spac...  8.55 us
    ppermute x3, starting transfers between devices, rotated(): lax.ppermute(array, axis, [((i + offset) % count, i) for i in range(count)])  3.06 us
    ppermute x2, starting transfers between devices, from_sides(): both = lax.ppermute(sends[0], axes, route(1) + route(-1))  2.14 us
    ppermute x4, waiting for transfers between devices, paired(): return lax.ppermute(array, 'gx', pairs)  1.72 us
    ppermute x2, waiting for transfers between devices, from_sides(): both = lax.ppermute(sends[0], axes, route(1) + route(-1))  1.18 us
  transfers between devices with their start and end apart: 9, of which 2 were waited for; matrix products, arithmetic and copies ran while one was open for 0% of the time, Pallas kernels for 20%

profile of v25, /device:TPU:8, one launch (start us, length us, event | category | flops | bytes accessed | tf_op | source)
XLA Modules:
  0.0 27.2 jit_solution(820162253148545420)
XLA Ops:
  0.6 1.3 %shard_map.95 = (f32[320,128]{1,0:T(8,128)S(1)}, f32[256,128]{1,0:T(8,128)S(1)}, f32[128,128]{1,0:T(8,128)S(1)}, f32[32,128]{1,0:T(8,128)S(1)}, f32[64,128]{1,0:...) custom-call(f32[4,4,32,128]{3,2,1,0:T(8,128)} %stored_hbm.1, ...), custom_call_target="tpu_custom_call" | custom-call | bytes 5166000 | tf_op jit(solution)/shard_map/pallas_call | solution.py:719
  2.0 2.7 %collective-permute-start = (f32[320,128]{1,0:T(8,128)S(1)}, f32[320,128]{1,0:T(8,128)S(1)}, u32[]{:S(2)}, u32[]{:S(2)}) collective-permute-start(f32[320,128]{1,0:T(8,128)S(1)} %get-tuple-element.33), channel_id=1, source_target_pairs={{8,0},{12,4},{0,8},{4,12},{9,1},{13,5},{1,9},{5,13},{10,2},{14,6},... | collective-permute-start | bytes 491528 | tf_op jit(solution)/shard_map/ppermute | solution.py:755
  4.6 1.5 %collective-permute-start.1 = (f32[160,128]{1,0:T(8,128)S(1)}, f32[160,128]{1,0:T(8,128)S(1)}, u32[]{:S(2)}, u32[]{:S(2)}) collective-permute-start(f32[160,128]{1,0:T(8,128)S(1)} %get-tuple-element.34), channel_id=1, source_target_pairs={{2,0},{0,2},{3,1},{1,3},{6,4},{4,6},{7,5},{5,7},{10,8},{8,10},{11,... | collective-permute-start | bytes 245768 | tf_op jit(solution)/shard_map/ppermute | solution.py:747
  6.1 0.0 collective-permute-start.3
  6.1 0.6 %collective-permute-start.2 = (f32[16,128]{1,0:T(8,128)S(1)}, f32[16,128]{1,0:T(8,128)S(1)}, u32[]{:S(2)}, u32[]{:S(2)}) collective-permute-start(f32[16,128]{1,0:T(8,128)S(1)} %get-tuple-element.35), channel_id=1, source_target_pairs={{2,1},{3,0},{0,3},{1,2},{6,5},{7,4},{4,7},{5,6},{10,9},{11,8},{8,1... | collective-permute-start | bytes 24584 | tf_op jit(solution)/shard_map/ppermute | solution.py:747
  6.8 1.2 %shard_map.96 = (f32[2,480,128]{2,1,0:T(8,128)S(1)}, f32[2,40,128]{2,1,0:T(8,128)S(1)}) custom-call(s32[3,1024]{1,0:T(4,128)S(1)} %get-tuple-element.40.receivers, f32[4,1024]{1,0:T(4,128)S(1)} %get-tuple-element.41.receiver_wave), custom_call_target="tpu_custom_call" | custom-call | bytes 4428000 | tf_op jit(solution)/shard_map/pallas_call | solution.py:719
  8.0 1.2 %collective-permute-done.2.corner_up.corner_down = f32[16,128]{1,0:T(8,128)S(1)} collective-permute-done((f32[16,128]{1,0:T(8,128)S(1)}, f32[16,128]{1,0:T(8,128)S(1)}, u32[]{:S(2)}, u32[]{:S(2)}) %collective-permute-start.2) | collective-permute-done | bytes 8224 | tf_op jit(solution)/shard_map/ppermute | solution.py:747
  9.2 0.0 collective-permute-done.3.other_ref
  9.2 0.0 collective-permute-done.1.from_up.from_down
  9.2 0.3 shard_map.97
  9.5 0.4 %collective-permute-start.4 = (f32[152,128]{1,0:T(8,128)S(1)}, f32[152,128]{1,0:T(8,128)S(1)}, u32[]{:S(2)}, u32[]{:S(2)}) collective-permute-start(f32[152,128]{1,0:T(8,128)S(1)} %get-tuple-element.43), channel_id=1, source_target_pairs={{8,0},{12,4},{0,8},{4,12},{9,1},{13,5},{1,9},{5,13},{10,2},{14,6},... | collective-permute-start | bytes 233480 | tf_op jit(solution)/shard_map/ppermute | solution.py:755
  9.9 0.5 %collective-permute-start.7 = (f32[464,128]{1,0:T(8,128)S(1)}, f32[464,128]{1,0:T(8,128)S(1)}, u32[]{:S(2)}, u32[]{:S(2)}) collective-permute-start(f32[464,128]{1,0:T(8,128)S(1)} %get-tuple-element.51), channel_id=1, source_target_pairs={{4,0},{0,4},{12,8},{8,12},{5,1},{1,5},{13,9},{9,13},{6,2},{2,6},{1... | collective-permute-start | bytes 712712 | tf_op jit(solution)/shard_map/ppermute | solution.py:764
  10.4 4.6 %collective-permute-start.8 = (f32[464,128]{1,0:T(8,128)S(1)}, f32[464,128]{1,0:T(8,128)S(1)}, u32[]{:S(2)}, u32[]{:S(2)}) collective-permute-start(f32[464,128]{1,0:T(8,128)S(1)} %get-tuple-element.52), channel_id=1, source_target_pairs={{0,0},{8,4},{4,8},{12,12},{1,1},{9,5},{5,9},{13,13},{2,2},{10,6},{... | collective-permute-start | bytes 712712 | tf_op jit(solution)/shard_map/ppermute | solution.py:764
  15.0 1.0 %shard_map.98 = (f32[2,320,128]{2,1,0:T(8,128)S(1)}, f32[2,40,128]{2,1,0:T(8,128)S(1)}) custom-call(s32[3,1024]{1,0:T(4,128)S(1)} %get-tuple-element.40.receivers, f32[4,1024]{1,0:T(4,128)S(1)} %get-tuple-element.41.receiver_wave, f32[304,128]{1,0:T(8,128)S(1)} %get-tuple-element.44._.adj_ref.late_ref), custom_call_target="tpu_custom_call" | custom-call | bytes 3690000 | tf_op jit(solution)/shard_map/pallas_call | solution.py:719
  16.0 0.0 collective-permute-done.4.late_ref
  16.1 0.0 collective-permute-done.wave_ref
  16.1 0.1 shard_map.99
  16.2 1.8 %collective-permute-start.5 = (f32[320,128]{1,0:T(8,128)S(1)}, f32[320,128]{1,0:T(8,128)S(1)}, u32[]{:S(2)}, u32[]{:S(2)}) collective-permute-start(f32[320,128]{1,0:T(8,128)S(1)} %get-tuple-element.48), channel_id=1, source_target_pairs={{4,0},{0,4},{12,8},{8,12},{5,1},{1,5},{13,9},{9,13},{6,2},{2,6},{1... | collective-permute-start | bytes 491528 | tf_op jit(solution)/shard_map/ppermute | solution.py:764
  17.9 3.0 %collective-permute-start.6 = (f32[320,128]{1,0:T(8,128)S(1)}, f32[320,128]{1,0:T(8,128)S(1)}, u32[]{:S(2)}, u32[]{:S(2)}) collective-permute-start(f32[320,128]{1,0:T(8,128)S(1)} %get-tuple-element.49), channel_id=1, source_target_pairs={{0,0},{8,4},{4,8},{12,12},{1,1},{9,5},{5,9},{13,13},{2,2},{10,6},{... | collective-permute-start | bytes 491528 | tf_op jit(solution)/shard_map/ppermute | solution.py:764
  20.9 0.5 %shard_map.102 = (f32[3,400,128]{2,1,0:T(8,128)S(1)}, f32[3,40,128]{2,1,0:T(8,128)S(1)}) custom-call(s32[3,64]{1,0:T(4,128)S(1)} %get-tuple-element.58.sources, f32[4,64]{1,0:T(4,128)S(1)} %get-tuple-element.59.source_wave, f32[304,128]{1,0:T(8,128)S(1)} %get-tuple-element.44._.adj_ref.late_ref), custom_call_target="tpu_custom_call" | custom-call | bytes 1845000 | tf_op jit(solution)/shard_map/pallas_call | solution.py:719
  21.5 0.0 collective-permute-done.7.even
  21.5 0.0 collective-permute-done.8.odd
  21.5 2.2 %shard_map.101 = (f32[4,4,32,128]{3,2,1,0:T(8,128)S(1)}, f32[4,4,4,32,128]{4,3,2,1,0:T(8,128)S(1)}, f32[3,12,40,128]{3,2,1,0:T(8,128)S(1)}, f32[3,40,128]{2,1,0:T(8,128)S(1)}) custom-call(f32[256,128]{1,0:T(8,128)S(1)} %get-tuple-element.50.ql_ref, f32[304,128]{1,0:T(8,128)S(1)} %get-tuple-element.44._.adj_ref.late_ref, ...), custom_call_target="tpu_custom_call" | custom-call | bytes 14391000 | tf_op jit(solution)/shard_map/pallas_call | solution.py:719
  23.7 0.0 collective-permute-done.5.even
  23.7 1.7 %collective-permute-done.6.odd = f32[320,128]{1,0:T(8,128)S(1)} collective-permute-done((f32[320,128]{1,0:T(8,128)S(1)}, f32[320,128]{1,0:T(8,128)S(1)}, u32[]{:S(2)}, u32[]{:S(2)}) %collective-permute-start.6) | collective-permute-done | bytes 163872 | tf_op jit(solution)/shard_map/ppermute | solution.py:764
  25.4 1.8 %shard_map.103 = (f32[2,4,32,128]{3,2,1,0:T(8,128)}, f32[4,4,32,128]{3,2,1,0:T(8,128)}) custom-call(f32[320,128]{1,0:T(8,128)S(1)} %collective-permute-done.wave_ref, f32[128,128]{1,0:T(8,128)S(1)} %get-tuple-element.46.own_s_ref, f32[144,128]{1,0:T(8,128)S(1)} %get-tuple-element.47.late_ref, f32[320,128]{1,0:T(8,128)S(1)} %collective-permute-done.5.even, ...), custom_call_target="tpu_custom_call" | custom-call | bytes 9225000 | tf_op jit(solution)/shard_map/pallas_call | solution.py:719
  (1 shorter events, 0.0 us)
Async XLA Ops:
  2.0 14.1 %collective-permute-start = (f32[320,128]{1,0:T(8,128)S(1)}, f32[320,128]{1,0:T(8,128)S(1)}, u32[]{:S(2)}, u32[]{:S(2)}) collective-permute-start(f32[320,128]{1,0:T(8,128)S(1)} %get-tuple-element.33), channel_id=1, source_target_pairs={{8,0},{12,4},{0,8},{4,12},{9,1},{13,5},{1,9},{5,13},{10,2},{14,6},... | collective-permute-start | bytes 491528 | tf_op jit(solution)/shard_map/ppermute | solution.py:755
  4.6 4.6 %collective-permute-start.1 = (f32[160,128]{1,0:T(8,128)S(1)}, f32[160,128]{1,0:T(8,128)S(1)}, u32[]{:S(2)}, u32[]{:S(2)}) collective-permute-start(f32[160,128]{1,0:T(8,128)S(1)} %get-tuple-element.34), channel_id=1, source_target_pairs={{2,0},{0,2},{3,1},{1,3},{6,4},{4,6},{7,5},{5,7},{10,8},{8,10},{11,... | collective-permute-start | bytes 245768 | tf_op jit(solution)/shard_map/ppermute | solution.py:747
  6.1 3.1 %collective-permute-start.3 = (f32[96,128]{1,0:T(8,128)S(1)}, f32[96,128]{1,0:T(8,128)S(1)}, u32[]{:S(2)}, u32[]{:S(2)}) collective-permute-start(f32[96,128]{1,0:T(8,128)S(1)} %get-tuple-element.36.strip_ref), channel_id=1, source_target_pairs={{1,0},{0,1},{3,2},{2,3},{5,4},{4,5},{7,6},{6,7},{9,8},{8,9},{11,10... | collective-permute-start | bytes 147464 | tf_op jit(solution)/shard_map/ppermute | solution.py:755
  6.1 3.1 %collective-permute-start.2 = (f32[16,128]{1,0:T(8,128)S(1)}, f32[16,128]{1,0:T(8,128)S(1)}, u32[]{:S(2)}, u32[]{:S(2)}) collective-permute-start(f32[16,128]{1,0:T(8,128)S(1)} %get-tuple-element.35), channel_id=1, source_target_pairs={{2,1},{3,0},{0,3},{1,2},{6,5},{7,4},{4,7},{5,6},{10,9},{11,8},{8,1... | collective-permute-start | bytes 24584 | tf_op jit(solution)/shard_map/ppermute | solution.py:747
  9.5 6.6 %collective-permute-start.4 = (f32[152,128]{1,0:T(8,128)S(1)}, f32[152,128]{1,0:T(8,128)S(1)}, u32[]{:S(2)}, u32[]{:S(2)}) collective-permute-start(f32[152,128]{1,0:T(8,128)S(1)} %get-tuple-element.43), channel_id=1, source_target_pairs={{8,0},{12,4},{0,8},{4,12},{9,1},{13,5},{1,9},{5,13},{10,2},{14,6},... | collective-permute-start | bytes 233480 | tf_op jit(solution)/shard_map/ppermute | solution.py:755
  9.9 11.6 %collective-permute-start.7 = (f32[464,128]{1,0:T(8,128)S(1)}, f32[464,128]{1,0:T(8,128)S(1)}, u32[]{:S(2)}, u32[]{:S(2)}) collective-permute-start(f32[464,128]{1,0:T(8,128)S(1)} %get-tuple-element.51), channel_id=1, source_target_pairs={{4,0},{0,4},{12,8},{8,12},{5,1},{1,5},{13,9},{9,13},{6,2},{2,6},{1... | collective-permute-start | bytes 712712 | tf_op jit(solution)/shard_map/ppermute | solution.py:764
  10.4 11.1 %collective-permute-start.8 = (f32[464,128]{1,0:T(8,128)S(1)}, f32[464,128]{1,0:T(8,128)S(1)}, u32[]{:S(2)}, u32[]{:S(2)}) collective-permute-start(f32[464,128]{1,0:T(8,128)S(1)} %get-tuple-element.52), channel_id=1, source_target_pairs={{0,0},{8,4},{4,8},{12,12},{1,1},{9,5},{5,9},{13,13},{2,2},{10,6},{... | collective-permute-start | bytes 712712 | tf_op jit(solution)/shard_map/ppermute | solution.py:764
  16.2 7.5 %collective-permute-start.5 = (f32[320,128]{1,0:T(8,128)S(1)}, f32[320,128]{1,0:T(8,128)S(1)}, u32[]{:S(2)}, u32[]{:S(2)}) collective-permute-start(f32[320,128]{1,0:T(8,128)S(1)} %get-tuple-element.48), channel_id=1, source_target_pairs={{4,0},{0,4},{12,8},{8,12},{5,1},{1,5},{13,9},{9,13},{6,2},{2,6},{1... | collective-permute-start | bytes 491528 | tf_op jit(solution)/shard_map/ppermute | solution.py:764
  17.9 7.5 %collective-permute-start.6 = (f32[320,128]{1,0:T(8,128)S(1)}, f32[320,128]{1,0:T(8,128)S(1)}, u32[]{:S(2)}, u32[]{:S(2)}) collective-permute-start(f32[320,128]{1,0:T(8,128)S(1)} %get-tuple-element.49), channel_id=1, source_target_pairs={{0,0},{8,4},{4,8},{12,12},{1,1},{9,5},{5,9},{13,13},{2,2},{10,6},{... | collective-permute-start | bytes 491528 | tf_op jit(solution)/shard_map/ppermute | solution.py:764
